TPU v7x, 32 devices: a whole 2x2x4 slice. The times are simulated.
32 devices in a mesh: ctx: 4 (over z), fsdp: 8 (over y, x, core).
Axes of the slice: x: 2, y: 2, z: 4, core: 2. Of those that a mesh axis runs over, the one named last changes fastest.
Arguments:
- inputs: float32 [8, 1024, 2048], P('fsdp', 'ctx'), may hold values from -6 to 6
- out_grad: float32 [8, 1024, 2048], P('fsdp', 'ctx'), may hold values from -6 to 6
- block_order: int32 [8, 8], P('fsdp'), may hold values from 0 to 7, each once within a row
- ln_gain: float32 [2048], replicated, may hold values from 0.5 to 1.5
- ln_beta: float32 [2048], replicated, may hold values from -2 to 2
- w_in: bfloat16 [2048, 14336], P('fsdp'), may hold values from -0.125 to 0.125
- b_in: float32 [14336], replicated, may hold values from -2 to 2
- w_out: bfloat16 [10240, 2048], P('fsdp'), may hold values from -0.125 to 0.125
- b_out: float32 [2048], replicated, may hold values from -2 to 2
Outputs:
- out_y: float32 [8, 1024, 2048], P('fsdp', 'ctx')
- d_input: float32 [8, 1024, 2048], P('fsdp', 'ctx')
- g_w_in: float32 [2048, 14336], P('fsdp')
- g_b_in: float32 [14336], P('fsdp')
- g_w_out: float32 [10240, 2048], P('fsdp')
- g_b_out: float32 [2048], P('fsdp')
- g_gain: float32 [2048], P('fsdp')
- g_beta: float32 [2048], P('fsdp')
Inputs may be any that keep to these rules, and one draw needn't show every extreme that they name: Each row of block_order names every block of a sequence once; stored slot j of a sequence holds positions block_order[j] * 128 to block_order[j] * 128 + 127.
All inputs are finite; a program needn't handle non-finite values.
Results may differ from a plain program's by a relative error of at most 0.0059.
Values may be sent and summed in bfloat16 or wider, within the bound.
No kernel may reach another device: no remote copies, remote signals or barrier semaphores. Data moves between devices by JAX's collectives and lax.ppermute only.
A program may use at most 704 MiB of HBM per device.

v0:
```python
import math

import jax
import jax.numpy as jnp
from jax import lax
from jax.sharding import PartitionSpec as P

D = 2048
HEADS = 32
HEAD_DIM = 64
ROT_DIM = 32


LN_EPS = 1e-05
NEG_BIG = -1e30
ROPE_BASE = 10000.0


def row_positions(blk_order, first_row, row_count, blk_size):
    row_index = first_row + jnp.arange(row_count, dtype=jnp.int32)
    slot_ids = row_index // blk_size
    table = (slot_ids[:, None] == jnp.arange(blk_order.shape[0], dtype=jnp.int32)[None, :]).astype(
        jnp.int32
    )
    picked = jnp.sum(table * blk_order[None, :], axis=1, dtype=jnp.int32)
    return picked * blk_size + row_index % blk_size


def rotary_tables(positions):
    half_rot = ROT_DIM // 2
    expon = jnp.arange(half_rot, dtype=jnp.float32) * (2.0 / ROT_DIM)
    freqs = ROPE_BASE ** (-expon)
    angles = positions.astype(jnp.float32)[:, None] * freqs[None, :]
    return (jnp.cos(angles)[:, None, :], jnp.sin(angles)[:, None, :])


def rotate(values, cosine, sine):
    half_rot = ROT_DIM // 2
    first = values[..., :half_rot]
    second = values[..., half_rot:ROT_DIM]
    return jnp.concatenate(
        [first * cosine - second * sine, second * cosine + first * sine, values[..., ROT_DIM:]],
        axis=-1,
    )


def rotate_back(grads, cosine, sine):
    half_rot = ROT_DIM // 2
    first = grads[..., :half_rot]
    second = grads[..., half_rot:ROT_DIM]
    return jnp.concatenate(
        [first * cosine + second * sine, second * cosine - first * sine, grads[..., ROT_DIM:]],
        axis=-1,
    )


def gelu_tanh(values):
    return jax.nn.gelu(values, approximate=True)


def contract_cols(left, right):
    return lax.dot_general(
        left, right, (((1,), (1,)), ((), ())), preferred_element_type=jnp.float32
    )


def contract_rows(left, right):
    return lax.dot_general(
        left, right, (((0,), (0,)), ((), ())), preferred_element_type=jnp.float32
    )


def shards(inputs, out_grad, block_order, ln_gain, ln_beta, w_in, b_in, w_out, b_out):
    seq_in = inputs[0]
    seq_grad = out_grad[0]
    blk_order = block_order[0]
    tok_rows = seq_in.shape[0]
    blk_size = tok_rows // 2
    seq_len = tok_rows * lax.axis_size("ctx")
    scale_val = 1.0 / math.sqrt(HEAD_DIM)
    positions = row_positions(blk_order, lax.axis_index("ctx") * tok_rows, tok_rows, blk_size)
    centred = seq_in - jnp.mean(seq_in, axis=1, keepdims=True)
    inv_std = lax.rsqrt(jnp.mean(centred * centred, axis=1, keepdims=True) + LN_EPS)
    x_hat = centred * inv_std
    normed = (x_hat * ln_gain + ln_beta).astype(jnp.bfloat16)
    columns = normed
    project = jnp.dot(
        columns,
        lax.all_gather(w_in, "fsdp", axis=0, tiled=True),
        preferred_element_type=jnp.float32,
    )
    project = project + b_in
    cosine, sine = rotary_tables(positions)
    query_b = rotate(project[:, :D].reshape(tok_rows, HEADS, HEAD_DIM), cosine, sine).astype(
        jnp.bfloat16
    )
    key_b = (
        rotate(project[:, D : 2 * D].reshape(tok_rows, HEADS, HEAD_DIM), cosine, sine)
        .astype(jnp.bfloat16)
        .reshape(tok_rows, D)
    )
    value_b = project[:, 2 * D : 3 * D].astype(jnp.bfloat16)
    pre_act = project[:, 3 * D :]
    act_b = gelu_tanh(pre_act).astype(jnp.bfloat16)
    all_keys, all_vals = (
        lax.all_gather(key_b, "ctx", axis=0, tiled=True),
        lax.all_gather(value_b, "ctx", axis=0, tiled=True),
    )
    size = math.gcd(seq_len, 512)
    nblk = seq_len // size
    key_stack = all_keys.reshape(nblk, size, HEADS, HEAD_DIM)
    val_stack = all_vals.reshape(nblk, size, HEADS, HEAD_DIM)
    blk_ids = jnp.arange(nblk, dtype=jnp.int32)

    def masked_scores(key_blk, blk_index):
        key_pos = row_positions(blk_order, blk_index * size, size, blk_size)
        allowed = key_pos[None, None, :] <= positions[None, :, None]
        scores = (
            jnp.einsum("thd,ghd->htg", query_b, key_blk, preferred_element_type=jnp.float32)
            * scale_val
        )
        return (allowed, jnp.where(allowed, scores, NEG_BIG))

    def total_block(state, items):
        top_val, weight_sum = state
        key_blk, blk_index = items
        allowed, scores = masked_scores(key_blk, blk_index)
        new_top = jnp.maximum(top_val, jnp.max(scores, axis=2))
        terms = jnp.where(allowed, jnp.exp(scores - new_top[:, :, None]), 0.0)
        weight_sum = weight_sum * jnp.exp(top_val - new_top) + jnp.sum(terms, axis=2)
        return ((new_top, weight_sum), None)

    start_state = (
        jnp.full((HEADS, tok_rows), NEG_BIG, jnp.float32),
        jnp.zeros((HEADS, tok_rows), jnp.float32),
    )
    (top_val, weight_sum), _ = lax.scan(total_block, start_state, (key_stack, blk_ids))
    log_sums = top_val + jnp.log(weight_sum)

    def value_block(accum, items):
        key_blk, val_blk, blk_index = items
        allowed, scores = masked_scores(key_blk, blk_index)
        probs = jnp.where(allowed, jnp.exp(scores - log_sums[:, :, None]), 0.0).astype(jnp.bfloat16)
        return (
            accum + jnp.einsum("htg,ghd->thd", probs, val_blk, preferred_element_type=jnp.float32),
            None,
        )

    zero_query = jnp.zeros((tok_rows, HEADS, HEAD_DIM), jnp.float32)
    accum, _ = lax.scan(value_block, zero_query, (key_stack, val_stack, blk_ids))
    att_b = accum.reshape(tok_rows, D).astype(jnp.bfloat16)
    cat_b = jnp.concatenate([att_b, act_b], axis=1)
    columns = cat_b
    mixed = jnp.dot(
        columns,
        lax.all_gather(w_out, "fsdp", axis=0, tiled=True),
        preferred_element_type=jnp.float32,
    )
    out_y = seq_in + mixed + b_out
    dy_b = seq_grad.astype(jnp.bfloat16)
    d_cat = contract_cols(dy_b, lax.all_gather(w_out, "fsdp", axis=0, tiled=True))
    g_w_out = lax.psum_scatter(contract_rows(cat_b, dy_b), "fsdp", scatter_dimension=0, tiled=True)
    g_b_out = jnp.sum(seq_grad, axis=0)
    d_att = d_cat[:, :D].astype(jnp.bfloat16).reshape(tok_rows, HEADS, HEAD_DIM)
    d_pre = jax.vjp(gelu_tanh, pre_act)[1](d_cat[:, D:])[0]
    att_f = att_b.astype(jnp.float32).reshape(tok_rows, HEADS, HEAD_DIM)
    delta = jnp.sum(d_att.astype(jnp.float32) * att_f, axis=2).T

    def block_terms(key_blk, val_blk, blk_index):
        allowed, scores = masked_scores(key_blk, blk_index)
        probs = jnp.where(allowed, jnp.exp(scores - log_sums[:, :, None]), 0.0)
        d_prob = jnp.einsum("thd,ghd->htg", d_att, val_blk, preferred_element_type=jnp.float32)
        d_score = (probs * (d_prob - delta[:, :, None]) * scale_val).astype(jnp.bfloat16)
        return (probs, d_score)

    def back_block(d_query, items):
        key_blk, val_blk, blk_index = items
        probs, d_score = block_terms(key_blk, val_blk, blk_index)
        d_val = jnp.einsum(
            "htg,thd->ghd", probs.astype(jnp.bfloat16), d_att, preferred_element_type=jnp.float32
        )
        d_query = d_query + jnp.einsum(
            "htg,ghd->thd", d_score, key_blk, preferred_element_type=jnp.float32
        )
        d_key = jnp.einsum("htg,thd->ghd", d_score, query_b, preferred_element_type=jnp.float32)
        return (d_query, (d_key.reshape(size, D), d_val.reshape(size, D)))

    d_query, (d_keys, d_vals) = lax.scan(back_block, zero_query, (key_stack, val_stack, blk_ids))
    own_keys, own_vals = (
        lax.psum_scatter(d_keys.reshape(seq_len, D), "ctx", scatter_dimension=0, tiled=True),
        lax.psum_scatter(d_vals.reshape(seq_len, D), "ctx", scatter_dimension=0, tiled=True),
    )
    dq_rot = rotate_back(d_query, cosine, sine).reshape(tok_rows, D)
    dk_rot = rotate_back(own_keys.reshape(tok_rows, HEADS, HEAD_DIM), cosine, sine).reshape(
        tok_rows, D
    )
    d_proj = jnp.concatenate([dq_rot, dk_rot, own_vals, d_pre], axis=1)
    g_b_in = jnp.sum(d_proj, axis=0)
    d_proj_b = d_proj.astype(jnp.bfloat16)
    g_w_in = lax.psum_scatter(
        contract_rows(normed, d_proj_b), "fsdp", scatter_dimension=0, tiled=True
    )
    d_norm = contract_cols(d_proj_b, lax.all_gather(w_in, "fsdp", axis=0, tiled=True))
    g_gain = jnp.sum(d_norm * x_hat, axis=0)
    g_beta = jnp.sum(d_norm, axis=0)
    gain_grad = d_norm * ln_gain
    d_input = seq_grad + inv_std * (
        gain_grad
        - jnp.mean(gain_grad, axis=1, keepdims=True)
        - x_hat * jnp.mean(gain_grad * x_hat, axis=1, keepdims=True)
    )
    g_w_in, g_w_out = lax.psum((g_w_in, g_w_out), "ctx")
    g_b_in, g_b_out, g_gain, g_beta = lax.psum((g_b_in, g_b_out, g_gain, g_beta), ("ctx", "fsdp"))
    shard_idx = lax.axis_index("fsdp")
    shard_count = lax.axis_size("fsdp")

    def own_part(vector):
        length_part = vector.shape[0] // shard_count
        return lax.dynamic_slice_in_dim(vector, shard_idx * length_part, length_part, 0)

    return (
        out_y[None],
        d_input[None],
        g_w_in,
        own_part(g_b_in),
        g_w_out,
        own_part(g_b_out),
        own_part(g_gain),
        own_part(g_beta),
    )


def solution(mesh):
    placed = (
        P("fsdp", "ctx", None),
        P("fsdp", "ctx", None),
        P("fsdp", None),
        P(),
        P(),
        P("fsdp", None),
        P(),
        P("fsdp", None),
        P(),
    )
    return jax.shard_map(
        shards,
        mesh=mesh,
        in_specs=placed,
        out_specs=(
            P("fsdp", "ctx", None),
            P("fsdp", "ctx", None),
            P("fsdp", None),
            P("fsdp"),
            P("fsdp", None),
            P("fsdp"),
            P("fsdp"),
            P("fsdp"),
        ),
        check_vma=False,
    )
```

profile of v0, /device:TPU:0, one launch (start us, length us, event | category | flops | bytes accessed | tf_op | source)
XLA Modules:
  0.0 3255.5 jit_solution(17638470050309141789)
XLA Ops:
  9.3 270.7 %all-gather.5.cloned.1.call-done = bf16[2048,14336]{1,0:T(8,128)(2,1)} async-done(((bf16[256,14336]{1,0:T(8,128)(2,1)}), bf16[2048,14336]{1,0:T(8,128)(2,1)}) %all-gather.5.cloned.1.call-update) | async-done | bytes 58720272 | tf_op jit(solution)/shard_map/all_gather | solution.py:89
  280.1 32.4 convolution_add_fusion
  329.8 149.3 %all-gather.11.cloned.1.call-done = bf16[10240,2048]{1,0:T(8,128)(2,1)} async-done(((bf16[1280,2048]{1,0:T(8,128)(2,1)}), bf16[10240,2048]{1,0:T(8,128)(2,1)}) %all-gather.11.cloned.1.call-update) | async-done | bytes 41943056 | tf_op jit(solution)/shard_map/all_gather | solution.py:156
  479.1 21.3 fusion.92
  506.0 55.5 %all-gather.7.cloned.1.call-done = bf16[1024,2048]{1,0:T(8,128)(2,1)} async-done(((bf16[256,2048]{1,0:T(8,128)(2,1)}), bf16[1024,2048]{1,0:T(8,128)(2,1)}) %all-gather.7.cloned.1.call-update) | async-done | bytes 4194320 | tf_op jit(solution)/shard_map/all_gather | solution.py:107
  561.5 12.9 reshape.389
  574.4 9.8 copy.83
  584.2 57.8 %all-gather.9.cloned.1.call-done = bf16[1024,2048]{0,1:T(8,128)(2,1)} async-done(((bf16[256,2048]{0,1:T(8,128)(2,1)}), bf16[1024,2048]{0,1:T(8,128)(2,1)}) %all-gather.9.cloned.1.call-update) | async-done | bytes 4194320 | tf_op jit(solution)/shard_map/all_gather | solution.py:106
  642.0 7.9 reshape.380
  655.0 39.4 %while.45 = (s32[]{:T(128)}, f32[32,256]{1,0:T(8,128)S(1)}, f32[32,256]{1,0:T(8,128)S(1)}, s32[2]{0:T(128)S(1)}, s32[1,8]{1,0:T(1,128)S(1)}, /*index=5*/s32[256]...) while((s32[]{:T(128)}, f32[32,256]{1,0:T(8,128)S(1)}, ...), condition=%wide.region_7.8_spmd.clone, body=%wide.region_3.7_spmd.clone.sunk | while | flops 570624512 | bytes 37532864 | solution.py:137
  656.5 10.0 fusion.146
  666.5 8.1 select_reduce_fusion.10
  676.2 10.0 fusion.146
  686.3 8.1 select_reduce_fusion.10
  694.5 35.5 %while.46 = (s32[]{:T(128)}, f32[256,32,64]{0,2,1:T(8,128)}, bf16[2,512,32,64]{1,3,2,0:T(8,128)(2,1)}, s32[2]{0:T(128)S(1)}, s32[1,8]{1,0:T(1,128)S(1)}, /*index...) while((s32[]{:T(128)}, f32[256,32,64]{0,2,1:T(8,128)}, ...), condition=%wide.region_10.11_spmd.clone, body=%wide.region_8.10_spmd.clone.sunk | while | flops 1095920128 | bytes 9747142 | solution.py:150
  709.7 9.1 bitcast_add_fusion.5
  720.3 9.7 bitcast_add_fusion.5
  733.3 135.8 %while.47 = (s32[]{:T(128)}, f32[256,32,64]{0,2,1:T(8,128)S(1)}, f32[2,512,2048]{2,1,0:T(8,128)}, f32[2,512,2048]{2,1,0:T(8,128)}, bf16[2,512,32,64]{1,3,2,0:T(8...) while((s32[]{:T(128)}, f32[256,32,64]{0,2,1:T(8,128)S(1)}, ...), condition=%wide.region_14.15_spmd.clone, body=%wide.region_12.14_spmd.clone.sunk | while | flops 2740087296 | bytes 153597232 | solution.py:188
  733.3 9.8 fusion.162
  744.6 11.8 fusion.164
  756.4 5.6 bitcast_add_fusion.6
  762.0 12.1 fusion.165
  774.2 5.5 copy.115
  779.6 8.0 fusion.166
  793.1 8.0 constant_dynamic-update-slice_fusion.3
  801.0 9.9 fusion.162
  812.4 11.8 fusion.164
  824.2 5.6 bitcast_add_fusion.6
  829.8 12.1 fusion.165
  841.9 5.5 copy.115
  847.4 8.0 fusion.166
  860.8 7.8 constant_dynamic-update-slice_fusion.3
  869.7 12.2 fusion.70
  883.4 32.2 fusion.71
  916.7 95.2 %reduce-scatter.7.cloned.1.call-done = f32[256,2048]{1,0:T(8,128)} async-done(((f32[1024,2048]{1,0:T(8,128)}), f32[256,2048]{1,0:T(8,128)}) %reduce-scatter.7.cloned.1.call-update) | async-done | bytes 2097168 | tf_op jit(solution)/shard_map/reduce_scatter | solution.py:190
  1025.7 133.7 %reduce-scatter.9.cloned.1.call-done = f32[256,2048]{1,0:T(8,128)} async-done(((f32[1024,2048]{1,0:T(8,128)}), f32[256,2048]{1,0:T(8,128)}) %reduce-scatter.9.cloned.1.call-update) | async-done | bytes 2097168 | tf_op jit(solution)/shard_map/reduce_scatter | solution.py:191
  1159.4 8.6 fusion.119
  1168.0 73.6 %fusion.83 = f32[2048,14336]{1,0:T(8,128)} fusion(f32[1,256,2048]{2,1,0:T(8,128)S(1)} %copy-done.1, f32[2048]{0:T(1024)S(1)} %copy-done.12, f32[2048]{0:T(1024)S(1)} %copy-done.10, f32[256]{0:T(256)S(1)} %copy-done.16, f32[256]{0:T(256)S(1)} %copy-done.14, bf16[256,14336]{1,0:T(8,128)(2,1)} %fusion.119), kind=kOutput, calls=%fused_computation.162 | convolution fusion | flops 15035006976 | bytes 126896128 | tf_op jit(solution)/shard_map/dot_general | solution.py:68
  1244.4 10.7 fusion.63
  1256.2 8.1 fusion.86.clone.4
  1264.3 29.7 multiply_reduce_fusion
  1294.1 332.0 %reduce-scatter.13.cloned.1.call-done = f32[1280,2048]{1,0:T(8,128)} async-done(((f32[10240,2048]{1,0:T(8,128)}), f32[1280,2048]{1,0:T(8,128)}) %reduce-scatter.13.cloned.1.call-update) | async-done | bytes 10485776
  1626.1 634.4 %reduce-scatter.11.cloned.1.call-done = f32[256,14336]{1,0:T(8,128)} async-done(((f32[2048,14336]{1,0:T(8,128)}), f32[256,14336]{1,0:T(8,128)}) %reduce-scatter.11.cloned.1.call-update) | async-done | bytes 14680080 | tf_op jit(solution)/shard_map/reduce_scatter | solution.py:200
  2261.7 20.7 fusion.75
  2286.7 101.5 %all-reduce.6.cloned.1.call-done = (f32[14336]{0:T(1024)}, f32[2048]{0:T(1024)}, f32[2048]{0:T(1024)}, f32[2048]{0:T(1024)}) async-done(((f32[14336]{0:T(1024)}, f32[2048]{0:T(1024)}, f32[2048]{0:T(1024)}, f32[2048]{0:T(1024)}), (f32[14336]{0:T(1024)}, f32[2048]{0:T(1024)}, f32[2048]{0:T(1024)}, f32[2048]{0:T(1024)})) %all-reduce.6.cloned.1.call-update) | async-done | bytes 81936 | tf_op jit(solution)/shard_map/psum | solution.py:213
  2393.5 833.0 %all-reduce.8.cloned.1.call-done = (f32[256,14336]{1,0:T(8,128)}, f32[1280,2048]{1,0:T(8,128)}) async-done(((f32[256,14336]{1,0:T(8,128)}, f32[1280,2048]{1,0:T(8,128)}), (f32[256,14336]{1,0:T(8,128)}, f32[1280,2048]{1,0:T(8,128)})) %all-reduce.8.cloned.1.call-update) | async-done | bytes 25165840 | tf_op jit(solution)/shard_map/psum | solution.py:212
  3226.5 12.2 copy.152
  3238.7 9.7 copy.153
  (158 shorter events, 81.1 us)
Async XLA Ops:
  7.2 1.6 copy-start
  7.2 272.9 %copy-start.22 = (f32[14336]{0:T(1024)S(1)}, f32[14336]{0:T(1024)}, u32[]{:S(2)}) copy-start(f32[14336]{0:T(1024)} %param.21) | copy-start | bytes 172036
  7.2 272.9 %copy-start.11 = (f32[2048]{0:T(1024)S(1)}, f32[2048]{0:T(1024)}, u32[]{:S(2)}) copy-start(f32[2048]{0:T(1024)} %param.19) | copy-start | bytes 24580
  7.2 272.9 %copy-start.9 = (f32[2048]{0:T(1024)S(1)}, f32[2048]{0:T(1024)}, u32[]{:S(2)}) copy-start(f32[2048]{0:T(1024)} %param.18) | copy-start | bytes 24580
  7.2 272.8 %all-gather.5.cloned.1.call-start = ((), (), s32[]{:S(2)}) async-start(), calls=%async_computation.4 | async-start | bytes 66060288 | tf_op jit(solution)/shard_map/all_gather | solution.py:89
  7.9 471.2 %all-gather.11.cloned.1.call-start = ((), (), s32[]{:S(2)}) async-start(), calls=%async_computation.7 | async-start | bytes 47185920 | tf_op jit(solution)/shard_map/all_gather | solution.py:156
  8.7 552.8 %all-gather.7.cloned.1.call-start = ((), (), s32[]{:S(2)}) async-start(), calls=%async_computation.5 | async-start | bytes 5242880 | tf_op jit(solution)/shard_map/all_gather | solution.py:107
  8.9 303.5 %copy-start.13 = (f32[256]{0:T(256)}, f32[256]{0:T(256)S(1)}, u32[]{:S(2)}) copy-start(f32[256]{0:T(256)S(1)} %broadcast_multiply_fusion.2) | copy-start | bytes 3076
  9.3 303.1 %copy-start.15 = (f32[256]{0:T(256)}, f32[256]{0:T(256)S(1)}, u32[]{:S(2)}) copy-start(f32[256]{0:T(256)S(1)} %add_rsqrt_fusion) | copy-start | bytes 3076
  9.3 305.9 %copy-start.21 = (s32[1,8]{1,0:T(1,128)S(1)}, s32[1,8]{1,0:T(1,128)}, u32[]{:S(2)}) copy-start(s32[1,8]{1,0:T(1,128)} %param.17) | copy-start | bytes 100
  315.2 326.9 %all-gather.9.cloned.1.call-start = ((), (), s32[]{:S(2)}) async-start(), calls=%async_computation.6 | async-start | bytes 5242880 | tf_op jit(solution)/shard_map/all_gather | solution.py:106
  315.5 10.0 copy-start.17
  315.5 10.0 copy-start.19
  329.4 682.5 %reduce-scatter.7.cloned.1.call-start = ((), (), s32[]{:S(2)}) async-start(), calls=%async_computation.8 | async-start | bytes 10485760 | tf_op jit(solution)/shard_map/reduce_scatter | solution.py:190
  733.3 11.4 copy-start.7
  733.3 11.4 copy-start.8
  801.0 11.4 copy-start.7
  801.0 11.4 copy-start.8
  869.1 290.2 %reduce-scatter.9.cloned.1.call-start = ((), (), s32[]{:S(2)}) async-start(), calls=%async_computation.9 | async-start | bytes 10485760 | tf_op jit(solution)/shard_map/reduce_scatter | solution.py:191
  869.7 756.5 %reduce-scatter.13.cloned.1.call-start = ((), (), s32[]{:S(2)}) async-start(), calls=%async_computation.11 | async-start | bytes 94371840
  883.4 32.2 copy-start.5
  915.6 100.5 %copy-start.18 = (f32[256,16]{0,1:T(8,128)S(1)}, f32[256,16]{0,1:T(8,128)}, u32[]{:S(2)}) copy-start(f32[256,16]{0,1:T(8,128)} %copy-done.17) | copy-start | bytes 49156
  915.6 100.5 %copy-start.20 = (f32[256,16]{0,1:T(8,128)S(1)}, f32[256,16]{0,1:T(8,128)}, u32[]{:S(2)}) copy-start(f32[256,16]{0,1:T(8,128)} %copy-done.19) | copy-start | bytes 49156
  915.6 1344.9 %reduce-scatter.11.cloned.1.call-start = ((), (), s32[]{:S(2)}) async-start(), calls=%async_computation.10 | async-start | bytes 132120576 | tf_op jit(solution)/shard_map/reduce_scatter | solution.py:200
  1159.3 8.6 copy-start.1
  1159.3 8.6 copy-start.10
  1159.3 8.6 copy-start.12
  1159.3 8.6 copy-start.14
  1159.3 8.6 copy-start.16
  1241.6 1146.6 %all-reduce.6.cloned.1.call-start = ((), (), s32[]{:S(2)}) async-start(), calls=%async_computation.12 | async-start | bytes 163840 | tf_op jit(solution)/shard_map/psum | solution.py:213
  1244.4 10.7 copy-start.2
  1244.4 10.8 copy-start.3
  1244.4 11.8 copy-start.4
  1294.0 1932.5 %all-reduce.8.cloned.1.call-start = ((), (), s32[]{:S(2)}) async-start(), calls=%async_computation.13 | async-start | bytes 50331648 | tf_op jit(solution)/shard_map/psum | solution.py:212
  2260.5 1.2 copy-start.6
  2260.5 1.2 copy-start.23
Sparse Core Ops, SparseCore 0:
  10.0 270.0 all-gather.4
  282.0 197.1 all-gather.10
  480.7 80.7 all-gather.6
  562.9 79.0 all-gather.8
  869.2 142.6 reduce-scatter.6
  1014.1 145.1 reduce-scatter.8
  1163.0 463.1 reduce-scatter.12
  1630.2 630.2 reduce-scatter.10
  2267.1 121.0 all-reduce.5
  2390.7 835.7 all-reduce.7
where the time goes:
time: 3260 us
  waiting for transfers between devices  2670 us (82%)
  matrix products  343 us (11%)
  local copies, waits for them, and re-layouts  135 us (4%)
  other arithmetic  77.9 us (2%)
    psum x1, waiting for transfers between devices, shards(): g_w_in, g_w_out = lax.psum((g_w_in, g_w_out), 'ctx')  833 us
    reduce_scatter x1, waiting for transfers between devices, shards(): lax.psum_scatter(contract_rows(normed, d_proj_b), 'fsdp', scatter_dimensi...  634 us
    unnamed x11, waiting for transfers between devices  334 us
    all_gather x1, waiting for transfers between devices, shards(): lax.all_gather(w_in, 'fsdp', axis=0, tiled=True)  271 us
    all_gather x1, waiting for transfers between devices, shards(): lax.all_gather(w_out, 'fsdp', axis=0, tiled=True)  149 us
    reduce_scatter x1, waiting for transfers between devices, shards(): lax.psum_scatter(d_vals.reshape(seq_len, D), 'ctx', scatter_dimension=0,...  134 us
    dot_general x2, matrix products, contract_rows(): lax.dot_general(left, right, (((0,), (0,)), ((), ())), preferred_element_...  106 us
    psum x1, waiting for transfers between devices, shards(): lax.psum((g_b_in, g_b_out, g_gain, g_beta), ('ctx', 'fsdp'))  101 us
  transfers between devices with their start and end apart: 10, of which 10 were waited for; matrix products, arithmetic and copies ran while one was open for 10% of the time, Pallas kernels for 0%

commit v1 on v0

v1 whole, which is shorter than its diff:
```python
import functools
import math

import jax
import jax.numpy as jnp
from jax import lax
from jax.experimental import pallas as pl
from jax.experimental.pallas import tpu as pltpu
from jax.sharding import PartitionSpec as P

D = 2048
HEADS = 32
HEAD_DIM = 64
ROT_DIM = 32

LN_EPS = 1e-05
NEG_BIG = -1e30
ROPE_BASE = 10000.0
BF = jnp.bfloat16
F32 = jnp.float32
VMEM_BYTES = 56 * 1024 * 1024


def plan(n_fsdp, n_ctx, cat_rows):
    shard = cat_rows // n_fsdp
    even = True
    att, act = [[] for _ in range(n_ctx)], [[] for _ in range(n_ctx)]
    for f in range(n_fsdp):
        a = min(max(D - shard * f, 0), shard)
        m = shard - a
        if a % (n_ctx * HEAD_DIM) or m % (n_ctx * 16):
            even = False
        for z in range(n_ctx):
            if a:
                att[z].append((shard * f + z * (a // n_ctx), a // n_ctx))
            if m:
                act[z].append((shard * f + a + z * (m // n_ctx), m // n_ctx))
    if not even:
        wide_a, wide_m = D // n_ctx, (cat_rows - D) // n_ctx
        att = [[(z * wide_a, wide_a)] for z in range(n_ctx)]
        act = [[(D + z * wide_m, wide_m)] for z in range(n_ctx)]
    return even, att, act


def in_runs(att, act):
    runs = [(part * D + s, n) for part in range(3) for s, n in att]
    return runs + [(2 * D + s, n) for s, n in act]


def pick_kernel(all_runs, z_ref, src_ref, dst_ref):
    for z, runs in enumerate(all_runs):

        @pl.when(z_ref[0] == z)
        def _():
            at = 0
            for start, size in runs:
                dst_ref[:, at : at + size] = src_ref[:, start : start + size]
                at += size


def pick_columns(src, z, all_runs):
    rows, cols = src.shape
    width = sum(n for _, n in all_runs[0])
    step = min(rows, 64)
    return pl.pallas_call(
        functools.partial(pick_kernel, all_runs),
        grid_spec=pltpu.PrefetchScalarGridSpec(
            num_scalar_prefetch=1,
            grid=(rows // step,),
            in_specs=[pl.BlockSpec((step, cols), lambda i, z_ref: (i, 0))],
            out_specs=pl.BlockSpec((step, width), lambda i, z_ref: (i, 0)),
        ),
        out_shape=jax.ShapeDtypeStruct((rows, width), src.dtype),
        compiler_params=pltpu.CompilerParams(vmem_limit_bytes=VMEM_BYTES),
        name="pick_columns",
    )(z[None], src)


def spread_kernel(all_runs, n_ctx, z_ref, *refs):
    srcs, dst_ref = refs[:-1], refs[-1]
    for z in range(n_ctx):

        @pl.when(z_ref[0] == z)
        def _():
            for j, src_ref in enumerate(srcs):
                at = 0
                for start, size in all_runs[(z - j) % n_ctx]:
                    dst_ref[:, start : start + size] = src_ref[:, at : at + size].astype(F32)
                    at += size


def spread_columns(parts, z, all_runs, cols):
    rows, width = parts[0].shape
    n_ctx = len(parts)
    step = min(rows, 64)
    return pl.pallas_call(
        functools.partial(spread_kernel, all_runs, n_ctx),
        grid_spec=pltpu.PrefetchScalarGridSpec(
            num_scalar_prefetch=1,
            grid=(rows // step,),
            in_specs=[pl.BlockSpec((step, width), lambda i, z_ref: (i, 0))] * n_ctx,
            out_specs=pl.BlockSpec((step, cols), lambda i, z_ref: (i, 0)),
        ),
        out_shape=jax.ShapeDtypeStruct((rows, cols), F32),
        compiler_params=pltpu.CompilerParams(vmem_limit_bytes=VMEM_BYTES),
        name="spread_columns",
    )(z[None], *parts)


def turn(u, c, s_up, s_down):
    half_rot = ROT_DIM // 2
    wide = u.shape[1]
    return (
        u * c
        + pltpu.roll(u, half_rot, 1) * s_up
        + pltpu.roll(u, wide - half_rot, 1) * s_down
    )


def dot(a, b, ca, cb):
    return lax.dot_general(a, b, (((ca,), (cb,)), ((), ())), preferred_element_type=F32)


def causal(size, keys, first):
    key_at = lax.broadcasted_iota(jnp.int32, (keys, size), 0)
    query_at = lax.broadcasted_iota(jnp.int32, (keys, size), 1) + first
    return key_at <= query_at


def att_kernel(q_ref, k_ref, v_ref, c_ref, u_ref, d_ref, qb_ref, kb_ref, vb_ref, att_ref, lse_ref):
    seq = q_ref.shape[0]
    size = math.gcd(seq, 256)
    c, su, sd = c_ref[...], u_ref[...], d_ref[...]
    qb_ref[...] = turn(q_ref[...], c, su, sd).astype(BF)
    kb_ref[...] = turn(k_ref[...], c, su, sd).astype(BF)
    vb_ref[...] = v_ref[...].astype(BF)
    scale = 1.0 / math.sqrt(HEAD_DIM)
    for i in range(seq // size):
        rows = slice(i * size, (i + 1) * size)
        keys = (i + 1) * size
        outs = []
        for h in range(2):
            lanes = slice(h * HEAD_DIM, (h + 1) * HEAD_DIM)
            s = dot(kb_ref[:keys, lanes], qb_ref[rows, lanes], 1, 1) * scale
            s = jnp.where(causal(size, keys, i * size), s, NEG_BIG)
            top = jnp.max(s, axis=0, keepdims=True)
            e = jnp.exp(s - top)
            total = jnp.sum(e, axis=0, keepdims=True)
            lse_ref[0, h : h + 1, rows] = top + jnp.log(total)
            p = (e * (1.0 / total)).astype(BF)
            outs.append(dot(p, vb_ref[:keys, lanes], 0, 0))
        att_ref[rows, :] = jnp.concatenate(outs, axis=1).astype(BF)


def attention(project, tables, n_heads):
    seq = project.shape[0]
    pairs = n_heads // 2
    wide = 2 * HEAD_DIM

    def col(base):
        return pl.BlockSpec((seq, wide), lambda p: (0, base + p))

    table = pl.BlockSpec((seq, wide), lambda p: (0, 0))
    own = jax.ShapeDtypeStruct((seq, n_heads * HEAD_DIM), BF)
    return pl.pallas_call(
        att_kernel,
        grid=(pairs,),
        in_specs=[col(0), col(pairs), col(2 * pairs), table, table, table],
        out_specs=[col(0)] * 4 + [pl.BlockSpec((1, 2, seq), lambda p: (p, 0, 0))],
        out_shape=[own] * 4 + [jax.ShapeDtypeStruct((pairs, 2, seq), F32)],
        compiler_params=pltpu.CompilerParams(vmem_limit_bytes=VMEM_BYTES),
        cost_estimate=pl.CostEstimate(
            flops=n_heads * seq * seq * 256, bytes_accessed=seq * n_heads * 64 * 20,
            transcendentals=n_heads * seq * seq // 2,
        ),
        name="attention",
    )(project, project, project, *tables)


def back_kernel(
    q_ref, k_ref, v_ref, att_ref, datt_ref, lse_ref, c_ref, u_ref, d_ref,
    dq_ref, dk_ref, dv_ref, sq_ref, sk_ref, sv_ref, aq, ak, av,
):
    seq = q_ref.shape[0]
    size = math.gcd(seq, 256)
    scale = 1.0 / math.sqrt(HEAD_DIM)
    ak[...] = jnp.zeros_like(ak)
    av[...] = jnp.zeros_like(av)
    for i in range(seq // size):
        rows = slice(i * size, (i + 1) * size)
        keys = (i + 1) * size
        dqs, dks, dvs = [], [], []
        prod = datt_ref[rows, :].astype(F32) * att_ref[rows, :].astype(F32)
        prod_t = prod.T
        for h in range(2):
            lanes = slice(h * HEAD_DIM, (h + 1) * HEAD_DIM)
            q, do = q_ref[rows, lanes], datt_ref[rows, lanes]
            k, v = k_ref[:keys, lanes], v_ref[:keys, lanes]
            delta = jnp.sum(prod_t[lanes, :], axis=0, keepdims=True)
            s = dot(k, q, 1, 1) * scale
            s = jnp.where(causal(size, keys, i * size), s, NEG_BIG)
            p = jnp.exp(s - lse_ref[0, h : h + 1, rows])
            dp = dot(v, do, 1, 1)
            ds = (p * (dp - delta) * scale).astype(BF)
            dvs.append(dot(p.astype(BF), do, 1, 0))
            dks.append(dot(ds, q, 1, 0))
            dqs.append(dot(ds, k, 0, 0))
        av[:keys, :] += jnp.concatenate(dvs, axis=1)
        ak[:keys, :] += jnp.concatenate(dks, axis=1)
        aq[rows, :] = jnp.concatenate(dqs, axis=1)
    c, su, sd = c_ref[...], -u_ref[...], -d_ref[...]
    dq = turn(aq[...], c, su, sd)
    dk = turn(ak[...], c, su, sd)
    dv = av[...]
    for g, out, tot in ((dq, dq_ref, sq_ref), (dk, dk_ref, sk_ref), (dv, dv_ref, sv_ref)):
        out[...] = g.astype(BF)
        tot[0] = jnp.sum(g, axis=0, keepdims=True)


def attention_back(q, k, v, att, d_att, lse, tables, n_heads):
    seq = q.shape[0]
    pairs = n_heads // 2
    wide = 2 * HEAD_DIM
    col = pl.BlockSpec((seq, wide), lambda p: (0, p))
    table = pl.BlockSpec((seq, wide), lambda p: (0, 0))
    own = jax.ShapeDtypeStruct((seq, n_heads * HEAD_DIM), BF)
    return pl.pallas_call(
        back_kernel,
        grid=(pairs,),
        in_specs=[col] * 5 + [pl.BlockSpec((1, 2, seq), lambda p: (p, 0, 0))] + [table] * 3,
        out_specs=[col] * 3 + [pl.BlockSpec((1, 1, wide), lambda p: (p, 0, 0))] * 3,
        out_shape=[own] * 3 + [jax.ShapeDtypeStruct((pairs, 1, wide), F32)] * 3,
        scratch_shapes=[pltpu.VMEM((seq, wide), F32)] * 3,
        compiler_params=pltpu.CompilerParams(vmem_limit_bytes=VMEM_BYTES),
        cost_estimate=pl.CostEstimate(
            flops=n_heads * seq * seq * 640, bytes_accessed=seq * n_heads * 64 * 16,
            transcendentals=n_heads * seq * seq // 2,
        ),
        name="attention_back",
    )(q, k, v, att, d_att, lse, *tables)


def ring(part):
    n = lax.axis_size("ctx")
    perm = [(i, (i + 1) % n) for i in range(n)]
    parts = [part]
    for _ in range(n - 1):
        parts.append(lax.ppermute(parts[-1], "ctx", perm))
    return parts


def ring_sum(take):
    n = lax.axis_size("ctx")
    perm = [(i, (i + 1) % n) for i in range(n)]
    run = take(1).astype(BF)
    for j in range(2, n):
        run = (take(j) + lax.ppermute(run, "ctx", perm).astype(F32)).astype(BF)
    return take(0) + lax.ppermute(run, "ctx", perm).astype(F32)


def swap(x, axis, bit):
    n = lax.axis_size(axis)
    return lax.ppermute(x, axis, [(i, i ^ bit) for i in range(n)])


def far_bits(n):
    return [1 << b for b in range(1, n.bit_length() - 1)]


def gather_near(shard):
    n = lax.axis_size("fsdp")
    rows = shard.shape[0]
    found = {}
    for half in range(2):
        order = far_bits(n)
        if half:
            order = order[::-1]
        lo = half * (rows // 2)
        have = {0: shard[lo : lo + rows // 2]}
        for bit in order:
            keys = sorted(have)
            got = swap(jnp.stack([have[k] for k in keys]), "fsdp", bit)
            for i, k in enumerate(keys):
                have[k ^ bit] = got[i]
        keys = sorted(have)
        got = swap(jnp.stack([have[k] for k in keys]), "fsdp", 1)
        for i, k in enumerate(keys):
            have[k ^ 1] = got[i]
        for k in range(n):
            found[k, half] = have[k]
    return [(found[k, 0], found[k, 1]) for k in range(n)]


def scatter_near(blocks):
    n = lax.axis_size("fsdp")
    rows = blocks[0].shape[0]
    halves = []
    for half in range(2):
        order = far_bits(n)
        if half:
            order = order[::-1]
        lo = half * (rows // 2)
        have = {k: blocks[k][lo : lo + rows // 2] for k in range(n)}
        for bit in [1] + order:
            away = sorted(k for k in have if k & bit)
            got = swap(jnp.stack([have[k] for k in away]), "fsdp", bit)
            for i, k in enumerate(away):
                mine = have[k ^ bit].astype(F32) + got[i].astype(F32)
                have[k ^ bit] = mine.astype(BF)
                del have[k]
        halves.append(have[0])
    return jnp.concatenate(halves, axis=0)


def sum_all(x, axes):
    for axis in axes:
        bit = 1
        while bit < lax.axis_size(axis):
            x = x + swap(x, axis, bit)
            bit *= 2
    return x


def gelu_tanh(values):
    return jax.nn.gelu(values, approximate=True)


def rotary_tables(seq):
    half_rot = ROT_DIM // 2
    expon = jnp.arange(half_rot, dtype=F32) * (2.0 / ROT_DIM)
    freqs = ROPE_BASE ** (-expon)
    angles = jnp.arange(seq, dtype=jnp.int32).astype(F32)[:, None] * freqs[None, :]
    cosine, sine = jnp.cos(angles), jnp.sin(angles)
    zero = jnp.zeros_like(sine)
    rest = jnp.zeros((seq, HEAD_DIM - ROT_DIM), F32)
    c = jnp.concatenate([cosine, cosine, rest + 1.0], axis=1)
    up = jnp.concatenate([zero, sine, rest], axis=1)
    down = jnp.concatenate([-sine, zero, rest], axis=1)
    return tuple(jnp.concatenate([t, t], axis=1) for t in (c, up, down))


def shards(inputs, out_grad, block_order, ln_gain, ln_beta, w_in, b_in, w_out, b_out):
    n_ctx, n_fsdp = lax.axis_size("ctx"), lax.axis_size("fsdp")
    z, f = lax.axis_index("ctx"), lax.axis_index("fsdp")
    seq_in, seq_grad, blk_order = inputs[0], out_grad[0], block_order[0]
    tok_rows = seq_in.shape[0]
    seq_len = tok_rows * n_ctx
    n_blk = blk_order.shape[0]
    blk_size = seq_len // n_blk
    per = n_blk // n_ctx
    wide_d = D // n_fsdp
    shard = w_out.shape[0]
    cat_rows = shard * n_fsdp
    in_cols = w_in.shape[1]
    n_heads = HEADS // n_ctx
    wide_a, wide_m = D // n_ctx, (cat_rows - D) // n_ctx
    even, att_runs, act_runs = plan(n_fsdp, n_ctx, cat_rows)
    z_runs = [in_runs(att_runs[i], act_runs[i]) for i in range(n_ctx)]

    def turned(x):
        return jnp.concatenate(
            [lax.dynamic_slice_in_dim(x, (f ^ k) * wide_d, wide_d, 1) for k in range(n_fsdp)], axis=1
        )

    def places(j):
        rank = lax.rem(z - j + n_ctx, n_ctx)
        return [blk_order[rank * per + i] * blk_size for i in range(per)]

    def in_order(parts):
        whole = jnp.zeros((seq_len, parts[0].shape[1]), parts[0].dtype)
        for j, part in enumerate(parts):
            for i, at in enumerate(places(j)):
                whole = lax.dynamic_update_slice_in_dim(
                    whole, part[i * blk_size : (i + 1) * blk_size], at, 0
                )
        return whole

    def taker(whole):
        def take(j):
            return jnp.concatenate(
                [lax.dynamic_slice_in_dim(whole, at, blk_size, 0) for at in places(j)], axis=0
            ).astype(F32)

        return take

    centred = seq_in - jnp.mean(seq_in, axis=1, keepdims=True)
    inv_std = lax.rsqrt(jnp.mean(centred * centred, axis=1, keepdims=True) + LN_EPS)
    x_hat = centred * inv_std
    normed_own = turned((x_hat * ln_gain + ln_beta).astype(BF))
    normed = in_order(ring(normed_own))
    dy_own = seq_grad.astype(BF)
    dy = in_order(ring(dy_own))

    w_in_blocks = gather_near(pick_columns(w_in, z, z_runs))
    w_in_all = jnp.concatenate([h for pair in w_in_blocks for h in pair], axis=0)
    b_in_z = jnp.stack([jnp.concatenate([b_in[s : s + n] for s, n in runs]) for runs in z_runs])[z]

    def own_rows(whole, rank, at_f):
        pieces = []
        a_0 = jnp.clip(D - shard * at_f, 0, shard)
        n_att = [min(max(D - shard * i, 0), shard) for i in range(n_fsdp)]
        share = shard // n_ctx
        del pieces, n_att
        first = lax.dynamic_slice_in_dim(whole, rank * share, share, 0)
        mixed = [i for i in range(n_fsdp) if 0 < min(max(D - shard * i, 0), shard) < shard]
        if not mixed:
            return first
        a = D - shard * mixed[0]
        m = shard - a
        both = jnp.concatenate(
            [
                lax.dynamic_slice_in_dim(whole, rank * (a // n_ctx), a // n_ctx, 0),
                lax.dynamic_slice_in_dim(whole, a + rank * (m // n_ctx), m // n_ctx, 0),
            ],
            axis=0,
        )
        return jnp.where(at_f == mixed[0], both, first)

    if even:
        share = shard // n_ctx
        w_out_blocks = gather_near(own_rows(w_out, z, f))
        w_out_z = jnp.zeros((cat_rows // n_ctx, D), BF)
        for k, pair in enumerate(w_out_blocks):
            for half in range(2):
                w_out_z = lax.dynamic_update_slice_in_dim(
                    w_out_z, pair[half], (f ^ k) * share + half * (share // 2), 0
                )
    else:
        w_all = lax.all_gather(w_out, "fsdp", axis=0, tiled=True)
        w_out_z = jnp.concatenate(
            [
                lax.dynamic_slice_in_dim(w_all, z * wide_a, wide_a, 0),
                lax.dynamic_slice_in_dim(w_all, D + z * wide_m, wide_m, 0),
            ],
            axis=0,
        )

    project = jnp.dot(normed, w_in_all, preferred_element_type=F32) + b_in_z
    tables = rotary_tables(seq_len)
    q_b, k_b, v_b, att_b, lse = attention(project, tables, n_heads)
    pre_act = project[:, 3 * wide_a :]
    act_b = gelu_tanh(pre_act).astype(BF)
    cat_b = jnp.concatenate([att_b, act_b], axis=1)
    mixed = ring_sum(taker(jnp.dot(cat_b, w_out_z, preferred_element_type=F32)))
    out_y = seq_in + mixed + b_out

    d_cat = dot(dy, w_out_z, 1, 1)
    g_out = dot(cat_b, dy, 0, 0).astype(BF)
    d_att = d_cat[:, :wide_a].astype(BF)
    d_pre = jax.vjp(gelu_tanh, pre_act)[1](d_cat[:, wide_a:])[0]
    d_pre_b = d_pre.astype(BF)
    g_in_pre = dot(normed, d_pre_b, 0, 0).astype(BF)

    if even:
        blocks = [
            lax.dynamic_slice_in_dim(g_out, (f ^ k) * share, share, 0) for k in range(n_fsdp)
        ]
        own = scatter_near(blocks)
        g_w_out = jnp.zeros((shard, D), F32)
        mixed_f = [i for i in range(n_fsdp) if 0 < min(max(D - shard * i, 0), shard) < shard]
        a = D - shard * mixed_f[0] if mixed_f else shard
        m = shard - a
        cut = a // n_ctx
        is_mixed = (f == mixed_f[0]) if mixed_f else False
        for j, part in enumerate(ring(own)):
            rank = lax.rem(z - j + n_ctx, n_ctx)
            part = part.astype(F32)
            at_a = jnp.where(is_mixed, rank * cut, rank * share)
            at_m = jnp.where(is_mixed, a + rank * (share - cut), rank * share + cut)
            g_w_out = lax.dynamic_update_slice_in_dim(g_w_out, part[:cut], at_a, 0)
            if m:
                g_w_out = lax.dynamic_update_slice_in_dim(g_w_out, part[cut:], at_m, 0)
    else:
        spread = jnp.zeros((cat_rows, D), BF)
        spread = lax.dynamic_update_slice_in_dim(spread, g_out[:wide_a], z * wide_a, 0)
        spread = lax.dynamic_update_slice_in_dim(spread, g_out[wide_a:], D + z * wide_m, 0)
        g_w_out = lax.psum_scatter(spread.astype(F32), "fsdp", scatter_dimension=0, tiled=True)
        g_w_out = lax.psum(g_w_out, "ctx")

    dq_b, dk_b, dv_b, s_q, s_k, s_v = attention_back(
        q_b, k_b, v_b, att_b, d_att, lse, tables, n_heads
    )
    d_qkv_b = jnp.concatenate([dq_b, dk_b, dv_b], axis=1)
    g_in_qkv = dot(normed, d_qkv_b, 0, 0).astype(BF)
    d_proj_b = jnp.concatenate([d_qkv_b, d_pre_b], axis=1)
    d_norm = turned(ring_sum(taker(dot(d_proj_b, w_in_all, 1, 1))))

    def by_rank(g):
        return [g[k * wide_d : (k + 1) * wide_d] for k in range(n_fsdp)]

    own_pre = ring(scatter_near(by_rank(g_in_pre)))
    own_qkv = ring(scatter_near(by_rank(g_in_qkv)))
    g_w_in = spread_columns(
        [jnp.concatenate([a, b], axis=1) for a, b in zip(own_qkv, own_pre)], z, z_runs, in_cols
    )

    g_b_in_z = jnp.concatenate(
        [s_q.reshape(-1), s_k.reshape(-1), s_v.reshape(-1), jnp.sum(d_pre, axis=0)]
    )
    masked = jnp.where(
        jnp.arange(n_ctx)[:, None] == z, g_b_in_z[None, :], jnp.zeros((), F32)
    )
    runs = sorted((s, n, i, at) for i in range(n_ctx) for s, n, at in run_offsets(z_runs[i]))
    g_b_in = sum_all(
        jnp.concatenate([masked[i, at : at + n] for _, n, i, at in runs]), ("fsdp", "ctx")
    )
    gain_grad = d_norm * ln_gain
    d_input = seq_grad + inv_std * (
        gain_grad
        - jnp.mean(gain_grad, axis=1, keepdims=True)
        - x_hat * jnp.mean(gain_grad * x_hat, axis=1, keepdims=True)
    )
    small = sum_all(
        jnp.stack(
            [jnp.sum(seq_grad, axis=0), jnp.sum(d_norm * x_hat, axis=0), jnp.sum(d_norm, axis=0)]
        ),
        ("fsdp", "ctx"),
    )

    def own_part(vector):
        length_part = vector.shape[0] // n_fsdp
        return lax.dynamic_slice_in_dim(vector, f * length_part, length_part, 0)

    return (
        out_y[None],
        d_input[None],
        g_w_in,
        own_part(g_b_in),
        g_w_out,
        own_part(small[0]),
        own_part(small[1]),
        own_part(small[2]),
    )


def run_offsets(runs):
    at, found = 0, []
    for start, size in runs:
        found.append((start, size, at))
        at += size
    return found


def solution(mesh):
    placed = (
        P("fsdp", "ctx", None),
        P("fsdp", "ctx", None),
        P("fsdp", None),
        P(),
        P(),
        P("fsdp", None),
        P(),
        P("fsdp", None),
        P(),
    )
    return jax.shard_map(
        shards,
        mesh=mesh,
        in_specs=placed,
        out_specs=(
            P("fsdp", "ctx", None),
            P("fsdp", "ctx", None),
            P("fsdp", None),
            P("fsdp"),
            P("fsdp", None),
            P("fsdp"),
            P("fsdp"),
            P("fsdp"),
        ),
        check_vma=False,
    )
```

time: 3260 us -> 855 us (0.26)
  waiting for transfers between devices: 2670 us -> 393 us
  matrix products: 343 us -> 114 us
  Pallas kernels: 0 us -> 51 us
  starting transfers between devices: 0.78 us -> 45.4 us
    psum x2 -> x0, waiting for transfers between devices: 934 us -> none  [the longest x1 833 us: shards(): g_w_in, g_w_out = lax.psum((g_w_in, g_w_out), 'ctx')]
    reduce_scatter x3 -> x0, waiting for transfers between devices: 863 us -> none  [the longest x1 634 us: shards(): lax.psum_scatter(contract_rows(normed, d_proj_b), 'fsdp', scatter_dimensi...]
    all_gather x4 -> x0, waiting for transfers between devices: 533 us -> none  [the longest x1 271 us: shards(): lax.all_gather(w_in, 'fsdp', axis=0, tiled=True)]
    ppermute x0 -> x61, waiting for transfers between devices: none -> 393 us  [the longest x15 171 us: ring(): parts.append(lax.ppermute(parts[-1], 'ctx', perm))]
    unnamed x11 -> x0, waiting for transfers between devices: 334 us -> none
    dot_general x20 -> x7, matrix products: 343 us -> 114 us  [the longest x5 79.5 us: dot(): lax.dot_general(a, b, (((ca,), (cb,)), ((), ())), preferred_element_type=...]
    pallas_call x0 -> x4, Pallas kernels: none -> 51 us  [the longest x1 21.6 us: attention_back(): pl.pallas_call(back_kernel, grid=(pairs,), in_specs=[col] * 5 + [pl.Block...]
    ppermute x0 -> x61, starting transfers between devices: none -> 45.4 us  [the longest x40 34 us: swap(): return lax.ppermute(x, axis, [(i, i ^ bit) for i in range(n)])]
  transfers between devices with their start and end apart: 10 -> 61, of which waited for: 10 -> 26; matrix products, arithmetic and copies ran while one was open for 10% -> 21% of each run, Pallas kernels for 0% -> 2%
where the time goes in v1:
time: 855 us; the launch traced here: 845 us
  waiting for transfers between devices  393 us (46%)
  local copies, waits for them, and re-layouts  150 us (18%)
  matrix products  114 us (13%)
  other arithmetic  85 us (10%)
  Pallas kernels  51 us (6%)
  starting transfers between devices  45.4 us (5%)
    ppermute x15, waiting for transfers between devices, ring(): parts.append(lax.ppermute(parts[-1], 'ctx', perm))  171 us
    ppermute x40, waiting for transfers between devices, swap(): return lax.ppermute(x, axis, [(i, i ^ bit) for i in range(n)])  136 us
    dot_general x5, matrix products, dot(): lax.dot_general(a, b, (((ca,), (cb,)), ((), ())), preferred_element_type=...  79.5 us
    unnamed x145, local copies, waits for them, and re-layouts  57.1 us
    ppermute x2, waiting for transfers between devices, ring_sum(): return take(0) + lax.ppermute(run, 'ctx', perm).astype(F32)  43.8 us
    ppermute x4, waiting for transfers between devices, ring_sum(): run = (take(j) + lax.ppermute(run, 'ctx', perm).astype(F32)).astype(BF)  42 us
    ppermute x40, starting transfers between devices, swap(): return lax.ppermute(x, axis, [(i, i ^ bit) for i in range(n)])  34 us
    another operation x20, other arithmetic, scatter_near(): got = swap(jnp.stack([have[k] for k in away]), 'fsdp', bit)  22.2 us
  transfers between devices with their start and end apart: 61, of which 26 were waited for; matrix products, arithmetic and copies ran while one was open for 21% of the time, Pallas kernels for 2%

profile of v1, /device:TPU:0, one launch (start us, length us, event | category | flops | bytes accessed | tf_op | source)
XLA Modules:
  0.0 845.0 jit_solution(17047682978103453966)
XLA Ops:
  4.8 5.4 broadcast_in_dim.55
  12.4 3.0 collective-permute-start.12
  20.2 5.1 pick_columns.1
  25.2 3.0 slice_bitcast_fusion.9
  47.6 2.5 broadcast.125.clone.1
  52.1 2.6 broadcast.125.clone
  82.1 15.4 %collective-permute-done.3 = bf16[1,128,3584]{2,1,0:T(8,128)(2,1)S(1)} collective-permute-done((bf16[1,128,3584]{2,1,0:T(8,128)(2,1)S(1)}, bf16[1,128,3584]{2,1,0:T(8,128)(2,1)S(1)}, u32[]{:S(2)}, u32[]{:S(2)}) %collective-permute-start.3) | collective-permute-done | bytes 917536 | tf_op jit(solution)/shard_map/ppermute | solution.py:263
  108.9 16.7 %collective-permute-done.13 = bf16[2,160,2048]{2,1,0:T(8,128)(2,1)S(1)} collective-permute-done((bf16[2,160,2048]{2,1,0:T(8,128)(2,1)S(1)}, bf16[2,160,2048]{2,1,0:T(8,128)(2,1)S(1)}, u32[]{:S(2)}, u32[]{:S(2)}) %collective-permute-start.13) | collective-permute-done | bytes 1310752 | tf_op jit(solution)/shard_map/ppermute | solution.py:263
  132.8 16.2 %collective-permute-done.1 = bf16[256,2048]{1,0:T(8,128)(2,1)S(1)} collective-permute-done((bf16[256,2048]{1,0:T(8,128)(2,1)}, bf16[256,2048]{1,0:T(8,128)(2,1)S(1)}, u32[]{:S(2)}, u32[]{:S(2)}) %collective-permute-start.1) | collective-permute-done | bytes 1048608 | tf_op jit(solution)/shard_map/ppermute | solution.py:248
  152.1 10.3 %collective-permute-done.7 = bf16[2,128,3584]{2,1,0:T(8,128)(2,1)S(1)} collective-permute-done((bf16[2,128,3584]{2,1,0:T(8,128)(2,1)S(1)}, bf16[2,128,3584]{2,1,0:T(8,128)(2,1)S(1)}, u32[]{:S(2)}, u32[]{:S(2)}) %collective-permute-start.7) | collective-permute-done | bytes 1835040 | tf_op jit(solution)/shard_map/ppermute | solution.py:263
  164.1 3.1 pad_maximum_fusion.2
  169.1 6.7 collective-permute-done.20
  177.5 15.0 %collective-permute-done.2 = bf16[256,2048]{1,0:T(8,128)(2,1)S(1)} collective-permute-done((bf16[256,2048]{1,0:T(8,128)(2,1)S(1)}, bf16[256,2048]{1,0:T(8,128)(2,1)S(1)}, u32[]{:S(2)}, u32[]{:S(2)}) %collective-permute-start.2) | collective-permute-done | bytes 1048608 | tf_op jit(solution)/shard_map/ppermute | solution.py:248
  208.8 15.0 %fusion.132 = f32[1024,2560]{1,0:T(8,128)S(1)} fusion(bf16[1024,2048]{1,0:T(8,128)(2,1)} %slice_dynamic-update-slice_fusion.10, bf16[2560,2048]{1,0:T(8,128)(2,1)} %fusion.86), kind=kOutput, calls=%fused_computation.454 | convolution fusion | flops 10737418240 | bytes 25165824 | tf_op jit(solution)/shard_map/dot_general | solution.py:121
  225.0 3.5 fusion.65
  249.5 20.2 %convolution_add_fusion.q_ref.k_ref.v_ref = f32[1024,3584]{1,0:T(8,128)S(1)} fusion(bf16[1024,2048]{1,0:T(8,128)(2,1)} %slice_dynamic-update-slice_fusion.16, bf16[2048,3584]{1,0:T(8,128)(2,1)} %fusion.56, f32[3584]{0:T(1024)S(1)} %fusion.114), kind=kOutput, calls=%fused_computation.3 | convolution fusion | flops 15036055552 | bytes 33568768 | tf_op jit(solution)/shard_map/dot_general | solution.py:438
  269.7 5.2 copy-done
  274.9 10.4 %fusion.121 = (f32[2048]{0:T(1024)S(1)}, bf16[1024,2048]{1,0:T(8,128)(2,1)}, bf16[1024,2048]{1,0:T(8,128)(2,1)}) fusion(f32[1024,3584]{1,0:T(8,128)S(1)} %convolution_add_fusion.q_ref.k_ref.v_ref, f32[1024,2560]{1,0:T(8,128)} %copy-done.5), kind=kLoop, calls=%fused_computation.444 | loop fusion | flops 48232448 | bytes 25174016 | tf_op jit(solution)/shard_map/reduce_sum | solution.py:498
  285.3 15.3 %attention.1 = (bf16[1024,512]{1,0:T(8,128)(2,1)}, bf16[1024,512]{1,0:T(8,128)(2,1)}, bf16[1024,512]{1,0:T(8,128)(2,1)}, bf16[1024,512]{1,0:T(8,128)(2,1)}, f32[4,2,1024]{2,1,0:T(2,128)}) custom-call(f32[1024,3584]{1,0:T(8,128)} %copy-done, f32[1024,3584]{1,0:T(8,128)} %copy-done, f32[1024,3584]{1,0:T(8,128)} %copy-done, f32[1024,128]{1,0:T(8,128)} %concatenate.134.c_ref, ...), custom_call_target="tpu_custom_call" | custom-call | flops 2147483648 | bytes 10485760 | tf_op jit(solution)/shard_map/attention/pallas_call | solution.py:165
  300.6 14.1 %fusion.14 = f32[1024,2048]{1,0:T(8,128)S(1)} fusion(bf16[2560,2048]{1,0:T(8,128)(2,1)} %fusion.86, bf16[1024,2048]{1,0:T(8,128)(2,1)S(1)} %copy-done.12, bf16[1024,512]{1,0:T(8,128)(2,1)} %get-tuple-element.19.att_ref), kind=kOutput, calls=%fused_computation.24 | convolution fusion | flops 10747904000 | bytes 24117248 | tf_op jit(solution)/shard_map/dot_general | solution.py:444
  317.1 21.6 %attention_back.1 = (bf16[1024,512]{1,0:T(8,128)(2,1)}, bf16[1024,512]{1,0:T(8,128)(2,1)}, bf16[1024,512]{1,0:T(8,128)(2,1)}, f32[4,1,128]{2,1,0:T(1,128)}, f32[4,1,128]{2,1,0:T(1,128)}, /*index=5*/f32[4,1,128]{2,1,0:T(1,128)}) custom-call(bf16[1024,512]{1,0:T(8,128)(2,1)} %get-tuple-element.20.q_ref, bf16[1024,512]{1,0:T(8,128)(2,1)} %get-tuple-element.21.k_ref, ...), custom_call_target="tpu_custom_call" | custom-call | flops 5368709120 | bytes 8388608 | tf_op jit(solution)/shard_map/attention_back/pallas_call | solution.py:227
  338.7 23.4 %fusion.6 = f32[1024,2048]{1,0:T(8,128)} fusion(bf16[2048,3584]{1,0:T(8,128)(2,1)} %fusion.56, bf16[1024,2048]{1,0:T(8,128)(2,1)} %get-tuple-element.71, bf16[1024,512]{1,0:T(8,128)(2,1)} %get-tuple-element.26, bf16[1024,512]{1,0:T(8,128)(2,1)} %get-tuple-element.25, bf16[1024,512]{1,0:T(8,128)(2,1)} %get-tuple-element.24), kind=kOutput, calls=%fused_computation.13 | convolution fusion | flops 15061745664 | bytes 30408704 | tf_op jit(solution)/shard_map/dot_general | solution.py:121
  363.9 5.7 constant_dynamic-slice_fusion.4
  369.7 15.9 %convolution_convert_fusion = bf16[2560,2048]{1,0:T(8,128)(2,1)} fusion(bf16[1024,2048]{1,0:T(8,128)(2,1)} %slice_dynamic-update-slice_fusion.10, bf16[1024,2048]{1,0:T(8,128)(2,1)S(1)} %copy-done.13, bf16[1024,512]{1,0:T(8,128)(2,1)S(1)} %copy-done.46), kind=kOutput, calls=%fused_computation.2 | convolution fusion | flops 10753146880 | bytes 19922944 | tf_op jit(solution)/shard_map/dot_general | solution.py:121
  386.1 11.6 %convolution_convert_fusion.2 = bf16[2048,1536]{1,0:T(8,128)(2,1)} fusion(bf16[1024,2048]{1,0:T(8,128)(2,1)} %slice_dynamic-update-slice_fusion.16, bf16[1024,512]{1,0:T(8,128)(2,1)S(1)} %copy-done.49, bf16[1024,512]{1,0:T(8,128)(2,1)S(1)} %copy-done.48, bf16[1024,512]{1,0:T(8,128)(2,1)S(1)} %copy-done.47), kind=kOutput, calls=%fused_computation.12 | convolution fusion | flops 6455033856 | bytes 13631488 | tf_op jit(solution)/shard_map/dot_general | solution.py:121
  397.6 13.6 %convolution_convert_fusion.1 = bf16[2048,2048]{1,0:T(8,128)(2,1)} fusion(bf16[1024,2048]{1,0:T(8,128)(2,1)} %slice_dynamic-update-slice_fusion.16, bf16[1024,2048]{1,0:T(8,128)(2,1)S(1)} %copy-done.11), kind=kOutput, calls=%fused_computation.11 | convolution fusion | flops 8594128896 | bytes 16777216 | tf_op jit(solution)/shard_map/dot_general | solution.py:121
  425.1 2.4 collective-permute-done.43
  433.6 23.8 %collective-permute-done.45 = f32[14336]{0:T(1024)S(1)} collective-permute-done((f32[14336]{0:T(1024)S(1)}, f32[14336]{0:T(1024)S(1)}, u32[]{:S(2)}, u32[]{:S(2)}) %collective-permute-start.45) | collective-permute-done | bytes 57376 | tf_op jit(solution)/shard_map/ppermute | solution.py:263
  459.7 3.0 collective-permute-done.46
  471.5 23.7 %collective-permute-done.16 = bf16[256,2048]{1,0:T(8,128)(2,1)S(1)} collective-permute-done((bf16[256,2048]{1,0:T(8,128)(2,1)S(1)}, bf16[256,2048]{1,0:T(8,128)(2,1)S(1)}, u32[]{:S(2)}, u32[]{:S(2)}) %collective-permute-start.16) | collective-permute-done | bytes 1048608 | tf_op jit(solution)/shard_map/ppermute | solution.py:257
  499.1 18.3 %collective-permute-done.22 = bf16[256,2048]{1,0:T(8,128)(2,1)} collective-permute-done((bf16[256,2048]{1,0:T(8,128)(2,1)S(1)}, bf16[256,2048]{1,0:T(8,128)(2,1)}, u32[]{:S(2)}, u32[]{:S(2)}) %collective-permute-start.22) | collective-permute-done | bytes 1048608 | tf_op jit(solution)/shard_map/ppermute | solution.py:257
  525.1 43.8 %collective-permute-done.23 = bf16[256,2048]{1,0:T(8,128)(2,1)S(1)} collective-permute-done((bf16[256,2048]{1,0:T(8,128)(2,1)S(1)}, bf16[256,2048]{1,0:T(8,128)(2,1)S(1)}, u32[]{:S(2)}, u32[]{:S(2)}) %collective-permute-start.23) | collective-permute-done | bytes 1048608 | tf_op jit(solution)/shard_map/ppermute | solution.py:258
  580.9 4.4 multiply_reduce_fusion
  590.3 7.6 collective-permute-done.26
  601.6 16.3 %collective-permute-done.57 = f32[3,2048]{1,0:T(4,128)S(1)} collective-permute-done((f32[3,2048]{1,0:T(4,128)S(1)}, f32[3,2048]{1,0:T(4,128)S(1)}, u32[]{:S(2)}, u32[]{:S(2)}) %collective-permute-start.57) | collective-permute-done | bytes 24608 | tf_op jit(solution)/shard_map/ppermute | solution.py:263
  622.9 3.1 collective-permute-done.59
  629.8 11.0 %collective-permute-done.32 = bf16[1,128,2048]{2,1,0:T(8,128)(2,1)S(1)} collective-permute-done((bf16[1,128,2048]{2,1,0:T(8,128)(2,1)S(1)}, bf16[1,128,2048]{2,1,0:T(8,128)(2,1)S(1)}, u32[]{:S(2)}, u32[]{:S(2)}) %collective-permute-start.32) | collective-permute-done | bytes 524320 | tf_op jit(solution)/shard_map/ppermute | solution.py:263
  644.2 5.5 collective-permute-done.49
  653.7 3.7 multiply_add_fusion
  659.4 18.5 %collective-permute-done.51 = bf16[2,160,2048]{2,1,0:T(8,128)(2,1)S(1)} collective-permute-done((bf16[2,160,2048]{2,1,0:T(8,128)(2,1)S(1)}, bf16[2,160,2048]{2,1,0:T(8,128)(2,1)S(1)}, u32[]{:S(2)}, u32[]{:S(2)}) %collective-permute-start.51) | collective-permute-done | bytes 1310752 | tf_op jit(solution)/shard_map/ppermute | solution.py:263
  683.2 19.1 %collective-permute-done.37 = bf16[256,2048]{1,0:T(8,128)(2,1)S(1)} collective-permute-done((bf16[256,2048]{1,0:T(8,128)(2,1)S(1)}, bf16[256,2048]{1,0:T(8,128)(2,1)S(1)}, u32[]{:S(2)}, u32[]{:S(2)}) %collective-permute-start.37) | collective-permute-done | bytes 1048608 | tf_op jit(solution)/shard_map/ppermute | solution.py:248
  705.6 36.0 %collective-permute-done.39 = bf16[256,2048]{1,0:T(8,128)(2,1)S(1)} collective-permute-done((bf16[256,2048]{1,0:T(8,128)(2,1)S(1)}, bf16[256,2048]{1,0:T(8,128)(2,1)S(1)}, u32[]{:S(2)}, u32[]{:S(2)}) %collective-permute-start.39) | collective-permute-done | bytes 1048608 | tf_op jit(solution)/shard_map/ppermute | solution.py:248
  743.4 4.1 copy-done.4
  747.5 22.2 %collective-permute-done.53 = bf16[320,2048]{1,0:T(8,128)(2,1)S(1)} collective-permute-done((bf16[320,2048]{1,0:T(8,128)(2,1)S(1)}, bf16[320,2048]{1,0:T(8,128)(2,1)S(1)}, u32[]{:S(2)}, u32[]{:S(2)}) %collective-permute-start.53) | collective-permute-done | bytes 1310752 | tf_op jit(solution)/shard_map/ppermute | solution.py:248
  771.0 21.1 %collective-permute-done.41 = bf16[256,2048]{1,0:T(8,128)(2,1)S(1)} collective-permute-done((bf16[256,2048]{1,0:T(8,128)(2,1)S(1)}, bf16[256,2048]{1,0:T(8,128)(2,1)S(1)}, u32[]{:S(2)}, u32[]{:S(2)}) %collective-permute-start.41) | collective-permute-done | bytes 1048608 | tf_op jit(solution)/shard_map/ppermute | solution.py:248
  793.5 9.0 %spread_columns.1 = f32[256,14336]{1,0:T(8,128)} custom-call(s32[1]{0:T(128)} %bitcast.9.z_ref, bf16[256,3584]{1,0:T(8,128)(2,1)} %maximum_maximum_fusion.refs_0_, bf16[256,3584]{1,0:T(8,128)(2,1)} %pad_maximum_fusion.13.refs_1_, bf16[256,3584]{1,0:T(8,128)(2,1)} %pad_maximum_fusion.14.refs_2_, bf16[256,3584]{1,0:T(8,128)(2,1)} %pad_maximum_fusion.15.refs_3_), custom_call_target="tpu_custom_call" | custom-call | tf_op jit(solution)/shard_map/spread_columns/pallas_call | solution.py:96
  804.1 11.5 %collective-permute-done.54 = bf16[320,2048]{1,0:T(8,128)(2,1)S(1)} collective-permute-done((bf16[320,2048]{1,0:T(8,128)(2,1)S(1)}, bf16[320,2048]{1,0:T(8,128)(2,1)S(1)}, u32[]{:S(2)}, u32[]{:S(2)}) %collective-permute-start.54) | collective-permute-done | bytes 1310752 | tf_op jit(solution)/shard_map/ppermute | solution.py:248
  819.4 22.7 %collective-permute-done.55 = bf16[320,2048]{1,0:T(8,128)(2,1)S(1)} collective-permute-done((bf16[320,2048]{1,0:T(8,128)(2,1)S(1)}, bf16[320,2048]{1,0:T(8,128)(2,1)S(1)}, u32[]{:S(2)}, u32[]{:S(2)}) %collective-permute-start.55) | collective-permute-done | bytes 1310752 | tf_op jit(solution)/shard_map/ppermute | solution.py:248
  (399 shorter events, 226.5 us)
Async XLA Ops:
  12.4 61.9 %collective-permute-start.12 = (bf16[1,160,2048]{2,1,0:T(8,128)(2,1)}, bf16[1,160,2048]{2,1,0:T(8,128)(2,1)}, u32[]{:S(2)}, u32[]{:S(2)}) collective-permute-start(bf16[1,160,2048]{2,1,0:T(8,128)(2,1)} %get-tuple-element.143), channel_id=1, source_target_pairs={{0,4},{1,5},{2,6},{3,7},{4,0},{5,1},{6,2},{7,3},{8,12},{9,13},{10,... | collective-permute-start | bytes 1966088 | tf_op jit(solution)/shard_map/ppermute | solution.py:263
  15.3 60.9 %collective-permute-start.9 = (bf16[1,160,2048]{2,1,0:T(8,128)(2,1)}, bf16[1,160,2048]{2,1,0:T(8,128)(2,1)}, u32[]{:S(2)}, u32[]{:S(2)}) collective-permute-start(bf16[1,160,2048]{2,1,0:T(8,128)(2,1)} %get-tuple-element.144), channel_id=1, source_target_pairs={{0,2},{1,3},{2,0},{3,1},{4,6},{5,7},{6,4},{7,5},{8,10},{9,11},{10,... | collective-permute-start | bytes 1966088 | tf_op jit(solution)/shard_map/ppermute | solution.py:263
  18.6 79.7 %collective-permute-start.18 = (bf16[256,2048]{1,0:T(8,128)(2,1)}, bf16[256,2048]{1,0:T(8,128)(2,1)}, u32[]{:S(2)}, u32[]{:S(2)}) collective-permute-start(bf16[256,2048]{1,0:T(8,128)(2,1)} %bitcast.45), channel_id=1, source_target_pairs={{0,8},{8,16},{16,24},{24,0},{1,9},{9,17},{17,25},{25,1},{2,10},{10... | collective-permute-start | bytes 3145736 | tf_op jit(solution)/shard_map/ppermute | solution.py:248
  28.2 51.0 %collective-permute-start.6 = (bf16[1,128,3584]{2,1,0:T(8,128)(2,1)}, bf16[1,128,3584]{2,1,0:T(8,128)(2,1)S(1)}, u32[]{:S(2)}, u32[]{:S(2)}) collective-permute-start(bf16[1,128,3584]{2,1,0:T(8,128)(2,1)} %get-tuple-element.137), channel_id=1, source_target_pairs={{0,4},{1,5},{2,6},{3,7},{4,0},{5,1},{6,2},{7,3},{8,12},{9,13},{10,... | collective-permute-start | bytes 2752520 | tf_op jit(solution)/shard_map/ppermute | solution.py:263
  42.4 61.2 %collective-permute-start = (bf16[256,2048]{1,0:T(8,128)(2,1)}, bf16[256,2048]{1,0:T(8,128)(2,1)}, u32[]{:S(2)}, u32[]{:S(2)}) collective-permute-start(bf16[256,2048]{1,0:T(8,128)(2,1)} %dynamic-slice_dynamic-update-slice_fusion.8), channel_id=1, source_target_pairs={{0,8},{8,16},{16,24},{24,0},{1,9},{9,17},{17,25},{25,1},{2,10},{10... | collective-permute-start | bytes 3145736 | tf_op jit(solution)/shard_map/ppermute | solution.py:248
  74.3 23.3 %collective-permute-start.3 = (bf16[1,128,3584]{2,1,0:T(8,128)(2,1)S(1)}, bf16[1,128,3584]{2,1,0:T(8,128)(2,1)S(1)}, u32[]{:S(2)}, u32[]{:S(2)}) collective-permute-start(bf16[1,128,3584]{2,1,0:T(8,128)(2,1)S(1)} %copy-done.9), channel_id=1, source_target_pairs={{0,2},{1,3},{2,0},{3,1},{4,6},{5,7},{6,4},{7,5},{8,10},{9,11},{10,... | collective-permute-start | bytes 2752520 | tf_op jit(solution)/shard_map/ppermute | solution.py:263
  76.2 49.4 %collective-permute-start.13 = (bf16[2,160,2048]{2,1,0:T(8,128)(2,1)S(1)}, bf16[2,160,2048]{2,1,0:T(8,128)(2,1)S(1)}, u32[]{:S(2)}, u32[]{:S(2)}) collective-permute-start(bf16[2,160,2048]{2,1,0:T(8,128)(2,1)S(1)} %pad_maximum_fusion.19), channel_id=1, source_target_pairs={{0,2},{1,3},{2,0},{3,1},{4,6},{5,7},{6,4},{7,5},{8,10},{9,11},{10,... | collective-permute-start | bytes 3932168 | tf_op jit(solution)/shard_map/ppermute | solution.py:263
  79.2 49.7 %collective-permute-start.10 = (bf16[2,160,2048]{2,1,0:T(8,128)(2,1)S(1)}, bf16[2,160,2048]{2,1,0:T(8,128)(2,1)S(1)}, u32[]{:S(2)}, u32[]{:S(2)}) collective-permute-start(bf16[2,160,2048]{2,1,0:T(8,128)(2,1)S(1)} %pad_maximum_fusion.18), channel_id=1, source_target_pairs={{0,4},{1,5},{2,6},{3,7},{4,0},{5,1},{6,2},{7,3},{8,12},{9,13},{10,... | collective-permute-start | bytes 3932168 | tf_op jit(solution)/shard_map/ppermute | solution.py:263
  97.6 64.8 %collective-permute-start.7 = (bf16[2,128,3584]{2,1,0:T(8,128)(2,1)S(1)}, bf16[2,128,3584]{2,1,0:T(8,128)(2,1)S(1)}, u32[]{:S(2)}, u32[]{:S(2)}) collective-permute-start(bf16[2,128,3584]{2,1,0:T(8,128)(2,1)S(1)} %pad_maximum_fusion.12), channel_id=1, source_target_pairs={{0,2},{1,3},{2,0},{3,1},{4,6},{5,7},{6,4},{7,5},{8,10},{9,11},{10,... | collective-permute-start | bytes 5505032 | tf_op jit(solution)/shard_map/ppermute | solution.py:263
  98.3 68.8 %collective-permute-start.4 = (bf16[2,128,3584]{2,1,0:T(8,128)(2,1)S(1)}, bf16[2,128,3584]{2,1,0:T(8,128)(2,1)S(1)}, u32[]{:S(2)}, u32[]{:S(2)}) collective-permute-start(bf16[2,128,3584]{2,1,0:T(8,128)(2,1)S(1)} %pad_maximum_fusion.11), channel_id=1, source_target_pairs={{0,4},{1,5},{2,6},{3,7},{4,0},{5,1},{6,2},{7,3},{8,12},{9,13},{10,... | collective-permute-start | bytes 5505032 | tf_op jit(solution)/shard_map/ppermute | solution.py:263
  103.7 26.9 %collective-permute-start.19 = (bf16[256,2048]{1,0:T(8,128)(2,1)}, bf16[256,2048]{1,0:T(8,128)(2,1)S(1)}, u32[]{:S(2)}, u32[]{:S(2)}) collective-permute-start(bf16[256,2048]{1,0:T(8,128)(2,1)} %collective-permute-done.18), channel_id=1, source_target_pairs={{0,8},{8,16},{16,24},{24,0},{1,9},{9,17},{17,25},{25,1},{2,10},{10... | collective-permute-start | bytes 3145736 | tf_op jit(solution)/shard_map/ppermute | solution.py:248
  125.7 23.3 %collective-permute-start.1 = (bf16[256,2048]{1,0:T(8,128)(2,1)}, bf16[256,2048]{1,0:T(8,128)(2,1)S(1)}, u32[]{:S(2)}, u32[]{:S(2)}) collective-permute-start(bf16[256,2048]{1,0:T(8,128)(2,1)} %collective-permute-done), channel_id=1, source_target_pairs={{0,8},{8,16},{16,24},{24,0},{1,9},{9,17},{17,25},{25,1},{2,10},{10... | collective-permute-start | bytes 3145736 | tf_op jit(solution)/shard_map/ppermute | solution.py:248
  128.9 66.2 %collective-permute-start.14 = (bf16[4,160,2048]{2,1,0:T(8,128)(2,1)S(1)}, bf16[4,160,2048]{2,1,0:T(8,128)(2,1)S(1)}, u32[]{:S(2)}, u32[]{:S(2)}) collective-permute-start(bf16[4,160,2048]{2,1,0:T(8,128)(2,1)S(1)} %pad_maximum_fusion.6), channel_id=1, source_target_pairs={{0,1},{1,0},{2,3},{3,2},{4,5},{5,4},{6,7},{7,6},{8,9},{9,8},{10,11... | collective-permute-start | bytes 7864328 | tf_op jit(solution)/shard_map/ppermute | solution.py:263
  130.6 63.7 %collective-permute-start.11 = (bf16[4,160,2048]{2,1,0:T(8,128)(2,1)S(1)}, bf16[4,160,2048]{2,1,0:T(8,128)(2,1)S(1)}, u32[]{:S(2)}, u32[]{:S(2)}) collective-permute-start(bf16[4,160,2048]{2,1,0:T(8,128)(2,1)S(1)} %pad_maximum_fusion.5), channel_id=1, source_target_pairs={{0,1},{1,0},{2,3},{3,2},{4,5},{5,4},{6,7},{7,6},{8,9},{9,8},{10,11... | collective-permute-start | bytes 7864328 | tf_op jit(solution)/shard_map/ppermute | solution.py:263
  149.0 26.9 %collective-permute-start.20 = (bf16[256,2048]{1,0:T(8,128)(2,1)S(1)}, bf16[256,2048]{1,0:T(8,128)(2,1)S(1)}, u32[]{:S(2)}, u32[]{:S(2)}) collective-permute-start(bf16[256,2048]{1,0:T(8,128)(2,1)S(1)} %collective-permute-done.19), channel_id=1, source_target_pairs={{0,8},{8,16},{16,24},{24,0},{1,9},{9,17},{17,25},{25,1},{2,10},{10... | collective-permute-start | bytes 3145736 | tf_op jit(solution)/shard_map/ppermute | solution.py:248
  162.4 30.2 %collective-permute-start.2 = (bf16[256,2048]{1,0:T(8,128)(2,1)S(1)}, bf16[256,2048]{1,0:T(8,128)(2,1)S(1)}, u32[]{:S(2)}, u32[]{:S(2)}) collective-permute-start(bf16[256,2048]{1,0:T(8,128)(2,1)S(1)} %collective-permute-done.1), channel_id=1, source_target_pairs={{0,8},{8,16},{16,24},{24,0},{1,9},{9,17},{17,25},{25,1},{2,10},{10... | collective-permute-start | bytes 3145736 | tf_op jit(solution)/shard_map/ppermute | solution.py:248
  167.1 61.3 %collective-permute-start.8 = (bf16[4,128,3584]{2,1,0:T(8,128)(2,1)}, bf16[4,128,3584]{2,1,0:T(8,128)(2,1)}, u32[]{:S(2)}, u32[]{:S(2)}) collective-permute-start(bf16[4,128,3584]{2,1,0:T(8,128)(2,1)} %pad_maximum_fusion.2), channel_id=1, source_target_pairs={{0,1},{1,0},{2,3},{3,2},{4,5},{5,4},{6,7},{7,6},{8,9},{9,8},{10,11... | collective-permute-start | bytes 11010056 | tf_op jit(solution)/shard_map/ppermute | solution.py:263
  175.9 49.1 %collective-permute-start.5 = (bf16[4,128,3584]{2,1,0:T(8,128)(2,1)}, bf16[4,128,3584]{2,1,0:T(8,128)(2,1)}, u32[]{:S(2)}, u32[]{:S(2)}) collective-permute-start(bf16[4,128,3584]{2,1,0:T(8,128)(2,1)} %pad_maximum_fusion.1), channel_id=1, source_target_pairs={{0,1},{1,0},{2,3},{3,2},{4,5},{5,4},{6,7},{7,6},{8,9},{9,8},{10,11... | collective-permute-start | bytes 11010056 | tf_op jit(solution)/shard_map/ppermute | solution.py:263
  412.3 51.2 %collective-permute-start.15 = (bf16[256,2048]{1,0:T(8,128)(2,1)}, bf16[256,2048]{1,0:T(8,128)(2,1)}, u32[]{:S(2)}, u32[]{:S(2)}) collective-permute-start(bf16[256,2048]{1,0:T(8,128)(2,1)} %pad_maximum_fusion.23), channel_id=1, source_target_pairs={{0,8},{8,16},{16,24},{24,0},{1,9},{9,17},{17,25},{25,1},{2,10},{10... | collective-permute-start | bytes 3145736 | tf_op jit(solution)/shard_map/ppermute | solution.py:257
  413.3 52.4 %collective-permute-start.21 = (bf16[256,2048]{1,0:T(8,128)(2,1)}, bf16[256,2048]{1,0:T(8,128)(2,1)}, u32[]{:S(2)}, u32[]{:S(2)}) collective-permute-start(bf16[256,2048]{1,0:T(8,128)(2,1)} %pad_maximum_fusion.24), channel_id=1, source_target_pairs={{0,8},{8,16},{16,24},{24,0},{1,9},{9,17},{17,25},{25,1},{2,10},{10... | collective-permute-start | bytes 3145736 | tf_op jit(solution)/shard_map/ppermute | solution.py:257
  417.3 50.1 %collective-permute-start.24 = (bf16[4,128,1536]{2,1,0:T(8,128)(2,1)}, bf16[4,128,1536]{2,1,0:T(8,128)(2,1)}, u32[]{:S(2)}, u32[]{:S(2)}) collective-permute-start(bf16[4,128,1536]{2,1,0:T(8,128)(2,1)} %pad_maximum_fusion.16), channel_id=1, source_target_pairs={{0,1},{1,0},{2,3},{3,2},{4,5},{5,4},{6,7},{7,6},{8,9},{9,8},{10,11... | collective-permute-start | bytes 4718600 | tf_op jit(solution)/shard_map/ppermute | solution.py:263
  420.5 48.4 %collective-permute-start.30 = (bf16[4,128,2048]{2,1,0:T(8,128)(2,1)}, bf16[4,128,2048]{2,1,0:T(8,128)(2,1)}, u32[]{:S(2)}, u32[]{:S(2)}) collective-permute-start(bf16[4,128,2048]{2,1,0:T(8,128)(2,1)} %pad_maximum_fusion.9), channel_id=1, source_target_pairs={{0,1},{1,0},{2,3},{3,2},{4,5},{5,4},{6,7},{7,6},{8,9},{9,8},{10,11... | collective-permute-start | bytes 6291464 | tf_op jit(solution)/shard_map/ppermute | solution.py:263
  431.8 25.6 %collective-permute-start.45 = (f32[14336]{0:T(1024)S(1)}, f32[14336]{0:T(1024)S(1)}, u32[]{:S(2)}, u32[]{:S(2)}) collective-permute-start(f32[14336]{0:T(1024)S(1)} %add.702), channel_id=1, source_target_pairs={{0,8},{8,0},{16,24},{24,16},{1,9},{9,1},{17,25},{25,17},{2,10},{10... | collective-permute-start | bytes 172040 | tf_op jit(solution)/shard_map/ppermute | solution.py:263
  462.7 59.5 %collective-permute-start.47 = (bf16[4,160,2048]{2,1,0:T(8,128)(2,1)S(1)}, bf16[4,160,2048]{2,1,0:T(8,128)(2,1)S(1)}, u32[]{:S(2)}, u32[]{:S(2)}) collective-permute-start(bf16[4,160,2048]{2,1,0:T(8,128)(2,1)S(1)} %pad_maximum_fusion.7), channel_id=1, source_target_pairs={{0,1},{1,0},{2,3},{3,2},{4,5},{5,4},{6,7},{7,6},{8,9},{9,8},{10,11... | collective-permute-start | bytes 7864328 | tf_op jit(solution)/shard_map/ppermute | solution.py:263
  463.4 180.8 %collective-permute-start.50 = (bf16[4,160,2048]{2,1,0:T(8,128)(2,1)}, bf16[4,160,2048]{2,1,0:T(8,128)(2,1)}, u32[]{:S(2)}, u32[]{:S(2)}) collective-permute-start(bf16[4,160,2048]{2,1,0:T(8,128)(2,1)} %pad_maximum_fusion.8), channel_id=1, source_target_pairs={{0,1},{1,0},{2,3},{3,2},{4,5},{5,4},{6,7},{7,6},{8,9},{9,8},{10,11... | collective-permute-start | bytes 7864328 | tf_op jit(solution)/shard_map/ppermute | solution.py:263
  465.7 53.3 %collective-permute-start.27 = (bf16[4,128,1536]{2,1,0:T(8,128)(2,1)S(1)}, bf16[4,128,1536]{2,1,0:T(8,128)(2,1)S(1)}, u32[]{:S(2)}, u32[]{:S(2)}) collective-permute-start(bf16[4,128,1536]{2,1,0:T(8,128)(2,1)S(1)} %pad_maximum_fusion.17), channel_id=1, source_target_pairs={{0,1},{1,0},{2,3},{3,2},{4,5},{5,4},{6,7},{7,6},{8,9},{9,8},{10,11... | collective-permute-start | bytes 4718600 | tf_op jit(solution)/shard_map/ppermute | solution.py:263
  467.4 27.8 %collective-permute-start.16 = (bf16[256,2048]{1,0:T(8,128)(2,1)S(1)}, bf16[256,2048]{1,0:T(8,128)(2,1)S(1)}, u32[]{:S(2)}, u32[]{:S(2)}) collective-permute-start(bf16[256,2048]{1,0:T(8,128)(2,1)S(1)} %fusion.24), channel_id=1, source_target_pairs={{0,8},{8,16},{16,24},{24,0},{1,9},{9,17},{17,25},{25,1},{2,10},{10... | collective-permute-start | bytes 3145736 | tf_op jit(solution)/shard_map/ppermute | solution.py:257
  469.0 48.4 %collective-permute-start.22 = (bf16[256,2048]{1,0:T(8,128)(2,1)S(1)}, bf16[256,2048]{1,0:T(8,128)(2,1)}, u32[]{:S(2)}, u32[]{:S(2)}) collective-permute-start(bf16[256,2048]{1,0:T(8,128)(2,1)S(1)} %fusion.26), channel_id=1, source_target_pairs={{0,8},{8,16},{16,24},{24,0},{1,9},{9,17},{17,25},{25,1},{2,10},{10... | collective-permute-start | bytes 3145736 | tf_op jit(solution)/shard_map/ppermute | solution.py:257
  495.2 23.8 %collective-permute-start.25 = (bf16[2,128,1536]{2,1,0:T(8,128)(2,1)S(1)}, bf16[2,128,1536]{2,1,0:T(8,128)(2,1)}, u32[]{:S(2)}, u32[]{:S(2)}) collective-permute-start(bf16[2,128,1536]{2,1,0:T(8,128)(2,1)S(1)} %pad_maximum_fusion.28), channel_id=1, source_target_pairs={{0,2},{1,3},{2,0},{3,1},{4,6},{5,7},{6,4},{7,5},{8,10},{9,11},{10,... | collective-permute-start | bytes 2359304 | tf_op jit(solution)/shard_map/ppermute | solution.py:263
  517.4 67.9 %collective-permute-start.33 = (bf16[4,128,2048]{2,1,0:T(8,128)(2,1)}, bf16[4,128,2048]{2,1,0:T(8,128)(2,1)}, u32[]{:S(2)}, u32[]{:S(2)}) collective-permute-start(bf16[4,128,2048]{2,1,0:T(8,128)(2,1)} %pad_maximum_fusion.10), channel_id=1, source_target_pairs={{0,1},{1,0},{2,3},{3,2},{4,5},{5,4},{6,7},{7,6},{8,9},{9,8},{10,11... | collective-permute-start | bytes 6291464 | tf_op jit(solution)/shard_map/ppermute | solution.py:263
  519.0 61.3 %collective-permute-start.17 = (bf16[256,2048]{1,0:T(8,128)(2,1)S(1)}, bf16[256,2048]{1,0:T(8,128)(2,1)}, u32[]{:S(2)}, u32[]{:S(2)}) collective-permute-start(bf16[256,2048]{1,0:T(8,128)(2,1)S(1)} %fusion.23), channel_id=1, source_target_pairs={{0,8},{8,16},{16,24},{24,0},{1,9},{9,17},{17,25},{25,1},{2,10},{10... | collective-permute-start | bytes 3145736 | tf_op jit(solution)/shard_map/ppermute | solution.py:258
  519.0 49.8 %collective-permute-start.23 = (bf16[256,2048]{1,0:T(8,128)(2,1)S(1)}, bf16[256,2048]{1,0:T(8,128)(2,1)S(1)}, u32[]{:S(2)}, u32[]{:S(2)}) collective-permute-start(bf16[256,2048]{1,0:T(8,128)(2,1)S(1)} %fusion.25), channel_id=1, source_target_pairs={{0,8},{8,16},{16,24},{24,0},{1,9},{9,17},{17,25},{25,1},{2,10},{10... | collective-permute-start | bytes 3145736 | tf_op jit(solution)/shard_map/ppermute | solution.py:258
  522.3 64.1 %collective-permute-start.31 = (bf16[2,128,2048]{2,1,0:T(8,128)(2,1)}, bf16[2,128,2048]{2,1,0:T(8,128)(2,1)}, u32[]{:S(2)}, u32[]{:S(2)}) collective-permute-start(bf16[2,128,2048]{2,1,0:T(8,128)(2,1)} %pad_maximum_fusion.25), channel_id=1, source_target_pairs={{0,2},{1,3},{2,0},{3,1},{4,6},{5,7},{6,4},{7,5},{8,10},{9,11},{10,... | collective-permute-start | bytes 3145736 | tf_op jit(solution)/shard_map/ppermute | solution.py:263
  568.9 30.1 %collective-permute-start.28 = (bf16[2,128,1536]{2,1,0:T(8,128)(2,1)}, bf16[2,128,1536]{2,1,0:T(8,128)(2,1)}, u32[]{:S(2)}, u32[]{:S(2)}) collective-permute-start(bf16[2,128,1536]{2,1,0:T(8,128)(2,1)} %pad_maximum_fusion.29), channel_id=1, source_target_pairs={{0,4},{1,5},{2,6},{3,7},{4,0},{5,1},{6,2},{7,3},{8,12},{9,13},{10,... | collective-permute-start | bytes 2359304 | tf_op jit(solution)/shard_map/ppermute | solution.py:263
  585.3 43.5 %collective-permute-start.48 = (bf16[2,160,2048]{2,1,0:T(8,128)(2,1)}, bf16[2,160,2048]{2,1,0:T(8,128)(2,1)S(1)}, u32[]{:S(2)}, u32[]{:S(2)}) collective-permute-start(bf16[2,160,2048]{2,1,0:T(8,128)(2,1)} %pad_maximum_fusion.20), channel_id=1, source_target_pairs={{0,2},{1,3},{2,0},{3,1},{4,6},{5,7},{6,4},{7,5},{8,10},{9,11},{10,... | collective-permute-start | bytes 3932168 | tf_op jit(solution)/shard_map/ppermute | solution.py:263
  589.3 51.5 %collective-permute-start.34 = (bf16[2,128,2048]{2,1,0:T(8,128)(2,1)S(1)}, bf16[2,128,2048]{2,1,0:T(8,128)(2,1)S(1)}, u32[]{:S(2)}, u32[]{:S(2)}) collective-permute-start(bf16[2,128,2048]{2,1,0:T(8,128)(2,1)S(1)} %pad_maximum_fusion.26), channel_id=1, source_target_pairs={{0,4},{1,5},{2,6},{3,7},{4,0},{5,1},{6,2},{7,3},{8,12},{9,13},{10,... | collective-permute-start | bytes 3145736 | tf_op jit(solution)/shard_map/ppermute | solution.py:263
  600.6 26.9 %collective-permute-start.29 = (bf16[1,128,1536]{2,1,0:T(8,128)(2,1)S(1)}, bf16[1,128,1536]{2,1,0:T(8,128)(2,1)S(1)}, u32[]{:S(2)}, u32[]{:S(2)}) collective-permute-start(bf16[1,128,1536]{2,1,0:T(8,128)(2,1)S(1)} %get-tuple-element.122), channel_id=1, source_target_pairs={{0,2},{1,3},{2,0},{3,1},{4,6},{5,7},{6,4},{7,5},{8,10},{9,11},{10,... | collective-permute-start | bytes 1179656 | tf_op jit(solution)/shard_map/ppermute | solution.py:263
  627.5 29.9 %collective-permute-start.60 = (f32[3,2048]{1,0:T(4,128)S(1)}, f32[3,2048]{1,0:T(4,128)S(1)}, u32[]{:S(2)}, u32[]{:S(2)}) collective-permute-start(f32[3,2048]{1,0:T(4,128)S(1)} %add.739), channel_id=1, source_target_pairs={{0,16},{8,24},{16,0},{24,8},{1,17},{9,25},{17,1},{25,9},{2,18},{10... | collective-permute-start | bytes 73736 | tf_op jit(solution)/shard_map/ppermute | solution.py:263
  652.1 25.7 %collective-permute-start.51 = (bf16[2,160,2048]{2,1,0:T(8,128)(2,1)S(1)}, bf16[2,160,2048]{2,1,0:T(8,128)(2,1)S(1)}, u32[]{:S(2)}, u32[]{:S(2)}) collective-permute-start(bf16[2,160,2048]{2,1,0:T(8,128)(2,1)S(1)} %pad_maximum_fusion.21), channel_id=1, source_target_pairs={{0,4},{1,5},{2,6},{3,7},{4,0},{5,1},{6,2},{7,3},{8,12},{9,13},{10,... | collective-permute-start | bytes 3932168 | tf_op jit(solution)/shard_map/ppermute | solution.py:263
  657.4 25.5 %collective-permute-start.38 = (bf16[256,1536]{1,0:T(8,128)(2,1)S(1)}, bf16[256,1536]{1,0:T(8,128)(2,1)S(1)}, u32[]{:S(2)}, u32[]{:S(2)}) collective-permute-start(bf16[256,1536]{1,0:T(8,128)(2,1)S(1)} %collective-permute-done.36), channel_id=1, source_target_pairs={{0,8},{8,16},{16,24},{24,0},{1,9},{9,17},{17,25},{25,1},{2,10},{10... | collective-permute-start | bytes 2359304 | tf_op jit(solution)/shard_map/ppermute | solution.py:248
  659.3 43.0 %collective-permute-start.37 = (bf16[256,2048]{1,0:T(8,128)(2,1)S(1)}, bf16[256,2048]{1,0:T(8,128)(2,1)S(1)}, u32[]{:S(2)}, u32[]{:S(2)}) collective-permute-start(bf16[256,2048]{1,0:T(8,128)(2,1)S(1)} %pad_maximum_fusion.27), channel_id=1, source_target_pairs={{0,8},{8,16},{16,24},{24,0},{1,9},{9,17},{17,25},{25,1},{2,10},{10... | collective-permute-start | bytes 3145736 | tf_op jit(solution)/shard_map/ppermute | solution.py:248
  679.3 23.0 %collective-permute-start.52 = (bf16[1,160,2048]{2,1,0:T(8,128)(2,1)S(1)}, bf16[1,160,2048]{2,1,0:T(8,128)(2,1)S(1)}, u32[]{:S(2)}, u32[]{:S(2)}) collective-permute-start(bf16[1,160,2048]{2,1,0:T(8,128)(2,1)S(1)} %fusion.85), channel_id=1, source_target_pairs={{0,2},{1,3},{2,0},{3,1},{4,6},{5,7},{6,4},{7,5},{8,10},{9,11},{10,... | collective-permute-start | bytes 1966088 | tf_op jit(solution)/shard_map/ppermute | solution.py:263
  682.9 88.1 %collective-permute-start.40 = (bf16[256,1536]{1,0:T(8,128)(2,1)S(1)}, bf16[256,1536]{1,0:T(8,128)(2,1)S(1)}, u32[]{:S(2)}, u32[]{:S(2)}) collective-permute-start(bf16[256,1536]{1,0:T(8,128)(2,1)S(1)} %collective-permute-done.38), channel_id=1, source_target_pairs={{0,8},{8,16},{16,24},{24,0},{1,9},{9,17},{17,25},{25,1},{2,10},{10... | collective-permute-start | bytes 2359304 | tf_op jit(solution)/shard_map/ppermute | solution.py:248
  702.2 39.3 %collective-permute-start.39 = (bf16[256,2048]{1,0:T(8,128)(2,1)S(1)}, bf16[256,2048]{1,0:T(8,128)(2,1)S(1)}, u32[]{:S(2)}, u32[]{:S(2)}) collective-permute-start(bf16[256,2048]{1,0:T(8,128)(2,1)S(1)} %collective-permute-done.37), channel_id=1, source_target_pairs={{0,8},{8,16},{16,24},{24,0},{1,9},{9,17},{17,25},{25,1},{2,10},{10... | collective-permute-start | bytes 3145736 | tf_op jit(solution)/shard_map/ppermute | solution.py:248
  704.2 65.5 %collective-permute-start.53 = (bf16[320,2048]{1,0:T(8,128)(2,1)S(1)}, bf16[320,2048]{1,0:T(8,128)(2,1)S(1)}, u32[]{:S(2)}, u32[]{:S(2)}) collective-permute-start(bf16[320,2048]{1,0:T(8,128)(2,1)S(1)} %get-tuple-element.139), channel_id=1, source_target_pairs={{0,8},{8,16},{16,24},{24,0},{1,9},{9,17},{17,25},{25,1},{2,10},{10... | collective-permute-start | bytes 3932168 | tf_op jit(solution)/shard_map/ppermute | solution.py:248
  741.6 50.6 %collective-permute-start.41 = (bf16[256,2048]{1,0:T(8,128)(2,1)S(1)}, bf16[256,2048]{1,0:T(8,128)(2,1)S(1)}, u32[]{:S(2)}, u32[]{:S(2)}) collective-permute-start(bf16[256,2048]{1,0:T(8,128)(2,1)S(1)} %collective-permute-done.39), channel_id=1, source_target_pairs={{0,8},{8,16},{16,24},{24,0},{1,9},{9,17},{17,25},{25,1},{2,10},{10... | collective-permute-start | bytes 3145736 | tf_op jit(solution)/shard_map/ppermute | solution.py:248
  769.7 46.0 %collective-permute-start.54 = (bf16[320,2048]{1,0:T(8,128)(2,1)S(1)}, bf16[320,2048]{1,0:T(8,128)(2,1)S(1)}, u32[]{:S(2)}, u32[]{:S(2)}) collective-permute-start(bf16[320,2048]{1,0:T(8,128)(2,1)S(1)} %collective-permute-done.53), channel_id=1, source_target_pairs={{0,8},{8,16},{16,24},{24,0},{1,9},{9,17},{17,25},{25,1},{2,10},{10... | collective-permute-start | bytes 3932168 | tf_op jit(solution)/shard_map/ppermute | solution.py:248
  815.6 26.5 %collective-permute-start.55 = (bf16[320,2048]{1,0:T(8,128)(2,1)S(1)}, bf16[320,2048]{1,0:T(8,128)(2,1)S(1)}, u32[]{:S(2)}, u32[]{:S(2)}) collective-permute-start(bf16[320,2048]{1,0:T(8,128)(2,1)S(1)} %collective-permute-done.54), channel_id=1, source_target_pairs={{0,8},{8,16},{16,24},{24,0},{1,9},{9,17},{17,25},{25,1},{2,10},{10... | collective-permute-start | bytes 3932168 | tf_op jit(solution)/shard_map/ppermute | solution.py:248
  (68 other events, 788.9 us)

commit v2 on v1

--- a/solution.py
+++ b/solution.py
@@ -19,6 +19,7 @@
 BF = jnp.bfloat16
 F32 = jnp.float32
 VMEM_BYTES = 56 * 1024 * 1024
+HBM_SPEC = pl.BlockSpec(memory_space=pltpu.HBM)
 
 
 def plan(n_fsdp, n_ctx, cat_rows):
@@ -47,6 +48,10 @@
     return runs + [(2 * D + s, n) for s, n in act]
 
 
+def key_order(n):
+    return list(range(0, n, 2)) + list(range(1, n, 2))
+
+
 def pick_kernel(all_runs, z_ref, src_ref, dst_ref):
     for z, runs in enumerate(all_runs):
 
@@ -77,7 +82,7 @@
 
 
 def spread_kernel(all_runs, n_ctx, z_ref, *refs):
-    srcs, dst_ref = refs[:-1], refs[-1]
+    srcs, dst_ref = refs[:n_ctx], refs[-1]
     for z in range(n_ctx):
 
         @pl.when(z_ref[0] == z)
@@ -89,22 +94,138 @@
                     at += size
 
 
-def spread_columns(parts, z, all_runs, cols):
+def spread_columns(whole, parts, z, all_runs, cols, first, width_out):
     rows, width = parts[0].shape
     n_ctx = len(parts)
     step = min(rows, 64)
+    fresh = whole is None
     return pl.pallas_call(
         functools.partial(spread_kernel, all_runs, n_ctx),
         grid_spec=pltpu.PrefetchScalarGridSpec(
             num_scalar_prefetch=1,
             grid=(rows // step,),
-            in_specs=[pl.BlockSpec((step, width), lambda i, z_ref: (i, 0))] * n_ctx,
-            out_specs=pl.BlockSpec((step, cols), lambda i, z_ref: (i, 0)),
+            in_specs=[pl.BlockSpec((step, width), lambda i, z_ref: (i, 0))] * n_ctx
+            + [pl.BlockSpec(memory_space=pl.ANY)] * (not fresh),
+            out_specs=pl.BlockSpec(
+                (pl.Element(step), pl.Element(width_out)), lambda i, z_ref: (i * step, first)
+            ),
         ),
         out_shape=jax.ShapeDtypeStruct((rows, cols), F32),
+        input_output_aliases={} if fresh else {1 + n_ctx: 0},
         compiler_params=pltpu.CompilerParams(vmem_limit_bytes=VMEM_BYTES),
         name="spread_columns",
-    )(z[None], *parts)
+    )(z[None], *parts, *([] if fresh else [whole]))
+
+
+def norm_kernel(n_fsdp, f_ref, x_ref, g_ref, gain_ref, beta_ref, out_ref, dy_ref, hold):
+    x = x_ref[...]
+    centred = x - jnp.mean(x, axis=1, keepdims=True)
+    inv_std = lax.rsqrt(jnp.mean(centred * centred, axis=1, keepdims=True) + LN_EPS)
+    hold[...] = (centred * inv_std * gain_ref[...] + beta_ref[...]).astype(BF)
+    wide = x.shape[1] // n_fsdp
+    for p, k in enumerate(key_order(n_fsdp)):
+        at = pl.multiple_of((f_ref[0] ^ k) * wide, wide)
+        out_ref[:, p * wide : (p + 1) * wide] = hold[:, pl.ds(at, wide)]
+    dy_ref[...] = g_ref[...].astype(BF)
+
+
+def norm(x, g, gain, beta, f, n_fsdp):
+    rows, cols = x.shape
+    step = min(rows, 64)
+    tile = pl.BlockSpec((step, cols), lambda i, f_ref: (i, 0))
+    line = pl.BlockSpec((1, cols), lambda i, f_ref: (0, 0))
+    own = jax.ShapeDtypeStruct((rows, cols), BF)
+    return pl.pallas_call(
+        functools.partial(norm_kernel, n_fsdp),
+        grid_spec=pltpu.PrefetchScalarGridSpec(
+            num_scalar_prefetch=1,
+            grid=(rows // step,),
+            in_specs=[tile, tile, line, line],
+            out_specs=[tile, tile],
+            scratch_shapes=[pltpu.VMEM((step, cols), BF)],
+        ),
+        out_shape=[own, own],
+        compiler_params=pltpu.CompilerParams(vmem_limit_bytes=VMEM_BYTES),
+        name="norm",
+    )(f[None], x, g, gain[None], beta[None])
+
+
+def put_kernel(cuts, fresh, at_ref, *refs):
+    n = len({i for i, _, _ in cuts})
+    srcs, dst, sems = refs[:n], refs[-2], refs[-1]
+    del fresh
+    copies = []
+    for c, (i, start, size) in enumerate(cuts):
+        copies.append(
+            pltpu.make_async_copy(
+                srcs[i].at[pl.ds(start, size)],
+                dst.at[pl.ds(pl.multiple_of(at_ref[c], 16), size)],
+                sems.at[c],
+            )
+        )
+    for copy in copies:
+        copy.start()
+    for copy in copies:
+        copy.wait()
+
+
+def put(whole, pieces, rows):
+    cuts, places = [], []
+    for i, (_, moves) in enumerate(pieces):
+        for start, size, at in moves:
+            cuts.append((i, start, size))
+            places.append(jnp.asarray(at, jnp.int32))
+    arrays = [p for p, _ in pieces]
+    fresh = whole is None
+    any_spec = pl.BlockSpec(memory_space=pl.ANY)
+    return pl.pallas_call(
+        functools.partial(put_kernel, tuple(cuts), fresh),
+        grid_spec=pltpu.PrefetchScalarGridSpec(
+            num_scalar_prefetch=1,
+            grid=(1,),
+            in_specs=[any_spec] * len(arrays) + [HBM_SPEC] * (not fresh),
+            out_specs=HBM_SPEC,
+            scratch_shapes=[pltpu.SemaphoreType.DMA((len(cuts),))],
+        ),
+        out_shape=jax.ShapeDtypeStruct((rows, arrays[0].shape[1]), arrays[0].dtype),
+        input_output_aliases={} if fresh else {1 + len(arrays): 0},
+        compiler_params=pltpu.CompilerParams(vmem_limit_bytes=4 * 1024 * 1024),
+        name="put",
+    )(jnp.stack(places), *arrays, *([] if fresh else [whole]))
+
+
+def split_kernel(n_fsdp, f_ref, src, away, home, sems):
+    rows = src.shape[0] // n_fsdp
+    copies = []
+    for s in range(n_fsdp):
+        key = f_ref[0] ^ s
+        at = pl.ds(pl.multiple_of(lax.shift_right_logical(key, 1) * rows, 16), rows)
+        cut = src.at[pl.ds(s * rows, rows)]
+        there = pltpu.make_async_copy(cut, away.at[at], sems.at[s])
+        here = pltpu.make_async_copy(cut, home.at[at], sems.at[s])
+        pl.when(lax.bitwise_and(key, 1) == 1)(there.start)
+        pl.when(lax.bitwise_and(key, 1) == 0)(here.start)
+        copies.append(here)
+    for copy in copies:
+        copy.wait()
+
+
+def split(whole, f, n_fsdp):
+    half = jax.ShapeDtypeStruct((whole.shape[0] // 2, whole.shape[1]), whole.dtype)
+    any_spec = pl.BlockSpec(memory_space=pl.ANY)
+    return pl.pallas_call(
+        functools.partial(split_kernel, n_fsdp),
+        grid_spec=pltpu.PrefetchScalarGridSpec(
+            num_scalar_prefetch=1,
+            grid=(1,),
+            in_specs=[any_spec],
+            out_specs=[HBM_SPEC] * 2,
+            scratch_shapes=[pltpu.SemaphoreType.DMA((n_fsdp,))],
+        ),
+        out_shape=[half, half],
+        compiler_params=pltpu.CompilerParams(vmem_limit_bytes=4 * 1024 * 1024),
+        name="split",
+    )(f[None], whole)
 
 
 def turn(u, c, s_up, s_down):
@@ -240,22 +361,13 @@
     )(q, k, v, att, d_att, lse, *tables)
 
 
-def ring(part):
+def after(x, *others):
+    return lax.optimization_barrier((x, *others))[0]
+
+
+def pass_on(x):
     n = lax.axis_size("ctx")
-    perm = [(i, (i + 1) % n) for i in range(n)]
-    parts = [part]
-    for _ in range(n - 1):
-        parts.append(lax.ppermute(parts[-1], "ctx", perm))
-    return parts
-
-
-def ring_sum(take):
-    n = lax.axis_size("ctx")
-    perm = [(i, (i + 1) % n) for i in range(n)]
-    run = take(1).astype(BF)
-    for j in range(2, n):
-        run = (take(j) + lax.ppermute(run, "ctx", perm).astype(F32)).astype(BF)
-    return take(0) + lax.ppermute(run, "ctx", perm).astype(F32)
+    return lax.ppermute(x, "ctx", [(i, (i + 1) % n) for i in range(n)])
 
 
 def swap(x, axis, bit):
@@ -263,73 +375,157 @@
     return lax.ppermute(x, axis, [(i, i ^ bit) for i in range(n)])
 
 
-def far_bits(n):
-    return [1 << b for b in range(1, n.bit_length() - 1)]
-
-
-def gather_near(shard):
+def near(x, bit):
+    return swap(x, "fsdp", bit)
+
+
+def far_keys(n):
+    return sorted((k for k in range(2, n, 2)), key=lambda k: (k.bit_count(), k))
+
+
+def top_bit(k):
+    return 1 << (k.bit_length() - 1)
+
+
+def low_bit(k):
+    return k & -k
+
+
+def halves(x):
+    rows = x.shape[0] // 2
+    return [x[:rows], x[rows:]]
+
+
+class Line:
+    def __init__(self):
+        self.due = []
+
+    def wait(self, *arrays):
+        self.due += list(arrays)
+
+    def tied(self, *xs):
+        got = list(lax.optimization_barrier((*xs, *self.due)))[: len(xs)]
+        self.due = got[:1]
+        return got[0] if len(xs) == 1 else got
+
+
+def ring_job(part, found):
+    for _ in range(lax.axis_size("ctx") - 1):
+        (part,) = yield [pass_on(part)]
+        found.append(part)
+
+
+def sum_job(take, found):
+    n = lax.axis_size("ctx")
+    run = take(1)
+    for j in range(2, n + 1):
+        (got,) = yield [pass_on(run.astype(BF))]
+        run = take(j % n) + got.astype(F32)
+    found.append(run)
+
+
+def gather_job(shard, found):
     n = lax.axis_size("fsdp")
-    rows = shard.shape[0]
-    found = {}
-    for half in range(2):
-        order = far_bits(n)
-        if half:
-            order = order[::-1]
-        lo = half * (rows // 2)
-        have = {0: shard[lo : lo + rows // 2]}
-        for bit in order:
-            keys = sorted(have)
-            got = swap(jnp.stack([have[k] for k in keys]), "fsdp", bit)
-            for i, k in enumerate(keys):
-                have[k ^ bit] = got[i]
-        keys = sorted(have)
-        got = swap(jnp.stack([have[k] for k in keys]), "fsdp", 1)
-        for i, k in enumerate(keys):
-            have[k ^ 1] = got[i]
-        for k in range(n):
-            found[k, half] = have[k]
-    return [(found[k, 0], found[k, 1]) for k in range(n)]
-
-
-def scatter_near(blocks):
+    have = {}
+    keys = far_keys(n)
+    fresh = [(0, None, shard)]
+    level = 0
+    while True:
+        level += 1
+        send = []
+        for k in keys:
+            if k.bit_count() != level:
+                continue
+            if level == 1:
+                send.append((k, None, near(shard, k)))
+            else:
+                for h, bit in ((0, top_bit(k)), (1, low_bit(k))):
+                    send.append((k, h, near(have[k ^ bit, h], bit)))
+        send += [(k | 1, h, near(x, 1)) for k, h, x in fresh if not k & 1]
+        if not send:
+            return
+        got = yield [x for _, _, x in send]
+        fresh = [(k, h, x) for (k, h, _), x in zip(send, got)]
+        found.extend(fresh)
+        for k, h, x in fresh:
+            if h is None:
+                have[k, 0], have[k, 1] = halves(x)
+            else:
+                have[k, h] = x
+
+
+def scatter_job(away, home, found):
     n = lax.axis_size("fsdp")
-    rows = blocks[0].shape[0]
-    halves = []
-    for half in range(2):
-        order = far_bits(n)
-        if half:
-            order = order[::-1]
-        lo = half * (rows // 2)
-        have = {k: blocks[k][lo : lo + rows // 2] for k in range(n)}
-        for bit in [1] + order:
-            away = sorted(k for k in have if k & bit)
-            got = swap(jnp.stack([have[k] for k in away]), "fsdp", bit)
-            for i, k in enumerate(away):
-                mine = have[k ^ bit].astype(F32) + got[i].astype(F32)
-                have[k ^ bit] = mine.astype(BF)
-                del have[k]
-        halves.append(have[0])
-    return jnp.concatenate(halves, axis=0)
-
-
-def sum_all(x, axes):
-    for axis in axes:
+    (got,) = yield [near(away, 1)]
+    home = home() if callable(home) else home
+    rows = home.shape[0] // (n // 2)
+    hold = {}
+    for i, k in enumerate(range(0, n, 2)):
+        for h in range(2):
+            at = i * rows + h * (rows // 2)
+            cut = slice(at, at + rows // 2)
+            hold[k, h] = home[cut].astype(F32) + got[cut].astype(F32)
+    for level in range(n.bit_length() - 2, 0, -1):
+        moves = []
+        for k in far_keys(n):
+            if k.bit_count() != level:
+                continue
+            if level > 1:
+                for h, bit in ((0, top_bit(k)), (1, low_bit(k))):
+                    moves.append((k ^ bit, h, near(hold[k, h].astype(BF), bit)))
+            else:
+                whole = jnp.concatenate([hold[k, 0], hold[k, 1]], axis=0).astype(BF)
+                moves.append((0, None, near(whole, k)))
+        got = yield [x for _, _, x in moves]
+        for (k, h, _), x in zip(moves, got):
+            if h is None:
+                for i, part in enumerate(halves(x)):
+                    hold[k, i] = hold[k, i] + part.astype(F32)
+            else:
+                hold[k, h] = hold[k, h] + x.astype(F32)
+    found.append(jnp.concatenate([hold[0, 0], hold[0, 1]], axis=0).astype(BF))
+
+
+def total_job(x, found):
+    for axis in ("fsdp", "ctx"):
         bit = 1
         while bit < lax.axis_size(axis):
-            x = x + swap(x, axis, bit)
+            (got,) = yield [swap(x, axis, bit)]
+            x = x + got
             bit *= 2
-    return x
+    found.append(x)
+
+
+class Move:
+    def __init__(self, line, job):
+        self.line, self.job, self.flight = line, job, next(job)
+
+    def step(self):
+        if self.flight is None:
+            return False
+        got = list(lax.optimization_barrier((*self.flight, *self.line.due)))[: len(self.flight)]
+        self.line.due = list(got)
+        try:
+            self.flight = self.job.send(got)
+        except StopIteration:
+            self.flight = None
+        return self.flight is not None
+
+    def end(self):
+        while self.step():
+            pass
 
 
 def gelu_tanh(values):
     return jax.nn.gelu(values, approximate=True)
 
 
-def rotary_tables(seq):
+def rotary_tables(positions):
+    seq = positions.shape[0]
     half_rot = ROT_DIM // 2
     expon = jnp.arange(half_rot, dtype=F32) * (2.0 / ROT_DIM)
     freqs = ROPE_BASE ** (-expon)
-    angles = jnp.arange(seq, dtype=jnp.int32).astype(F32)[:, None] * freqs[None, :]
+    angles = positions.astype(F32)[:, None] * freqs[None, :]
     cosine, sine = jnp.cos(angles), jnp.sin(angles)
     zero = jnp.zeros_like(sine)
     rest = jnp.zeros((seq, HEAD_DIM - ROT_DIM), F32)
@@ -357,23 +553,12 @@
     even, att_runs, act_runs = plan(n_fsdp, n_ctx, cat_rows)
     z_runs = [in_runs(att_runs[i], act_runs[i]) for i in range(n_ctx)]
 
-    def turned(x):
-        return jnp.concatenate(
-            [lax.dynamic_slice_in_dim(x, (f ^ k) * wide_d, wide_d, 1) for k in range(n_fsdp)], axis=1
-        )
+    def position_of(k):
+        return lax.shift_right_logical(k, 1) + lax.bitwise_and(k, 1) * (n_fsdp // 2)
 
     def places(j):
         rank = lax.rem(z - j + n_ctx, n_ctx)
         return [blk_order[rank * per + i] * blk_size for i in range(per)]
-
-    def in_order(parts):
-        whole = jnp.zeros((seq_len, parts[0].shape[1]), parts[0].dtype)
-        for j, part in enumerate(parts):
-            for i, at in enumerate(places(j)):
-                whole = lax.dynamic_update_slice_in_dim(
-                    whole, part[i * blk_size : (i + 1) * blk_size], at, 0
-                )
-        return whole
 
     def taker(whole):
         def take(j):
@@ -383,49 +568,88 @@
 
         return take
 
-    centred = seq_in - jnp.mean(seq_in, axis=1, keepdims=True)
-    inv_std = lax.rsqrt(jnp.mean(centred * centred, axis=1, keepdims=True) + LN_EPS)
-    x_hat = centred * inv_std
-    normed_own = turned((x_hat * ln_gain + ln_beta).astype(BF))
-    normed = in_order(ring(normed_own))
-    dy_own = seq_grad.astype(BF)
-    dy = in_order(ring(dy_own))
-
-    w_in_blocks = gather_near(pick_columns(w_in, z, z_runs))
-    w_in_all = jnp.concatenate([h for pair in w_in_blocks for h in pair], axis=0)
-    b_in_z = jnp.stack([jnp.concatenate([b_in[s : s + n] for s, n in runs]) for runs in z_runs])[z]
-
-    def own_rows(whole, rank, at_f):
+    line = Line()
+    rest = n_ctx - 1
+    keys_at = {k: p for p, k in enumerate(key_order(n_fsdp))}
+    share = shard // n_ctx
+    mixed_f = [i for i in range(n_fsdp) if 0 < D - shard * i < shard]
+    cut = (D - shard * mixed_f[0]) // n_ctx if mixed_f else share
+    cut_m = share - cut
+    is_mixed = (f == mixed_f[0]) if mixed_f else False
+
+    def places_of(j, part):
+        return (part, [(i * blk_size, blk_size, at) for i, at in enumerate(places(j))])
+
+    def put_on(whole, pieces, rows):
+        pieces = [(line.tied(pieces[0][0]), pieces[0][1])] + pieces[1:]
+        whole = put(whole, pieces, rows)
+        line.wait(whole)
+        return whole
+
+    def put_w_in(whole, parts):
         pieces = []
-        a_0 = jnp.clip(D - shard * at_f, 0, shard)
-        n_att = [min(max(D - shard * i, 0), shard) for i in range(n_fsdp)]
-        share = shard // n_ctx
-        del pieces, n_att
-        first = lax.dynamic_slice_in_dim(whole, rank * share, share, 0)
-        mixed = [i for i in range(n_fsdp) if 0 < min(max(D - shard * i, 0), shard) < shard]
-        if not mixed:
+        for k, h, x in parts:
+            rows = x.shape[0]
+            pieces.append((x, [(0, rows, keys_at[k] * wide_d + (h or 0) * rows)]))
+        return put_on(whole, pieces, D)
+
+    def put_w_out(whole, parts):
+        pieces = []
+        for k, h, x in parts:
+            rows = x.shape[0]
+            pieces.append((x, [(0, rows, (f ^ k) * share + (h or 0) * rows)]))
+        return put_on(whole, pieces, cat_rows // n_ctx)
+
+    def own_rows(whole):
+        first = lax.dynamic_slice_in_dim(whole, z * share, share, 0)
+        if not cut_m:
             return first
-        a = D - shard * mixed[0]
-        m = shard - a
         both = jnp.concatenate(
             [
-                lax.dynamic_slice_in_dim(whole, rank * (a // n_ctx), a // n_ctx, 0),
-                lax.dynamic_slice_in_dim(whole, a + rank * (m // n_ctx), m // n_ctx, 0),
+                lax.dynamic_slice_in_dim(whole, z * cut, cut, 0),
+                lax.dynamic_slice_in_dim(whole, cut * n_ctx + z * cut_m, cut_m, 0),
             ],
             axis=0,
         )
-        return jnp.where(at_f == mixed[0], both, first)
-
-    if even:
-        share = shard // n_ctx
-        w_out_blocks = gather_near(own_rows(w_out, z, f))
-        w_out_z = jnp.zeros((cat_rows // n_ctx, D), BF)
-        for k, pair in enumerate(w_out_blocks):
-            for half in range(2):
-                w_out_z = lax.dynamic_update_slice_in_dim(
-                    w_out_z, pair[half], (f ^ k) * share + half * (share // 2), 0
-                )
-    else:
+        return jnp.where(is_mixed, both, first)
+
+    normed_parts, dy_parts, w_in_parts, w_out_parts = [], [], [], []
+    w_in_own = pick_columns(w_in, z, z_runs)
+    w_in_move = Move(line, gather_job(w_in_own, w_in_parts))
+    line.wait(w_in_own)
+    normed_own, dy_own = norm(line.tied(seq_in), seq_grad, ln_gain, ln_beta, f, n_fsdp)
+    normed_ring = Move(line, ring_job(normed_own, normed_parts))
+    line.wait(normed_own)
+    w_in_all = put_w_in(None, [(0, None, w_in_own)])
+    normed = put_on(None, [places_of(0, normed_own)], seq_len)
+    tables = rotary_tables(line.tied(jnp.arange(seq_len, dtype=jnp.int32)))
+    line.wait(*tables)
+    b_in_z = jnp.stack([jnp.concatenate([b_in[s : s + n] for s, n in runs]) for runs in z_runs])[z]
+    w_out_own = None
+    if even:
+        w_out_own = own_rows(line.tied(w_out))
+        line.wait(w_out_own)
+
+    def w_in_round():
+        nonlocal w_in_all
+        had = len(w_in_parts)
+        w_in_move.step()
+        if len(w_in_parts) > had:
+            w_in_all = put_w_in(w_in_all, w_in_parts[had:])
+
+    dy_ring = w_out_move = None
+    for j in range(1, n_ctx):
+        normed_ring.step()
+        if j == rest:
+            dy_ring = Move(line, ring_job(line.tied(dy_own), dy_parts))
+        normed = put_on(normed, [places_of(j, normed_parts[j - 1])], seq_len)
+        w_in_round()
+        if j == 2 and even:
+            w_out_move = Move(line, gather_job(line.tied(w_out_own), w_out_parts))
+    while w_in_move.flight is not None:
+        w_in_round()
+
+    if not even:
         w_all = lax.all_gather(w_out, "fsdp", axis=0, tiled=True)
         w_out_z = jnp.concatenate(
             [
@@ -434,88 +658,173 @@
             ],
             axis=0,
         )
-
-    project = jnp.dot(normed, w_in_all, preferred_element_type=F32) + b_in_z
-    tables = rotary_tables(seq_len)
-    q_b, k_b, v_b, att_b, lse = attention(project, tables, n_heads)
-    pre_act = project[:, 3 * wide_a :]
+    wide_q = 3 * wide_a
+    normed = line.tied(normed)
+    qkv = jnp.dot(normed, w_in_all[:, :wide_q], preferred_element_type=F32) + b_in_z[:wide_q]
+    line.wait(qkv)
+    q_b, k_b, v_b, att_b, lse = attention(line.tied(qkv), tables, n_heads)
+    line.wait(att_b)
+    dy_ring.step()
+    if even:
+        w_out_move.step()
+    normed_t = line.tied(normed)
+    pre_act = jnp.dot(normed_t, w_in_all[:, wide_q:], preferred_element_type=F32) + b_in_z[wide_q:]
     act_b = gelu_tanh(pre_act).astype(BF)
-    cat_b = jnp.concatenate([att_b, act_b], axis=1)
-    mixed = ring_sum(taker(jnp.dot(cat_b, w_out_z, preferred_element_type=F32)))
-    out_y = seq_in + mixed + b_out
-
-    d_cat = dot(dy, w_out_z, 1, 1)
-    g_out = dot(cat_b, dy, 0, 0).astype(BF)
+    line.wait(act_b, pre_act)
+    if even:
+        w_out_move.step()
+        cat_b = jnp.concatenate([line.tied(att_b), act_b], axis=1)
+        line.wait(cat_b)
+        w_out_move.end()
+        w_out_z = put_w_out(None, [(0, None, w_out_own)] + w_out_parts)
+    else:
+        cat_b = jnp.concatenate([line.tied(att_b), act_b], axis=1)
+    dy_ring.step()
+    out_part = jnp.dot(line.tied(cat_b), w_out_z, preferred_element_type=F32)
+    line.wait(out_part)
+    out_sum, norm_sum = [], []
+    out_move = Move(line, sum_job(taker(out_part), out_sum))
+
+    dy_ring.end()
+    dy = put_on(
+        None, [places_of(j, part) for j, part in enumerate([dy_own] + dy_parts)], seq_len
+    )
+    d_cat = dot(line.tied(dy), w_out_z, 1, 1)
+    line.wait(d_cat)
+    out_move.step()
+    d_cat = line.tied(d_cat)
     d_att = d_cat[:, :wide_a].astype(BF)
     d_pre = jax.vjp(gelu_tanh, pre_act)[1](d_cat[:, wide_a:])[0]
     d_pre_b = d_pre.astype(BF)
-    g_in_pre = dot(normed, d_pre_b, 0, 0).astype(BF)
-
-    if even:
-        blocks = [
-            lax.dynamic_slice_in_dim(g_out, (f ^ k) * share, share, 0) for k in range(n_fsdp)
-        ]
-        own = scatter_near(blocks)
+    sum_pre = jnp.sum(d_pre, axis=0)
+    line.wait(d_pre_b, d_att, sum_pre)
+
+    dq_b, dk_b, dv_b, s_q, s_k, s_v = attention_back(
+        q_b, k_b, v_b, att_b, line.tied(d_att), lse, tables, n_heads
+    )
+    line.wait(dq_b)
+    out_move.step()
+    d_proj_b = jnp.concatenate([line.tied(dq_b), dk_b, dv_b, d_pre_b], axis=1)
+    d_norm_part = dot(d_proj_b, w_in_all, 1, 1)
+    line.wait(d_norm_part)
+    norm_move = Move(line, sum_job(taker(d_norm_part), norm_sum))
+    out_move.end()
+
+    def weight_sum(left, right):
+        return dot(line.tied(left), right, 0, 0).astype(BF)
+
+    half = D // 2
+    out_own, pre_own, qkv_own = [], [], []
+    g_out = weight_sum(cat_b, dy)
+    line.wait(g_out)
+    if even:
+        away, home = split(line.tied(g_out), f, n_fsdp)
+        line.wait(away)
+        out_scatter = Move(line, scatter_job(away, home, out_own))
+    pre_away = weight_sum(normed[:, half:], d_pre_b)
+    line.wait(pre_away)
+    pre_scatter = Move(line, scatter_job(pre_away, lambda: pre_home, pre_own))
+    norm_move.step()
+    if even:
+        out_scatter.step()
+    pre_home = weight_sum(normed[:, :half], d_pre_b)
+    line.wait(pre_home)
+    qkv_away = weight_sum(normed[:, half:], d_proj_b[:, :wide_q])
+    line.wait(qkv_away)
+    qkv_scatter = Move(line, scatter_job(qkv_away, lambda: qkv_home, qkv_own))
+    norm_move.step()
+    qkv_home = weight_sum(normed[:, :half], d_proj_b[:, :wide_q])
+    line.wait(qkv_home)
+    if even:
+        out_scatter.step()
+    pre_scatter.step()
+    norm_move.end()
+    if even:
+        out_scatter.end()
+        out_parts = [out_own[0]]
+        out_ring = Move(line, ring_job(out_own[0], out_parts))
+    pre_scatter.step()
+
+    seq_in_t = line.tied(seq_in)
+    centred = seq_in_t - jnp.mean(seq_in_t, axis=1, keepdims=True)
+    inv_std = lax.rsqrt(jnp.mean(centred * centred, axis=1, keepdims=True) + LN_EPS)
+    x_hat = centred * inv_std
+    d_norm = jnp.concatenate(
+        [
+            lax.dynamic_slice_in_dim(norm_sum[0], position_of(f ^ i) * wide_d, wide_d, 1)
+            for i in range(n_fsdp)
+        ],
+        axis=1,
+    )
+    small = jnp.stack(
+        [jnp.sum(seq_grad, axis=0), jnp.sum(d_norm * x_hat, axis=0), jnp.sum(d_norm, axis=0)]
+    )
+    gain_grad = d_norm * ln_gain
+    d_input = seq_grad + inv_std * (
+        gain_grad
+        - jnp.mean(gain_grad, axis=1, keepdims=True)
+        - x_hat * jnp.mean(gain_grad * x_hat, axis=1, keepdims=True)
+    )
+    out_y = seq_in + out_sum[0] + b_out
+
+    g_b_in_z = jnp.concatenate([s_q.reshape(-1), s_k.reshape(-1), s_v.reshape(-1), sum_pre])
+    masked = jnp.where(
+        jnp.arange(n_ctx)[:, None] == z, g_b_in_z[None, :], jnp.zeros((), F32)
+    )
+    runs = sorted((s, n, i, at) for i in range(n_ctx) for s, n, at in run_offsets(z_runs[i]))
+    vector = jnp.concatenate([small.reshape(-1)] + [masked[i, at : at + n] for _, n, i, at in runs])
+    vectors = []
+    vector_move = Move(line, total_job(vector, vectors))
+    line.wait(vector, d_input, out_y)
+
+    pre_runs = [[(s - 3 * D, n) for s, n in runs if s >= 3 * D] for runs in z_runs]
+    qkv_runs = [[(s, n) for s, n in runs if s < 3 * D] for runs in z_runs]
+    if even:
+        out_ring.step()
+    qkv_scatter.step()
+    pre_scatter.end()
+    pre_parts = [pre_own[0]]
+    pre_ring = Move(line, ring_job(pre_own[0], pre_parts))
+    if even:
+        out_ring.step()
+    qkv_scatter.end()
+    qkv_parts = [qkv_own[0]]
+    vector_move.step()
+    pre_ring.step()
+    if even:
+        out_ring.step()
+    vector_move.step()
+    qkv_ring = Move(line, ring_job(qkv_own[0], qkv_parts))
+    pre_ring.step()
+    vector_move.step()
+    pre_ring.end()
+    g_w_in = spread_columns(None, pre_parts, z, pre_runs, in_cols, 3 * D, in_cols - 3 * D)
+    line.wait(g_w_in)
+    qkv_ring.step()
+    vector_move.step()
+    if even:
         g_w_out = jnp.zeros((shard, D), F32)
-        mixed_f = [i for i in range(n_fsdp) if 0 < min(max(D - shard * i, 0), shard) < shard]
-        a = D - shard * mixed_f[0] if mixed_f else shard
-        m = shard - a
-        cut = a // n_ctx
-        is_mixed = (f == mixed_f[0]) if mixed_f else False
-        for j, part in enumerate(ring(own)):
+        for j, part in enumerate(out_parts):
             rank = lax.rem(z - j + n_ctx, n_ctx)
             part = part.astype(F32)
             at_a = jnp.where(is_mixed, rank * cut, rank * share)
-            at_m = jnp.where(is_mixed, a + rank * (share - cut), rank * share + cut)
             g_w_out = lax.dynamic_update_slice_in_dim(g_w_out, part[:cut], at_a, 0)
-            if m:
+            if cut_m:
+                at_m = jnp.where(is_mixed, cut * n_ctx + rank * cut_m, rank * share + cut)
                 g_w_out = lax.dynamic_update_slice_in_dim(g_w_out, part[cut:], at_m, 0)
+        line.wait(g_w_out)
     else:
         spread = jnp.zeros((cat_rows, D), BF)
         spread = lax.dynamic_update_slice_in_dim(spread, g_out[:wide_a], z * wide_a, 0)
         spread = lax.dynamic_update_slice_in_dim(spread, g_out[wide_a:], D + z * wide_m, 0)
         g_w_out = lax.psum_scatter(spread.astype(F32), "fsdp", scatter_dimension=0, tiled=True)
         g_w_out = lax.psum(g_w_out, "ctx")
-
-    dq_b, dk_b, dv_b, s_q, s_k, s_v = attention_back(
-        q_b, k_b, v_b, att_b, d_att, lse, tables, n_heads
-    )
-    d_qkv_b = jnp.concatenate([dq_b, dk_b, dv_b], axis=1)
-    g_in_qkv = dot(normed, d_qkv_b, 0, 0).astype(BF)
-    d_proj_b = jnp.concatenate([d_qkv_b, d_pre_b], axis=1)
-    d_norm = turned(ring_sum(taker(dot(d_proj_b, w_in_all, 1, 1))))
-
-    def by_rank(g):
-        return [g[k * wide_d : (k + 1) * wide_d] for k in range(n_fsdp)]
-
-    own_pre = ring(scatter_near(by_rank(g_in_pre)))
-    own_qkv = ring(scatter_near(by_rank(g_in_qkv)))
-    g_w_in = spread_columns(
-        [jnp.concatenate([a, b], axis=1) for a, b in zip(own_qkv, own_pre)], z, z_runs, in_cols
-    )
-
-    g_b_in_z = jnp.concatenate(
-        [s_q.reshape(-1), s_k.reshape(-1), s_v.reshape(-1), jnp.sum(d_pre, axis=0)]
-    )
-    masked = jnp.where(
-        jnp.arange(n_ctx)[:, None] == z, g_b_in_z[None, :], jnp.zeros((), F32)
-    )
-    runs = sorted((s, n, i, at) for i in range(n_ctx) for s, n, at in run_offsets(z_runs[i]))
-    g_b_in = sum_all(
-        jnp.concatenate([masked[i, at : at + n] for _, n, i, at in runs]), ("fsdp", "ctx")
-    )
-    gain_grad = d_norm * ln_gain
-    d_input = seq_grad + inv_std * (
-        gain_grad
-        - jnp.mean(gain_grad, axis=1, keepdims=True)
-        - x_hat * jnp.mean(gain_grad * x_hat, axis=1, keepdims=True)
-    )
-    small = sum_all(
-        jnp.stack(
-            [jnp.sum(seq_grad, axis=0), jnp.sum(d_norm * x_hat, axis=0), jnp.sum(d_norm, axis=0)]
-        ),
-        ("fsdp", "ctx"),
-    )
+    qkv_ring.step()
+    vector_move.end()
+    qkv_ring.end()
+    g_w_in = spread_columns(g_w_in, qkv_parts, z, qkv_runs, in_cols, 0, 3 * D)
+    small = vectors[0][: 3 * D].reshape(3, D)
+    g_b_in = vectors[0][3 * D :]
 
     def own_part(vector):
         length_part = vector.shape[0] // n_fsdp

time: 855 us -> 666 us (0.78)
  waiting for transfers between devices: 393 us -> 239 us
  local copies, waits for them, and re-layouts: 150 us -> 103 us
  Pallas kernels: 51 us -> 77.5 us
  other arithmetic: 85 us -> 67.4 us
    ppermute x21, waiting for transfers between devices: 256 us -> 161 us  [pass_on(): return lax.ppermute(x, 'ctx', [(i, (i + 1) % n) for i in range(n)])]
    ppermute x40 -> x38, waiting for transfers between devices: 136 us -> 78 us  [swap(): return lax.ppermute(x, axis, [(i, i ^ bit) for i in range(n)])]
    dynamic_update_slice x31 -> x0, local copies, waits for them, and re-layouts: 36.3 us -> none  [the longest x16 20.9 us: in_order(): lax.dynamic_update_slice_in_dim(whole, part[i * blk_size:(i + 1) * blk_si...]
    pallas_call x0 -> x12, Pallas kernels: none -> 23.8 us  [the longest x10 18.3 us: put(): pl.pallas_call(functools.partial(put_kernel, tuple(cuts), fresh), grid_sp...]
    another operation x28 -> x11, other arithmetic: 34.8 us -> 15.5 us  [the longest x20 22.2 us: scatter_near(): got = swap(jnp.stack([have[k] for k in away]), 'fsdp', bit)]
    another operation x9 -> x4, local copies, waits for them, and re-layouts: 14.8 us -> 0.47 us
    dot_general x5 -> x7, matrix products: 79.5 us -> 76.1 us  [dot(): lax.dot_general(a, b, (((ca,), (cb,)), ((), ())), preferred_element_type=...]
    dot_general x2 -> x3, matrix products: 34.3 us -> 37 us  [the longest x1 15.5 us: shards(): jnp.dot(normed_t, w_in_all[:, wide_q:], preferred_element_type=F32)]
  transfers between devices with their start and end apart: 61 -> 59, of which waited for: 26 -> 25; matrix products, arithmetic and copies ran while one was open for 21% -> 32% of each run, Pallas kernels for 2% -> 10%
where the time goes in v2:
time: 666 us; the launch traced here: 656 us
  waiting for transfers between devices  239 us (36%)
  matrix products  113 us (17%)
  local copies, waits for them, and re-layouts  103 us (15%)
  Pallas kernels  77.5 us (12%)
  other arithmetic  67.4 us (10%)
  starting transfers between devices  49.4 us (7%)
  between operations  7.23 us (1%)
    ppermute x21, waiting for transfers between devices, pass_on(): return lax.ppermute(x, 'ctx', [(i, (i + 1) % n) for i in range(n)])  161 us
    ppermute x38, waiting for transfers between devices, swap(): return lax.ppermute(x, axis, [(i, i ^ bit) for i in range(n)])  78 us
    dot_general x7, matrix products, dot(): lax.dot_general(a, b, (((ca,), (cb,)), ((), ())), preferred_element_type=...  76.1 us
    unnamed x143, local copies, waits for them, and re-layouts  56.5 us
    ppermute x38, starting transfers between devices, swap(): return lax.ppermute(x, axis, [(i, i ^ bit) for i in range(n)])  36.1 us
    pallas_call x1, Pallas kernels, attention_back(): pl.pallas_call(back_kernel, grid=(pairs,), in_specs=[col] * 5 + [pl.Block...  21.8 us
    pallas_call x10, Pallas kernels, put(): pl.pallas_call(functools.partial(put_kernel, tuple(cuts), fresh), grid_sp...  18.3 us
    dot_general x1, matrix products, shards(): jnp.dot(normed_t, w_in_all[:, wide_q:], preferred_element_type=F32)  15.5 us
  transfers between devices with their start and end apart: 59, of which 25 were waited for; matrix products, arithmetic and copies ran while one was open for 32% of the time, Pallas kernels for 10%

profile of v2, /device:TPU:0, one launch (start us, length us, event | category | flops | bytes accessed | tf_op | source)
XLA Modules:
  0.0 656.2 jit_solution(5838694753052514394)
XLA Ops:
  0.6 5.1 pick_columns.1.refs_0_
  10.2 4.6 norm.1
  16.6 5.5 copy-done
  44.0 5.1 collective-permute-done.2.refs_0_
  58.7 5.2 copy-done.1
  63.9 3.2 put.13.refs_4_
  67.1 5.5 copy-done.2
  72.5 5.7 collective-permute-done.1.refs_0_
  85.8 5.2 copy-done.3
  94.8 5.5 copy-done.4
  106.5 6.6 %copy-done.5 = bf16[2048,3584]{1,0:T(8,128)(2,1)S(1)} copy-done((bf16[2048,3584]{1,0:T(8,128)(2,1)S(1)}, bf16[2048,3584]{1,0:T(8,128)(2,1)}, u32[]{:S(2)}) %copy-start.5) | copy-done | bytes 14680088
  115.1 5.5 copy-done.6
  120.6 10.4 %fusion.21.q_ref.k_ref.v_ref = f32[1024,1536]{1,0:T(8,128)} fusion(bf16[1024,2048]{1,0:T(8,128)(2,1)S(1)} %put.16, bf16[2048,3584]{1,0:T(8,128)(2,1)} %copy-done.6, f32[1536]{0:T(1024)S(1)} %slice_reduce_fusion), kind=kOutput, calls=%fused_computation.24 | convolution fusion | flops 6444023808 | bytes 16783360 | tf_op jit(solution)/shard_map/dot_general | solution.py:663
  131.0 15.2 %attention.1 = (bf16[1024,512]{1,0:T(8,128)(2,1)}, bf16[1024,512]{1,0:T(8,128)(2,1)}, bf16[1024,512]{1,0:T(8,128)(2,1)}, bf16[1024,512]{1,0:T(8,128)(2,1)}, f32[4,2,1024]{2,1,0:T(2,128)}) custom-call(f32[1024,1536]{1,0:T(8,128)} %fusion.21.q_ref.k_ref.v_ref, f32[1024,1536]{1,0:T(8,128)} %fusion.21.q_ref.k_ref.v_ref, f32[1024,1536]{1,0:T(8,128)} %fusion.21.q_ref.k_ref.v_ref, ...), custom_call_target="tpu_custom_call" | custom-call | flops 2147483648 | bytes 10485760 | tf_op jit(solution)/shard_map/attention/pallas_call | solution.py:286
  150.6 15.5 %multiply_convert_fusion = (bf16[1024,2048]{1,0:T(8,128)(2,1)}, f32[1024,2048]{1,0:T(8,128)}) fusion(f32[2048]{0:T(1024)S(1)} %bitcast.89, bf16[1024,2048]{1,0:T(8,128)(2,1)S(1)} %put.16, bf16[2048,3584]{1,0:T(8,128)(2,1)} %copy-done.6), kind=kOutput, calls=%fused_computation.11 | convolution fusion | flops 8610906112 | bytes 25174016 | tf_op jit(solution)/shard_map/dot_general | solution.py:671
  172.1 5.4 pad_maximum_fusion
  177.5 3.4 put.18
  181.4 11.1 %fusion.45 = f32[1024,2048]{1,0:T(8,128)S(1)} fusion(bf16[1024,2560]{1,0:T(8,128)(2,1)S(1)} %copy-done.31, bf16[2560,2048]{1,0:T(8,128)(2,1)S(1)} %put.18), kind=kOutput, calls=%fused_computation.203 | convolution fusion | flops 10737418240 | bytes 24117248 | tf_op jit(solution)/shard_map/dot_general | solution.py:683
  199.1 10.0 %collective-permute-done.24.refs_3_ = bf16[256,2048]{1,0:T(8,128)(2,1)S(1)} collective-permute-done((bf16[256,2048]{1,0:T(8,128)(2,1)}, bf16[256,2048]{1,0:T(8,128)(2,1)S(1)}, u32[]{:S(2)}, u32[]{:S(2)}) %collective-permute-start.24) | collective-permute-done | bytes 1048608 | tf_op jit(solution)/shard_map/ppermute | solution.py:370
  211.6 13.7 %fusion.46 = f32[1024,2560]{1,0:T(8,128)} fusion(bf16[1024,2048]{1,0:T(8,128)(2,1)S(1)} %put.19, bf16[2560,2048]{1,0:T(8,128)(2,1)S(1)} %put.18), kind=kOutput, calls=%fused_computation.204 | convolution fusion | flops 10737418240 | bytes 25165824 | tf_op jit(solution)/shard_map/dot_general | solution.py:242
  225.3 5.4 collective-permute-done.23
  232.5 11.2 %fusion.36 = (f32[2048]{0:T(1024)S(1)}, bf16[1024,2048]{1,0:T(8,128)(2,1)}) fusion(f32[1024,2048]{1,0:T(8,128)} %get-tuple-element.387, f32[1024,2560]{1,0:T(8,128)} %fusion.46), kind=kLoop, calls=%fused_computation.195 | loop fusion | flops 44038144 | bytes 20979712 | tf_op jit(solution)/shard_map/reduce_sum | solution.py:699
  246.4 21.8 %attention_back.1 = (bf16[1024,512]{1,0:T(8,128)(2,1)}, bf16[1024,512]{1,0:T(8,128)(2,1)}, bf16[1024,512]{1,0:T(8,128)(2,1)}, f32[4,1,128]{2,1,0:T(1,128)}, f32[4,1,128]{2,1,0:T(1,128)}, /*index=5*/f32[4,1,128]{2,1,0:T(1,128)}) custom-call(bf16[1024,512]{1,0:T(8,128)(2,1)} %get-tuple-element.164.q_ref, bf16[1024,512]{1,0:T(8,128)(2,1)} %get-tuple-element.165.k_ref, ...), custom_call_target="tpu_custom_call" | custom-call | flops 5368709120 | bytes 8388608 | tf_op jit(solution)/shard_map/attention_back/pallas_call | solution.py:348
  270.9 22.1 %fusion.8 = f32[1024,2048]{1,0:T(8,128)} fusion(bf16[2048,3584]{1,0:T(8,128)(2,1)} %copy-done.6, bf16[1024,2048]{1,0:T(8,128)(2,1)} %get-tuple-element.259, bf16[1024,512]{1,0:T(8,128)(2,1)S(1)} %copy-done.48, bf16[1024,512]{1,0:T(8,128)(2,1)S(1)} %copy-done.49, bf16[1024,512]{1,0:T(8,128)(2,1)} %get-tuple-element.170), kind=kOutput, calls=%fused_computation.12 | convolution fusion | flops 15061745664 | bytes 30408704 | tf_op jit(solution)/shard_map/dot_general | solution.py:242
  296.0 14.3 %convolution_convert_fusion.src = bf16[2560,2048]{1,0:T(8,128)(2,1)S(1)} fusion(bf16[1024,2560]{1,0:T(8,128)(2,1)} %pad_maximum_fusion, bf16[1024,2048]{1,0:T(8,128)(2,1)} %copy-done.14), kind=kOutput, calls=%fused_computation.2 | convolution fusion | flops 10742661120 | bytes 19922944 | tf_op jit(solution)/shard_map/dot_general | solution.py:242
  324.5 6.2 convolution_convert_fusion.4
  330.7 14.6 %collective-permute-done.28 = bf16[256,2048]{1,0:T(8,128)(2,1)} collective-permute-done((bf16[256,2048]{1,0:T(8,128)(2,1)}, bf16[256,2048]{1,0:T(8,128)(2,1)}, u32[]{:S(2)}, u32[]{:S(2)}) %collective-permute-start.28) | collective-permute-done | bytes 1048608 | tf_op jit(solution)/shard_map/ppermute | solution.py:370
  351.9 4.9 convolution_convert_fusion.3
  356.8 8.2 %convolution_convert_fusion.2 = bf16[1024,1536]{1,0:T(8,128)(2,1)} fusion(bf16[1024,1024]{1,0:T(8,128)(2,1)S(1)} %copy-done.47, bf16[1024,1536]{1,0:T(8,128)(2,1)} %constant_dynamic-update-slice_fusion), kind=kOutput, calls=%fused_computation.26 | convolution fusion | flops 3222798336 | bytes 8388608 | tf_op jit(solution)/shard_map/dot_general | solution.py:242
  365.0 8.4 %collective-permute-done.32 = bf16[256,2048]{1,0:T(8,128)(2,1)S(1)} collective-permute-done((bf16[256,2048]{1,0:T(8,128)(2,1)}, bf16[256,2048]{1,0:T(8,128)(2,1)S(1)}, u32[]{:S(2)}, u32[]{:S(2)}) %collective-permute-start.32) | collective-permute-done | bytes 1048608 | tf_op jit(solution)/shard_map/ppermute | solution.py:370
  377.2 6.7 %convolution_convert_fusion.1 = bf16[1024,1536]{1,0:T(8,128)(2,1)} fusion(bf16[1024,1024]{1,0:T(8,128)(2,1)S(1)} %copy-done.45, bf16[1024,1536]{1,0:T(8,128)(2,1)} %constant_dynamic-update-slice_fusion), kind=kOutput, calls=%fused_computation.25 | convolution fusion | flops 3222798336 | bytes 8388608 | tf_op jit(solution)/shard_map/dot_general | solution.py:242
  384.0 6.2 collective-permute-done.30
  399.3 30.7 %collective-permute-done.35 = bf16[320,2048]{1,0:T(8,128)(2,1)S(1)} collective-permute-done((bf16[320,2048]{1,0:T(8,128)(2,1)S(1)}, bf16[320,2048]{1,0:T(8,128)(2,1)S(1)}, u32[]{:S(2)}, u32[]{:S(2)}) %collective-permute-start.35) | collective-permute-done | bytes 1310752 | tf_op jit(solution)/shard_map/ppermute | solution.py:375
  437.6 3.6 add_convert_fusion.11
  447.0 4.3 multiply_add_fusion
  451.3 13.4 %collective-permute-done.39 = bf16[320,2048]{1,0:T(8,128)(2,1)S(1)} collective-permute-done((bf16[320,2048]{1,0:T(8,128)(2,1)}, bf16[320,2048]{1,0:T(8,128)(2,1)S(1)}, u32[]{:S(2)}, u32[]{:S(2)}) %collective-permute-start.39) | collective-permute-done | bytes 1310752 | tf_op jit(solution)/shard_map/ppermute | solution.py:370
  473.7 24.5 %collective-permute-done.42 = bf16[320,2048]{1,0:T(8,128)(2,1)S(1)} collective-permute-done((bf16[320,2048]{1,0:T(8,128)(2,1)S(1)}, bf16[320,2048]{1,0:T(8,128)(2,1)S(1)}, u32[]{:S(2)}, u32[]{:S(2)}) %collective-permute-start.42) | collective-permute-done | bytes 1310752 | tf_op jit(solution)/shard_map/ppermute | solution.py:370
  502.4 5.4 broadcast_in_dim.73
  513.4 7.3 %collective-permute-done.48.refs_1_ = bf16[256,2048]{1,0:T(8,128)(2,1)S(1)} collective-permute-done((bf16[256,2048]{1,0:T(8,128)(2,1)S(1)}, bf16[256,2048]{1,0:T(8,128)(2,1)S(1)}, u32[]{:S(2)}, u32[]{:S(2)}) %collective-permute-start.48) | collective-permute-done | bytes 1048608 | tf_op jit(solution)/shard_map/ppermute | solution.py:370
  526.2 22.6 %collective-permute-done.52 = bf16[320,2048]{1,0:T(8,128)(2,1)S(1)} collective-permute-done((bf16[320,2048]{1,0:T(8,128)(2,1)S(1)}, bf16[320,2048]{1,0:T(8,128)(2,1)S(1)}, u32[]{:S(2)}, u32[]{:S(2)}) %collective-permute-start.52) | collective-permute-done | bytes 1310752 | tf_op jit(solution)/shard_map/ppermute | solution.py:370
  548.8 17.9 %collective-permute-done.50.refs_2_ = bf16[256,2048]{1,0:T(8,128)(2,1)S(1)} collective-permute-done((bf16[256,2048]{1,0:T(8,128)(2,1)S(1)}, bf16[256,2048]{1,0:T(8,128)(2,1)S(1)}, u32[]{:S(2)}, u32[]{:S(2)}) %collective-permute-start.50) | collective-permute-done | bytes 1048608 | tf_op jit(solution)/shard_map/ppermute | solution.py:370
  574.4 20.2 %collective-permute-done.53.refs_3_ = bf16[256,2048]{1,0:T(8,128)(2,1)S(1)} collective-permute-done((bf16[256,2048]{1,0:T(8,128)(2,1)S(1)}, bf16[256,2048]{1,0:T(8,128)(2,1)S(1)}, u32[]{:S(2)}, u32[]{:S(2)}) %collective-permute-start.53) | collective-permute-done | bytes 1048608 | tf_op jit(solution)/shard_map/ppermute | solution.py:370
  595.6 6.1 spread_columns.2.refs_4_
  601.7 5.3 collective-permute-done.47.refs_1_
  611.1 11.9 %collective-permute-done.56 = f32[20480]{0:T(1024)S(1)} collective-permute-done((f32[20480]{0:T(1024)S(1)}, f32[20480]{0:T(1024)S(1)}, u32[]{:S(2)}, u32[]{:S(2)}) %collective-permute-start.56) | collective-permute-done | bytes 81952 | tf_op jit(solution)/shard_map/ppermute | solution.py:375
  623.0 6.9 %collective-permute-start.58 = (f32[20480]{0:T(1024)S(1)}, f32[20480]{0:T(1024)S(1)}, u32[]{:S(2)}, u32[]{:S(2)}) collective-permute-start(f32[20480]{0:T(1024)S(1)} %add.618), channel_id=1, source_target_pairs={{0,16},{8,24},{16,0},{24,8},{1,17},{9,25},{17,1},{25,9},{2,18},{10... | collective-permute-start | bytes 245768 | tf_op jit(solution)/shard_map/ppermute | solution.py:375
  630.0 17.0 %collective-permute-done.58 = f32[20480]{0:T(1024)S(1)} collective-permute-done((f32[20480]{0:T(1024)S(1)}, f32[20480]{0:T(1024)S(1)}, u32[]{:S(2)}, u32[]{:S(2)}) %collective-permute-start.58) | collective-permute-done | bytes 81952 | tf_op jit(solution)/shard_map/ppermute | solution.py:375
  650.5 5.5 spread_columns.3
  (357 shorter events, 169.3 us)
Async XLA Ops:
  5.7 43.3 %collective-permute-start.2 = (bf16[256,3584]{1,0:T(8,128)(2,1)}, bf16[256,3584]{1,0:T(8,128)(2,1)}, u32[]{:S(2)}, u32[]{:S(2)}) collective-permute-start(bf16[256,3584]{1,0:T(8,128)(2,1)} %pick_columns.1.refs_0_), channel_id=1, source_target_pairs={{0,2},{1,3},{2,0},{3,1},{4,6},{5,7},{6,4},{7,5},{8,10},{9,11},{10,... | collective-permute-start | bytes 5505032 | tf_op jit(solution)/shard_map/ppermute | solution.py:375
  8.7 41.8 %collective-permute-start.3 = (bf16[256,3584]{1,0:T(8,128)(2,1)}, bf16[256,3584]{1,0:T(8,128)(2,1)}, u32[]{:S(2)}, u32[]{:S(2)}) collective-permute-start(bf16[256,3584]{1,0:T(8,128)(2,1)} %pick_columns.1.refs_0_), channel_id=1, source_target_pairs={{0,4},{1,5},{2,6},{3,7},{4,0},{5,1},{6,2},{7,3},{8,12},{9,13},{10,... | collective-permute-start | bytes 5505032 | tf_op jit(solution)/shard_map/ppermute | solution.py:375
  10.2 40.3 %collective-permute-start.4 = (bf16[256,3584]{1,0:T(8,128)(2,1)}, bf16[256,3584]{1,0:T(8,128)(2,1)}, u32[]{:S(2)}, u32[]{:S(2)}) collective-permute-start(bf16[256,3584]{1,0:T(8,128)(2,1)} %pick_columns.1.refs_0_), channel_id=1, source_target_pairs={{0,1},{1,0},{2,3},{3,2},{4,5},{5,4},{6,7},{7,6},{8,9},{9,8},{10,11... | collective-permute-start | bytes 5505032 | tf_op jit(solution)/shard_map/ppermute | solution.py:375
  14.8 28.1 %collective-permute-start = (bf16[256,2048]{1,0:T(8,128)(2,1)}, bf16[256,2048]{1,0:T(8,128)(2,1)S(1)}, u32[]{:S(2)}, u32[]{:S(2)}) collective-permute-start(bf16[256,2048]{1,0:T(8,128)(2,1)} %get-tuple-element.116.refs_0_), channel_id=1, source_target_pairs={{0,8},{8,16},{16,24},{24,0},{1,9},{9,17},{17,25},{25,1},{2,10},{10... | collective-permute-start | bytes 3145736 | tf_op jit(solution)/shard_map/ppermute | solution.py:370
  50.5 31.6 %collective-permute-start.8 = (bf16[256,3584]{1,0:T(8,128)(2,1)}, bf16[256,3584]{1,0:T(8,128)(2,1)S(1)}, u32[]{:S(2)}, u32[]{:S(2)}) collective-permute-start(bf16[256,3584]{1,0:T(8,128)(2,1)} %collective-permute-done.2.refs_0_), channel_id=1, source_target_pairs={{0,1},{1,0},{2,3},{3,2},{4,5},{5,4},{6,7},{7,6},{8,9},{9,8},{10,11... | collective-permute-start | bytes 5505032 | tf_op jit(solution)/shard_map/ppermute | solution.py:375
  50.5 31.6 %collective-permute-start.9 = (bf16[256,3584]{1,0:T(8,128)(2,1)}, bf16[256,3584]{1,0:T(8,128)(2,1)S(1)}, u32[]{:S(2)}, u32[]{:S(2)}) collective-permute-start(bf16[256,3584]{1,0:T(8,128)(2,1)} %collective-permute-done.3.refs_1_), channel_id=1, source_target_pairs={{0,1},{1,0},{2,3},{3,2},{4,5},{5,4},{6,7},{7,6},{8,9},{9,8},{10,11... | collective-permute-start | bytes 5505032 | tf_op jit(solution)/shard_map/ppermute | solution.py:375
  51.0 27.2 %collective-permute-start.1 = (bf16[256,2048]{1,0:T(8,128)(2,1)}, bf16[256,2048]{1,0:T(8,128)(2,1)}, u32[]{:S(2)}, u32[]{:S(2)}) collective-permute-start(bf16[256,2048]{1,0:T(8,128)(2,1)} %copy-done.21), channel_id=1, source_target_pairs={{0,8},{8,16},{16,24},{24,0},{1,9},{9,17},{17,25},{25,1},{2,10},{10... | collective-permute-start | bytes 3145736 | tf_op jit(solution)/shard_map/ppermute | solution.py:370
  55.1 26.9 %collective-permute-start.6 = (bf16[128,3584]{1,0:T(8,128)(2,1)S(1)}, bf16[128,3584]{1,0:T(8,128)(2,1)}, u32[]{:S(2)}, u32[]{:S(2)}) collective-permute-start(bf16[128,3584]{1,0:T(8,128)(2,1)S(1)} %slice.579), channel_id=1, source_target_pairs={{0,4},{1,5},{2,6},{3,7},{4,0},{5,1},{6,2},{7,3},{8,12},{9,13},{10,... | collective-permute-start | bytes 2752520 | tf_op jit(solution)/shard_map/ppermute | solution.py:375
  56.6 25.4 %collective-permute-start.7 = (bf16[128,3584]{1,0:T(8,128)(2,1)S(1)}, bf16[128,3584]{1,0:T(8,128)(2,1)}, u32[]{:S(2)}, u32[]{:S(2)}) collective-permute-start(bf16[128,3584]{1,0:T(8,128)(2,1)S(1)} %slice.580), channel_id=1, source_target_pairs={{0,2},{1,3},{2,0},{3,1},{4,6},{5,7},{6,4},{7,5},{8,10},{9,11},{10,... | collective-permute-start | bytes 2752520 | tf_op jit(solution)/shard_map/ppermute | solution.py:375
  78.2 26.4 %collective-permute-start.5 = (bf16[256,2048]{1,0:T(8,128)(2,1)}, bf16[256,2048]{1,0:T(8,128)(2,1)}, u32[]{:S(2)}, u32[]{:S(2)}) collective-permute-start(bf16[256,2048]{1,0:T(8,128)(2,1)} %collective-permute-done.1.refs_0_), channel_id=1, source_target_pairs={{0,8},{8,16},{16,24},{24,0},{1,9},{9,17},{17,25},{25,1},{2,10},{10... | collective-permute-start | bytes 3145736 | tf_op jit(solution)/shard_map/ppermute | solution.py:370
  83.3 23.2 %collective-permute-start.10 = (bf16[128,3584]{1,0:T(8,128)(2,1)}, bf16[128,3584]{1,0:T(8,128)(2,1)}, u32[]{:S(2)}, u32[]{:S(2)}) collective-permute-start(bf16[128,3584]{1,0:T(8,128)(2,1)} %collective-permute-done.6.refs_0_), channel_id=1, source_target_pairs={{0,1},{1,0},{2,3},{3,2},{4,5},{5,4},{6,7},{7,6},{8,9},{9,8},{10,11... | collective-permute-start | bytes 2752520 | tf_op jit(solution)/shard_map/ppermute | solution.py:375
  83.3 23.2 %collective-permute-start.11 = (bf16[128,3584]{1,0:T(8,128)(2,1)}, bf16[128,3584]{1,0:T(8,128)(2,1)}, u32[]{:S(2)}, u32[]{:S(2)}) collective-permute-start(bf16[128,3584]{1,0:T(8,128)(2,1)} %collective-permute-done.7.refs_1_), channel_id=1, source_target_pairs={{0,1},{1,0},{2,3},{3,2},{4,5},{5,4},{6,7},{7,6},{8,9},{9,8},{10,11... | collective-permute-start | bytes 2752520 | tf_op jit(solution)/shard_map/ppermute | solution.py:375
  100.3 46.3 %collective-permute-start.12 = (bf16[320,2048]{1,0:T(8,128)(2,1)S(1)}, bf16[320,2048]{1,0:T(8,128)(2,1)S(1)}, u32[]{:S(2)}, u32[]{:S(2)}) collective-permute-start(bf16[320,2048]{1,0:T(8,128)(2,1)S(1)} %maximum_select_fusion.refs_0_), channel_id=1, source_target_pairs={{0,2},{1,3},{2,0},{3,1},{4,6},{5,7},{6,4},{7,5},{8,10},{9,11},{10,... | collective-permute-start | bytes 3932168 | tf_op jit(solution)/shard_map/ppermute | solution.py:375
  100.8 45.8 %collective-permute-start.13 = (bf16[320,2048]{1,0:T(8,128)(2,1)S(1)}, bf16[320,2048]{1,0:T(8,128)(2,1)}, u32[]{:S(2)}, u32[]{:S(2)}) collective-permute-start(bf16[320,2048]{1,0:T(8,128)(2,1)S(1)} %maximum_select_fusion.refs_0_), channel_id=1, source_target_pairs={{0,4},{1,5},{2,6},{3,7},{4,0},{5,1},{6,2},{7,3},{8,12},{9,13},{10,... | collective-permute-start | bytes 3932168 | tf_op jit(solution)/shard_map/ppermute | solution.py:375
  104.6 42.0 %collective-permute-start.14 = (bf16[320,2048]{1,0:T(8,128)(2,1)S(1)}, bf16[320,2048]{1,0:T(8,128)(2,1)}, u32[]{:S(2)}, u32[]{:S(2)}) collective-permute-start(bf16[320,2048]{1,0:T(8,128)(2,1)S(1)} %maximum_select_fusion.refs_0_), channel_id=1, source_target_pairs={{0,1},{1,0},{2,3},{3,2},{4,5},{5,4},{6,7},{7,6},{8,9},{9,8},{10,11... | collective-permute-start | bytes 3932168 | tf_op jit(solution)/shard_map/ppermute | solution.py:375
  106.4 39.8 %collective-permute-start.15 = (bf16[256,2048]{1,0:T(8,128)(2,1)}, bf16[256,2048]{1,0:T(8,128)(2,1)}, u32[]{:S(2)}, u32[]{:S(2)}) collective-permute-start(bf16[256,2048]{1,0:T(8,128)(2,1)} %get-tuple-element.159.refs_0_), channel_id=1, source_target_pairs={{0,8},{8,16},{16,24},{24,0},{1,9},{9,17},{17,25},{25,1},{2,10},{10... | collective-permute-start | bytes 3145736 | tf_op jit(solution)/shard_map/ppermute | solution.py:370
  146.2 34.8 %collective-permute-start.20 = (bf16[256,2048]{1,0:T(8,128)(2,1)}, bf16[256,2048]{1,0:T(8,128)(2,1)}, u32[]{:S(2)}, u32[]{:S(2)}) collective-permute-start(bf16[256,2048]{1,0:T(8,128)(2,1)} %collective-permute-done.15.refs_1_), channel_id=1, source_target_pairs={{0,8},{8,16},{16,24},{24,0},{1,9},{9,17},{17,25},{25,1},{2,10},{10... | collective-permute-start | bytes 3145736 | tf_op jit(solution)/shard_map/ppermute | solution.py:370
  146.7 20.3 %collective-permute-start.18 = (bf16[320,2048]{1,0:T(8,128)(2,1)S(1)}, bf16[320,2048]{1,0:T(8,128)(2,1)S(1)}, u32[]{:S(2)}, u32[]{:S(2)}) collective-permute-start(bf16[320,2048]{1,0:T(8,128)(2,1)S(1)} %collective-permute-done.12.refs_1_), channel_id=1, source_target_pairs={{0,1},{1,0},{2,3},{3,2},{4,5},{5,4},{6,7},{7,6},{8,9},{9,8},{10,11... | collective-permute-start | bytes 3932168 | tf_op jit(solution)/shard_map/ppermute | solution.py:375
  148.4 19.6 %collective-permute-start.19 = (bf16[320,2048]{1,0:T(8,128)(2,1)}, bf16[320,2048]{1,0:T(8,128)(2,1)S(1)}, u32[]{:S(2)}, u32[]{:S(2)}) collective-permute-start(bf16[320,2048]{1,0:T(8,128)(2,1)} %collective-permute-done.13.refs_2_), channel_id=1, source_target_pairs={{0,1},{1,0},{2,3},{3,2},{4,5},{5,4},{6,7},{7,6},{8,9},{9,8},{10,11... | collective-permute-start | bytes 3932168 | tf_op jit(solution)/shard_map/ppermute | solution.py:375
  181.0 28.1 %collective-permute-start.24 = (bf16[256,2048]{1,0:T(8,128)(2,1)}, bf16[256,2048]{1,0:T(8,128)(2,1)S(1)}, u32[]{:S(2)}, u32[]{:S(2)}) collective-permute-start(bf16[256,2048]{1,0:T(8,128)(2,1)} %collective-permute-done.20.refs_2_), channel_id=1, source_target_pairs={{0,8},{8,16},{16,24},{24,0},{1,9},{9,17},{17,25},{25,1},{2,10},{10... | collective-permute-start | bytes 3145736 | tf_op jit(solution)/shard_map/ppermute | solution.py:370
  193.7 37.0 %collective-permute-start.23 = (bf16[256,2048]{1,0:T(8,128)(2,1)}, bf16[256,2048]{1,0:T(8,128)(2,1)}, u32[]{:S(2)}, u32[]{:S(2)}) collective-permute-start(bf16[256,2048]{1,0:T(8,128)(2,1)} %pad_maximum_fusion.4), channel_id=1, source_target_pairs={{0,8},{8,16},{16,24},{24,0},{1,9},{9,17},{17,25},{25,1},{2,10},{10... | collective-permute-start | bytes 3145736 | tf_op jit(solution)/shard_map/ppermute | solution.py:370
  232.3 35.9 %collective-permute-start.25 = (bf16[256,2048]{1,0:T(8,128)(2,1)S(1)}, bf16[256,2048]{1,0:T(8,128)(2,1)S(1)}, u32[]{:S(2)}, u32[]{:S(2)}) collective-permute-start(bf16[256,2048]{1,0:T(8,128)(2,1)S(1)} %fusion.27), channel_id=1, source_target_pairs={{0,8},{8,16},{16,24},{24,0},{1,9},{9,17},{17,25},{25,1},{2,10},{10... | collective-permute-start | bytes 3145736 | tf_op jit(solution)/shard_map/ppermute | solution.py:370
  269.5 26.5 %collective-permute-start.26 = (bf16[256,2048]{1,0:T(8,128)(2,1)}, bf16[256,2048]{1,0:T(8,128)(2,1)}, u32[]{:S(2)}, u32[]{:S(2)}) collective-permute-start(bf16[256,2048]{1,0:T(8,128)(2,1)} %fusion.26), channel_id=1, source_target_pairs={{0,8},{8,16},{16,24},{24,0},{1,9},{9,17},{17,25},{25,1},{2,10},{10... | collective-permute-start | bytes 3145736 | tf_op jit(solution)/shard_map/ppermute | solution.py:370
  311.3 39.8 %collective-permute-start.27 = (bf16[1280,2048]{1,0:T(8,128)(2,1)S(1)}, bf16[1280,2048]{1,0:T(8,128)(2,1)}, u32[]{:S(2)}, u32[]{:S(2)}) collective-permute-start(bf16[1280,2048]{1,0:T(8,128)(2,1)S(1)} %get-tuple-element.176), channel_id=1, source_target_pairs={{0,1},{1,0},{2,3},{3,2},{4,5},{5,4},{6,7},{7,6},{8,9},{9,8},{10,11... | collective-permute-start | bytes 15728648 | tf_op jit(solution)/shard_map/ppermute | solution.py:375
  318.4 26.9 %collective-permute-start.28 = (bf16[256,2048]{1,0:T(8,128)(2,1)}, bf16[256,2048]{1,0:T(8,128)(2,1)}, u32[]{:S(2)}, u32[]{:S(2)}) collective-permute-start(bf16[256,2048]{1,0:T(8,128)(2,1)} %pad_maximum_fusion.5), channel_id=1, source_target_pairs={{0,8},{8,16},{16,24},{24,0},{1,9},{9,17},{17,25},{25,1},{2,10},{10... | collective-permute-start | bytes 3145736 | tf_op jit(solution)/shard_map/ppermute | solution.py:370
  330.7 59.5 %collective-permute-start.29 = (bf16[1024,2048]{1,0:T(8,128)(2,1)}, bf16[1024,2048]{1,0:T(8,128)(2,1)S(1)}, u32[]{:S(2)}, u32[]{:S(2)}) collective-permute-start(bf16[1024,2048]{1,0:T(8,128)(2,1)} %convolution_convert_fusion.4), channel_id=1, source_target_pairs={{0,1},{1,0},{2,3},{3,2},{4,5},{5,4},{6,7},{7,6},{8,9},{9,8},{10,11... | collective-permute-start | bytes 12582920 | tf_op jit(solution)/shard_map/ppermute | solution.py:375
  347.9 25.5 %collective-permute-start.32 = (bf16[256,2048]{1,0:T(8,128)(2,1)}, bf16[256,2048]{1,0:T(8,128)(2,1)S(1)}, u32[]{:S(2)}, u32[]{:S(2)}) collective-permute-start(bf16[256,2048]{1,0:T(8,128)(2,1)} %fusion.28), channel_id=1, source_target_pairs={{0,8},{8,16},{16,24},{24,0},{1,9},{9,17},{17,25},{25,1},{2,10},{10... | collective-permute-start | bytes 3145736 | tf_op jit(solution)/shard_map/ppermute | solution.py:370
  365.0 99.7 %collective-permute-start.38 = (bf16[1024,1536]{1,0:T(8,128)(2,1)}, bf16[1024,1536]{1,0:T(8,128)(2,1)}, u32[]{:S(2)}, u32[]{:S(2)}) collective-permute-start(bf16[1024,1536]{1,0:T(8,128)(2,1)} %convolution_convert_fusion.2), channel_id=1, source_target_pairs={{0,1},{1,0},{2,3},{3,2},{4,5},{5,4},{6,7},{7,6},{8,9},{9,8},{10,11... | collective-permute-start | bytes 9437192 | tf_op jit(solution)/shard_map/ppermute | solution.py:375
  373.7 24.6 %collective-permute-start.37 = (bf16[256,2048]{1,0:T(8,128)(2,1)S(1)}, bf16[256,2048]{1,0:T(8,128)(2,1)S(1)}, u32[]{:S(2)}, u32[]{:S(2)}) collective-permute-start(bf16[256,2048]{1,0:T(8,128)(2,1)S(1)} %fusion.29), channel_id=1, source_target_pairs={{0,8},{8,16},{16,24},{24,0},{1,9},{9,17},{17,25},{25,1},{2,10},{10... | collective-permute-start | bytes 3145736 | tf_op jit(solution)/shard_map/ppermute | solution.py:370
  390.6 41.7 %collective-permute-start.33 = (bf16[128,2048]{1,0:T(8,128)(2,1)S(1)}, bf16[128,2048]{1,0:T(8,128)(2,1)S(1)}, u32[]{:S(2)}, u32[]{:S(2)}) collective-permute-start(bf16[128,2048]{1,0:T(8,128)(2,1)S(1)} %get-tuple-element.275), channel_id=1, source_target_pairs={{0,4},{1,5},{2,6},{3,7},{4,0},{5,1},{6,2},{7,3},{8,12},{9,13},{10,... | collective-permute-start | bytes 1572872 | tf_op jit(solution)/shard_map/ppermute | solution.py:375
  392.4 40.7 %collective-permute-start.34 = (bf16[128,2048]{1,0:T(8,128)(2,1)S(1)}, bf16[128,2048]{1,0:T(8,128)(2,1)}, u32[]{:S(2)}, u32[]{:S(2)}) collective-permute-start(bf16[128,2048]{1,0:T(8,128)(2,1)S(1)} %get-tuple-element.274), channel_id=1, source_target_pairs={{0,2},{1,3},{2,0},{3,1},{4,6},{5,7},{6,4},{7,5},{8,10},{9,11},{10,... | collective-permute-start | bytes 1572872 | tf_op jit(solution)/shard_map/ppermute | solution.py:375
  396.7 33.4 %collective-permute-start.35 = (bf16[320,2048]{1,0:T(8,128)(2,1)S(1)}, bf16[320,2048]{1,0:T(8,128)(2,1)S(1)}, u32[]{:S(2)}, u32[]{:S(2)}) collective-permute-start(bf16[320,2048]{1,0:T(8,128)(2,1)S(1)} %pad_maximum_fusion.1), channel_id=1, source_target_pairs={{0,2},{1,3},{2,0},{3,1},{4,6},{5,7},{6,4},{7,5},{8,10},{9,11},{10,... | collective-permute-start | bytes 3932168 | tf_op jit(solution)/shard_map/ppermute | solution.py:375
  398.3 31.8 %collective-permute-start.36 = (bf16[320,2048]{1,0:T(8,128)(2,1)S(1)}, bf16[320,2048]{1,0:T(8,128)(2,1)S(1)}, u32[]{:S(2)}, u32[]{:S(2)}) collective-permute-start(bf16[320,2048]{1,0:T(8,128)(2,1)S(1)} %pad_maximum_fusion.2), channel_id=1, source_target_pairs={{0,4},{1,5},{2,6},{3,7},{4,0},{5,1},{6,2},{7,3},{8,12},{9,13},{10,... | collective-permute-start | bytes 3932168 | tf_op jit(solution)/shard_map/ppermute | solution.py:375
  435.6 29.2 %collective-permute-start.39 = (bf16[320,2048]{1,0:T(8,128)(2,1)}, bf16[320,2048]{1,0:T(8,128)(2,1)S(1)}, u32[]{:S(2)}, u32[]{:S(2)}) collective-permute-start(bf16[320,2048]{1,0:T(8,128)(2,1)} %get-tuple-element.303), channel_id=1, source_target_pairs={{0,8},{8,16},{16,24},{24,0},{1,9},{9,17},{17,25},{25,1},{2,10},{10... | collective-permute-start | bytes 3932168 | tf_op jit(solution)/shard_map/ppermute | solution.py:370
  442.3 25.0 %collective-permute-start.43 = (bf16[256,2048]{1,0:T(8,128)(2,1)}, bf16[256,2048]{1,0:T(8,128)(2,1)}, u32[]{:S(2)}, u32[]{:S(2)}) collective-permute-start(bf16[256,2048]{1,0:T(8,128)(2,1)} %pad_maximum_fusion.6), channel_id=1, source_target_pairs={{0,2},{1,3},{2,0},{3,1},{4,6},{5,7},{6,4},{7,5},{8,10},{9,11},{10,... | collective-permute-start | bytes 3145736 | tf_op jit(solution)/shard_map/ppermute | solution.py:375
  444.5 23.9 %collective-permute-start.44 = (bf16[256,2048]{1,0:T(8,128)(2,1)}, bf16[256,2048]{1,0:T(8,128)(2,1)}, u32[]{:S(2)}, u32[]{:S(2)}) collective-permute-start(bf16[256,2048]{1,0:T(8,128)(2,1)} %pad_maximum_fusion.7), channel_id=1, source_target_pairs={{0,4},{1,5},{2,6},{3,7},{4,0},{5,1},{6,2},{7,3},{8,12},{9,13},{10,... | collective-permute-start | bytes 3145736 | tf_op jit(solution)/shard_map/ppermute | solution.py:375
  464.7 33.5 %collective-permute-start.42 = (bf16[320,2048]{1,0:T(8,128)(2,1)S(1)}, bf16[320,2048]{1,0:T(8,128)(2,1)S(1)}, u32[]{:S(2)}, u32[]{:S(2)}) collective-permute-start(bf16[320,2048]{1,0:T(8,128)(2,1)S(1)} %collective-permute-done.39), channel_id=1, source_target_pairs={{0,8},{8,16},{16,24},{24,0},{1,9},{9,17},{17,25},{25,1},{2,10},{10... | collective-permute-start | bytes 3932168 | tf_op jit(solution)/shard_map/ppermute | solution.py:370
  464.7 48.7 %collective-permute-start.49 = (f32[20480]{0:T(1024)S(1)}, f32[20480]{0:T(1024)S(1)}, u32[]{:S(2)}, u32[]{:S(2)}) collective-permute-start(f32[20480]{0:T(1024)S(1)} %concatenate.134), channel_id=1, source_target_pairs={{0,1},{1,0},{2,3},{3,2},{4,5},{5,4},{6,7},{7,6},{8,9},{9,8},{10,11... | collective-permute-start | bytes 245768 | tf_op jit(solution)/shard_map/ppermute | solution.py:375
  466.3 32.0 %collective-permute-start.40 = (bf16[128,1536]{1,0:T(8,128)(2,1)S(1)}, bf16[128,1536]{1,0:T(8,128)(2,1)S(1)}, u32[]{:S(2)}, u32[]{:S(2)}) collective-permute-start(bf16[128,1536]{1,0:T(8,128)(2,1)S(1)} %get-tuple-element.299), channel_id=1, source_target_pairs={{0,4},{1,5},{2,6},{3,7},{4,0},{5,1},{6,2},{7,3},{8,12},{9,13},{10,... | collective-permute-start | bytes 1179656 | tf_op jit(solution)/shard_map/ppermute | solution.py:375
  467.3 31.0 %collective-permute-start.41 = (bf16[128,1536]{1,0:T(8,128)(2,1)S(1)}, bf16[128,1536]{1,0:T(8,128)(2,1)S(1)}, u32[]{:S(2)}, u32[]{:S(2)}) collective-permute-start(bf16[128,1536]{1,0:T(8,128)(2,1)S(1)} %get-tuple-element.298), channel_id=1, source_target_pairs={{0,2},{1,3},{2,0},{3,1},{4,6},{5,7},{6,4},{7,5},{8,10},{9,11},{10,... | collective-permute-start | bytes 1179656 | tf_op jit(solution)/shard_map/ppermute | solution.py:375
  471.3 49.4 %collective-permute-start.48 = (bf16[256,2048]{1,0:T(8,128)(2,1)S(1)}, bf16[256,2048]{1,0:T(8,128)(2,1)S(1)}, u32[]{:S(2)}, u32[]{:S(2)}) collective-permute-start(bf16[256,2048]{1,0:T(8,128)(2,1)S(1)} %pad_maximum_fusion.8.refs_0_), channel_id=1, source_target_pairs={{0,8},{8,16},{16,24},{24,0},{1,9},{9,17},{17,25},{25,1},{2,10},{10... | collective-permute-start | bytes 3145736 | tf_op jit(solution)/shard_map/ppermute | solution.py:370
  510.4 38.4 %collective-permute-start.52 = (bf16[320,2048]{1,0:T(8,128)(2,1)S(1)}, bf16[320,2048]{1,0:T(8,128)(2,1)S(1)}, u32[]{:S(2)}, u32[]{:S(2)}) collective-permute-start(bf16[320,2048]{1,0:T(8,128)(2,1)S(1)} %collective-permute-done.42), channel_id=1, source_target_pairs={{0,8},{8,16},{16,24},{24,0},{1,9},{9,17},{17,25},{25,1},{2,10},{10... | collective-permute-start | bytes 3932168 | tf_op jit(solution)/shard_map/ppermute | solution.py:370
  520.7 46.0 %collective-permute-start.50 = (bf16[256,2048]{1,0:T(8,128)(2,1)S(1)}, bf16[256,2048]{1,0:T(8,128)(2,1)S(1)}, u32[]{:S(2)}, u32[]{:S(2)}) collective-permute-start(bf16[256,2048]{1,0:T(8,128)(2,1)S(1)} %collective-permute-done.48.refs_1_), channel_id=1, source_target_pairs={{0,8},{8,16},{16,24},{24,0},{1,9},{9,17},{17,25},{25,1},{2,10},{10... | collective-permute-start | bytes 3145736 | tf_op jit(solution)/shard_map/ppermute | solution.py:370
  523.5 25.3 %collective-permute-start.51 = (f32[20480]{0:T(1024)S(1)}, f32[20480]{0:T(1024)S(1)}, u32[]{:S(2)}, u32[]{:S(2)}) collective-permute-start(f32[20480]{0:T(1024)S(1)} %add.599), channel_id=1, source_target_pairs={{0,2},{1,3},{2,0},{3,1},{4,6},{5,7},{6,4},{7,5},{8,10},{9,11},{10,... | collective-permute-start | bytes 245768 | tf_op jit(solution)/shard_map/ppermute | solution.py:375
  566.7 27.9 %collective-permute-start.53 = (bf16[256,2048]{1,0:T(8,128)(2,1)S(1)}, bf16[256,2048]{1,0:T(8,128)(2,1)S(1)}, u32[]{:S(2)}, u32[]{:S(2)}) collective-permute-start(bf16[256,2048]{1,0:T(8,128)(2,1)S(1)} %collective-permute-done.50.refs_2_), channel_id=1, source_target_pairs={{0,8},{8,16},{16,24},{24,0},{1,9},{9,17},{17,25},{25,1},{2,10},{10... | collective-permute-start | bytes 3145736 | tf_op jit(solution)/shard_map/ppermute | solution.py:370
  566.8 40.2 %collective-permute-start.47 = (bf16[256,1536]{1,0:T(8,128)(2,1)S(1)}, bf16[256,1536]{1,0:T(8,128)(2,1)S(1)}, u32[]{:S(2)}, u32[]{:S(2)}) collective-permute-start(bf16[256,1536]{1,0:T(8,128)(2,1)S(1)} %pad_maximum_fusion.11.refs_0_), channel_id=1, source_target_pairs={{0,8},{8,16},{16,24},{24,0},{1,9},{9,17},{17,25},{25,1},{2,10},{10... | collective-permute-start | bytes 2359304 | tf_op jit(solution)/shard_map/ppermute | solution.py:370
  623.0 26.6 %collective-permute-start.57 = (bf16[256,1536]{1,0:T(8,128)(2,1)S(1)}, bf16[256,1536]{1,0:T(8,128)(2,1)S(1)}, u32[]{:S(2)}, u32[]{:S(2)}) collective-permute-start(bf16[256,1536]{1,0:T(8,128)(2,1)S(1)} %collective-permute-done.55.refs_2_), channel_id=1, source_target_pairs={{0,8},{8,16},{16,24},{24,0},{1,9},{9,17},{17,25},{25,1},{2,10},{10... | collective-permute-start | bytes 2359304 | tf_op jit(solution)/shard_map/ppermute | solution.py:370
  623.0 23.9 %collective-permute-start.58 = (f32[20480]{0:T(1024)S(1)}, f32[20480]{0:T(1024)S(1)}, u32[]{:S(2)}, u32[]{:S(2)}) collective-permute-start(f32[20480]{0:T(1024)S(1)} %add.618), channel_id=1, source_target_pairs={{0,16},{8,24},{16,0},{24,8},{1,17},{9,25},{17,1},{25,9},{2,18},{10... | collective-permute-start | bytes 245768 | tf_op jit(solution)/shard_map/ppermute | solution.py:375
  (79 other events, 754.0 us)

commit v3 on v2

v3 whole, which is shorter than its diff:
```python
import functools
import math

import jax
import jax.numpy as jnp
from jax import lax
from jax.experimental import pallas as pl
from jax.experimental.pallas import tpu as pltpu
from jax.sharding import PartitionSpec as P

D = 2048
HEADS = 32
HEAD_DIM = 64
ROT_DIM = 32

LN_EPS = 1e-05
NEG_BIG = -1e30
ROPE_BASE = 10000.0
BF = jnp.bfloat16
F32 = jnp.float32
VMEM_BYTES = 56 * 1024 * 1024
HBM_SPEC = pl.BlockSpec(memory_space=pltpu.HBM)


def plan(n_fsdp, n_ctx, cat_rows):
    shard = cat_rows // n_fsdp
    even = True
    att, act = [[] for _ in range(n_ctx)], [[] for _ in range(n_ctx)]
    for f in range(n_fsdp):
        a = min(max(D - shard * f, 0), shard)
        m = shard - a
        if a % (n_ctx * HEAD_DIM) or m % (n_ctx * 16):
            even = False
        for z in range(n_ctx):
            if a:
                att[z].append((shard * f + z * (a // n_ctx), a // n_ctx))
            if m:
                act[z].append((shard * f + a + z * (m // n_ctx), m // n_ctx))
    if not even:
        wide_a, wide_m = D // n_ctx, (cat_rows - D) // n_ctx
        att = [[(z * wide_a, wide_a)] for z in range(n_ctx)]
        act = [[(D + z * wide_m, wide_m)] for z in range(n_ctx)]
    return even, att, act


def in_runs(att, act):
    runs = [(part * D + s, n) for part in range(3) for s, n in att]
    return runs + [(2 * D + s, n) for s, n in act]


def key_order(n):
    return list(range(0, n, 2)) + list(range(1, n, 2))


def pick_kernel(all_runs, z_ref, src_ref, dst_ref):
    for z, runs in enumerate(all_runs):

        @pl.when(z_ref[0] == z)
        def _():
            at = 0
            for start, size in runs:
                dst_ref[:, at : at + size] = src_ref[:, start : start + size]
                at += size


def pick_columns(src, z, all_runs):
    rows, cols = src.shape
    width = sum(n for _, n in all_runs[0])
    step = min(rows, 64)
    return pl.pallas_call(
        functools.partial(pick_kernel, all_runs),
        grid_spec=pltpu.PrefetchScalarGridSpec(
            num_scalar_prefetch=1,
            grid=(rows // step,),
            in_specs=[pl.BlockSpec((step, cols), lambda i, z_ref: (i, 0))],
            out_specs=pl.BlockSpec((step, width), lambda i, z_ref: (i, 0)),
        ),
        out_shape=jax.ShapeDtypeStruct((rows, width), src.dtype),
        **big("pick_columns", 0, 2 * rows * (cols + width)),
    )(z[None], src)


def spread_kernel(all_runs, n_ctx, z_ref, *refs):
    srcs, dst_ref = refs[:n_ctx], refs[-1]
    for z in range(n_ctx):

        @pl.when(z_ref[0] == z)
        def _():
            for j, src_ref in enumerate(srcs):
                at = 0
                for start, size in all_runs[(z - j) % n_ctx]:
                    dst_ref[:, start : start + size] = src_ref[:, at : at + size].astype(F32)
                    at += size


def spread_columns(whole, parts, z, all_runs, cols, first, width_out):
    rows, width = parts[0].shape
    n_ctx = len(parts)
    step = min(rows, 64)
    fresh = whole is None
    return pl.pallas_call(
        functools.partial(spread_kernel, all_runs, n_ctx),
        grid_spec=pltpu.PrefetchScalarGridSpec(
            num_scalar_prefetch=1,
            grid=(rows // step,),
            in_specs=[pl.BlockSpec((step, width), lambda i, z_ref: (i, 0))] * n_ctx
            + [pl.BlockSpec(memory_space=pl.ANY)] * (not fresh),
            out_specs=pl.BlockSpec(
                (pl.Element(step), pl.Element(width_out)), lambda i, z_ref: (i * step, first)
            ),
        ),
        out_shape=jax.ShapeDtypeStruct((rows, cols), F32),
        input_output_aliases={} if fresh else {1 + n_ctx: 0},
        **big("spread_columns", 0, rows * width_out * 6),
    )(z[None], *parts, *([] if fresh else [whole]))


def norm_kernel(n_fsdp, f_ref, x_ref, g_ref, gain_ref, beta_ref, out_ref, dy_ref, hold):
    x = x_ref[...]
    centred = x - jnp.mean(x, axis=1, keepdims=True)
    inv_std = lax.rsqrt(jnp.mean(centred * centred, axis=1, keepdims=True) + LN_EPS)
    hold[...] = (centred * inv_std * gain_ref[...] + beta_ref[...]).astype(BF)
    wide = x.shape[1] // n_fsdp
    for p, k in enumerate(key_order(n_fsdp)):
        at = pl.multiple_of((f_ref[0] ^ k) * wide, wide)
        out_ref[:, p * wide : (p + 1) * wide] = hold[:, pl.ds(at, wide)]
    dy_ref[...] = g_ref[...].astype(BF)


def norm(x, g, gain, beta, f, n_fsdp):
    rows, cols = x.shape
    step = min(rows, 64)
    tile = pl.BlockSpec((step, cols), lambda i, f_ref: (i, 0))
    line = pl.BlockSpec((1, cols), lambda i, f_ref: (0, 0))
    own = jax.ShapeDtypeStruct((rows, cols), BF)
    return pl.pallas_call(
        functools.partial(norm_kernel, n_fsdp),
        grid_spec=pltpu.PrefetchScalarGridSpec(
            num_scalar_prefetch=1,
            grid=(rows // step,),
            in_specs=[tile, tile, line, line],
            out_specs=[tile, tile],
            scratch_shapes=[pltpu.VMEM((step, cols), BF)],
        ),
        out_shape=[own, own],
        **big("norm", 0, 12 * rows * cols),
    )(f[None], x, g, gain[None], beta[None])


def turn(u, c, s_up, s_down):
    half_rot = ROT_DIM // 2
    wide = u.shape[1]
    return (
        u * c
        + pltpu.roll(u, half_rot, 1) * s_up
        + pltpu.roll(u, wide - half_rot, 1) * s_down
    )


def dot(a, b, ca, cb):
    return lax.dot_general(a, b, (((ca,), (cb,)), ((), ())), preferred_element_type=F32)


def causal(size, keys, first):
    key_at = lax.broadcasted_iota(jnp.int32, (keys, size), 0)
    query_at = lax.broadcasted_iota(jnp.int32, (keys, size), 1) + first
    return key_at <= query_at


def att_kernel(q_ref, k_ref, v_ref, c_ref, u_ref, d_ref, qb_ref, kb_ref, vb_ref, att_ref, lse_ref):
    seq = q_ref.shape[0]
    size = math.gcd(seq, 256)
    c, su, sd = c_ref[...], u_ref[...], d_ref[...]
    qb_ref[...] = turn(q_ref[...], c, su, sd).astype(BF)
    kb_ref[...] = turn(k_ref[...], c, su, sd).astype(BF)
    vb_ref[...] = v_ref[...].astype(BF)
    scale = 1.0 / math.sqrt(HEAD_DIM)
    for i in range(seq // size):
        rows = slice(i * size, (i + 1) * size)
        keys = (i + 1) * size
        outs = []
        for h in range(2):
            lanes = slice(h * HEAD_DIM, (h + 1) * HEAD_DIM)
            s = dot(kb_ref[:keys, lanes], qb_ref[rows, lanes], 1, 1) * scale
            s = jnp.where(causal(size, keys, i * size), s, NEG_BIG)
            top = jnp.max(s, axis=0, keepdims=True)
            e = jnp.exp(s - top)
            total = jnp.sum(e, axis=0, keepdims=True)
            lse_ref[0, h : h + 1, rows] = top + jnp.log(total)
            p = (e * (1.0 / total)).astype(BF)
            outs.append(dot(p, vb_ref[:keys, lanes], 0, 0))
        att_ref[rows, :] = jnp.concatenate(outs, axis=1).astype(BF)


def attention(project, tables, n_heads, cat_width):
    seq = project.shape[0]
    pairs = n_heads // 2
    wide = 2 * HEAD_DIM

    def col(base):
        return pl.BlockSpec((seq, wide), lambda p: (0, base + p))

    table = pl.BlockSpec((seq, wide), lambda p: (0, 0))
    own = jax.ShapeDtypeStruct((seq, n_heads * HEAD_DIM), BF)
    return pl.pallas_call(
        att_kernel,
        grid=(pairs,),
        in_specs=[col(0), col(pairs), col(2 * pairs), table, table, table],
        out_specs=[col(0)] * 4 + [pl.BlockSpec((1, 2, seq), lambda p: (p, 0, 0))],
        out_shape=[own] * 3
        + [
            jax.ShapeDtypeStruct((seq, cat_width), BF),
            jax.ShapeDtypeStruct((pairs, 2, seq), F32),
        ],
        **big("attention", n_heads * seq * seq * 256, seq * n_heads * 64 * 20),
    )(project, project, project, *tables)


def back_kernel(
    pairs, q_ref, k_ref, v_ref, att_ref, datt_ref, lse_ref, c_ref, u_ref, d_ref, dproj_in,
    dproj_ref, sq_ref, sk_ref, sv_ref, aq, ak, av, hold, sems,
):
    del dproj_in
    seq = q_ref.shape[0]
    size = math.gcd(seq, 256)
    scale = 1.0 / math.sqrt(HEAD_DIM)
    ak[...] = jnp.zeros_like(ak)
    av[...] = jnp.zeros_like(av)
    for i in range(seq // size):
        rows = slice(i * size, (i + 1) * size)
        keys = (i + 1) * size
        dqs, dks, dvs = [], [], []
        prod = datt_ref[rows, :].astype(F32) * att_ref[rows, :].astype(F32)
        prod_t = prod.T
        for h in range(2):
            lanes = slice(h * HEAD_DIM, (h + 1) * HEAD_DIM)
            q, do = q_ref[rows, lanes], datt_ref[rows, lanes]
            k, v = k_ref[:keys, lanes], v_ref[:keys, lanes]
            delta = jnp.sum(prod_t[lanes, :], axis=0, keepdims=True)
            s = dot(k, q, 1, 1) * scale
            s = jnp.where(causal(size, keys, i * size), s, NEG_BIG)
            p = jnp.exp(s - lse_ref[0, h : h + 1, rows])
            dp = dot(v, do, 1, 1)
            ds = (p * (dp - delta) * scale).astype(BF)
            dvs.append(dot(p.astype(BF), do, 1, 0))
            dks.append(dot(ds, q, 1, 0))
            dqs.append(dot(ds, k, 0, 0))
        av[:keys, :] += jnp.concatenate(dvs, axis=1)
        ak[:keys, :] += jnp.concatenate(dks, axis=1)
        aq[rows, :] = jnp.concatenate(dqs, axis=1)
    wide = q_ref.shape[1]
    copies = []
    for i, (acc, total) in enumerate(((aq, sq_ref), (ak, sk_ref), (av, sv_ref))):
        g = acc[...]
        if i < 2:
            g = turn(g, c_ref[...], -u_ref[...], -d_ref[...])
        hold[i] = g.astype(BF)
        total[...] = jnp.sum(g, axis=0, keepdims=True)
        at = pl.multiple_of((i * pairs + pl.program_id(0)) * wide, wide)
        copies.append(
            pltpu.make_async_copy(hold.at[i], dproj_ref.at[:, pl.ds(at, wide)], sems.at[i])
        )
        copies[-1].start()
    for copy in copies:
        copy.wait()


def attention_back(q, k, v, cat, d_att, lse, tables, d_proj, n_heads):
    seq = q.shape[0]
    pairs = n_heads // 2
    wide = 2 * HEAD_DIM
    col = pl.BlockSpec((seq, wide), lambda p: (0, p))
    table = pl.BlockSpec((seq, wide), lambda p: (0, 0))
    line = pl.BlockSpec((1, wide), lambda p: (0, p))
    return pl.pallas_call(
        functools.partial(back_kernel, pairs),
        grid=(pairs,),
        in_specs=[col] * 5
        + [pl.BlockSpec((1, 2, seq), lambda p: (p, 0, 0))]
        + [table] * 3
        + [HBM_SPEC],
        out_specs=[HBM_SPEC] + [line] * 3,
        out_shape=[jax.ShapeDtypeStruct(d_proj.shape, BF)]
        + [jax.ShapeDtypeStruct((1, n_heads * HEAD_DIM), F32)] * 3,
        input_output_aliases={9: 0},
        scratch_shapes=[pltpu.VMEM((seq, wide), F32)] * 3
        + [pltpu.VMEM((3, seq, wide), BF), pltpu.SemaphoreType.DMA((3,))],
        **big("attention_back", n_heads * seq * seq * 640, seq * n_heads * 64 * 16),
    )(q, k, v, cat, d_att, lse, *tables, d_proj)


def grads_kernel(n_split, f_ref, left_ref, right_ref, *refs):
    outs, left_t = refs[:-1], refs[-1]

    @pl.when(pl.program_id(0) == 0)
    def _():
        left_t[...] = left_ref[...].T

    g = dot(left_t[...], right_ref[...], 1, 0).astype(BF)
    if len(outs) == 1:
        outs[0][...] = g
        return
    rows = g.shape[0] // n_split
    for s in range(n_split):
        key = lax.bitwise_xor(f_ref[0], s)
        at = pl.ds(pl.multiple_of(lax.shift_right_logical(key, 1) * rows, 16), rows)
        for i, out in enumerate(outs):

            @pl.when(lax.bitwise_and(key, 1) == 1 - i)
            def _():
                out[at, :] = g[s * rows : (s + 1) * rows]


def grads(left, block, wide, right, first, width, f, n_split=None):
    rows = left.shape[0]
    tile = math.gcd(512, math.gcd(width, first) if first else width)
    n_out = 2 if n_split else 1
    return pl.pallas_call(
        functools.partial(grads_kernel, n_split),
        grid_spec=pltpu.PrefetchScalarGridSpec(
            num_scalar_prefetch=1,
            grid=(width // tile,),
            in_specs=[
                pl.BlockSpec((rows, wide), lambda i, f_ref: (0, block)),
                pl.BlockSpec((rows, tile), lambda i, f_ref: (0, first // tile + i)),
            ],
            out_specs=[pl.BlockSpec((wide // n_out, tile), lambda i, f_ref: (0, i))] * n_out,
            scratch_shapes=[pltpu.VMEM((wide, rows), BF)],
        ),
        out_shape=[jax.ShapeDtypeStruct((wide // n_out, width), BF)] * n_out,
        **big("grads", 2 * rows * wide * width, 2 * rows * (wide + width) + 2 * wide * width),
    )(f[None], left, right)


def chunks(rows):
    step = math.gcd(rows, 256)
    return [slice(at, at + step) for at in range(0, rows, step)]


def gelu_parts(u):
    c = math.sqrt(2.0 / math.pi)
    square = u * u
    t = jnp.tanh(c * (u + 0.044715 * u * square))
    value = 0.5 * u * (1.0 + t)
    slope = 0.5 * (1.0 + t) + 0.5 * u * (1.0 - t * t) * (c * (1.0 + 3 * 0.044715 * square))
    return value, slope


def cost(flops, nbytes):
    return pl.CostEstimate(flops=flops, bytes_accessed=nbytes, transcendentals=0)


def big(name_of, flops, nbytes):
    return {
        "compiler_params": pltpu.CompilerParams(vmem_limit_bytes=VMEM_BYTES),
        "cost_estimate": cost(flops // 8, nbytes // 8),
        "name": name_of,
    }


def lay(parts, cuts, at_ref, base, dst):
    for c, (i, start, size) in enumerate(cuts):
        at = pl.multiple_of(at_ref[base + c], 16)
        dst[pl.ds(at, size), :] = parts[i][start : start + size, :]


def qkv_kernel(x_cuts, n_x, w_cuts, n_w, at_ref, *refs):
    xs, ws, b_ref = refs[:n_x], refs[n_x : n_x + n_w], refs[n_x + n_w]
    out_ref, x_ref, w_ref = refs[n_x + n_w + 1 :]

    @pl.when(pl.program_id(0) == 0)
    def _():
        lay(xs, x_cuts, at_ref, 0, x_ref)

    lay(ws, w_cuts, at_ref, len(x_cuts), w_ref)
    out_ref[...] = dot(x_ref[...], w_ref[...], 1, 0) + b_ref[...]


def qkv_project(xs, x_cuts, ws, w_cuts, places, b, rows, width, tile):
    deep, full = xs[0].shape[1], ws[0].shape[1]
    return pl.pallas_call(
        functools.partial(qkv_kernel, x_cuts, len(xs), w_cuts, len(ws)),
        grid_spec=pltpu.PrefetchScalarGridSpec(
            num_scalar_prefetch=1,
            grid=(width // tile,),
            in_specs=[pl.BlockSpec(x.shape, lambda i, at: (0, 0)) for x in xs]
            + [pl.BlockSpec((w.shape[0], tile), lambda i, at: (0, i)) for w in ws]
            + [pl.BlockSpec((1, tile), lambda i, at: (0, i))],
            out_specs=[
                pl.BlockSpec((rows, tile), lambda i, at: (0, i)),
                pl.BlockSpec((rows, deep), lambda i, at: (0, 0)),
                pl.BlockSpec((deep, tile), lambda i, at: (0, i)),
            ],
        ),
        out_shape=[
            jax.ShapeDtypeStruct((rows, width), F32),
            jax.ShapeDtypeStruct((rows, deep), BF),
            jax.ShapeDtypeStruct((deep, full), BF),
        ],
        **big("qkv_project", 2 * rows * deep * width, 2 * deep * (rows + width) + 4 * rows * width),
    )(places, *xs, *ws, b)


def pre_kernel(w_cuts, n_w, at_ref, x_ref, *refs):
    ws, b_ref = refs[:n_w], refs[n_w]
    slope_ref, cat_ref, w_ref = refs[-3:]
    lay(ws, w_cuts, at_ref, 0, w_ref)
    for rows in chunks(x_ref.shape[0]):
        pre = dot(x_ref[rows, :], w_ref[...], 1, 0) + b_ref[...]
        value, slope = gelu_parts(pre)
        slope_ref[rows, :] = slope
        cat_ref[rows, :] = value.astype(BF)


def pre_project(x, ws, w_cuts, places, b, cat, w_all, skip, tile):
    rows, deep = x.shape
    width = w_all.shape[1] - skip
    first, cat_first = skip // tile, (cat.shape[1] - width) // tile
    n_w = len(ws)
    return pl.pallas_call(
        functools.partial(pre_kernel, w_cuts, n_w),
        grid_spec=pltpu.PrefetchScalarGridSpec(
            num_scalar_prefetch=1,
            grid=(width // tile,),
            in_specs=[pl.BlockSpec((rows, deep), lambda i, at: (0, 0))]
            + [pl.BlockSpec((w.shape[0], tile), lambda i, at: (0, first + i)) for w in ws]
            + [pl.BlockSpec((1, tile), lambda i, at: (0, first + i))]
            + [pl.BlockSpec(memory_space=pl.ANY)] * 2,
            out_specs=[
                pl.BlockSpec((rows, tile), lambda i, at: (0, i)),
                pl.BlockSpec((rows, tile), lambda i, at: (0, cat_first + i)),
                pl.BlockSpec((deep, tile), lambda i, at: (0, first + i)),
            ],
        ),
        out_shape=[
            jax.ShapeDtypeStruct((rows, width), F32),
            jax.ShapeDtypeStruct(cat.shape, BF),
            jax.ShapeDtypeStruct(w_all.shape, BF),
        ],
        input_output_aliases={3 + n_w: 1, 4 + n_w: 2},
        **big("pre_project", 2 * rows * deep * width, 2 * deep * (rows + width) + 6 * rows * width),
    )(places, x, *ws, b, cat, w_all)


def give_shares(at_ref, acc, outs, per, blk_size):
    for j, out in enumerate(outs):
        for i in range(per):
            at = pl.multiple_of(at_ref[j * per + i], blk_size)
            out[i * blk_size : (i + 1) * blk_size, :] = acc[pl.ds(at, blk_size), :].astype(out.dtype)


def share_shapes(n_ctx, own, width):
    ups, downs = reach(n_ctx)
    kinds = [BF if j in (n_ctx - ups, downs) and j else F32 for j in range(n_ctx)]
    return [jax.ShapeDtypeStruct((own, width), kind) for kind in kinds]


def out_kernel(w_cuts, n_w, n_ctx, per, blk_size, at_ref, x_ref, *refs):
    ws, outs, w_ref, acc = refs[:n_w], refs[n_w : n_w + n_ctx], refs[-2], refs[-1]
    lay(ws, w_cuts, at_ref, n_ctx * per, w_ref)
    acc[...] = dot(x_ref[...], w_ref[...], 1, 0)
    give_shares(at_ref, acc, outs, per, blk_size)


def out_shares_of(x, ws, w_cuts, places, n_rows, n_ctx, blk_size):
    rows, deep = x.shape
    width = ws[0].shape[1]
    tile = min(512, width)
    per = n_rows // n_ctx
    own = rows // n_ctx
    col = pl.BlockSpec((own, tile), lambda i, at: (0, i))
    return pl.pallas_call(
        functools.partial(out_kernel, w_cuts, len(ws), n_ctx, per, blk_size),
        grid_spec=pltpu.PrefetchScalarGridSpec(
            num_scalar_prefetch=1,
            grid=(width // tile,),
            in_specs=[pl.BlockSpec((rows, deep), lambda i, at: (0, 0))]
            + [pl.BlockSpec((w.shape[0], tile), lambda i, at: (0, i)) for w in ws],
            out_specs=[col] * n_ctx + [pl.BlockSpec((deep, tile), lambda i, at: (0, i))],
            scratch_shapes=[pltpu.VMEM((rows, tile), F32)],
        ),
        out_shape=share_shapes(n_ctx, own, width) + [jax.ShapeDtypeStruct((deep, width), BF)],
        **big("out_shares", 2 * rows * deep * width, 2 * deep * (rows + width) + 3 * rows * width),
    )(places, x, *ws)


def norm_share_kernel(n_ctx, per, blk_size, at_ref, x_ref, w_ref, *refs):
    refs[-1][...] = dot(x_ref[...], w_ref[...], 1, 1)
    give_shares(at_ref, refs[-1], refs[:-1], per, blk_size)


def norm_shares_of(x, w, row_places, n_ctx, blk_size):
    rows, deep = x.shape
    width = w.shape[0]
    tile = min(256, width)
    per = row_places.shape[0] // n_ctx
    own = rows // n_ctx
    return pl.pallas_call(
        functools.partial(norm_share_kernel, n_ctx, per, blk_size),
        grid_spec=pltpu.PrefetchScalarGridSpec(
            num_scalar_prefetch=1,
            grid=(width // tile,),
            in_specs=[
                pl.BlockSpec((rows, deep), lambda i, at: (0, 0)),
                pl.BlockSpec((tile, deep), lambda i, at: (i, 0)),
            ],
            out_specs=[pl.BlockSpec((own, tile), lambda i, at: (0, i))] * n_ctx,
            scratch_shapes=[pltpu.VMEM((rows, tile), F32)],
        ),
        out_shape=share_shapes(n_ctx, own, width),
        **big("norm_shares", 2 * rows * deep * width, 2 * deep * (rows + width) + 3 * rows * width),
    )(row_places, x, w)


def d_cat_kernel(cuts, at_ref, g_ref, w_ref, slope_ref, datt_ref, dproj_ref, sum_ref, x_ref):
    @pl.when(pl.program_id(0) == 0)
    def _():
        lay([g_ref], cuts, at_ref, 0, x_ref)
        datt_ref[...] = dot(x_ref[...], w_ref[...], 1, 1).astype(BF)

    @pl.when(pl.program_id(0) > 0)
    def _():
        total = 0.0
        for rows in chunks(x_ref.shape[0]):
            d_pre = slope_ref[rows, :] * dot(x_ref[rows, :], w_ref[...], 1, 1)
            dproj_ref[rows, :] = d_pre.astype(BF)
            total = total + jnp.sum(d_pre, axis=0, keepdims=True)
        sum_ref[...] = total


def d_cat_parts(g, cuts, places, w, slope, wide_a):
    rows, deep = g.shape
    width = slope.shape[1]
    tile = wide_a
    total = 3 * wide_a + width

    def col(i):
        return jnp.maximum(i - 1, 0)

    return pl.pallas_call(
        functools.partial(d_cat_kernel, cuts),
        grid_spec=pltpu.PrefetchScalarGridSpec(
            num_scalar_prefetch=1,
            grid=(1 + width // tile,),
            in_specs=[
                pl.BlockSpec((rows, deep), lambda i, at: (0, 0)),
                pl.BlockSpec((tile, deep), lambda i, at: (i, 0)),
                pl.BlockSpec((rows, tile), lambda i, at: (0, col(i))),
            ],
            out_specs=[
                pl.BlockSpec((rows, tile), lambda i, at: (0, 0)),
                pl.BlockSpec((rows, tile), lambda i, at: (0, 3 + col(i))),
                pl.BlockSpec((1, tile), lambda i, at: (0, col(i))),
                pl.BlockSpec((rows, deep), lambda i, at: (0, 0)),
            ],
        ),
        out_shape=[
            jax.ShapeDtypeStruct((rows, tile), BF),
            jax.ShapeDtypeStruct((rows, total), BF),
            jax.ShapeDtypeStruct((1, width), F32),
            jax.ShapeDtypeStruct((rows, deep), BF),
        ],
        **big("d_cat_parts", 2 * rows * deep * (width + tile), 2 * deep * rows + (2 * deep + 6 * rows) * width),
    )(places, g, w, slope)


def after(x, *others):
    return lax.optimization_barrier((x, *others))[0]


def pass_on(x, hops):
    n = lax.axis_size("ctx")
    return lax.ppermute(x, "ctx", [(i, (i + hops) % n) for i in range(n)])


def reach(n):
    return n // 2, n - 1 - n // 2


def swap(x, axis, bit):
    n = lax.axis_size(axis)
    return lax.ppermute(x, axis, [(i, i ^ bit) for i in range(n)])


def near(x, bit):
    return swap(x, "fsdp", bit)


def far_keys(n):
    return sorted((k for k in range(2, n, 2)), key=lambda k: (k.bit_count(), k))


def top_bit(k):
    return 1 << (k.bit_length() - 1)


def low_bit(k):
    return k & -k


def halves(x):
    rows = x.shape[0] // 2
    return [x[:rows], x[rows:]]


class Line:
    def __init__(self):
        self.due = []

    def wait(self, *arrays):
        self.due += list(arrays)

    def tied(self, *xs):
        got = list(lax.optimization_barrier((*xs, *self.due)))[: len(xs)]
        self.due = got[:1]
        return got[0] if len(xs) == 1 else got


def ring_job(part, found):
    n = lax.axis_size("ctx")
    ups, downs = reach(n)
    found[0] = up = down = part
    for hop in range(1, ups + 1):
        if hop <= downs:
            up, down = yield [pass_on(up, 1), pass_on(down, -1)]
            found[n - hop] = down
        else:
            (up,) = yield [pass_on(up, 1)]
        found[hop] = up


def sum_job(parts, found):
    n = lax.axis_size("ctx")
    ups, downs = reach(n)
    up, down = parts[n - ups], parts[downs] if downs else None
    total = parts[0]
    for hop in range(ups):
        send = [pass_on(up.astype(BF), 1)]
        if hop < downs:
            send.append(pass_on(down.astype(BF), -1))
        got = yield send
        left = ups - 1 - hop
        if left:
            up = parts[n - left].astype(F32) + got[0].astype(F32)
        else:
            total = total + got[0].astype(F32)
        if hop < downs:
            left = downs - 1 - hop
            if left:
                down = parts[left].astype(F32) + got[1].astype(F32)
            else:
                total = total + got[1].astype(F32)
    found.append(total)


def total_job(x, found):
    for axis in ("fsdp", "ctx"):
        bit = 1
        while bit < lax.axis_size(axis):
            (got,) = yield [swap(x, axis, bit)]
            x = x + got
            bit *= 2
    found.append(x)


def gather_job(shard, found):
    n = lax.axis_size("fsdp")
    have = {}
    keys = far_keys(n)
    fresh = [(0, None, shard)]
    found.extend(fresh)
    level = 0
    while True:
        level += 1
        send = []
        for k in keys:
            if k.bit_count() != level:
                continue
            if level == 1:
                send.append((k, None, near(shard, k)))
            else:
                for h, bit in ((0, top_bit(k)), (1, low_bit(k))):
                    send.append((k, h, near(have[k ^ bit, h], bit)))
        send += [(k | 1, h, near(x, 1)) for k, h, x in fresh if not k & 1]
        if not send:
            return
        got = yield [x for _, _, x in send]
        fresh = [(k, h, x) for (k, h, _), x in zip(send, got)]
        found.extend(fresh)
        for k, h, x in fresh:
            if not k & 1:
                if h is None:
                    have[k, 0], have[k, 1] = halves(x)
                else:
                    have[k, h] = x


def gather_order(n):
    got = [(0, None)]
    fresh = list(got)
    level = 0
    while True:
        level += 1
        new = []
        for k in far_keys(n):
            if k.bit_count() == level:
                new += [(k, None)] if level == 1 else [(k, 0), (k, 1)]
        new += [(k | 1, h) for k, h in fresh if not k & 1]
        if not new:
            return got
        got += new
        fresh = new


def scatter_job(away, home, found):
    n = lax.axis_size("fsdp")
    (got,) = yield [near(away, 1)]
    home = home() if callable(home) else home
    rows = home.shape[0] // (n // 2)
    hold = {}
    for i, k in enumerate(range(0, n, 2)):
        for h in range(2):
            at = i * rows + h * (rows // 2)
            cut = slice(at, at + rows // 2)
            hold[k, h] = home[cut].astype(F32) + got[cut].astype(F32)
    for level in range(n.bit_length() - 2, 0, -1):
        moves = []
        for k in far_keys(n):
            if k.bit_count() != level:
                continue
            if level > 1:
                for h, bit in ((0, top_bit(k)), (1, low_bit(k))):
                    moves.append((k ^ bit, h, near(hold[k, h].astype(BF), bit)))
            else:
                whole = jnp.concatenate([hold[k, 0], hold[k, 1]], axis=0).astype(BF)
                moves.append((0, None, near(whole, k)))
        got = yield [x for _, _, x in moves]
        for (k, h, _), x in zip(moves, got):
            if h is None:
                for i, part in enumerate(halves(x)):
                    hold[k, i] = hold[k, i] + part.astype(F32)
            else:
                hold[k, h] = hold[k, h] + x.astype(F32)
    found.append(jnp.concatenate([hold[0, 0], hold[0, 1]], axis=0).astype(BF))


class Move:
    def __init__(self, line, job):
        self.line, self.job, self.flight = line, job, next(job)

    def step(self, *more):
        moves = [m for m in (self, *more) if m.flight is not None]
        flights = [x for m in moves for x in m.flight]
        if not moves:
            return
        got = list(lax.optimization_barrier((*flights, *self.line.due)))[: len(flights)]
        self.line.due = list(got)
        for m in moves:
            own, got = got[: len(m.flight)], got[len(m.flight) :]
            try:
                m.flight = m.job.send(own)
            except StopIteration:
                m.flight = None

    def end(self, *more):
        while self.flight is not None:
            self.step(*more)


def gelu_tanh(values):
    return jax.nn.gelu(values, approximate=True)


def rotary_tables(positions):
    seq = positions.shape[0]
    half_rot = ROT_DIM // 2
    expon = jnp.arange(half_rot, dtype=F32) * (2.0 / ROT_DIM)
    freqs = ROPE_BASE ** (-expon)
    angles = positions.astype(F32)[:, None] * freqs[None, :]
    cosine, sine = jnp.cos(angles), jnp.sin(angles)
    zero = jnp.zeros_like(sine)
    rest = jnp.zeros((seq, HEAD_DIM - ROT_DIM), F32)
    c = jnp.concatenate([cosine, cosine, rest + 1.0], axis=1)
    up = jnp.concatenate([zero, sine, rest], axis=1)
    down = jnp.concatenate([-sine, zero, rest], axis=1)
    return tuple(jnp.concatenate([t, t], axis=1) for t in (c, up, down))


def shards(inputs, out_grad, block_order, ln_gain, ln_beta, w_in, b_in, w_out, b_out):
    n_ctx, n_fsdp = lax.axis_size("ctx"), lax.axis_size("fsdp")
    z, f = lax.axis_index("ctx"), lax.axis_index("fsdp")
    seq_in, seq_grad, blk_order = inputs[0], out_grad[0], block_order[0]
    tok_rows = seq_in.shape[0]
    seq_len = tok_rows * n_ctx
    n_blk = blk_order.shape[0]
    blk_size = seq_len // n_blk
    per = n_blk // n_ctx
    wide_d = D // n_fsdp
    shard = w_out.shape[0]
    cat_rows = shard * n_fsdp
    in_cols = w_in.shape[1]
    n_heads = HEADS // n_ctx
    wide_a, wide_m = D // n_ctx, (cat_rows - D) // n_ctx
    even, att_runs, act_runs = plan(n_fsdp, n_ctx, cat_rows)
    z_runs = [in_runs(att_runs[i], act_runs[i]) for i in range(n_ctx)]

    def position_of(k):
        return lax.shift_right_logical(k, 1) + lax.bitwise_and(k, 1) * (n_fsdp // 2)

    rank_places = blk_order * blk_size
    ranks = lax.rem(z - jnp.arange(n_ctx, dtype=jnp.int32) + n_ctx, n_ctx)
    picks = (ranks[:, None] == jnp.arange(n_ctx, dtype=jnp.int32)[None, :]).astype(jnp.int32)
    row_places = jnp.sum(
        picks[:, :, None] * rank_places.reshape(1, n_ctx, per), axis=1, dtype=jnp.int32
    ).reshape(-1)

    line = Line()
    keys_at = {k: p for p, k in enumerate(key_order(n_fsdp))}
    share = shard // n_ctx
    mixed_f = [i for i in range(n_fsdp) if 0 < D - shard * i < shard]
    cut = (D - shard * mixed_f[0]) // n_ctx if mixed_f else share
    cut_m = share - cut
    is_mixed = (f == mixed_f[0]) if mixed_f else False

    def own_rows(whole):
        first = lax.dynamic_slice_in_dim(whole, z * share, share, 0)
        if not cut_m:
            return first
        both = jnp.concatenate(
            [
                lax.dynamic_slice_in_dim(whole, z * cut, cut, 0),
                lax.dynamic_slice_in_dim(whole, cut * n_ctx + z * cut_m, cut_m, 0),
            ],
            axis=0,
        )
        return jnp.where(is_mixed, both, first)

    def cuts_of(found):
        return [x for _, _, x in found], tuple((i, 0, x.shape[0]) for i, (_, _, x) in enumerate(found))

    order = gather_order(n_fsdp)
    w_at = jnp.asarray(
        [keys_at[k] * wide_d + (h or 0) * (wide_d // 2) for k, h in order], jnp.int32
    )
    o_keys = jnp.asarray([k for k, _ in order], jnp.int32)
    o_at = lax.bitwise_xor(f, o_keys) * share + jnp.asarray(
        [(h or 0) * (share // 2) for _, h in order], jnp.int32
    )
    qkv_at = jnp.concatenate([row_places, w_at])
    o_at = jnp.concatenate([row_places, o_at if even else jnp.zeros((1,), jnp.int32)])

    normed_parts, w_in_parts, w_out_parts = {}, [], []
    w_in_own = pick_columns(w_in, z, z_runs)
    w_in_move = Move(line, gather_job(w_in_own, w_in_parts))
    line.wait(w_in_own)
    normed_own, dy_own = norm(line.tied(seq_in), seq_grad, ln_gain, ln_beta, f, n_fsdp)
    normed_ring = Move(line, ring_job(normed_own, normed_parts))
    line.wait(normed_own)
    tables = rotary_tables(line.tied(jnp.arange(seq_len, dtype=jnp.int32)))
    line.wait(*tables)
    b_in_z = jnp.stack([jnp.concatenate([b_in[s : s + n] for s, n in runs]) for runs in z_runs])[z]
    b_in_z = b_in_z[None]
    w_out_own = own_rows(line.tied(w_out)) if even else w_out
    line.wait(w_out_own, b_in_z, qkv_at, o_at, w_at, rank_places, row_places)

    while normed_ring.flight is not None:
        normed_ring.step(w_in_move)
    dy_all = lax.all_gather(after(dy_own, *line.due), "ctx", axis=0, tiled=True)
    if even:
        w_out_move = Move(line, gather_job(line.tied(w_out_own), w_out_parts))
    w_in_move.end()

    wide_q = 3 * wide_a
    x_cuts = [(j, i * blk_size, blk_size) for j in range(n_ctx) for i in range(per)]
    w_arrays, w_cuts = cuts_of(w_in_parts)
    xs = [normed_parts[j] for j in range(n_ctx)]
    qkv, normed, w_in_all = qkv_project(
        [line.tied(xs[0])] + xs[1:], tuple(x_cuts), w_arrays, w_cuts, qkv_at,
        b_in_z, seq_len, wide_q, wide_a,
    )
    line.wait(qkv)
    q_b, k_b, v_b, cat_b, lse = attention(line.tied(qkv), tables, n_heads, cat_rows // n_ctx)
    line.wait(cat_b)
    if even:
        w_out_move.step()
    slope, cat_b, w_in_all = pre_project(
        line.tied(normed), w_arrays, w_cuts, w_at, b_in_z, cat_b, w_in_all, wide_q, wide_a
    )
    line.wait(cat_b)
    if even:
        w_out_move.end()
        o_arrays, o_cuts = cuts_of(w_out_parts)
    else:
        w_all = lax.all_gather(w_out, "fsdp", axis=0, tiled=True)
        w_all = jnp.concatenate(
            [
                lax.dynamic_slice_in_dim(w_all, z * wide_a, wide_a, 0),
                lax.dynamic_slice_in_dim(w_all, D + z * wide_m, wide_m, 0),
            ],
            axis=0,
        )
        o_arrays, o_cuts = [w_all], ((0, 0, cat_rows // n_ctx),)
    *out_shares, w_out_z = out_shares_of(
        line.tied(cat_b), o_arrays, o_cuts, o_at, n_ctx * per, n_ctx, blk_size
    )
    line.wait(*out_shares)
    out_sum, norm_sum = [], []
    out_move = Move(line, sum_job(line.tied(*out_shares), out_sum))

    row_cuts = tuple((0, i * blk_size, blk_size) for i in range(n_blk))
    line.wait(dy_all)
    d_att, d_proj, sum_pre, dy = d_cat_parts(
        line.tied(dy_all), row_cuts, rank_places, w_out_z, slope, wide_a
    )
    line.wait(d_att)
    away, home = grads(line.tied(cat_b), 0, cat_rows // n_ctx, dy, 0, D, f, n_fsdp)
    line.wait(away)
    out_move.step()
    out_own, pre_own, qkv_own = [], [], []
    out_moves = [Move(line, scatter_job(line.tied(away), home, out_own))] if even else []

    d_proj, *sum_qkv = attention_back(
        q_b, k_b, v_b, cat_b, line.tied(d_att), lse, tables, d_proj, n_heads
    )
    line.wait(d_proj)
    out_move.step(*out_moves)
    norm_shares = norm_shares_of(line.tied(d_proj), w_in_all, row_places, n_ctx, blk_size)
    line.wait(*norm_shares)
    out_move.end()
    if even:
        out_moves[0].step()
    norm_move = Move(line, sum_job(line.tied(*norm_shares), norm_sum))

    half = D // 2
    pre_parts, qkv_parts = {}, {}
    (pre_away,) = grads(line.tied(normed), 1, half, d_proj, wide_q, wide_m, f)
    (pre_home,) = grads(after(normed, pre_away), 0, half, d_proj, wide_q, wide_m, f)
    (qkv_away,) = grads(after(normed, pre_home), 1, half, d_proj, 0, wide_q, f)
    (qkv_home,) = grads(after(normed, qkv_away), 0, half, d_proj, 0, wide_q, f)
    line.wait(qkv_home)
    norm_move.step(*out_moves)
    if even:
        out_all = lax.all_gather(line.tied(out_own[0]), "ctx", axis=0)
    pre_scatter = Move(line, scatter_job(line.tied(pre_away), pre_home, pre_own))
    qkv_scatter = Move(line, scatter_job(line.tied(qkv_away), qkv_home, qkv_own))
    pre_scatter.step()
    pre_scatter.step()
    norm_move.end()

    seq_in_t = line.tied(seq_in)
    centred = seq_in_t - jnp.mean(seq_in_t, axis=1, keepdims=True)
    inv_std = lax.rsqrt(jnp.mean(centred * centred, axis=1, keepdims=True) + LN_EPS)
    x_hat = centred * inv_std
    d_norm = jnp.concatenate(
        [
            lax.dynamic_slice_in_dim(norm_sum[0], position_of(f ^ i) * wide_d, wide_d, 1)
            for i in range(n_fsdp)
        ],
        axis=1,
    )
    small = jnp.stack(
        [jnp.sum(seq_grad, axis=0), jnp.sum(d_norm * x_hat, axis=0), jnp.sum(d_norm, axis=0)]
    )
    gain_grad = d_norm * ln_gain
    d_input = seq_grad + inv_std * (
        gain_grad
        - jnp.mean(gain_grad, axis=1, keepdims=True)
        - x_hat * jnp.mean(gain_grad * x_hat, axis=1, keepdims=True)
    )
    out_y = seq_in + out_sum[0] + b_out

    g_b_in_z = jnp.concatenate([x[0] for x in (*sum_qkv, sum_pre)])
    masked = jnp.where(
        jnp.arange(n_ctx)[:, None] == z, g_b_in_z[None, :], jnp.zeros((), F32)
    )
    runs = sorted((s, n, i, at) for i in range(n_ctx) for s, n, at in run_offsets(z_runs[i]))
    vector = jnp.concatenate([small.reshape(-1)] + [masked[i, at : at + n] for _, n, i, at in runs])
    vectors = []
    vector_move = Move(line, total_job(vector, vectors))
    line.wait(d_input, out_y)

    pre_runs = [[(s - 3 * D, n) for s, n in runs if s >= 3 * D] for runs in z_runs]
    qkv_runs = [[(s, n) for s, n in runs if s < 3 * D] for runs in z_runs]
    pre_scatter.end(qkv_scatter, vector_move)
    pre_ring = Move(line, ring_job(line.tied(pre_own[0]), pre_parts))
    qkv_scatter.step()
    qkv_scatter.end(vector_move)
    if even:
        g_w_out = jnp.zeros((shard, D), F32)
        for rank in range(n_ctx):
            part = out_all[rank].astype(F32)
            at_a = jnp.where(is_mixed, rank * cut, rank * share)
            g_w_out = lax.dynamic_update_slice_in_dim(g_w_out, part[:cut], at_a, 0)
            if cut_m:
                at_m = jnp.where(is_mixed, cut * n_ctx + rank * cut_m, rank * share + cut)
                g_w_out = lax.dynamic_update_slice_in_dim(g_w_out, part[cut:], at_m, 0)
    else:
        blocks = jnp.concatenate([home, away], axis=0).reshape(n_fsdp, -1, D)
        g_out = jnp.concatenate(
            [lax.dynamic_index_in_dim(blocks, position_of(f ^ i), 0, False) for i in range(n_fsdp)]
        )
        spread = jnp.zeros((cat_rows, D), BF)
        spread = lax.dynamic_update_slice_in_dim(spread, g_out[:wide_a], z * wide_a, 0)
        spread = lax.dynamic_update_slice_in_dim(spread, g_out[wide_a:], D + z * wide_m, 0)
        g_w_out = lax.psum_scatter(spread.astype(F32), "fsdp", scatter_dimension=0, tiled=True)
        g_w_out = lax.psum(g_w_out, "ctx")
    pre_ring.step(vector_move)
    pre_ring.end(vector_move)
    qkv_ring = Move(line, ring_job(line.tied(qkv_own[0]), qkv_parts))
    in_turn = range(n_ctx)
    g_w_in = spread_columns(
        None,
        [line.tied(pre_parts[0])] + [pre_parts[j] for j in in_turn[1:]],
        z, pre_runs, in_cols, 3 * D, in_cols - 3 * D,
    )
    line.wait(g_w_in)
    vector_move.end(qkv_ring)
    qkv_ring.end()
    g_w_in = spread_columns(
        g_w_in, [qkv_parts[j] for j in in_turn], z, qkv_runs, in_cols, 0, 3 * D
    )
    vector = vectors[0]
    small = vector[: 3 * D].reshape(3, D)
    g_b_in = vector[3 * D :]

    def own_part(vector):
        length_part = vector.shape[0] // n_fsdp
        return lax.dynamic_slice_in_dim(vector, f * length_part, length_part, 0)

    return (
        out_y[None],
        d_input[None],
        g_w_in,
        own_part(g_b_in),
        g_w_out,
        own_part(small[0]),
        own_part(small[1]),
        own_part(small[2]),
    )


def run_offsets(runs):
    at, found = 0, []
    for start, size in runs:
        found.append((start, size, at))
        at += size
    return found


def solution(mesh):
    placed = (
        P("fsdp", "ctx", None),
        P("fsdp", "ctx", None),
        P("fsdp", None),
        P(),
        P(),
        P("fsdp", None),
        P(),
        P("fsdp", None),
        P(),
    )
    return jax.shard_map(
        shards,
        mesh=mesh,
        in_specs=placed,
        out_specs=(
            P("fsdp", "ctx", None),
            P("fsdp", "ctx", None),
            P("fsdp", None),
            P("fsdp"),
            P("fsdp", None),
            P("fsdp"),
            P("fsdp"),
            P("fsdp"),
        ),
        check_vma=False,
    )
```

time: 666 us -> 612 us (0.919)
  Pallas kernels: 77.5 us -> 210 us
  matrix products: 113 us -> 0 us
  local copies, waits for them, and re-layouts: 103 us -> 37.8 us
  other arithmetic: 67.4 us -> 56.1 us
  waiting for transfers between devices: 239 us -> 228 us
  starting transfers between devices: 49.4 us -> 59.5 us
  between operations: 7.23 us -> 15.4 us
    pallas_call x12 -> x11, Pallas kernels: 41 us -> 173 us  [the longest x5 52.6 us: grads(): pl.pallas_call(functools.partial(grads_kernel, n_split), grid_spec=pltpu....]
    dot_general x10 -> x0, matrix products: 113 us -> none  [the longest x7 76.1 us: dot(): lax.dot_general(a, b, (((ca,), (cb,)), ((), ())), preferred_element_type=...]
    unnamed x143 -> x127, local copies, waits for them, and re-layouts: 56.5 us -> 5.95 us
    ppermute x21 -> x15, waiting for transfers between devices: 161 us -> 129 us  [pass_on(): return lax.ppermute(x, 'ctx', [(i, (i + hops) % n) for i in range(n)])]
    ppermute x38, waiting for transfers between devices: 78 us -> 98.4 us  [swap(): return lax.ppermute(x, axis, [(i, i ^ bit) for i in range(n)])]
    ppermute x21 -> x15, starting transfers between devices: 13.3 us -> 30.6 us  [pass_on(): return lax.ppermute(x, 'ctx', [(i, (i + hops) % n) for i in range(n)])]
    reduce_sum x1, other arithmetic: 11.2 us -> 0.14 us  [shards(): jnp.sum(picks[:, :, None] * rank_places.reshape(1, n_ctx, per), axis=1, d...]
    ppermute x38, starting transfers between devices: 36.1 us -> 28.4 us  [swap(): return lax.ppermute(x, axis, [(i, i ^ bit) for i in range(n)])]
  transfers between devices with their start and end apart: 59 -> 55, of which waited for: 25 -> 26; matrix products, arithmetic and copies ran while one was open for 32% -> 13% of each run, Pallas kernels for 10% -> 32%
where the time goes in v3:
time: 612 us; the launch traced here: 606 us
  waiting for transfers between devices  228 us (37%)
  Pallas kernels  210 us (34%)
  starting transfers between devices  59.5 us (10%)
  other arithmetic  56.1 us (9%)
  local copies, waits for them, and re-layouts  37.8 us (6%)
  between operations  15.4 us (3%)
    ppermute x15, waiting for transfers between devices, pass_on(): return lax.ppermute(x, 'ctx', [(i, (i + hops) % n) for i in range(n)])  129 us
    ppermute x38, waiting for transfers between devices, swap(): return lax.ppermute(x, axis, [(i, i ^ bit) for i in range(n)])  98.4 us
    pallas_call x5, Pallas kernels, grads(): pl.pallas_call(functools.partial(grads_kernel, n_split), grid_spec=pltpu....  52.6 us
    ppermute x15, starting transfers between devices, pass_on(): return lax.ppermute(x, 'ctx', [(i, (i + hops) % n) for i in range(n)])  30.6 us
    ppermute x38, starting transfers between devices, swap(): return lax.ppermute(x, axis, [(i, i ^ bit) for i in range(n)])  28.4 us
    pallas_call x1, Pallas kernels, attention_back(): pl.pallas_call(functools.partial(back_kernel, pairs), grid=(pairs,), in_s...  24.9 us
    pallas_call x1, Pallas kernels, norm_shares_of(): pl.pallas_call(functools.partial(norm_share_kernel, n_ctx, per, blk_size)...  22.5 us
    pallas_call x1, Pallas kernels, pre_project(): pl.pallas_call(functools.partial(pre_kernel, w_cuts, n_w), grid_spec=pltp...  21.1 us
  transfers between devices with their start and end apart: 55, of which 26 were waited for; matrix products, arithmetic and copies ran while one was open for 13% of the time, Pallas kernels for 32%

profile of v3, /device:TPU:0, one launch (start us, length us, event | category | flops | bytes accessed | tf_op | source)
XLA Modules:
  0.0 606.4 jit_solution(10654385698995275591)
XLA Ops:
  7.2 5.1 pick_columns.1.refs_4_.refs_0_
  12.3 4.8 norm.1
  17.1 3.1 collective-permute-start
  27.6 3.0 fusion.11
  46.5 21.1 %collective-permute-done.1.refs_3_ = bf16[256,2048]{1,0:T(8,128)(2,1)} collective-permute-done((bf16[256,2048]{1,0:T(8,128)(2,1)}, bf16[256,2048]{1,0:T(8,128)(2,1)}, u32[]{:S(2)}, u32[]{:S(2)}) %collective-permute-start.1) | collective-permute-done | bytes 1048608 | tf_op jit(solution)/shard_map/ppermute | solution.py:573
  74.8 19.0 %collective-permute-done.6.refs_8_.refs_4_ = bf16[128,3584]{1,0:T(8,128)(2,1)S(1)} collective-permute-done((bf16[128,3584]{1,0:T(8,128)(2,1)S(1)}, bf16[128,3584]{1,0:T(8,128)(2,1)S(1)}, u32[]{:S(2)}, u32[]{:S(2)}) %collective-permute-start.6) | collective-permute-done | bytes 917536 | tf_op jit(solution)/shard_map/ppermute | solution.py:582
  100.5 3.7 collective-permute-done.10.refs_12_.refs_8_
  106.8 13.4 %qkv_project.1 = (f32[1024,1536]{1,0:T(8,128)}, bf16[1024,2048]{1,0:T(8,128)(2,1)}, bf16[2048,3584]{1,0:T(8,128)(2,1)}) custom-call(s32[18]{0:T(128)} %get-tuple-element.388.at_ref, bf16[256,2048]{1,0:T(8,128)(2,1)} %get-tuple-element.143.refs_0_, bf16[256,2048]{1,0:T(8,128)(2,1)} %collective-permute-done.refs_1_, bf16[256,2048]{1,0:T(8,128)(2,1)} %copy-done.23, ...), custom_call_target="tpu_custom_call" | custom-call | flops 805306368 | bytes 2097152 | tf_op jit(solution)/shard_map/qkv_project/pallas_call | solution.py:381
  120.2 15.2 %attention.1 = (bf16[1024,512]{1,0:T(8,128)(2,1)}, bf16[1024,512]{1,0:T(8,128)(2,1)}, bf16[1024,512]{1,0:T(8,128)(2,1)}, bf16[1024,2560]{1,0:T(8,128)(2,1)}, f32[4,2,1024]{2,1,0:T(2,128)}) custom-call(f32[1024,1536]{1,0:T(8,128)} %get-tuple-element.146.q_ref.k_ref.v_ref, f32[1024,1536]{1,0:T(8,128)} %get-tuple-element.146.q_ref.k_ref.v_ref, ...), custom_call_target="tpu_custom_call" | custom-call | flops 268435456 | bytes 1310720 | tf_op jit(solution)/shard_map/attention/pallas_call | solution.py:205
  138.6 21.1 %pre_project.1 = (f32[1024,2048]{1,0:T(8,128)}, bf16[1024,2560]{1,0:T(8,128)(2,1)}, bf16[2048,3584]{1,0:T(8,128)(2,1)}) custom-call(s32[10]{0:T(128)} %constant.102.clone.at_ref, bf16[1024,2048]{1,0:T(8,128)(2,1)} %get-tuple-element.206.x_ref.left_ref, ...), custom_call_target="tpu_custom_call", output_to_operand_aliasing={{1}: (13, {}), {2}: (14, {})} | custom-call | flops 1073741824 | bytes 3145728 | tf_op jit(solution)/shard_map/pre_project/pallas_call | solution.py:420
  163.8 19.2 %out_shares.1 = (f32[256,2048]{1,0:T(8,128)}, bf16[256,2048]{1,0:T(8,128)(2,1)}, bf16[256,2048]{1,0:T(8,128)(2,1)}, f32[256,2048]{1,0:T(8,128)}, bf16[2560,2048]{1,0:T(8,128)(2,1)}) custom-call(s32[18]{0:T(128)} %get-tuple-element.389.at_ref, bf16[1024,2560]{1,0:T(8,128)(2,1)} %get-tuple-element.174.x_ref.left_ref.att_ref, bf16[320,2048]{1,0:T(8,128)(2,1)} %copy-done.6, ...), custom_call_target="tpu_custom_call" | custom-call | flops 1342177280 | bytes 2752512 | tf_op jit(solution)/shard_map/out_shares/pallas_call | solution.py:472
  184.0 3.1 collective-permute-start.22
  187.1 19.3 %d_cat_parts.1 = (bf16[1024,512]{1,0:T(8,128)(2,1)}, bf16[1024,3584]{1,0:T(8,128)(2,1)}, f32[1,2048]{1,0:T(1,128)}, bf16[1024,2048]{1,0:T(8,128)(2,1)}) custom-call(s32[8]{0:T(128)} %get-tuple-element.386.at_ref, bf16[1024,2048]{1,0:T(8,128)(2,1)} %all-gather.4.cloned.1.call-done.g_ref, bf16[2560,2048]{1,0:T(8,128)(2,1)} %get-tuple-element.171.w_ref, ...), custom_call_target="tpu_custom_call" | custom-call | flops 1342177280 | bytes 3145728 | tf_op jit(solution)/shard_map/d_cat_parts/pallas_call | solution.py:540
  206.5 19.0 %grads.5 = (bf16[1280,2048]{1,0:T(8,128)(2,1)}, bf16[1280,2048]{1,0:T(8,128)(2,1)}) custom-call(s32[1]{0:T(128)} %bitcast.1.f_ref, bf16[1024,2560]{1,0:T(8,128)(2,1)} %get-tuple-element.174.x_ref.left_ref.att_ref, bf16[1024,2048]{1,0:T(8,128)(2,1)} %get-tuple-element.175.right_ref), custom_call_target="tpu_custom_call" | custom-call | flops 1342177280 | bytes 2490368 | tf_op jit(solution)/shard_map/grads/pallas_call | solution.py:318
  225.5 6.2 %collective-permute-done.22 = bf16[256,2048]{1,0:T(8,128)(2,1)S(1)} collective-permute-done((bf16[256,2048]{1,0:T(8,128)(2,1)}, bf16[256,2048]{1,0:T(8,128)(2,1)S(1)}, u32[]{:S(2)}, u32[]{:S(2)}) %collective-permute-start.22) | collective-permute-done | bytes 1048608 | tf_op jit(solution)/shard_map/ppermute | solution.py:573
  231.8 2.9 add_convert_fusion.1
  236.4 24.9 %attention_back.1 = (bf16[1024,3584]{1,0:T(8,128)(2,1)}, f32[1,512]{1,0:T(1,128)}, f32[1,512]{1,0:T(1,128)}, f32[1,512]{1,0:T(1,128)}) custom-call(bf16[1024,512]{1,0:T(8,128)(2,1)} %get-tuple-element.182.q_ref, bf16[1024,512]{1,0:T(8,128)(2,1)} %get-tuple-element.183.k_ref, ...), custom_call_target="tpu_custom_call", output_to_operand_aliasing={{0}: (9, {})} | custom-call | flops 671088640 | bytes 1048576 | tf_op jit(solution)/shard_map/attention_back/pallas_call | solution.py:275
  262.2 3.0 add_convert_fusion.8
  267.4 22.5 %norm_shares.1 = (f32[256,2048]{1,0:T(8,128)}, bf16[256,2048]{1,0:T(8,128)(2,1)}, bf16[256,2048]{1,0:T(8,128)(2,1)}, f32[256,2048]{1,0:T(8,128)}) custom-call(s32[8]{0:T(128)} %copy-done.38, bf16[1024,3584]{1,0:T(8,128)(2,1)} %get-tuple-element.190.x_ref.right_ref, bf16[2048,3584]{1,0:T(8,128)(2,1)} %get-tuple-element.191.w_ref), custom_call_target="tpu_custom_call" | custom-call | flops 1879048192 | bytes 3538944 | tf_op jit(solution)/shard_map/norm_shares/pallas_call | solution.py:498
  290.0 3.0 add_convert_fusion.5
  295.2 4.1 collective-permute-start.28
  299.2 9.0 %grads.6 = bf16[1024,2048]{1,0:T(8,128)(2,1)} custom-call(s32[1]{0:T(128)} %bitcast.1.f_ref, bf16[1024,2048]{1,0:T(8,128)(2,1)} %get-tuple-element.206.x_ref.left_ref, bf16[1024,3584]{1,0:T(8,128)(2,1)} %get-tuple-element.190.x_ref.right_ref), custom_call_target="tpu_custom_call" | custom-call | flops 536870912 | bytes 1310720 | tf_op jit(solution)/shard_map/grads/pallas_call | solution.py:318
  308.2 9.0 %grads.7 = bf16[1024,2048]{1,0:T(8,128)(2,1)} custom-call(s32[1]{0:T(128)} %bitcast.1.f_ref, bf16[1024,2048]{1,0:T(8,128)(2,1)} %get-tuple-element.206.x_ref.left_ref, bf16[1024,3584]{1,0:T(8,128)(2,1)} %get-tuple-element.190.x_ref.right_ref), custom_call_target="tpu_custom_call" | custom-call | flops 536870912 | bytes 1310720 | tf_op jit(solution)/shard_map/grads/pallas_call | solution.py:318
  317.2 7.8 %grads.8 = bf16[1024,1536]{1,0:T(8,128)(2,1)} custom-call(s32[1]{0:T(128)} %bitcast.1.f_ref, bf16[1024,2048]{1,0:T(8,128)(2,1)} %get-tuple-element.206.x_ref.left_ref, bf16[1024,3584]{1,0:T(8,128)(2,1)} %get-tuple-element.190.x_ref.right_ref), custom_call_target="tpu_custom_call" | custom-call | flops 402653184 | bytes 1048576 | tf_op jit(solution)/shard_map/grads/pallas_call | solution.py:318
  325.0 7.7 %grads.9 = bf16[1024,1536]{1,0:T(8,128)(2,1)} custom-call(s32[1]{0:T(128)} %bitcast.1.f_ref, bf16[1024,2048]{1,0:T(8,128)(2,1)} %get-tuple-element.206.x_ref.left_ref, bf16[1024,3584]{1,0:T(8,128)(2,1)} %get-tuple-element.190.x_ref.right_ref), custom_call_target="tpu_custom_call" | custom-call | flops 402653184 | bytes 1048576 | tf_op jit(solution)/shard_map/grads/pallas_call | solution.py:318
  332.8 8.9 %collective-permute-done.28 = bf16[256,2048]{1,0:T(8,128)(2,1)} collective-permute-done((bf16[256,2048]{1,0:T(8,128)(2,1)}, bf16[256,2048]{1,0:T(8,128)(2,1)}, u32[]{:S(2)}, u32[]{:S(2)}) %collective-permute-start.28) | collective-permute-done | bytes 1048608 | tf_op jit(solution)/shard_map/ppermute | solution.py:573
  341.7 3.1 add_convert_fusion.3
  347.5 3.3 add_convert_fusion
  361.0 9.5 %collective-permute-done.33 = bf16[128,2048]{1,0:T(8,128)(2,1)S(1)} collective-permute-done((bf16[128,2048]{1,0:T(8,128)(2,1)}, bf16[128,2048]{1,0:T(8,128)(2,1)S(1)}, u32[]{:S(2)}, u32[]{:S(2)}) %collective-permute-start.33) | collective-permute-done | bytes 524320 | tf_op jit(solution)/shard_map/ppermute | solution.py:582
  371.3 3.5 add_convert_fusion.13
  376.0 9.3 %collective-permute-done.31 = bf16[256,2048]{1,0:T(8,128)(2,1)} collective-permute-done((bf16[256,2048]{1,0:T(8,128)(2,1)}, bf16[256,2048]{1,0:T(8,128)(2,1)}, u32[]{:S(2)}, u32[]{:S(2)}) %collective-permute-start.31) | collective-permute-done | bytes 1048608 | tf_op jit(solution)/shard_map/ppermute | solution.py:573
  393.8 4.5 multiply_add_fusion
  398.2 9.0 %collective-permute-done.35 = bf16[256,2048]{1,0:T(8,128)(2,1)} collective-permute-done((bf16[256,2048]{1,0:T(8,128)(2,1)}, bf16[256,2048]{1,0:T(8,128)(2,1)}, u32[]{:S(2)}, u32[]{:S(2)}) %collective-permute-start.35) | collective-permute-done | bytes 1048608 | tf_op jit(solution)/shard_map/ppermute | solution.py:582
  407.2 5.1 collective-permute-done.36
  418.2 3.3 collective-permute-done.39
  421.5 3.2 collective-permute-done.40
  429.2 7.9 %collective-permute-start.44 = (bf16[256,2048]{1,0:T(8,128)(2,1)S(1)}, bf16[256,2048]{1,0:T(8,128)(2,1)S(1)}, u32[]{:S(2)}, u32[]{:S(2)}) collective-permute-start(bf16[256,2048]{1,0:T(8,128)(2,1)S(1)} %pad_maximum_fusion.5.refs_0_), channel_id=1, source_target_pairs={{0,8},{8,16},{16,24},{24,0},{1,9},{9,17},{17,25},{25,1},{2,10},{10... | collective-permute-start | bytes 3145736 | tf_op jit(solution)/shard_map/ppermute | solution.py:573
  438.1 3.5 collective-permute-done.43
  444.7 38.4 %collective-permute-done.44.refs_1_ = bf16[256,2048]{1,0:T(8,128)(2,1)S(1)} collective-permute-done((bf16[256,2048]{1,0:T(8,128)(2,1)S(1)}, bf16[256,2048]{1,0:T(8,128)(2,1)S(1)}, u32[]{:S(2)}, u32[]{:S(2)}) %collective-permute-start.44) | collective-permute-done | bytes 1048608 | tf_op jit(solution)/shard_map/ppermute | solution.py:573
  483.1 24.4 %collective-permute-done.45.refs_3_ = bf16[256,2048]{1,0:T(8,128)(2,1)} collective-permute-done((bf16[256,2048]{1,0:T(8,128)(2,1)S(1)}, bf16[256,2048]{1,0:T(8,128)(2,1)}, u32[]{:S(2)}, u32[]{:S(2)}) %collective-permute-start.45) | collective-permute-done | bytes 1048608 | tf_op jit(solution)/shard_map/ppermute | solution.py:573
  509.0 3.9 fusion.3
  513.0 5.5 dynamic_update_slice.24
  521.8 9.8 %collective-permute-done.48 = f32[20480]{0:T(1024)S(1)} collective-permute-done((f32[20480]{0:T(1024)S(1)}, f32[20480]{0:T(1024)S(1)}, u32[]{:S(2)}, u32[]{:S(2)}) %collective-permute-start.48) | collective-permute-done | bytes 81952 | tf_op jit(solution)/shard_map/ppermute | solution.py:582
  533.5 4.0 collective-permute-start.51
  539.9 6.1 %spread_columns.2.refs_4_ = f32[256,14336]{1,0:T(8,128)} custom-call(s32[1]{0:T(128)} %bitcast.2.z_ref, bf16[256,2048]{1,0:T(8,128)(2,1)} %copy-done.7, bf16[256,2048]{1,0:T(8,128)(2,1)} %copy-done.24, bf16[256,2048]{1,0:T(8,128)(2,1)} %copy-done.25, bf16[256,2048]{1,0:T(8,128)(2,1)} %collective-permute-done.45.refs_3_), custom_call_target="tpu_custom_call" | custom-call | bytes 1572864 | tf_op jit(solution)/shard_map/spread_columns/pallas_call | solution.py:101
  546.1 25.6 %collective-permute-done.49 = f32[20480]{0:T(1024)S(1)} collective-permute-done((f32[20480]{0:T(1024)S(1)}, f32[20480]{0:T(1024)S(1)}, u32[]{:S(2)}, u32[]{:S(2)}) %collective-permute-start.49) | collective-permute-done | bytes 81952 | tf_op jit(solution)/shard_map/ppermute | solution.py:582
  576.9 16.1 %collective-permute-done.52.refs_2_ = bf16[256,1536]{1,0:T(8,128)(2,1)S(1)} collective-permute-done((bf16[256,1536]{1,0:T(8,128)(2,1)S(1)}, bf16[256,1536]{1,0:T(8,128)(2,1)S(1)}, u32[]{:S(2)}, u32[]{:S(2)}) %collective-permute-start.52) | collective-permute-done | bytes 786464 | tf_op jit(solution)/shard_map/ppermute | solution.py:573
  593.9 5.5 spread_columns.3
  (310 shorter events, 107.1 us)
Async XLA Ops:
  7.2 179.9 %all-gather.4.cloned.1.call-start = ((), (), s32[]{:S(2)}) async-start(), calls=%async_computation | async-start | bytes 5242880 | tf_op jit(solution)/shard_map/all_gather | solution.py:868
  17.1 29.4 %collective-permute-start = (bf16[256,2048]{1,0:T(8,128)(2,1)}, bf16[256,2048]{1,0:T(8,128)(2,1)}, u32[]{:S(2)}, u32[]{:S(2)}) collective-permute-start(bf16[256,2048]{1,0:T(8,128)(2,1)} %get-tuple-element.143.refs_0_), channel_id=1, source_target_pairs={{0,8},{8,16},{16,24},{24,0},{1,9},{9,17},{17,25},{25,1},{2,10},{10... | collective-permute-start | bytes 3145736 | tf_op jit(solution)/shard_map/ppermute | solution.py:573
  20.1 47.4 %collective-permute-start.1 = (bf16[256,2048]{1,0:T(8,128)(2,1)}, bf16[256,2048]{1,0:T(8,128)(2,1)}, u32[]{:S(2)}, u32[]{:S(2)}) collective-permute-start(bf16[256,2048]{1,0:T(8,128)(2,1)} %get-tuple-element.143.refs_0_), channel_id=1, source_target_pairs={{0,24},{8,0},{16,8},{24,16},{1,25},{9,1},{17,9},{25,17},{2,26},{10... | collective-permute-start | bytes 3145736 | tf_op jit(solution)/shard_map/ppermute | solution.py:573
  22.2 45.3 %collective-permute-start.2 = (bf16[256,3584]{1,0:T(8,128)(2,1)S(1)}, bf16[256,3584]{1,0:T(8,128)(2,1)}, u32[]{:S(2)}, u32[]{:S(2)}) collective-permute-start(bf16[256,3584]{1,0:T(8,128)(2,1)S(1)} %copy-done.2), channel_id=1, source_target_pairs={{0,2},{1,3},{2,0},{3,1},{4,6},{5,7},{6,4},{7,5},{8,10},{9,11},{10,... | collective-permute-start | bytes 5505032 | tf_op jit(solution)/shard_map/ppermute | solution.py:582
  23.8 43.7 %collective-permute-start.3 = (bf16[256,3584]{1,0:T(8,128)(2,1)S(1)}, bf16[256,3584]{1,0:T(8,128)(2,1)}, u32[]{:S(2)}, u32[]{:S(2)}) collective-permute-start(bf16[256,3584]{1,0:T(8,128)(2,1)S(1)} %copy-done.2), channel_id=1, source_target_pairs={{0,4},{1,5},{2,6},{3,7},{4,0},{5,1},{6,2},{7,3},{8,12},{9,13},{10,... | collective-permute-start | bytes 5505032 | tf_op jit(solution)/shard_map/ppermute | solution.py:582
  25.4 42.2 %collective-permute-start.4 = (bf16[256,3584]{1,0:T(8,128)(2,1)S(1)}, bf16[256,3584]{1,0:T(8,128)(2,1)}, u32[]{:S(2)}, u32[]{:S(2)}) collective-permute-start(bf16[256,3584]{1,0:T(8,128)(2,1)S(1)} %copy-done.2), channel_id=1, source_target_pairs={{0,1},{1,0},{2,3},{3,2},{4,5},{5,4},{6,7},{7,6},{8,9},{9,8},{10,11... | collective-permute-start | bytes 5505032 | tf_op jit(solution)/shard_map/ppermute | solution.py:582
  67.5 27.7 %collective-permute-start.8 = (bf16[256,3584]{1,0:T(8,128)(2,1)}, bf16[256,3584]{1,0:T(8,128)(2,1)S(1)}, u32[]{:S(2)}, u32[]{:S(2)}) collective-permute-start(bf16[256,3584]{1,0:T(8,128)(2,1)} %collective-permute-done.2.refs_5_.refs_1_), channel_id=1, source_target_pairs={{0,1},{1,0},{2,3},{3,2},{4,5},{5,4},{6,7},{7,6},{8,9},{9,8},{10,11... | collective-permute-start | bytes 5505032 | tf_op jit(solution)/shard_map/ppermute | solution.py:582
  67.6 27.7 %collective-permute-start.9 = (bf16[256,3584]{1,0:T(8,128)(2,1)}, bf16[256,3584]{1,0:T(8,128)(2,1)}, u32[]{:S(2)}, u32[]{:S(2)}) collective-permute-start(bf16[256,3584]{1,0:T(8,128)(2,1)} %collective-permute-done.3.refs_6_.refs_2_), channel_id=1, source_target_pairs={{0,1},{1,0},{2,3},{3,2},{4,5},{5,4},{6,7},{7,6},{8,9},{9,8},{10,11... | collective-permute-start | bytes 5505032 | tf_op jit(solution)/shard_map/ppermute | solution.py:582
  68.1 27.2 %collective-permute-start.5 = (bf16[256,2048]{1,0:T(8,128)(2,1)}, bf16[256,2048]{1,0:T(8,128)(2,1)S(1)}, u32[]{:S(2)}, u32[]{:S(2)}) collective-permute-start(bf16[256,2048]{1,0:T(8,128)(2,1)} %collective-permute-done.refs_1_), channel_id=1, source_target_pairs={{0,8},{8,16},{16,24},{24,0},{1,9},{9,17},{17,25},{25,1},{2,10},{10... | collective-permute-start | bytes 3145736 | tf_op jit(solution)/shard_map/ppermute | solution.py:573
  71.7 22.1 %collective-permute-start.6 = (bf16[128,3584]{1,0:T(8,128)(2,1)S(1)}, bf16[128,3584]{1,0:T(8,128)(2,1)S(1)}, u32[]{:S(2)}, u32[]{:S(2)}) collective-permute-start(bf16[128,3584]{1,0:T(8,128)(2,1)S(1)} %slice.635), channel_id=1, source_target_pairs={{0,4},{1,5},{2,6},{3,7},{4,0},{5,1},{6,2},{7,3},{8,12},{9,13},{10,... | collective-permute-start | bytes 2752520 | tf_op jit(solution)/shard_map/ppermute | solution.py:582
  73.3 21.8 %collective-permute-start.7 = (bf16[128,3584]{1,0:T(8,128)(2,1)S(1)}, bf16[128,3584]{1,0:T(8,128)(2,1)S(1)}, u32[]{:S(2)}, u32[]{:S(2)}) collective-permute-start(bf16[128,3584]{1,0:T(8,128)(2,1)S(1)} %slice.636), channel_id=1, source_target_pairs={{0,2},{1,3},{2,0},{3,1},{4,6},{5,7},{6,4},{7,5},{8,10},{9,11},{10,... | collective-permute-start | bytes 2752520 | tf_op jit(solution)/shard_map/ppermute | solution.py:582
  96.5 412.5 %all-gather.6.cloned.1.call-start = ((), (), s32[]{:S(2)}) async-start(), calls=%async_computation.1 | async-start | bytes 6553600 | tf_op jit(solution)/shard_map/all_gather | solution.py:943
  97.1 38.4 %collective-permute-start.12 = (bf16[320,2048]{1,0:T(8,128)(2,1)S(1)}, bf16[320,2048]{1,0:T(8,128)(2,1)S(1)}, u32[]{:S(2)}, u32[]{:S(2)}) collective-permute-start(bf16[320,2048]{1,0:T(8,128)(2,1)S(1)} %maximum_select_fusion.refs_0_), channel_id=1, source_target_pairs={{0,2},{1,3},{2,0},{3,1},{4,6},{5,7},{6,4},{7,5},{8,10},{9,11},{10,... | collective-permute-start | bytes 3932168 | tf_op jit(solution)/shard_map/ppermute | solution.py:582
  98.6 36.8 %collective-permute-start.13 = (bf16[320,2048]{1,0:T(8,128)(2,1)S(1)}, bf16[320,2048]{1,0:T(8,128)(2,1)S(1)}, u32[]{:S(2)}, u32[]{:S(2)}) collective-permute-start(bf16[320,2048]{1,0:T(8,128)(2,1)S(1)} %maximum_select_fusion.refs_0_), channel_id=1, source_target_pairs={{0,4},{1,5},{2,6},{3,7},{4,0},{5,1},{6,2},{7,3},{8,12},{9,13},{10,... | collective-permute-start | bytes 3932168 | tf_op jit(solution)/shard_map/ppermute | solution.py:582
  100.0 35.5 %collective-permute-start.14 = (bf16[320,2048]{1,0:T(8,128)(2,1)S(1)}, bf16[320,2048]{1,0:T(8,128)(2,1)}, u32[]{:S(2)}, u32[]{:S(2)}) collective-permute-start(bf16[320,2048]{1,0:T(8,128)(2,1)S(1)} %maximum_select_fusion.refs_0_), channel_id=1, source_target_pairs={{0,1},{1,0},{2,3},{3,2},{4,5},{5,4},{6,7},{7,6},{8,9},{9,8},{10,11... | collective-permute-start | bytes 3932168 | tf_op jit(solution)/shard_map/ppermute | solution.py:582
  135.5 24.3 %collective-permute-start.17 = (bf16[320,2048]{1,0:T(8,128)(2,1)S(1)}, bf16[320,2048]{1,0:T(8,128)(2,1)S(1)}, u32[]{:S(2)}, u32[]{:S(2)}) collective-permute-start(bf16[320,2048]{1,0:T(8,128)(2,1)S(1)} %collective-permute-done.12.refs_1_), channel_id=1, source_target_pairs={{0,1},{1,0},{2,3},{3,2},{4,5},{5,4},{6,7},{7,6},{8,9},{9,8},{10,11... | collective-permute-start | bytes 3932168 | tf_op jit(solution)/shard_map/ppermute | solution.py:582
  135.7 24.1 %collective-permute-start.18 = (bf16[320,2048]{1,0:T(8,128)(2,1)S(1)}, bf16[320,2048]{1,0:T(8,128)(2,1)S(1)}, u32[]{:S(2)}, u32[]{:S(2)}) collective-permute-start(bf16[320,2048]{1,0:T(8,128)(2,1)S(1)} %collective-permute-done.13.refs_2_), channel_id=1, source_target_pairs={{0,1},{1,0},{2,3},{3,2},{4,5},{5,4},{6,7},{7,6},{8,9},{9,8},{10,11... | collective-permute-start | bytes 3932168 | tf_op jit(solution)/shard_map/ppermute | solution.py:582
  137.2 22.6 %collective-permute-start.15 = (bf16[160,2048]{1,0:T(8,128)(2,1)}, bf16[160,2048]{1,0:T(8,128)(2,1)S(1)}, u32[]{:S(2)}, u32[]{:S(2)}) collective-permute-start(bf16[160,2048]{1,0:T(8,128)(2,1)} %slice.637), channel_id=1, source_target_pairs={{0,4},{1,5},{2,6},{3,7},{4,0},{5,1},{6,2},{7,3},{8,12},{9,13},{10,... | collective-permute-start | bytes 1966088 | tf_op jit(solution)/shard_map/ppermute | solution.py:582
  137.9 21.9 %collective-permute-start.16 = (bf16[160,2048]{1,0:T(8,128)(2,1)S(1)}, bf16[160,2048]{1,0:T(8,128)(2,1)S(1)}, u32[]{:S(2)}, u32[]{:S(2)}) collective-permute-start(bf16[160,2048]{1,0:T(8,128)(2,1)S(1)} %slice.638), channel_id=1, source_target_pairs={{0,2},{1,3},{2,0},{3,1},{4,6},{5,7},{6,4},{7,5},{8,10},{9,11},{10,... | collective-permute-start | bytes 1966088 | tf_op jit(solution)/shard_map/ppermute | solution.py:582
  183.1 42.4 %collective-permute-start.21 = (bf16[256,2048]{1,0:T(8,128)(2,1)}, bf16[256,2048]{1,0:T(8,128)(2,1)}, u32[]{:S(2)}, u32[]{:S(2)}) collective-permute-start(bf16[256,2048]{1,0:T(8,128)(2,1)} %get-tuple-element.166), channel_id=1, source_target_pairs={{0,8},{8,16},{16,24},{24,0},{1,9},{9,17},{17,25},{25,1},{2,10},{10... | collective-permute-start | bytes 3145736 | tf_op jit(solution)/shard_map/ppermute | solution.py:573
  184.0 47.7 %collective-permute-start.22 = (bf16[256,2048]{1,0:T(8,128)(2,1)}, bf16[256,2048]{1,0:T(8,128)(2,1)S(1)}, u32[]{:S(2)}, u32[]{:S(2)}) collective-permute-start(bf16[256,2048]{1,0:T(8,128)(2,1)} %get-tuple-element.167), channel_id=1, source_target_pairs={{0,24},{8,0},{16,8},{24,16},{1,25},{9,1},{17,9},{25,17},{2,26},{10... | collective-permute-start | bytes 3145736 | tf_op jit(solution)/shard_map/ppermute | solution.py:573
  231.7 30.4 %collective-permute-start.24 = (bf16[1280,2048]{1,0:T(8,128)(2,1)}, bf16[1280,2048]{1,0:T(8,128)(2,1)}, u32[]{:S(2)}, u32[]{:S(2)}) collective-permute-start(bf16[1280,2048]{1,0:T(8,128)(2,1)} %get-tuple-element.180), channel_id=1, source_target_pairs={{0,1},{1,0},{2,3},{3,2},{4,5},{5,4},{6,7},{7,6},{8,9},{9,8},{10,11... | collective-permute-start | bytes 15728648 | tf_op jit(solution)/shard_map/ppermute | solution.py:582
  234.7 27.5 %collective-permute-start.23 = (bf16[256,2048]{1,0:T(8,128)(2,1)}, bf16[256,2048]{1,0:T(8,128)(2,1)S(1)}, u32[]{:S(2)}, u32[]{:S(2)}) collective-permute-start(bf16[256,2048]{1,0:T(8,128)(2,1)} %add_convert_fusion.1), channel_id=1, source_target_pairs={{0,8},{8,16},{16,24},{24,0},{1,9},{9,17},{17,25},{25,1},{2,10},{10... | collective-permute-start | bytes 3145736 | tf_op jit(solution)/shard_map/ppermute | solution.py:573
  265.2 24.8 %collective-permute-start.25 = (bf16[160,2048]{1,0:T(8,128)(2,1)}, bf16[160,2048]{1,0:T(8,128)(2,1)S(1)}, u32[]{:S(2)}, u32[]{:S(2)}) collective-permute-start(bf16[160,2048]{1,0:T(8,128)(2,1)} %get-tuple-element.293), channel_id=1, source_target_pairs={{0,4},{1,5},{2,6},{3,7},{4,0},{5,1},{6,2},{7,3},{8,12},{9,13},{10,... | collective-permute-start | bytes 1966088 | tf_op jit(solution)/shard_map/ppermute | solution.py:582
  265.9 24.0 %collective-permute-start.26 = (bf16[160,2048]{1,0:T(8,128)(2,1)S(1)}, bf16[160,2048]{1,0:T(8,128)(2,1)S(1)}, u32[]{:S(2)}, u32[]{:S(2)}) collective-permute-start(bf16[160,2048]{1,0:T(8,128)(2,1)S(1)} %get-tuple-element.292), channel_id=1, source_target_pairs={{0,2},{1,3},{2,0},{3,1},{4,6},{5,7},{6,4},{7,5},{8,10},{9,11},{10,... | collective-permute-start | bytes 1966088 | tf_op jit(solution)/shard_map/ppermute | solution.py:582
  293.1 48.6 %collective-permute-start.29 = (bf16[320,2048]{1,0:T(8,128)(2,1)S(1)}, bf16[320,2048]{1,0:T(8,128)(2,1)}, u32[]{:S(2)}, u32[]{:S(2)}) collective-permute-start(bf16[320,2048]{1,0:T(8,128)(2,1)S(1)} %pad_maximum_fusion), channel_id=1, source_target_pairs={{0,2},{1,3},{2,0},{3,1},{4,6},{5,7},{6,4},{7,5},{8,10},{9,11},{10,... | collective-permute-start | bytes 3932168 | tf_op jit(solution)/shard_map/ppermute | solution.py:582
  293.8 47.9 %collective-permute-start.30 = (bf16[320,2048]{1,0:T(8,128)(2,1)S(1)}, bf16[320,2048]{1,0:T(8,128)(2,1)}, u32[]{:S(2)}, u32[]{:S(2)}) collective-permute-start(bf16[320,2048]{1,0:T(8,128)(2,1)S(1)} %pad_maximum_fusion.1), channel_id=1, source_target_pairs={{0,4},{1,5},{2,6},{3,7},{4,0},{5,1},{6,2},{7,3},{8,12},{9,13},{10,... | collective-permute-start | bytes 3932168 | tf_op jit(solution)/shard_map/ppermute | solution.py:582
  295.1 37.6 %collective-permute-start.27 = (bf16[256,2048]{1,0:T(8,128)(2,1)}, bf16[256,2048]{1,0:T(8,128)(2,1)}, u32[]{:S(2)}, u32[]{:S(2)}) collective-permute-start(bf16[256,2048]{1,0:T(8,128)(2,1)} %get-tuple-element.200), channel_id=1, source_target_pairs={{0,8},{8,16},{16,24},{24,0},{1,9},{9,17},{17,25},{25,1},{2,10},{10... | collective-permute-start | bytes 3145736 | tf_op jit(solution)/shard_map/ppermute | solution.py:573
  295.2 46.5 %collective-permute-start.28 = (bf16[256,2048]{1,0:T(8,128)(2,1)}, bf16[256,2048]{1,0:T(8,128)(2,1)}, u32[]{:S(2)}, u32[]{:S(2)}) collective-permute-start(bf16[256,2048]{1,0:T(8,128)(2,1)} %get-tuple-element.201), channel_id=1, source_target_pairs={{0,24},{8,0},{16,8},{24,16},{1,25},{9,1},{17,9},{25,17},{2,26},{10... | collective-permute-start | bytes 3145736 | tf_op jit(solution)/shard_map/ppermute | solution.py:573
  350.9 34.4 %collective-permute-start.31 = (bf16[256,2048]{1,0:T(8,128)(2,1)}, bf16[256,2048]{1,0:T(8,128)(2,1)}, u32[]{:S(2)}, u32[]{:S(2)}) collective-permute-start(bf16[256,2048]{1,0:T(8,128)(2,1)} %add_convert_fusion), channel_id=1, source_target_pairs={{0,8},{8,16},{16,24},{24,0},{1,9},{9,17},{17,25},{25,1},{2,10},{10... | collective-permute-start | bytes 3145736 | tf_op jit(solution)/shard_map/ppermute | solution.py:573
  356.3 14.2 %collective-permute-start.33 = (bf16[128,2048]{1,0:T(8,128)(2,1)}, bf16[128,2048]{1,0:T(8,128)(2,1)S(1)}, u32[]{:S(2)}, u32[]{:S(2)}) collective-permute-start(bf16[128,2048]{1,0:T(8,128)(2,1)} %get-tuple-element.299), channel_id=1, source_target_pairs={{0,4},{1,5},{2,6},{3,7},{4,0},{5,1},{6,2},{7,3},{8,12},{9,13},{10,... | collective-permute-start | bytes 1572872 | tf_op jit(solution)/shard_map/ppermute | solution.py:582
  357.5 13.8 %collective-permute-start.34 = (bf16[128,2048]{1,0:T(8,128)(2,1)S(1)}, bf16[128,2048]{1,0:T(8,128)(2,1)}, u32[]{:S(2)}, u32[]{:S(2)}) collective-permute-start(bf16[128,2048]{1,0:T(8,128)(2,1)S(1)} %get-tuple-element.298), channel_id=1, source_target_pairs={{0,2},{1,3},{2,0},{3,1},{4,6},{5,7},{6,4},{7,5},{8,10},{9,11},{10,... | collective-permute-start | bytes 1572872 | tf_op jit(solution)/shard_map/ppermute | solution.py:582
  361.0 37.3 %collective-permute-start.37 = (bf16[1024,1536]{1,0:T(8,128)(2,1)}, bf16[1024,1536]{1,0:T(8,128)(2,1)}, u32[]{:S(2)}, u32[]{:S(2)}) collective-permute-start(bf16[1024,1536]{1,0:T(8,128)(2,1)} %grads.8), channel_id=1, source_target_pairs={{0,1},{1,0},{2,3},{3,2},{4,5},{5,4},{6,7},{7,6},{8,9},{9,8},{10,11... | collective-permute-start | bytes 9437192 | tf_op jit(solution)/shard_map/ppermute | solution.py:582
  385.4 21.8 %collective-permute-start.35 = (bf16[256,2048]{1,0:T(8,128)(2,1)}, bf16[256,2048]{1,0:T(8,128)(2,1)}, u32[]{:S(2)}, u32[]{:S(2)}) collective-permute-start(bf16[256,2048]{1,0:T(8,128)(2,1)} %pad_maximum_fusion.3), channel_id=1, source_target_pairs={{0,2},{1,3},{2,0},{3,1},{4,6},{5,7},{6,4},{7,5},{8,10},{9,11},{10,... | collective-permute-start | bytes 3145736 | tf_op jit(solution)/shard_map/ppermute | solution.py:582
  390.3 22.1 %collective-permute-start.36 = (bf16[256,2048]{1,0:T(8,128)(2,1)}, bf16[256,2048]{1,0:T(8,128)(2,1)S(1)}, u32[]{:S(2)}, u32[]{:S(2)}) collective-permute-start(bf16[256,2048]{1,0:T(8,128)(2,1)} %pad_maximum_fusion.4), channel_id=1, source_target_pairs={{0,4},{1,5},{2,6},{3,7},{4,0},{5,1},{6,2},{7,3},{8,12},{9,13},{10,... | collective-permute-start | bytes 3145736 | tf_op jit(solution)/shard_map/ppermute | solution.py:582
  413.7 7.8 %collective-permute-start.39 = (bf16[128,1536]{1,0:T(8,128)(2,1)S(1)}, bf16[128,1536]{1,0:T(8,128)(2,1)S(1)}, u32[]{:S(2)}, u32[]{:S(2)}) collective-permute-start(bf16[128,1536]{1,0:T(8,128)(2,1)S(1)} %get-tuple-element.307), channel_id=1, source_target_pairs={{0,4},{1,5},{2,6},{3,7},{4,0},{5,1},{6,2},{7,3},{8,12},{9,13},{10,... | collective-permute-start | bytes 1179656 | tf_op jit(solution)/shard_map/ppermute | solution.py:582
  415.1 9.6 %collective-permute-start.40 = (bf16[128,1536]{1,0:T(8,128)(2,1)S(1)}, bf16[128,1536]{1,0:T(8,128)(2,1)S(1)}, u32[]{:S(2)}, u32[]{:S(2)}) collective-permute-start(bf16[128,1536]{1,0:T(8,128)(2,1)S(1)} %get-tuple-element.306), channel_id=1, source_target_pairs={{0,2},{1,3},{2,0},{3,1},{4,6},{5,7},{6,4},{7,5},{8,10},{9,11},{10,... | collective-permute-start | bytes 1179656 | tf_op jit(solution)/shard_map/ppermute | solution.py:582
  426.6 15.0 %collective-permute-start.41 = (bf16[256,1536]{1,0:T(8,128)(2,1)S(1)}, bf16[256,1536]{1,0:T(8,128)(2,1)}, u32[]{:S(2)}, u32[]{:S(2)}) collective-permute-start(bf16[256,1536]{1,0:T(8,128)(2,1)S(1)} %pad_maximum_fusion.6), channel_id=1, source_target_pairs={{0,2},{1,3},{2,0},{3,1},{4,6},{5,7},{6,4},{7,5},{8,10},{9,11},{10,... | collective-permute-start | bytes 2359304 | tf_op jit(solution)/shard_map/ppermute | solution.py:582
  428.1 13.6 %collective-permute-start.42 = (bf16[256,1536]{1,0:T(8,128)(2,1)}, bf16[256,1536]{1,0:T(8,128)(2,1)}, u32[]{:S(2)}, u32[]{:S(2)}) collective-permute-start(bf16[256,1536]{1,0:T(8,128)(2,1)} %pad_maximum_fusion.7), channel_id=1, source_target_pairs={{0,4},{1,5},{2,6},{3,7},{4,0},{5,1},{6,2},{7,3},{8,12},{9,13},{10,... | collective-permute-start | bytes 2359304 | tf_op jit(solution)/shard_map/ppermute | solution.py:582
  429.2 53.9 %collective-permute-start.44 = (bf16[256,2048]{1,0:T(8,128)(2,1)S(1)}, bf16[256,2048]{1,0:T(8,128)(2,1)S(1)}, u32[]{:S(2)}, u32[]{:S(2)}) collective-permute-start(bf16[256,2048]{1,0:T(8,128)(2,1)S(1)} %pad_maximum_fusion.5.refs_0_), channel_id=1, source_target_pairs={{0,8},{8,16},{16,24},{24,0},{1,9},{9,17},{17,25},{25,1},{2,10},{10... | collective-permute-start | bytes 3145736 | tf_op jit(solution)/shard_map/ppermute | solution.py:573
  437.1 70.4 %collective-permute-start.45 = (bf16[256,2048]{1,0:T(8,128)(2,1)S(1)}, bf16[256,2048]{1,0:T(8,128)(2,1)}, u32[]{:S(2)}, u32[]{:S(2)}) collective-permute-start(bf16[256,2048]{1,0:T(8,128)(2,1)S(1)} %pad_maximum_fusion.5.refs_0_), channel_id=1, source_target_pairs={{0,24},{8,0},{16,8},{24,16},{1,25},{9,1},{17,9},{25,17},{2,26},{10... | collective-permute-start | bytes 3145736 | tf_op jit(solution)/shard_map/ppermute | solution.py:573
  441.7 65.8 %collective-permute-start.46 = (f32[20480]{0:T(1024)S(1)}, f32[20480]{0:T(1024)S(1)}, u32[]{:S(2)}, u32[]{:S(2)}) collective-permute-start(f32[20480]{0:T(1024)S(1)} %add.359), channel_id=1, source_target_pairs={{0,4},{1,5},{2,6},{3,7},{4,0},{5,1},{6,2},{7,3},{8,12},{9,13},{10,... | collective-permute-start | bytes 245768 | tf_op jit(solution)/shard_map/ppermute | solution.py:582
  507.5 26.1 %collective-permute-start.47 = (bf16[256,2048]{1,0:T(8,128)(2,1)S(1)}, bf16[256,2048]{1,0:T(8,128)(2,1)S(1)}, u32[]{:S(2)}, u32[]{:S(2)}) collective-permute-start(bf16[256,2048]{1,0:T(8,128)(2,1)S(1)} %collective-permute-done.44.refs_1_), channel_id=1, source_target_pairs={{0,8},{8,16},{16,24},{24,0},{1,9},{9,17},{17,25},{25,1},{2,10},{10... | collective-permute-start | bytes 3145736 | tf_op jit(solution)/shard_map/ppermute | solution.py:573
  508.4 23.3 %collective-permute-start.48 = (f32[20480]{0:T(1024)S(1)}, f32[20480]{0:T(1024)S(1)}, u32[]{:S(2)}, u32[]{:S(2)}) collective-permute-start(f32[20480]{0:T(1024)S(1)} %add.360), channel_id=1, source_target_pairs={{0,8},{8,0},{16,24},{24,16},{1,9},{9,1},{17,25},{25,17},{2,10},{10... | collective-permute-start | bytes 245768 | tf_op jit(solution)/shard_map/ppermute | solution.py:582
  533.5 38.1 %collective-permute-start.50 = (bf16[256,1536]{1,0:T(8,128)(2,1)S(1)}, bf16[256,1536]{1,0:T(8,128)(2,1)S(1)}, u32[]{:S(2)}, u32[]{:S(2)}) collective-permute-start(bf16[256,1536]{1,0:T(8,128)(2,1)S(1)} %pad_maximum_fusion.8.refs_0_), channel_id=1, source_target_pairs={{0,8},{8,16},{16,24},{24,0},{1,9},{9,17},{17,25},{25,1},{2,10},{10... | collective-permute-start | bytes 2359304 | tf_op jit(solution)/shard_map/ppermute | solution.py:573
  533.5 38.1 %collective-permute-start.51 = (bf16[256,1536]{1,0:T(8,128)(2,1)S(1)}, bf16[256,1536]{1,0:T(8,128)(2,1)S(1)}, u32[]{:S(2)}, u32[]{:S(2)}) collective-permute-start(bf16[256,1536]{1,0:T(8,128)(2,1)S(1)} %pad_maximum_fusion.8.refs_0_), channel_id=1, source_target_pairs={{0,24},{8,0},{16,8},{24,16},{1,25},{9,1},{17,9},{25,17},{2,26},{10... | collective-permute-start | bytes 2359304 | tf_op jit(solution)/shard_map/ppermute | solution.py:573
  538.8 32.9 %collective-permute-start.49 = (f32[20480]{0:T(1024)S(1)}, f32[20480]{0:T(1024)S(1)}, u32[]{:S(2)}, u32[]{:S(2)}) collective-permute-start(f32[20480]{0:T(1024)S(1)} %add.361), channel_id=1, source_target_pairs={{0,16},{8,24},{16,0},{24,8},{1,17},{9,25},{17,1},{25,9},{2,18},{10... | collective-permute-start | bytes 245768 | tf_op jit(solution)/shard_map/ppermute | solution.py:582
  571.7 21.3 %collective-permute-start.52 = (bf16[256,1536]{1,0:T(8,128)(2,1)S(1)}, bf16[256,1536]{1,0:T(8,128)(2,1)S(1)}, u32[]{:S(2)}, u32[]{:S(2)}) collective-permute-start(bf16[256,1536]{1,0:T(8,128)(2,1)S(1)} %collective-permute-done.50.refs_1_), channel_id=1, source_target_pairs={{0,8},{8,16},{16,24},{24,0},{1,9},{9,17},{17,25},{25,1},{2,10},{10... | collective-permute-start | bytes 2359304 | tf_op jit(solution)/shard_map/ppermute | solution.py:573
  (67 other events, 593.3 us)
Sparse Core Ops, SparseCore 0:
  96.6 80.1 all-gather.3
  361.1 142.0 all-gather.5

commit v4 on v3

--- a/solution.py
+++ b/solution.py
@@ -289,8 +289,8 @@
     )(q, k, v, cat, d_att, lse, *tables, d_proj)
 
 
-def grads_kernel(n_split, f_ref, left_ref, right_ref, *refs):
-    outs, left_t = refs[:-1], refs[-1]
+def grads_kernel(n_split, n_late, f_ref, left_ref, right_ref, *refs):
+    outs, left_t = refs[n_late:-1], refs[-1]
 
     @pl.when(pl.program_id(0) == 0)
     def _():
@@ -311,25 +311,26 @@
                 out[at, :] = g[s * rows : (s + 1) * rows]
 
 
-def grads(left, block, wide, right, first, width, f, n_split=None):
+def grads(left, block, wide, right, first, width, f, n_split=None, late=()):
     rows = left.shape[0]
     tile = math.gcd(512, math.gcd(width, first) if first else width)
     n_out = 2 if n_split else 1
     return pl.pallas_call(
-        functools.partial(grads_kernel, n_split),
+        functools.partial(grads_kernel, n_split, len(late)),
         grid_spec=pltpu.PrefetchScalarGridSpec(
             num_scalar_prefetch=1,
             grid=(width // tile,),
             in_specs=[
                 pl.BlockSpec((rows, wide), lambda i, f_ref: (0, block)),
                 pl.BlockSpec((rows, tile), lambda i, f_ref: (0, first // tile + i)),
-            ],
+            ]
+            + [pl.BlockSpec(memory_space=pl.ANY)] * len(late),
             out_specs=[pl.BlockSpec((wide // n_out, tile), lambda i, f_ref: (0, i))] * n_out,
             scratch_shapes=[pltpu.VMEM((wide, rows), BF)],
         ),
         out_shape=[jax.ShapeDtypeStruct((wide // n_out, width), BF)] * n_out,
         **big("grads", 2 * rows * wide * width, 2 * rows * (wide + width) + 2 * wide * width),
-    )(f[None], left, right)
+    )(f[None], left, right, *late)
 
 
 def chunks(rows):
@@ -353,7 +354,7 @@
 def big(name_of, flops, nbytes):
     return {
         "compiler_params": pltpu.CompilerParams(vmem_limit_bytes=VMEM_BYTES),
-        "cost_estimate": cost(flops // 8, nbytes // 8),
+        "cost_estimate": cost(flops // 64, nbytes // 64),
         "name": name_of,
     }
 
@@ -442,61 +443,55 @@
     )(places, x, *ws, b, cat, w_all)
 
 
-def give_shares(at_ref, acc, outs, per, blk_size):
-    for j, out in enumerate(outs):
-        for i in range(per):
-            at = pl.multiple_of(at_ref[j * per + i], blk_size)
-            out[i * blk_size : (i + 1) * blk_size, :] = acc[pl.ds(at, blk_size), :].astype(out.dtype)
-
-
-def share_shapes(n_ctx, own, width):
-    ups, downs = reach(n_ctx)
-    kinds = [BF if j in (n_ctx - ups, downs) and j else F32 for j in range(n_ctx)]
-    return [jax.ShapeDtypeStruct((own, width), kind) for kind in kinds]
-
-
-def out_kernel(w_cuts, n_w, n_ctx, per, blk_size, at_ref, x_ref, *refs):
-    ws, outs, w_ref, acc = refs[:n_w], refs[n_w : n_w + n_ctx], refs[-2], refs[-1]
-    lay(ws, w_cuts, at_ref, n_ctx * per, w_ref)
+def by_rank(at_ref, acc, out, blk_size):
+    for i in range(acc.shape[0] // blk_size):
+        at = pl.multiple_of(at_ref[i], blk_size)
+        out[i * blk_size : (i + 1) * blk_size, :] = acc[pl.ds(at, blk_size), :].astype(out.dtype)
+
+
+def out_kernel(w_cuts, n_w, n_blk, blk_size, at_ref, x_ref, *refs):
+    ws, out_ref, w_ref, acc = refs[:n_w], refs[-3], refs[-2], refs[-1]
+    lay(ws, w_cuts, at_ref, n_blk, w_ref)
     acc[...] = dot(x_ref[...], w_ref[...], 1, 0)
-    give_shares(at_ref, acc, outs, per, blk_size)
-
-
-def out_shares_of(x, ws, w_cuts, places, n_rows, n_ctx, blk_size):
+    by_rank(at_ref, acc, out_ref, blk_size)
+
+
+def out_project(x, ws, w_cuts, places, n_blk, blk_size):
     rows, deep = x.shape
     width = ws[0].shape[1]
     tile = min(512, width)
-    per = n_rows // n_ctx
-    own = rows // n_ctx
-    col = pl.BlockSpec((own, tile), lambda i, at: (0, i))
-    return pl.pallas_call(
-        functools.partial(out_kernel, w_cuts, len(ws), n_ctx, per, blk_size),
+    return pl.pallas_call(
+        functools.partial(out_kernel, w_cuts, len(ws), n_blk, blk_size),
         grid_spec=pltpu.PrefetchScalarGridSpec(
             num_scalar_prefetch=1,
             grid=(width // tile,),
             in_specs=[pl.BlockSpec((rows, deep), lambda i, at: (0, 0))]
             + [pl.BlockSpec((w.shape[0], tile), lambda i, at: (0, i)) for w in ws],
-            out_specs=[col] * n_ctx + [pl.BlockSpec((deep, tile), lambda i, at: (0, i))],
+            out_specs=[
+                pl.BlockSpec((rows, tile), lambda i, at: (0, i)),
+                pl.BlockSpec((deep, tile), lambda i, at: (0, i)),
+            ],
             scratch_shapes=[pltpu.VMEM((rows, tile), F32)],
         ),
-        out_shape=share_shapes(n_ctx, own, width) + [jax.ShapeDtypeStruct((deep, width), BF)],
-        **big("out_shares", 2 * rows * deep * width, 2 * deep * (rows + width) + 3 * rows * width),
+        out_shape=[
+            jax.ShapeDtypeStruct((rows, width), BF),
+            jax.ShapeDtypeStruct((deep, width), BF),
+        ],
+        **big("out_project", 2 * rows * deep * width, 2 * deep * (rows + width) + 3 * rows * width),
     )(places, x, *ws)
 
 
-def norm_share_kernel(n_ctx, per, blk_size, at_ref, x_ref, w_ref, *refs):
-    refs[-1][...] = dot(x_ref[...], w_ref[...], 1, 1)
-    give_shares(at_ref, refs[-1], refs[:-1], per, blk_size)
-
-
-def norm_shares_of(x, w, row_places, n_ctx, blk_size):
+def norm_kernel_back(blk_size, at_ref, x_ref, w_ref, out_ref, acc):
+    acc[...] = dot(x_ref[...], w_ref[...], 1, 1)
+    by_rank(at_ref, acc, out_ref, blk_size)
+
+
+def norm_back(x, w, places, blk_size):
     rows, deep = x.shape
     width = w.shape[0]
     tile = min(256, width)
-    per = row_places.shape[0] // n_ctx
-    own = rows // n_ctx
-    return pl.pallas_call(
-        functools.partial(norm_share_kernel, n_ctx, per, blk_size),
+    return pl.pallas_call(
+        functools.partial(norm_kernel_back, blk_size),
         grid_spec=pltpu.PrefetchScalarGridSpec(
             num_scalar_prefetch=1,
             grid=(width // tile,),
@@ -504,12 +499,12 @@
                 pl.BlockSpec((rows, deep), lambda i, at: (0, 0)),
                 pl.BlockSpec((tile, deep), lambda i, at: (i, 0)),
             ],
-            out_specs=[pl.BlockSpec((own, tile), lambda i, at: (0, i))] * n_ctx,
+            out_specs=pl.BlockSpec((rows, tile), lambda i, at: (0, i)),
             scratch_shapes=[pltpu.VMEM((rows, tile), F32)],
         ),
-        out_shape=share_shapes(n_ctx, own, width),
-        **big("norm_shares", 2 * rows * deep * width, 2 * deep * (rows + width) + 3 * rows * width),
-    )(row_places, x, w)
+        out_shape=jax.ShapeDtypeStruct((rows, width), BF),
+        **big("norm_back", 2 * rows * deep * width, 2 * deep * (rows + width) + 3 * rows * width),
+    )(places, x, w)
 
 
 def d_cat_kernel(cuts, at_ref, g_ref, w_ref, slope_ref, datt_ref, dproj_ref, sum_ref, x_ref):
@@ -528,11 +523,13 @@
         sum_ref[...] = total
 
 
-def d_cat_parts(g, cuts, places, w, slope, wide_a):
+def d_cat_parts(g, places, w, slope, wide_a):
     rows, deep = g.shape
     width = slope.shape[1]
     tile = wide_a
     total = 3 * wide_a + width
+    blk = rows // places.shape[0]
+    cuts = tuple((0, i * blk, blk) for i in range(places.shape[0]))
 
     def col(i):
         return jnp.maximum(i - 1, 0)
@@ -564,6 +561,32 @@
     )(places, g, w, slope)
 
 
+def join_kernel(n_parts, sizes, at_ref, *refs):
+    dst = refs[-1]
+    for j in range(n_parts):
+        first = 0
+        for i, size in enumerate(sizes):
+            at = pl.multiple_of(at_ref[j * len(sizes) + i], 16)
+            dst[pl.ds(at, size), :] = refs[j][first : first + size, :].astype(F32)
+            first += size
+
+
+def join_rows(parts, places, sizes):
+    rows, width = parts[0].shape
+    tile = min(512, width)
+    return pl.pallas_call(
+        functools.partial(join_kernel, len(parts), sizes),
+        grid_spec=pltpu.PrefetchScalarGridSpec(
+            num_scalar_prefetch=1,
+            grid=(width // tile,),
+            in_specs=[pl.BlockSpec((rows, tile), lambda i, at: (0, i))] * len(parts),
+            out_specs=pl.BlockSpec((rows * len(parts), tile), lambda i, at: (0, i)),
+        ),
+        out_shape=jax.ShapeDtypeStruct((rows * len(parts), width), F32),
+        **big("join_rows", 0, 6 * rows * len(parts) * width),
+    )(places, *parts)
+
+
 def after(x, *others):
     return lax.optimization_barrier((x, *others))[0]
 
@@ -627,30 +650,6 @@
         else:
             (up,) = yield [pass_on(up, 1)]
         found[hop] = up
-
-
-def sum_job(parts, found):
-    n = lax.axis_size("ctx")
-    ups, downs = reach(n)
-    up, down = parts[n - ups], parts[downs] if downs else None
-    total = parts[0]
-    for hop in range(ups):
-        send = [pass_on(up.astype(BF), 1)]
-        if hop < downs:
-            send.append(pass_on(down.astype(BF), -1))
-        got = yield send
-        left = ups - 1 - hop
-        if left:
-            up = parts[n - left].astype(F32) + got[0].astype(F32)
-        else:
-            total = total + got[0].astype(F32)
-        if hop < downs:
-            left = downs - 1 - hop
-            if left:
-                down = parts[left].astype(F32) + got[1].astype(F32)
-            else:
-                total = total + got[1].astype(F32)
-    found.append(total)
 
 
 def total_job(x, found):
@@ -847,7 +846,7 @@
         [(h or 0) * (share // 2) for _, h in order], jnp.int32
     )
     qkv_at = jnp.concatenate([row_places, w_at])
-    o_at = jnp.concatenate([row_places, o_at if even else jnp.zeros((1,), jnp.int32)])
+    o_at = jnp.concatenate([rank_places, o_at if even else jnp.zeros((1,), jnp.int32)])
 
     normed_parts, w_in_parts, w_out_parts = {}, [], []
     w_in_own = pick_columns(w_in, z, z_runs)
@@ -900,52 +899,55 @@
             axis=0,
         )
         o_arrays, o_cuts = [w_all], ((0, 0, cat_rows // n_ctx),)
-    *out_shares, w_out_z = out_shares_of(
-        line.tied(cat_b), o_arrays, o_cuts, o_at, n_ctx * per, n_ctx, blk_size
-    )
-    line.wait(*out_shares)
-    out_sum, norm_sum = [], []
-    out_move = Move(line, sum_job(line.tied(*out_shares), out_sum))
-
-    row_cuts = tuple((0, i * blk_size, blk_size) for i in range(n_blk))
+    out_part, w_out_z = out_project(line.tied(cat_b), o_arrays, o_cuts, o_at, n_blk, blk_size)
+    line.wait(out_part)
+
+    def ctx_sum(x):
+        return lax.psum_scatter(x, "ctx", scatter_dimension=0, tiled=True)
+
+    out_sum = ctx_sum(out_part)
+
     line.wait(dy_all)
     d_att, d_proj, sum_pre, dy = d_cat_parts(
-        line.tied(dy_all), row_cuts, rank_places, w_out_z, slope, wide_a
+        line.tied(dy_all), rank_places, w_out_z, slope, wide_a
     )
     line.wait(d_att)
+    d_proj, *sum_qkv = attention_back(
+        q_b, k_b, v_b, cat_b, line.tied(d_att), lse, tables, d_proj, n_heads
+    )
+    line.wait(d_proj)
+    norm_part = norm_back(line.tied(d_proj), w_in_all, rank_places, blk_size)
+    line.wait(norm_part)
+    norm_sum = ctx_sum(norm_part)
+
+    half = D // 2
+    out_own, pre_own, qkv_own = [], [], []
+    out_parts, pre_parts, qkv_parts = {}, {}, {}
     away, home = grads(line.tied(cat_b), 0, cat_rows // n_ctx, dy, 0, D, f, n_fsdp)
     line.wait(away)
-    out_move.step()
-    out_own, pre_own, qkv_own = [], [], []
-    out_moves = [Move(line, scatter_job(line.tied(away), home, out_own))] if even else []
-
-    d_proj, *sum_qkv = attention_back(
-        q_b, k_b, v_b, cat_b, line.tied(d_att), lse, tables, d_proj, n_heads
-    )
-    line.wait(d_proj)
-    out_move.step(*out_moves)
-    norm_shares = norm_shares_of(line.tied(d_proj), w_in_all, row_places, n_ctx, blk_size)
-    line.wait(*norm_shares)
-    out_move.end()
+    out_scatter = Move(line, scatter_job(line.tied(away), home, out_own)) if even else None
+    (pre_away,) = grads(line.tied(normed), 1, half, d_proj, wide_q, wide_m, f)
+    line.wait(pre_away)
     if even:
-        out_moves[0].step()
-    norm_move = Move(line, sum_job(line.tied(*norm_shares), norm_sum))
-
-    half = D // 2
-    pre_parts, qkv_parts = {}, {}
-    (pre_away,) = grads(line.tied(normed), 1, half, d_proj, wide_q, wide_m, f)
-    (pre_home,) = grads(after(normed, pre_away), 0, half, d_proj, wide_q, wide_m, f)
-    (qkv_away,) = grads(after(normed, pre_home), 1, half, d_proj, 0, wide_q, f)
-    (qkv_home,) = grads(after(normed, qkv_away), 0, half, d_proj, 0, wide_q, f)
+        out_scatter.step()
+    (pre_home,) = grads(line.tied(normed), 0, half, d_proj, wide_q, wide_m, f, late=(out_sum,))
+    line.wait(pre_home)
+    (qkv_away,) = grads(line.tied(normed), 1, half, d_proj, 0, wide_q, f)
+    line.wait(qkv_away)
+    if even:
+        out_scatter.step()
+    pre_scatter = Move(line, scatter_job(line.tied(pre_away), pre_home, pre_own))
+    (qkv_home,) = grads(line.tied(normed), 0, half, d_proj, 0, wide_q, f)
     line.wait(qkv_home)
-    norm_move.step(*out_moves)
     if even:
-        out_all = lax.all_gather(line.tied(out_own[0]), "ctx", axis=0)
-    pre_scatter = Move(line, scatter_job(line.tied(pre_away), pre_home, pre_own))
+        out_scatter.step(pre_scatter)
+        out_ring = Move(line, ring_job(line.tied(out_own[0]), out_parts))
+    else:
+        pre_scatter.step()
     qkv_scatter = Move(line, scatter_job(line.tied(qkv_away), qkv_home, qkv_own))
     pre_scatter.step()
-    pre_scatter.step()
-    norm_move.end()
+
+    norm_sum = line.tied(norm_sum)
 
     seq_in_t = line.tied(seq_in)
     centred = seq_in_t - jnp.mean(seq_in_t, axis=1, keepdims=True)
@@ -953,7 +955,7 @@
     x_hat = centred * inv_std
     d_norm = jnp.concatenate(
         [
-            lax.dynamic_slice_in_dim(norm_sum[0], position_of(f ^ i) * wide_d, wide_d, 1)
+            lax.dynamic_slice_in_dim(norm_sum.astype(F32), position_of(f ^ i) * wide_d, wide_d, 1)
             for i in range(n_fsdp)
         ],
         axis=1,
@@ -967,7 +969,7 @@
         - jnp.mean(gain_grad, axis=1, keepdims=True)
         - x_hat * jnp.mean(gain_grad * x_hat, axis=1, keepdims=True)
     )
-    out_y = seq_in + out_sum[0] + b_out
+    out_y = seq_in + out_sum.astype(F32) + b_out
 
     g_b_in_z = jnp.concatenate([x[0] for x in (*sum_qkv, sum_pre)])
     masked = jnp.where(
@@ -975,25 +977,33 @@
     )
     runs = sorted((s, n, i, at) for i in range(n_ctx) for s, n, at in run_offsets(z_runs[i]))
     vector = jnp.concatenate([small.reshape(-1)] + [masked[i, at : at + n] for _, n, i, at in runs])
-    vectors = []
-    vector_move = Move(line, total_job(vector, vectors))
-    line.wait(d_input, out_y)
+    line.wait(d_input)
 
     pre_runs = [[(s - 3 * D, n) for s, n in runs if s >= 3 * D] for runs in z_runs]
     qkv_runs = [[(s, n) for s, n in runs if s < 3 * D] for runs in z_runs]
-    pre_scatter.end(qkv_scatter, vector_move)
+    if even:
+        out_ring.step(pre_scatter, qkv_scatter)
+    else:
+        pre_scatter.step(qkv_scatter)
+    pre_scatter.end()
     pre_ring = Move(line, ring_job(line.tied(pre_own[0]), pre_parts))
-    qkv_scatter.step()
-    qkv_scatter.end(vector_move)
+    vectors = []
     if even:
-        g_w_out = jnp.zeros((shard, D), F32)
-        for rank in range(n_ctx):
-            part = out_all[rank].astype(F32)
-            at_a = jnp.where(is_mixed, rank * cut, rank * share)
-            g_w_out = lax.dynamic_update_slice_in_dim(g_w_out, part[:cut], at_a, 0)
+        out_ring.end(qkv_scatter)
+    vector_move = Move(line, total_job(line.tied(vector), vectors))
+    if even:
+        at = []
+        for j in range(n_ctx):
+            rank = lax.rem(z - j + n_ctx, n_ctx)
+            at.append(jnp.where(is_mixed, rank * cut, rank * share))
             if cut_m:
-                at_m = jnp.where(is_mixed, cut * n_ctx + rank * cut_m, rank * share + cut)
-                g_w_out = lax.dynamic_update_slice_in_dim(g_w_out, part[cut:], at_m, 0)
+                at.append(jnp.where(is_mixed, cut * n_ctx + rank * cut_m, rank * share + cut))
+        g_w_out = join_rows(
+            [line.tied(out_parts[0])] + [out_parts[j] for j in range(1, n_ctx)],
+            jnp.stack(at).astype(jnp.int32),
+            (cut, cut_m) if cut_m else (cut,),
+        )
+        line.wait(g_w_out)
     else:
         blocks = jnp.concatenate([home, away], axis=0).reshape(n_fsdp, -1, D)
         g_out = jnp.concatenate(
@@ -1004,9 +1014,11 @@
         spread = lax.dynamic_update_slice_in_dim(spread, g_out[wide_a:], D + z * wide_m, 0)
         g_w_out = lax.psum_scatter(spread.astype(F32), "fsdp", scatter_dimension=0, tiled=True)
         g_w_out = lax.psum(g_w_out, "ctx")
-    pre_ring.step(vector_move)
+    pre_ring.step(qkv_scatter, vector_move)
+    qkv_scatter.end()
+    qkv_ring = Move(line, ring_job(line.tied(qkv_own[0]), qkv_parts))
     pre_ring.end(vector_move)
-    qkv_ring = Move(line, ring_job(line.tied(qkv_own[0]), qkv_parts))
+    vector_move.step()
     in_turn = range(n_ctx)
     g_w_in = spread_columns(
         None,
@@ -1014,8 +1026,9 @@
         z, pre_runs, in_cols, 3 * D, in_cols - 3 * D,
     )
     line.wait(g_w_in)
-    vector_move.end(qkv_ring)
-    qkv_ring.end()
+    qkv_ring.step(vector_move)
+    qkv_ring.end(vector_move)
+    vector_move.end()
     g_w_in = spread_columns(
         g_w_in, [qkv_parts[j] for j in in_turn], z, qkv_runs, in_cols, 0, 3 * D
     )

time: 612 us -> 587 us (0.959)
  local copies, waits for them, and re-layouts: 37.8 us -> 24.5 us
  other arithmetic: 56.1 us -> 43.3 us
  starting transfers between devices: 59.5 us -> 49.2 us
  Pallas kernels: 210 us -> 218 us
    ppermute x15 -> x12, waiting for transfers between devices: 129 us -> 144 us  [pass_on(): return lax.ppermute(x, 'ctx', [(i, (i + hops) % n) for i in range(n)])]
    dynamic_update_slice x8 -> x0, local copies, waits for them, and re-layouts: 13.6 us -> none  [the longest x4 9.39 us: shards(): g_w_out = lax.dynamic_update_slice_in_dim(g_w_out, part[:cut], at_a, 0)]
    ppermute x38, waiting for transfers between devices: 98.4 us -> 87.2 us  [swap(): return lax.ppermute(x, axis, [(i, i ^ bit) for i in range(n)])]
    ppermute x15 -> x12, starting transfers between devices: 30.6 us -> 20.2 us  [pass_on(): return lax.ppermute(x, 'ctx', [(i, (i + hops) % n) for i in range(n)])]
    pallas_call x7 -> x8, Pallas kernels: 94.3 us -> 102 us  [the longest x5 53.1 us: grads(): pl.pallas_call(functools.partial(grads_kernel, n_split, len(late)), grid_...]
    convert_element_type x3 -> x1, other arithmetic: 10.2 us -> 2.79 us  [shards(): norm_sum.astype(F32)]
  transfers between devices with their start and end apart: 55 -> 53, of which waited for: 26 -> 27; matrix products, arithmetic and copies ran while one was open for 13% -> 10% of each run, Pallas kernels for 32% -> 35%
where the time goes in v4:
time: 587 us; the launch traced here: 581 us
  waiting for transfers between devices  231 us (39%)
  Pallas kernels  218 us (37%)
  starting transfers between devices  49.2 us (8%)
  other arithmetic  43.3 us (7%)
  local copies, waits for them, and re-layouts  24.5 us (4%)
  between operations  15.3 us (3%)
    ppermute x12, waiting for transfers between devices, pass_on(): return lax.ppermute(x, 'ctx', [(i, (i + hops) % n) for i in range(n)])  144 us
    ppermute x38, waiting for transfers between devices, swap(): return lax.ppermute(x, axis, [(i, i ^ bit) for i in range(n)])  87.2 us
    pallas_call x5, Pallas kernels, grads(): pl.pallas_call(functools.partial(grads_kernel, n_split, len(late)), grid_...  53.1 us
    ppermute x38, starting transfers between devices, swap(): return lax.ppermute(x, axis, [(i, i ^ bit) for i in range(n)])  28.2 us
    pallas_call x1, Pallas kernels, attention_back(): pl.pallas_call(functools.partial(back_kernel, pairs), grid=(pairs,), in_s...  24.9 us
    pallas_call x1, Pallas kernels, norm_back(): pl.pallas_call(functools.partial(norm_kernel_back, blk_size), grid_spec=p...  22.5 us
    pallas_call x1, Pallas kernels, pre_project(): pl.pallas_call(functools.partial(pre_kernel, w_cuts, n_w), grid_spec=pltp...  21 us
    ppermute x12, starting transfers between devices, pass_on(): return lax.ppermute(x, 'ctx', [(i, (i + hops) % n) for i in range(n)])  20.2 us
  transfers between devices with their start and end apart: 53, of which 27 were waited for; matrix products, arithmetic and copies ran while one was open for 10% of the time, Pallas kernels for 35%

profile of v4, /device:TPU:0, one launch (start us, length us, event | category | flops | bytes accessed | tf_op | source)
XLA Modules:
  0.0 581.1 jit_solution(6321495427075259019)
XLA Ops:
  7.2 5.1 pick_columns.1.refs_4_.refs_0_
  12.3 4.8 norm.1
  17.1 3.1 collective-permute-start
  27.0 3.0 fusion
  31.1 2.6 concatenate.84.u_ref
  33.7 2.6 concatenate.85.d_ref
  46.5 21.1 %collective-permute-done.1.refs_3_ = bf16[256,2048]{1,0:T(8,128)(2,1)} collective-permute-done((bf16[256,2048]{1,0:T(8,128)(2,1)}, bf16[256,2048]{1,0:T(8,128)(2,1)}, u32[]{:S(2)}, u32[]{:S(2)}) %collective-permute-start.1) | collective-permute-done | bytes 1048608 | tf_op jit(solution)/shard_map/ppermute | solution.py:596
  74.8 19.0 %collective-permute-done.6.refs_8_.refs_4_ = bf16[128,3584]{1,0:T(8,128)(2,1)S(1)} collective-permute-done((bf16[128,3584]{1,0:T(8,128)(2,1)S(1)}, bf16[128,3584]{1,0:T(8,128)(2,1)S(1)}, u32[]{:S(2)}, u32[]{:S(2)}) %collective-permute-start.6) | collective-permute-done | bytes 917536 | tf_op jit(solution)/shard_map/ppermute | solution.py:605
  100.4 3.7 collective-permute-done.10.refs_12_.refs_8_
  106.8 13.4 %qkv_project.1 = (f32[1024,1536]{1,0:T(8,128)}, bf16[1024,2048]{1,0:T(8,128)(2,1)}, bf16[2048,3584]{1,0:T(8,128)(2,1)}) custom-call(s32[18]{0:T(128)} %get-tuple-element.355.at_ref, bf16[256,2048]{1,0:T(8,128)(2,1)} %get-tuple-element.128.refs_0_, bf16[256,2048]{1,0:T(8,128)(2,1)} %collective-permute-done.refs_1_, bf16[256,2048]{1,0:T(8,128)(2,1)} %copy-done.22, ...), custom_call_target="tpu_custom_call" | custom-call | flops 100663296 | bytes 262144 | tf_op jit(solution)/shard_map/qkv_project/pallas_call | solution.py:382
  120.2 15.2 %attention.1 = (bf16[1024,512]{1,0:T(8,128)(2,1)}, bf16[1024,512]{1,0:T(8,128)(2,1)}, bf16[1024,512]{1,0:T(8,128)(2,1)}, bf16[1024,2560]{1,0:T(8,128)(2,1)}, f32[4,2,1024]{2,1,0:T(2,128)}) custom-call(f32[1024,1536]{1,0:T(8,128)} %get-tuple-element.131.q_ref.k_ref.v_ref, f32[1024,1536]{1,0:T(8,128)} %get-tuple-element.131.q_ref.k_ref.v_ref, ...), custom_call_target="tpu_custom_call" | custom-call | flops 33554432 | bytes 163840 | tf_op jit(solution)/shard_map/attention/pallas_call | solution.py:205
  138.6 21.0 %pre_project.1 = (f32[1024,2048]{1,0:T(8,128)}, bf16[1024,2560]{1,0:T(8,128)(2,1)}, bf16[2048,3584]{1,0:T(8,128)(2,1)}) custom-call(s32[10]{0:T(128)} %constant.89.clone.at_ref, bf16[1024,2048]{1,0:T(8,128)(2,1)} %get-tuple-element.174.x_ref.left_ref, bf16[256,3584]{1,0:T(8,128)(2,1)} %pick_columns.1.refs_4_.refs_0_, ...), custom_call_target="tpu_custom_call", output_to_operand_aliasing={{1}: (13, {}), {2}: (14, {})} | custom-call | flops 134217728 | bytes 393216 | tf_op jit(solution)/shard_map/pre_project/pallas_call | solution.py:421
  163.7 19.1 %out_project.1 = (bf16[1024,2048]{1,0:T(8,128)(2,1)}, bf16[2560,2048]{1,0:T(8,128)(2,1)}) custom-call(s32[18]{0:T(128)} %get-tuple-element.354.at_ref, bf16[1024,2560]{1,0:T(8,128)(2,1)} %get-tuple-element.162.x_ref.att_ref.left_ref, bf16[320,2048]{1,0:T(8,128)(2,1)} %copy-done.8, bf16[320,2048]{1,0:T(8,128)(2,1)} %copy-done.16, ...), custom_call_target="tpu_custom_call" | custom-call | flops 167772160 | bytes 344064 | tf_op jit(solution)/shard_map/out_project/pallas_call | solution.py:463
  183.1 19.3 %d_cat_parts.1 = (bf16[1024,512]{1,0:T(8,128)(2,1)}, bf16[1024,3584]{1,0:T(8,128)(2,1)}, f32[1,2048]{1,0:T(1,128)}, bf16[1024,2048]{1,0:T(8,128)(2,1)}) custom-call(s32[8]{0:T(128)} %copy-done.33, bf16[1024,2048]{1,0:T(8,128)(2,1)} %all-gather.2.cloned.1.call-done.g_ref, bf16[2560,2048]{1,0:T(8,128)(2,1)} %get-tuple-element.153.w_ref, ...), custom_call_target="tpu_custom_call" | custom-call | flops 167772160 | bytes 393216 | tf_op jit(solution)/shard_map/d_cat_parts/pallas_call | solution.py:537
  202.4 24.9 %attention_back.1 = (bf16[1024,3584]{1,0:T(8,128)(2,1)}, f32[1,512]{1,0:T(1,128)}, f32[1,512]{1,0:T(1,128)}, f32[1,512]{1,0:T(1,128)}) custom-call(bf16[1024,512]{1,0:T(8,128)(2,1)} %get-tuple-element.147.q_ref, bf16[1024,512]{1,0:T(8,128)(2,1)} %get-tuple-element.148.k_ref, ...), custom_call_target="tpu_custom_call", output_to_operand_aliasing={{0}: (9, {})} | custom-call | flops 83886080 | bytes 131072 | tf_op jit(solution)/shard_map/attention_back/pallas_call | solution.py:275
  227.3 22.5 %norm_back.1 = bf16[1024,2048]{1,0:T(8,128)(2,1)} custom-call(s32[8]{0:T(128)} %copy-done.33, bf16[1024,3584]{1,0:T(8,128)(2,1)} %get-tuple-element.160.x_ref.right_ref, bf16[2048,3584]{1,0:T(8,128)(2,1)} %get-tuple-element.161.w_ref), custom_call_target="tpu_custom_call" | custom-call | flops 234881024 | bytes 442368 | tf_op jit(solution)/shard_map/norm_back/pallas_call | solution.py:493
  249.8 19.0 %grads.5 = (bf16[1280,2048]{1,0:T(8,128)(2,1)}, bf16[1280,2048]{1,0:T(8,128)(2,1)}) custom-call(s32[1]{0:T(128)} %bitcast.2.f_ref, bf16[1024,2560]{1,0:T(8,128)(2,1)} %get-tuple-element.162.x_ref.att_ref.left_ref, bf16[1024,2048]{1,0:T(8,128)(2,1)} %get-tuple-element.163.right_ref), custom_call_target="tpu_custom_call" | custom-call | flops 167772160 | bytes 311296 | tf_op jit(solution)/shard_map/grads/pallas_call | solution.py:318
  269.0 9.3 %grads.6 = bf16[1024,2048]{1,0:T(8,128)(2,1)} custom-call(s32[1]{0:T(128)} %bitcast.2.f_ref, bf16[1024,2048]{1,0:T(8,128)(2,1)} %get-tuple-element.174.x_ref.left_ref, bf16[1024,3584]{1,0:T(8,128)(2,1)} %get-tuple-element.160.x_ref.right_ref), custom_call_target="tpu_custom_call" | custom-call | flops 67108864 | bytes 163840 | tf_op jit(solution)/shard_map/grads/pallas_call | solution.py:318
  278.3 2.1 add_convert_fusion.6
  283.3 9.1 %grads.7 = bf16[1024,2048]{1,0:T(8,128)(2,1)} custom-call(s32[1]{0:T(128)} %bitcast.2.f_ref, bf16[1024,2048]{1,0:T(8,128)(2,1)} %get-tuple-element.174.x_ref.left_ref, bf16[1024,3584]{1,0:T(8,128)(2,1)} %get-tuple-element.160.x_ref.right_ref, bf16[256,2048]{1,0:T(8,128)(2,1)} %reduce-scatter.3.cloned.1.call-done.refs_0_), custom_call_target="tpu_custom_call" | custom-call | flops 67108864 | bytes 163840 | tf_op jit(solution)/shard_map/grads/pallas_call | solution.py:318
  292.4 7.7 %grads.8 = bf16[1024,1536]{1,0:T(8,128)(2,1)} custom-call(s32[1]{0:T(128)} %bitcast.2.f_ref, bf16[1024,2048]{1,0:T(8,128)(2,1)} %get-tuple-element.174.x_ref.left_ref, bf16[1024,3584]{1,0:T(8,128)(2,1)} %get-tuple-element.160.x_ref.right_ref), custom_call_target="tpu_custom_call" | custom-call | flops 50331648 | bytes 131072 | tf_op jit(solution)/shard_map/grads/pallas_call | solution.py:318
  300.2 3.8 add_convert_fusion.3
  306.9 7.9 %grads.9 = bf16[1024,1536]{1,0:T(8,128)(2,1)} custom-call(s32[1]{0:T(128)} %bitcast.2.f_ref, bf16[1024,2048]{1,0:T(8,128)(2,1)} %get-tuple-element.174.x_ref.left_ref, bf16[1024,3584]{1,0:T(8,128)(2,1)} %get-tuple-element.160.x_ref.right_ref), custom_call_target="tpu_custom_call" | custom-call | flops 50331648 | bytes 131072 | tf_op jit(solution)/shard_map/grads/pallas_call | solution.py:318
  314.8 20.7 %collective-permute-done.24 = bf16[320,2048]{1,0:T(8,128)(2,1)} collective-permute-done((bf16[320,2048]{1,0:T(8,128)(2,1)S(1)}, bf16[320,2048]{1,0:T(8,128)(2,1)}, u32[]{:S(2)}, u32[]{:S(2)}) %collective-permute-start.24) | collective-permute-done | bytes 1310752 | tf_op jit(solution)/shard_map/ppermute | solution.py:605
  341.1 3.5 add_convert_fusion.1
  345.4 3.2 collective-permute-start.30
  348.6 3.8 collective-permute-done.27
  352.9 2.8 convert_element_type.281
  355.7 4.7 add_convert_fusion.11
  369.6 8.8 %collective-permute-done.29.refs_1_ = bf16[320,2048]{1,0:T(8,128)(2,1)} collective-permute-done((bf16[320,2048]{1,0:T(8,128)(2,1)S(1)}, bf16[320,2048]{1,0:T(8,128)(2,1)}, u32[]{:S(2)}, u32[]{:S(2)}) %collective-permute-start.29) | collective-permute-done | bytes 1310752 | tf_op jit(solution)/shard_map/ppermute | solution.py:596
  378.4 24.5 %collective-permute-done.30.refs_3_ = bf16[320,2048]{1,0:T(8,128)(2,1)} collective-permute-done((bf16[320,2048]{1,0:T(8,128)(2,1)S(1)}, bf16[320,2048]{1,0:T(8,128)(2,1)}, u32[]{:S(2)}, u32[]{:S(2)}) %collective-permute-start.30) | collective-permute-done | bytes 1310752 | tf_op jit(solution)/shard_map/ppermute | solution.py:596
  407.5 2.2 add_convert_fusion.9
  411.4 2.2 collective-permute-start.35
  413.7 3.2 collective-permute-done.37
  416.9 20.1 %collective-permute-done.36.refs_2_ = bf16[320,2048]{1,0:T(8,128)(2,1)} collective-permute-done((bf16[320,2048]{1,0:T(8,128)(2,1)}, bf16[320,2048]{1,0:T(8,128)(2,1)}, u32[]{:S(2)}, u32[]{:S(2)}) %collective-permute-start.36) | collective-permute-done | bytes 1310752 | tf_op jit(solution)/shard_map/ppermute | solution.py:596
  443.6 7.6 %join_rows.1 = f32[1280,2048]{1,0:T(8,128)} custom-call(s32[8]{0:T(128)} %stack.71.at_ref, bf16[320,2048]{1,0:T(8,128)(2,1)} %copy-done.7, bf16[320,2048]{1,0:T(8,128)(2,1)} %collective-permute-done.29.refs_1_, bf16[320,2048]{1,0:T(8,128)(2,1)} %collective-permute-done.36.refs_2_, bf16[320,2048]{1,0:T(8,128)(2,1)} %collective-permute-done.30.refs_3_), custom_call_target="tpu_custom_call" | custom-call | bytes 245760 | tf_op jit(solution)/shard_map/join_rows/pallas_call | solution.py:577
  451.2 8.1 %collective-permute-done.34.refs_1_ = bf16[256,2048]{1,0:T(8,128)(2,1)} collective-permute-done((bf16[256,2048]{1,0:T(8,128)(2,1)S(1)}, bf16[256,2048]{1,0:T(8,128)(2,1)}, u32[]{:S(2)}, u32[]{:S(2)}) %collective-permute-start.34) | collective-permute-done | bytes 1048608 | tf_op jit(solution)/shard_map/ppermute | solution.py:596
  459.4 20.0 %collective-permute-done.35.refs_3_ = bf16[256,2048]{1,0:T(8,128)(2,1)} collective-permute-done((bf16[256,2048]{1,0:T(8,128)(2,1)S(1)}, bf16[256,2048]{1,0:T(8,128)(2,1)}, u32[]{:S(2)}, u32[]{:S(2)}) %collective-permute-start.35) | collective-permute-done | bytes 1048608 | tf_op jit(solution)/shard_map/ppermute | solution.py:596
  479.9 2.2 add_convert_fusion.17
  482.9 3.2 collective-permute-start.43
  486.8 3.8 collective-permute-done.45
  490.6 17.0 %collective-permute-done.44.refs_2_ = bf16[256,2048]{1,0:T(8,128)(2,1)S(1)} collective-permute-done((bf16[256,2048]{1,0:T(8,128)(2,1)}, bf16[256,2048]{1,0:T(8,128)(2,1)S(1)}, u32[]{:S(2)}, u32[]{:S(2)}) %collective-permute-start.44) | collective-permute-done | bytes 1048608 | tf_op jit(solution)/shard_map/ppermute | solution.py:596
  508.5 3.6 collective-permute-done.46
  512.2 6.2 %spread_columns.2.refs_4_ = f32[256,14336]{1,0:T(8,128)} custom-call(s32[1]{0:T(128)} %bitcast.3.z_ref, bf16[256,2048]{1,0:T(8,128)(2,1)} %copy-done.10, bf16[256,2048]{1,0:T(8,128)(2,1)} %collective-permute-done.34.refs_1_, bf16[256,2048]{1,0:T(8,128)(2,1)} %copy-done.23, bf16[256,2048]{1,0:T(8,128)(2,1)} %collective-permute-done.35.refs_3_), custom_call_target="tpu_custom_call" | custom-call | bytes 196608 | tf_op jit(solution)/shard_map/spread_columns/pallas_call | solution.py:101
  518.5 6.0 %collective-permute-done.42.refs_1_ = bf16[256,1536]{1,0:T(8,128)(2,1)} collective-permute-done((bf16[256,1536]{1,0:T(8,128)(2,1)S(1)}, bf16[256,1536]{1,0:T(8,128)(2,1)}, u32[]{:S(2)}, u32[]{:S(2)}) %collective-permute-start.42) | collective-permute-done | bytes 786464 | tf_op jit(solution)/shard_map/ppermute | solution.py:596
  524.4 15.9 %collective-permute-done.43.refs_3_ = bf16[256,1536]{1,0:T(8,128)(2,1)S(1)} collective-permute-done((bf16[256,1536]{1,0:T(8,128)(2,1)S(1)}, bf16[256,1536]{1,0:T(8,128)(2,1)S(1)}, u32[]{:S(2)}, u32[]{:S(2)}) %collective-permute-start.43) | collective-permute-done | bytes 786464 | tf_op jit(solution)/shard_map/ppermute | solution.py:596
  544.8 21.2 %collective-permute-done.49 = f32[20480]{0:T(1024)S(1)} collective-permute-done((f32[20480]{0:T(1024)S(1)}, f32[20480]{0:T(1024)S(1)}, u32[]{:S(2)}, u32[]{:S(2)}) %collective-permute-start.49) | collective-permute-done | bytes 81952 | tf_op jit(solution)/shard_map/ppermute | solution.py:605
  566.0 5.5 spread_columns.3
  (285 shorter events, 86.2 us)
Async XLA Ops:
  7.2 175.9 %all-gather.2.cloned.1.call-start = ((), (), s32[]{:S(2)}) async-start(), calls=%async_computation.3 | async-start | bytes 5242880 | tf_op jit(solution)/shard_map/all_gather | solution.py:867
  17.1 29.4 %collective-permute-start = (bf16[256,2048]{1,0:T(8,128)(2,1)}, bf16[256,2048]{1,0:T(8,128)(2,1)}, u32[]{:S(2)}, u32[]{:S(2)}) collective-permute-start(bf16[256,2048]{1,0:T(8,128)(2,1)} %get-tuple-element.128.refs_0_), channel_id=1, source_target_pairs={{0,8},{8,16},{16,24},{24,0},{1,9},{9,17},{17,25},{25,1},{2,10},{10... | collective-permute-start | bytes 3145736 | tf_op jit(solution)/shard_map/ppermute | solution.py:596
  20.1 47.4 %collective-permute-start.1 = (bf16[256,2048]{1,0:T(8,128)(2,1)}, bf16[256,2048]{1,0:T(8,128)(2,1)}, u32[]{:S(2)}, u32[]{:S(2)}) collective-permute-start(bf16[256,2048]{1,0:T(8,128)(2,1)} %get-tuple-element.128.refs_0_), channel_id=1, source_target_pairs={{0,24},{8,0},{16,8},{24,16},{1,25},{9,1},{17,9},{25,17},{2,26},{10... | collective-permute-start | bytes 3145736 | tf_op jit(solution)/shard_map/ppermute | solution.py:596
  22.2 45.3 %collective-permute-start.2 = (bf16[256,3584]{1,0:T(8,128)(2,1)S(1)}, bf16[256,3584]{1,0:T(8,128)(2,1)}, u32[]{:S(2)}, u32[]{:S(2)}) collective-permute-start(bf16[256,3584]{1,0:T(8,128)(2,1)S(1)} %copy-done.3), channel_id=1, source_target_pairs={{0,2},{1,3},{2,0},{3,1},{4,6},{5,7},{6,4},{7,5},{8,10},{9,11},{10,... | collective-permute-start | bytes 5505032 | tf_op jit(solution)/shard_map/ppermute | solution.py:605
  23.8 43.7 %collective-permute-start.3 = (bf16[256,3584]{1,0:T(8,128)(2,1)S(1)}, bf16[256,3584]{1,0:T(8,128)(2,1)}, u32[]{:S(2)}, u32[]{:S(2)}) collective-permute-start(bf16[256,3584]{1,0:T(8,128)(2,1)S(1)} %copy-done.3), channel_id=1, source_target_pairs={{0,4},{1,5},{2,6},{3,7},{4,0},{5,1},{6,2},{7,3},{8,12},{9,13},{10,... | collective-permute-start | bytes 5505032 | tf_op jit(solution)/shard_map/ppermute | solution.py:605
  25.4 42.2 %collective-permute-start.4 = (bf16[256,3584]{1,0:T(8,128)(2,1)S(1)}, bf16[256,3584]{1,0:T(8,128)(2,1)}, u32[]{:S(2)}, u32[]{:S(2)}) collective-permute-start(bf16[256,3584]{1,0:T(8,128)(2,1)S(1)} %copy-done.3), channel_id=1, source_target_pairs={{0,1},{1,0},{2,3},{3,2},{4,5},{5,4},{6,7},{7,6},{8,9},{9,8},{10,11... | collective-permute-start | bytes 5505032 | tf_op jit(solution)/shard_map/ppermute | solution.py:605
  67.5 27.7 %collective-permute-start.8 = (bf16[256,3584]{1,0:T(8,128)(2,1)}, bf16[256,3584]{1,0:T(8,128)(2,1)S(1)}, u32[]{:S(2)}, u32[]{:S(2)}) collective-permute-start(bf16[256,3584]{1,0:T(8,128)(2,1)} %collective-permute-done.2.refs_5_.refs_1_), channel_id=1, source_target_pairs={{0,1},{1,0},{2,3},{3,2},{4,5},{5,4},{6,7},{7,6},{8,9},{9,8},{10,11... | collective-permute-start | bytes 5505032 | tf_op jit(solution)/shard_map/ppermute | solution.py:605
  67.6 27.7 %collective-permute-start.9 = (bf16[256,3584]{1,0:T(8,128)(2,1)}, bf16[256,3584]{1,0:T(8,128)(2,1)}, u32[]{:S(2)}, u32[]{:S(2)}) collective-permute-start(bf16[256,3584]{1,0:T(8,128)(2,1)} %collective-permute-done.3.refs_6_.refs_2_), channel_id=1, source_target_pairs={{0,1},{1,0},{2,3},{3,2},{4,5},{5,4},{6,7},{7,6},{8,9},{9,8},{10,11... | collective-permute-start | bytes 5505032 | tf_op jit(solution)/shard_map/ppermute | solution.py:605
  68.1 27.2 %collective-permute-start.5 = (bf16[256,2048]{1,0:T(8,128)(2,1)}, bf16[256,2048]{1,0:T(8,128)(2,1)S(1)}, u32[]{:S(2)}, u32[]{:S(2)}) collective-permute-start(bf16[256,2048]{1,0:T(8,128)(2,1)} %collective-permute-done.refs_1_), channel_id=1, source_target_pairs={{0,8},{8,16},{16,24},{24,0},{1,9},{9,17},{17,25},{25,1},{2,10},{10... | collective-permute-start | bytes 3145736 | tf_op jit(solution)/shard_map/ppermute | solution.py:596
  71.7 22.1 %collective-permute-start.6 = (bf16[128,3584]{1,0:T(8,128)(2,1)S(1)}, bf16[128,3584]{1,0:T(8,128)(2,1)S(1)}, u32[]{:S(2)}, u32[]{:S(2)}) collective-permute-start(bf16[128,3584]{1,0:T(8,128)(2,1)S(1)} %slice.575), channel_id=1, source_target_pairs={{0,4},{1,5},{2,6},{3,7},{4,0},{5,1},{6,2},{7,3},{8,12},{9,13},{10,... | collective-permute-start | bytes 2752520 | tf_op jit(solution)/shard_map/ppermute | solution.py:605
  73.3 21.8 %collective-permute-start.7 = (bf16[128,3584]{1,0:T(8,128)(2,1)S(1)}, bf16[128,3584]{1,0:T(8,128)(2,1)S(1)}, u32[]{:S(2)}, u32[]{:S(2)}) collective-permute-start(bf16[128,3584]{1,0:T(8,128)(2,1)S(1)} %slice.576), channel_id=1, source_target_pairs={{0,2},{1,3},{2,0},{3,1},{4,6},{5,7},{6,4},{7,5},{8,10},{9,11},{10,... | collective-permute-start | bytes 2752520 | tf_op jit(solution)/shard_map/ppermute | solution.py:605
  96.4 186.9 %reduce-scatter.3.cloned.1.call-start = ((), (), s32[]{:S(2)}) async-start(), calls=%async_computation.2 | async-start | bytes 5242880 | tf_op jit(solution)/shard_map/reduce_scatter | solution.py:906
  96.9 38.5 %collective-permute-start.12 = (bf16[320,2048]{1,0:T(8,128)(2,1)S(1)}, bf16[320,2048]{1,0:T(8,128)(2,1)S(1)}, u32[]{:S(2)}, u32[]{:S(2)}) collective-permute-start(bf16[320,2048]{1,0:T(8,128)(2,1)S(1)} %maximum_select_fusion.refs_0_), channel_id=1, source_target_pairs={{0,2},{1,3},{2,0},{3,1},{4,6},{5,7},{6,4},{7,5},{8,10},{9,11},{10,... | collective-permute-start | bytes 3932168 | tf_op jit(solution)/shard_map/ppermute | solution.py:605
  98.5 36.9 %collective-permute-start.13 = (bf16[320,2048]{1,0:T(8,128)(2,1)S(1)}, bf16[320,2048]{1,0:T(8,128)(2,1)S(1)}, u32[]{:S(2)}, u32[]{:S(2)}) collective-permute-start(bf16[320,2048]{1,0:T(8,128)(2,1)S(1)} %maximum_select_fusion.refs_0_), channel_id=1, source_target_pairs={{0,4},{1,5},{2,6},{3,7},{4,0},{5,1},{6,2},{7,3},{8,12},{9,13},{10,... | collective-permute-start | bytes 3932168 | tf_op jit(solution)/shard_map/ppermute | solution.py:605
  99.9 35.5 %collective-permute-start.14 = (bf16[320,2048]{1,0:T(8,128)(2,1)S(1)}, bf16[320,2048]{1,0:T(8,128)(2,1)}, u32[]{:S(2)}, u32[]{:S(2)}) collective-permute-start(bf16[320,2048]{1,0:T(8,128)(2,1)S(1)} %maximum_select_fusion.refs_0_), channel_id=1, source_target_pairs={{0,1},{1,0},{2,3},{3,2},{4,5},{5,4},{6,7},{7,6},{8,9},{9,8},{10,11... | collective-permute-start | bytes 3932168 | tf_op jit(solution)/shard_map/ppermute | solution.py:605
  100.4 5.4 collective-permute-start.11
  135.5 24.2 %collective-permute-start.17 = (bf16[320,2048]{1,0:T(8,128)(2,1)S(1)}, bf16[320,2048]{1,0:T(8,128)(2,1)S(1)}, u32[]{:S(2)}, u32[]{:S(2)}) collective-permute-start(bf16[320,2048]{1,0:T(8,128)(2,1)S(1)} %collective-permute-done.12.refs_1_), channel_id=1, source_target_pairs={{0,1},{1,0},{2,3},{3,2},{4,5},{5,4},{6,7},{7,6},{8,9},{9,8},{10,11... | collective-permute-start | bytes 3932168 | tf_op jit(solution)/shard_map/ppermute | solution.py:605
  135.7 24.0 %collective-permute-start.18 = (bf16[320,2048]{1,0:T(8,128)(2,1)S(1)}, bf16[320,2048]{1,0:T(8,128)(2,1)S(1)}, u32[]{:S(2)}, u32[]{:S(2)}) collective-permute-start(bf16[320,2048]{1,0:T(8,128)(2,1)S(1)} %collective-permute-done.13.refs_2_), channel_id=1, source_target_pairs={{0,1},{1,0},{2,3},{3,2},{4,5},{5,4},{6,7},{7,6},{8,9},{9,8},{10,11... | collective-permute-start | bytes 3932168 | tf_op jit(solution)/shard_map/ppermute | solution.py:605
  137.2 22.4 %collective-permute-start.15 = (bf16[160,2048]{1,0:T(8,128)(2,1)}, bf16[160,2048]{1,0:T(8,128)(2,1)S(1)}, u32[]{:S(2)}, u32[]{:S(2)}) collective-permute-start(bf16[160,2048]{1,0:T(8,128)(2,1)} %slice.577), channel_id=1, source_target_pairs={{0,4},{1,5},{2,6},{3,7},{4,0},{5,1},{6,2},{7,3},{8,12},{9,13},{10,... | collective-permute-start | bytes 1966088 | tf_op jit(solution)/shard_map/ppermute | solution.py:605
  137.8 21.8 %collective-permute-start.16 = (bf16[160,2048]{1,0:T(8,128)(2,1)S(1)}, bf16[160,2048]{1,0:T(8,128)(2,1)S(1)}, u32[]{:S(2)}, u32[]{:S(2)}) collective-permute-start(bf16[160,2048]{1,0:T(8,128)(2,1)S(1)} %slice.578), channel_id=1, source_target_pairs={{0,2},{1,3},{2,0},{3,1},{4,6},{5,7},{6,4},{7,5},{8,10},{9,11},{10,... | collective-permute-start | bytes 1966088 | tf_op jit(solution)/shard_map/ppermute | solution.py:605
  182.8 170.1 %reduce-scatter.5.cloned.1.call-start = ((), (), s32[]{:S(2)}) async-start(), calls=%async_computation.4 | async-start | bytes 5242880 | tf_op jit(solution)/shard_map/reduce_scatter | solution.py:906
  268.8 9.5 %collective-permute-start.21 = (bf16[1280,2048]{1,0:T(8,128)(2,1)}, bf16[1280,2048]{1,0:T(8,128)(2,1)}, u32[]{:S(2)}, u32[]{:S(2)}) collective-permute-start(bf16[1280,2048]{1,0:T(8,128)(2,1)} %get-tuple-element.165), channel_id=1, source_target_pairs={{0,1},{1,0},{2,3},{3,2},{4,5},{5,4},{6,7},{7,6},{8,9},{9,8},{10,11... | collective-permute-start | bytes 15728648 | tf_op jit(solution)/shard_map/ppermute | solution.py:605
  280.5 19.6 %collective-permute-start.22 = (bf16[160,2048]{1,0:T(8,128)(2,1)S(1)}, bf16[160,2048]{1,0:T(8,128)(2,1)S(1)}, u32[]{:S(2)}, u32[]{:S(2)}) collective-permute-start(bf16[160,2048]{1,0:T(8,128)(2,1)S(1)} %get-tuple-element.263), channel_id=1, source_target_pairs={{0,4},{1,5},{2,6},{3,7},{4,0},{5,1},{6,2},{7,3},{8,12},{9,13},{10,... | collective-permute-start | bytes 1966088 | tf_op jit(solution)/shard_map/ppermute | solution.py:605
  281.8 18.3 %collective-permute-start.23 = (bf16[160,2048]{1,0:T(8,128)(2,1)S(1)}, bf16[160,2048]{1,0:T(8,128)(2,1)S(1)}, u32[]{:S(2)}, u32[]{:S(2)}) collective-permute-start(bf16[160,2048]{1,0:T(8,128)(2,1)S(1)} %get-tuple-element.262), channel_id=1, source_target_pairs={{0,2},{1,3},{2,0},{3,1},{4,6},{5,7},{6,4},{7,5},{8,10},{9,11},{10,... | collective-permute-start | bytes 1966088 | tf_op jit(solution)/shard_map/ppermute | solution.py:605
  300.1 36.9 %collective-permute-start.26 = (bf16[1024,2048]{1,0:T(8,128)(2,1)}, bf16[1024,2048]{1,0:T(8,128)(2,1)}, u32[]{:S(2)}, u32[]{:S(2)}) collective-permute-start(bf16[1024,2048]{1,0:T(8,128)(2,1)} %grads.6), channel_id=1, source_target_pairs={{0,1},{1,0},{2,3},{3,2},{4,5},{5,4},{6,7},{7,6},{8,9},{9,8},{10,11... | collective-permute-start | bytes 12582920 | tf_op jit(solution)/shard_map/ppermute | solution.py:605
  304.2 31.3 %collective-permute-start.24 = (bf16[320,2048]{1,0:T(8,128)(2,1)S(1)}, bf16[320,2048]{1,0:T(8,128)(2,1)}, u32[]{:S(2)}, u32[]{:S(2)}) collective-permute-start(bf16[320,2048]{1,0:T(8,128)(2,1)S(1)} %pad_maximum_fusion), channel_id=1, source_target_pairs={{0,2},{1,3},{2,0},{3,1},{4,6},{5,7},{6,4},{7,5},{8,10},{9,11},{10,... | collective-permute-start | bytes 3932168 | tf_op jit(solution)/shard_map/ppermute | solution.py:605
  305.8 31.2 %collective-permute-start.25 = (bf16[320,2048]{1,0:T(8,128)(2,1)}, bf16[320,2048]{1,0:T(8,128)(2,1)}, u32[]{:S(2)}, u32[]{:S(2)}) collective-permute-start(bf16[320,2048]{1,0:T(8,128)(2,1)} %pad_maximum_fusion.1), channel_id=1, source_target_pairs={{0,4},{1,5},{2,6},{3,7},{4,0},{5,1},{6,2},{7,3},{8,12},{9,13},{10,... | collective-permute-start | bytes 3932168 | tf_op jit(solution)/shard_map/ppermute | solution.py:605
  339.0 13.4 %collective-permute-start.27 = (bf16[128,2048]{1,0:T(8,128)(2,1)S(1)}, bf16[128,2048]{1,0:T(8,128)(2,1)}, u32[]{:S(2)}, u32[]{:S(2)}) collective-permute-start(bf16[128,2048]{1,0:T(8,128)(2,1)S(1)} %get-tuple-element.269), channel_id=1, source_target_pairs={{0,4},{1,5},{2,6},{3,7},{4,0},{5,1},{6,2},{7,3},{8,12},{9,13},{10,... | collective-permute-start | bytes 1572872 | tf_op jit(solution)/shard_map/ppermute | solution.py:605
  339.8 13.0 %collective-permute-start.28 = (bf16[128,2048]{1,0:T(8,128)(2,1)S(1)}, bf16[128,2048]{1,0:T(8,128)(2,1)}, u32[]{:S(2)}, u32[]{:S(2)}) collective-permute-start(bf16[128,2048]{1,0:T(8,128)(2,1)S(1)} %get-tuple-element.268), channel_id=1, source_target_pairs={{0,2},{1,3},{2,0},{3,1},{4,6},{5,7},{6,4},{7,5},{8,10},{9,11},{10,... | collective-permute-start | bytes 1572872 | tf_op jit(solution)/shard_map/ppermute | solution.py:605
  344.7 33.7 %collective-permute-start.29 = (bf16[320,2048]{1,0:T(8,128)(2,1)S(1)}, bf16[320,2048]{1,0:T(8,128)(2,1)}, u32[]{:S(2)}, u32[]{:S(2)}) collective-permute-start(bf16[320,2048]{1,0:T(8,128)(2,1)S(1)} %pad_maximum_fusion.2.refs_0_), channel_id=1, source_target_pairs={{0,8},{8,16},{16,24},{24,0},{1,9},{9,17},{17,25},{25,1},{2,10},{10... | collective-permute-start | bytes 3932168 | tf_op jit(solution)/shard_map/ppermute | solution.py:596
  345.4 57.6 %collective-permute-start.30 = (bf16[320,2048]{1,0:T(8,128)(2,1)S(1)}, bf16[320,2048]{1,0:T(8,128)(2,1)}, u32[]{:S(2)}, u32[]{:S(2)}) collective-permute-start(bf16[320,2048]{1,0:T(8,128)(2,1)S(1)} %pad_maximum_fusion.2.refs_0_), channel_id=1, source_target_pairs={{0,24},{8,0},{16,8},{24,16},{1,25},{9,1},{17,9},{25,17},{2,26},{10... | collective-permute-start | bytes 3932168 | tf_op jit(solution)/shard_map/ppermute | solution.py:596
  348.6 54.3 %collective-permute-start.33 = (bf16[1024,1536]{1,0:T(8,128)(2,1)}, bf16[1024,1536]{1,0:T(8,128)(2,1)}, u32[]{:S(2)}, u32[]{:S(2)}) collective-permute-start(bf16[1024,1536]{1,0:T(8,128)(2,1)} %grads.8), channel_id=1, source_target_pairs={{0,1},{1,0},{2,3},{3,2},{4,5},{5,4},{6,7},{7,6},{8,9},{9,8},{10,11... | collective-permute-start | bytes 9437192 | tf_op jit(solution)/shard_map/ppermute | solution.py:605
  362.0 40.9 %collective-permute-start.31 = (bf16[256,2048]{1,0:T(8,128)(2,1)S(1)}, bf16[256,2048]{1,0:T(8,128)(2,1)S(1)}, u32[]{:S(2)}, u32[]{:S(2)}) collective-permute-start(bf16[256,2048]{1,0:T(8,128)(2,1)S(1)} %pad_maximum_fusion.3), channel_id=1, source_target_pairs={{0,2},{1,3},{2,0},{3,1},{4,6},{5,7},{6,4},{7,5},{8,10},{9,11},{10,... | collective-permute-start | bytes 3145736 | tf_op jit(solution)/shard_map/ppermute | solution.py:605
  363.5 39.5 %collective-permute-start.32 = (bf16[256,2048]{1,0:T(8,128)(2,1)S(1)}, bf16[256,2048]{1,0:T(8,128)(2,1)S(1)}, u32[]{:S(2)}, u32[]{:S(2)}) collective-permute-start(bf16[256,2048]{1,0:T(8,128)(2,1)S(1)} %pad_maximum_fusion.4), channel_id=1, source_target_pairs={{0,4},{1,5},{2,6},{3,7},{4,0},{5,1},{6,2},{7,3},{8,12},{9,13},{10,... | collective-permute-start | bytes 3145736 | tf_op jit(solution)/shard_map/ppermute | solution.py:605
  403.0 34.0 %collective-permute-start.36 = (bf16[320,2048]{1,0:T(8,128)(2,1)}, bf16[320,2048]{1,0:T(8,128)(2,1)}, u32[]{:S(2)}, u32[]{:S(2)}) collective-permute-start(bf16[320,2048]{1,0:T(8,128)(2,1)} %collective-permute-done.29.refs_1_), channel_id=1, source_target_pairs={{0,8},{8,16},{16,24},{24,0},{1,9},{9,17},{17,25},{25,1},{2,10},{10... | collective-permute-start | bytes 3932168 | tf_op jit(solution)/shard_map/ppermute | solution.py:596
  406.2 10.6 %collective-permute-start.37 = (bf16[128,1536]{1,0:T(8,128)(2,1)S(1)}, bf16[128,1536]{1,0:T(8,128)(2,1)S(1)}, u32[]{:S(2)}, u32[]{:S(2)}) collective-permute-start(bf16[128,1536]{1,0:T(8,128)(2,1)S(1)} %get-tuple-element.277), channel_id=1, source_target_pairs={{0,4},{1,5},{2,6},{3,7},{4,0},{5,1},{6,2},{7,3},{8,12},{9,13},{10,... | collective-permute-start | bytes 1179656 | tf_op jit(solution)/shard_map/ppermute | solution.py:605
  407.0 10.0 %collective-permute-start.38 = (bf16[128,1536]{1,0:T(8,128)(2,1)S(1)}, bf16[128,1536]{1,0:T(8,128)(2,1)S(1)}, u32[]{:S(2)}, u32[]{:S(2)}) collective-permute-start(bf16[128,1536]{1,0:T(8,128)(2,1)S(1)} %get-tuple-element.276), channel_id=1, source_target_pairs={{0,2},{1,3},{2,0},{3,1},{4,6},{5,7},{6,4},{7,5},{8,10},{9,11},{10,... | collective-permute-start | bytes 1179656 | tf_op jit(solution)/shard_map/ppermute | solution.py:605
  409.8 49.6 %collective-permute-start.34 = (bf16[256,2048]{1,0:T(8,128)(2,1)S(1)}, bf16[256,2048]{1,0:T(8,128)(2,1)}, u32[]{:S(2)}, u32[]{:S(2)}) collective-permute-start(bf16[256,2048]{1,0:T(8,128)(2,1)S(1)} %pad_maximum_fusion.5.refs_0_), channel_id=1, source_target_pairs={{0,8},{8,16},{16,24},{24,0},{1,9},{9,17},{17,25},{25,1},{2,10},{10... | collective-permute-start | bytes 3145736 | tf_op jit(solution)/shard_map/ppermute | solution.py:596
  411.4 67.9 %collective-permute-start.35 = (bf16[256,2048]{1,0:T(8,128)(2,1)S(1)}, bf16[256,2048]{1,0:T(8,128)(2,1)}, u32[]{:S(2)}, u32[]{:S(2)}) collective-permute-start(bf16[256,2048]{1,0:T(8,128)(2,1)S(1)} %pad_maximum_fusion.5.refs_0_), channel_id=1, source_target_pairs={{0,24},{8,0},{16,8},{24,16},{1,25},{9,1},{17,9},{25,17},{2,26},{10... | collective-permute-start | bytes 3145736 | tf_op jit(solution)/shard_map/ppermute | solution.py:596
  439.8 39.5 %collective-permute-start.39 = (bf16[256,1536]{1,0:T(8,128)(2,1)}, bf16[256,1536]{1,0:T(8,128)(2,1)}, u32[]{:S(2)}, u32[]{:S(2)}) collective-permute-start(bf16[256,1536]{1,0:T(8,128)(2,1)} %pad_maximum_fusion.6), channel_id=1, source_target_pairs={{0,2},{1,3},{2,0},{3,1},{4,6},{5,7},{6,4},{7,5},{8,10},{9,11},{10,... | collective-permute-start | bytes 2359304 | tf_op jit(solution)/shard_map/ppermute | solution.py:605
  441.4 37.9 %collective-permute-start.40 = (bf16[256,1536]{1,0:T(8,128)(2,1)}, bf16[256,1536]{1,0:T(8,128)(2,1)}, u32[]{:S(2)}, u32[]{:S(2)}) collective-permute-start(bf16[256,1536]{1,0:T(8,128)(2,1)} %pad_maximum_fusion.7), channel_id=1, source_target_pairs={{0,4},{1,5},{2,6},{3,7},{4,0},{5,1},{6,2},{7,3},{8,12},{9,13},{10,... | collective-permute-start | bytes 2359304 | tf_op jit(solution)/shard_map/ppermute | solution.py:605
  442.8 36.5 %collective-permute-start.41 = (f32[20480]{0:T(1024)S(1)}, f32[20480]{0:T(1024)S(1)}, u32[]{:S(2)}, u32[]{:S(2)}) collective-permute-start(f32[20480]{0:T(1024)S(1)} %concatenate.101), channel_id=1, source_target_pairs={{0,1},{1,0},{2,3},{3,2},{4,5},{5,4},{6,7},{7,6},{8,9},{9,8},{10,11... | collective-permute-start | bytes 245768 | tf_op jit(solution)/shard_map/ppermute | solution.py:605
  479.3 28.2 %collective-permute-start.44 = (bf16[256,2048]{1,0:T(8,128)(2,1)}, bf16[256,2048]{1,0:T(8,128)(2,1)S(1)}, u32[]{:S(2)}, u32[]{:S(2)}) collective-permute-start(bf16[256,2048]{1,0:T(8,128)(2,1)} %collective-permute-done.34.refs_1_), channel_id=1, source_target_pairs={{0,8},{8,16},{16,24},{24,0},{1,9},{9,17},{17,25},{25,1},{2,10},{10... | collective-permute-start | bytes 3145736 | tf_op jit(solution)/shard_map/ppermute | solution.py:596
  482.2 42.2 %collective-permute-start.42 = (bf16[256,1536]{1,0:T(8,128)(2,1)S(1)}, bf16[256,1536]{1,0:T(8,128)(2,1)}, u32[]{:S(2)}, u32[]{:S(2)}) collective-permute-start(bf16[256,1536]{1,0:T(8,128)(2,1)S(1)} %pad_maximum_fusion.8.refs_0_), channel_id=1, source_target_pairs={{0,8},{8,16},{16,24},{24,0},{1,9},{9,17},{17,25},{25,1},{2,10},{10... | collective-permute-start | bytes 2359304 | tf_op jit(solution)/shard_map/ppermute | solution.py:596
  482.9 57.4 %collective-permute-start.43 = (bf16[256,1536]{1,0:T(8,128)(2,1)S(1)}, bf16[256,1536]{1,0:T(8,128)(2,1)S(1)}, u32[]{:S(2)}, u32[]{:S(2)}) collective-permute-start(bf16[256,1536]{1,0:T(8,128)(2,1)S(1)} %pad_maximum_fusion.8.refs_0_), channel_id=1, source_target_pairs={{0,24},{8,0},{16,8},{24,16},{1,25},{9,1},{17,9},{25,17},{2,26},{10... | collective-permute-start | bytes 2359304 | tf_op jit(solution)/shard_map/ppermute | solution.py:596
  512.1 29.8 %collective-permute-start.47 = (f32[20480]{0:T(1024)S(1)}, f32[20480]{0:T(1024)S(1)}, u32[]{:S(2)}, u32[]{:S(2)}) collective-permute-start(f32[20480]{0:T(1024)S(1)} %add.384), channel_id=1, source_target_pairs={{0,8},{8,0},{16,24},{24,16},{1,9},{9,1},{17,25},{25,17},{2,10},{10... | collective-permute-start | bytes 245768 | tf_op jit(solution)/shard_map/ppermute | solution.py:605
  541.9 24.0 %collective-permute-start.48 = (bf16[256,1536]{1,0:T(8,128)(2,1)}, bf16[256,1536]{1,0:T(8,128)(2,1)}, u32[]{:S(2)}, u32[]{:S(2)}) collective-permute-start(bf16[256,1536]{1,0:T(8,128)(2,1)} %collective-permute-done.42.refs_1_), channel_id=1, source_target_pairs={{0,8},{8,16},{16,24},{24,0},{1,9},{9,17},{17,25},{25,1},{2,10},{10... | collective-permute-start | bytes 2359304 | tf_op jit(solution)/shard_map/ppermute | solution.py:596
  541.9 24.0 %collective-permute-start.49 = (f32[20480]{0:T(1024)S(1)}, f32[20480]{0:T(1024)S(1)}, u32[]{:S(2)}, u32[]{:S(2)}) collective-permute-start(f32[20480]{0:T(1024)S(1)} %add.385), channel_id=1, source_target_pairs={{0,16},{8,24},{16,0},{24,8},{1,17},{9,25},{17,1},{25,9},{2,18},{10... | collective-permute-start | bytes 245768 | tf_op jit(solution)/shard_map/ppermute | solution.py:605
  (59 other events, 456.4 us)
Sparse Core Ops, SparseCore 0:
  96.5 80.1 all-gather.1
  182.9 76.1 reduce-scatter.2
  269.1 76.4 reduce-scatter.4

commit v5 on v4

--- a/solution.py
+++ b/solution.py
@@ -66,7 +66,7 @@
 def pick_columns(src, z, all_runs):
     rows, cols = src.shape
     width = sum(n for _, n in all_runs[0])
-    step = min(rows, 64)
+    step = min(rows, 128)
     return pl.pallas_call(
         functools.partial(pick_kernel, all_runs),
         grid_spec=pltpu.PrefetchScalarGridSpec(
@@ -96,7 +96,7 @@
 def spread_columns(whole, parts, z, all_runs, cols, first, width_out):
     rows, width = parts[0].shape
     n_ctx = len(parts)
-    step = min(rows, 64)
+    step = min(rows, 128)
     fresh = whole is None
     return pl.pallas_call(
         functools.partial(spread_kernel, all_runs, n_ctx),
@@ -129,7 +129,7 @@
 
 def norm(x, g, gain, beta, f, n_fsdp):
     rows, cols = x.shape
-    step = min(rows, 64)
+    step = min(rows, 128)
     tile = pl.BlockSpec((step, cols), lambda i, f_ref: (i, 0))
     line = pl.BlockSpec((1, cols), lambda i, f_ref: (0, 0))
     own = jax.ShapeDtypeStruct((rows, cols), BF)
@@ -404,13 +404,12 @@
 
 def pre_kernel(w_cuts, n_w, at_ref, x_ref, *refs):
     ws, b_ref = refs[:n_w], refs[n_w]
-    slope_ref, cat_ref, w_ref = refs[-3:]
+    pre_ref, cat_ref, w_ref = refs[-3:]
     lay(ws, w_cuts, at_ref, 0, w_ref)
     for rows in chunks(x_ref.shape[0]):
         pre = dot(x_ref[rows, :], w_ref[...], 1, 0) + b_ref[...]
-        value, slope = gelu_parts(pre)
-        slope_ref[rows, :] = slope
-        cat_ref[rows, :] = value.astype(BF)
+        pre_ref[rows, :] = pre
+        cat_ref[rows, :] = gelu_parts(pre)[0].astype(BF)
 
 
 def pre_project(x, ws, w_cuts, places, b, cat, w_all, skip, tile):
@@ -507,7 +506,7 @@
     )(places, x, w)
 
 
-def d_cat_kernel(cuts, at_ref, g_ref, w_ref, slope_ref, datt_ref, dproj_ref, sum_ref, x_ref):
+def d_cat_kernel(cuts, at_ref, g_ref, w_ref, pre_ref, datt_ref, dproj_ref, sum_ref, x_ref):
     @pl.when(pl.program_id(0) == 0)
     def _():
         lay([g_ref], cuts, at_ref, 0, x_ref)
@@ -517,15 +516,15 @@
     def _():
         total = 0.0
         for rows in chunks(x_ref.shape[0]):
-            d_pre = slope_ref[rows, :] * dot(x_ref[rows, :], w_ref[...], 1, 1)
+            d_pre = gelu_parts(pre_ref[rows, :])[1] * dot(x_ref[rows, :], w_ref[...], 1, 1)
             dproj_ref[rows, :] = d_pre.astype(BF)
             total = total + jnp.sum(d_pre, axis=0, keepdims=True)
         sum_ref[...] = total
 
 
-def d_cat_parts(g, places, w, slope, wide_a):
+def d_cat_parts(g, places, w, pre_act, wide_a):
     rows, deep = g.shape
-    width = slope.shape[1]
+    width = pre_act.shape[1]
     tile = wide_a
     total = 3 * wide_a + width
     blk = rows // places.shape[0]
@@ -558,7 +557,7 @@
             jax.ShapeDtypeStruct((rows, deep), BF),
         ],
         **big("d_cat_parts", 2 * rows * deep * (width + tile), 2 * deep * rows + (2 * deep + 6 * rows) * width),
-    )(places, g, w, slope)
+    )(places, g, w, pre_act)
 
 
 def join_kernel(n_parts, sizes, at_ref, *refs):
@@ -865,9 +864,9 @@
     while normed_ring.flight is not None:
         normed_ring.step(w_in_move)
     dy_all = lax.all_gather(after(dy_own, *line.due), "ctx", axis=0, tiled=True)
+    w_in_move.end()
     if even:
         w_out_move = Move(line, gather_job(line.tied(w_out_own), w_out_parts))
-    w_in_move.end()
 
     wide_q = 3 * wide_a
     x_cuts = [(j, i * blk_size, blk_size) for j in range(n_ctx) for i in range(per)]
@@ -882,7 +881,7 @@
     line.wait(cat_b)
     if even:
         w_out_move.step()
-    slope, cat_b, w_in_all = pre_project(
+    pre_act, cat_b, w_in_all = pre_project(
         line.tied(normed), w_arrays, w_cuts, w_at, b_in_z, cat_b, w_in_all, wide_q, wide_a
     )
     line.wait(cat_b)
@@ -909,7 +908,7 @@
 
     line.wait(dy_all)
     d_att, d_proj, sum_pre, dy = d_cat_parts(
-        line.tied(dy_all), rank_places, w_out_z, slope, wide_a
+        line.tied(dy_all), rank_places, w_out_z, pre_act, wide_a
     )
     line.wait(d_att)
     d_proj, *sum_qkv = attention_back(

time: 587 us -> 583 us (level)
  transfers between devices with their start and end apart: 53 -> 53, of which waited for: 27 -> 28; matrix products, arithmetic and copies ran while one was open for 10% -> 10% of each run, Pallas kernels for 35% -> 35%
where the time goes in v5:
time: 583 us; the launch traced here: 577 us
  waiting for transfers between devices  230 us (39%)
  Pallas kernels  216 us (37%)
  starting transfers between devices  49.2 us (8%)
  other arithmetic  43.3 us (7%)
  local copies, waits for them, and re-layouts  23.5 us (4%)
  between operations  15.3 us (3%)
    ppermute x12, waiting for transfers between devices, pass_on(): return lax.ppermute(x, 'ctx', [(i, (i + hops) % n) for i in range(n)])  145 us
    ppermute x38, waiting for transfers between devices, swap(): return lax.ppermute(x, axis, [(i, i ^ bit) for i in range(n)])  85.1 us
    pallas_call x5, Pallas kernels, grads(): pl.pallas_call(functools.partial(grads_kernel, n_split, len(late)), grid_...  53.1 us
    ppermute x38, starting transfers between devices, swap(): return lax.ppermute(x, axis, [(i, i ^ bit) for i in range(n)])  28.4 us
    pallas_call x1, Pallas kernels, attention_back(): pl.pallas_call(functools.partial(back_kernel, pairs), grid=(pairs,), in_s...  24.8 us
    pallas_call x1, Pallas kernels, d_cat_parts(): pl.pallas_call(functools.partial(d_cat_kernel, cuts), grid_spec=pltpu.Pre...  22.9 us
    pallas_call x1, Pallas kernels, norm_back(): pl.pallas_call(functools.partial(norm_kernel_back, blk_size), grid_spec=p...  22.5 us
    ppermute x12, starting transfers between devices, pass_on(): return lax.ppermute(x, 'ctx', [(i, (i + hops) % n) for i in range(n)])  20 us
  transfers between devices with their start and end apart: 53, of which 28 were waited for; matrix products, arithmetic and copies ran while one was open for 10% of the time, Pallas kernels for 35%

profile of v5, /device:TPU:0, one launch (start us, length us, event | category | flops | bytes accessed | tf_op | source)
XLA Modules:
  0.0 576.8 jit_solution(16733512712995435431)
XLA Ops:
  7.2 4.3 pick_columns.1.refs_4_.refs_0_
  11.6 3.8 norm.1
  15.4 3.1 collective-permute-start
  25.3 3.0 fusion
  29.4 2.6 concatenate.84.u_ref
  31.9 2.6 concatenate.85.d_ref
  44.8 21.0 %collective-permute-done.1.refs_3_ = bf16[256,2048]{1,0:T(8,128)(2,1)} collective-permute-done((bf16[256,2048]{1,0:T(8,128)(2,1)}, bf16[256,2048]{1,0:T(8,128)(2,1)}, u32[]{:S(2)}, u32[]{:S(2)}) %collective-permute-start.1) | collective-permute-done | bytes 1048608 | tf_op jit(solution)/shard_map/ppermute | solution.py:595
  73.1 19.0 %collective-permute-done.6.refs_8_.refs_4_ = bf16[128,3584]{1,0:T(8,128)(2,1)S(1)} collective-permute-done((bf16[128,3584]{1,0:T(8,128)(2,1)S(1)}, bf16[128,3584]{1,0:T(8,128)(2,1)S(1)}, u32[]{:S(2)}, u32[]{:S(2)}) %collective-permute-start.6) | collective-permute-done | bytes 917536 | tf_op jit(solution)/shard_map/ppermute | solution.py:604
  95.8 2.2 collective-permute-done.10.refs_12_.refs_8_
  102.2 13.8 %qkv_project.1 = (f32[1024,1536]{1,0:T(8,128)}, bf16[1024,2048]{1,0:T(8,128)(2,1)}, bf16[2048,3584]{1,0:T(8,128)(2,1)}) custom-call(s32[18]{0:T(128)} %get-tuple-element.355.at_ref, bf16[256,2048]{1,0:T(8,128)(2,1)} %get-tuple-element.128.refs_0_, bf16[256,2048]{1,0:T(8,128)(2,1)} %collective-permute-done.refs_1_, bf16[256,2048]{1,0:T(8,128)(2,1)} %copy-done.22, ...), custom_call_target="tpu_custom_call" | custom-call | flops 100663296 | bytes 262144 | tf_op jit(solution)/shard_map/qkv_project/pallas_call | solution.py:382
  116.0 15.2 %attention.1 = (bf16[1024,512]{1,0:T(8,128)(2,1)}, bf16[1024,512]{1,0:T(8,128)(2,1)}, bf16[1024,512]{1,0:T(8,128)(2,1)}, bf16[1024,2560]{1,0:T(8,128)(2,1)}, f32[4,2,1024]{2,1,0:T(2,128)}) custom-call(f32[1024,1536]{1,0:T(8,128)} %get-tuple-element.131.q_ref.k_ref.v_ref, f32[1024,1536]{1,0:T(8,128)} %get-tuple-element.131.q_ref.k_ref.v_ref, ...), custom_call_target="tpu_custom_call" | custom-call | flops 33554432 | bytes 163840 | tf_op jit(solution)/shard_map/attention/pallas_call | solution.py:205
  134.9 18.6 %pre_project.1 = (f32[1024,2048]{1,0:T(8,128)}, bf16[1024,2560]{1,0:T(8,128)(2,1)}, bf16[2048,3584]{1,0:T(8,128)(2,1)}) custom-call(s32[10]{0:T(128)} %constant.89.clone.at_ref, bf16[1024,2048]{1,0:T(8,128)(2,1)} %get-tuple-element.174.x_ref.left_ref, bf16[256,3584]{1,0:T(8,128)(2,1)} %pick_columns.1.refs_4_.refs_0_, ...), custom_call_target="tpu_custom_call", output_to_operand_aliasing={{1}: (13, {}), {2}: (14, {})} | custom-call | flops 134217728 | bytes 393216 | tf_op jit(solution)/shard_map/pre_project/pallas_call | solution.py:420
  157.5 19.1 %out_project.1 = (bf16[1024,2048]{1,0:T(8,128)(2,1)}, bf16[2560,2048]{1,0:T(8,128)(2,1)}) custom-call(s32[18]{0:T(128)} %get-tuple-element.354.at_ref, bf16[1024,2560]{1,0:T(8,128)(2,1)} %get-tuple-element.162.x_ref.att_ref.left_ref, bf16[320,2048]{1,0:T(8,128)(2,1)} %copy-done.8, bf16[320,2048]{1,0:T(8,128)(2,1)} %copy-done.16, ...), custom_call_target="tpu_custom_call" | custom-call | flops 167772160 | bytes 344064 | tf_op jit(solution)/shard_map/out_project/pallas_call | solution.py:462
  176.9 22.9 %d_cat_parts.1 = (bf16[1024,512]{1,0:T(8,128)(2,1)}, bf16[1024,3584]{1,0:T(8,128)(2,1)}, f32[1,2048]{1,0:T(1,128)}, bf16[1024,2048]{1,0:T(8,128)(2,1)}) custom-call(s32[8]{0:T(128)} %copy-done.33, bf16[1024,2048]{1,0:T(8,128)(2,1)} %all-gather.2.cloned.1.call-done.g_ref, bf16[2560,2048]{1,0:T(8,128)(2,1)} %get-tuple-element.153.w_ref, ...), custom_call_target="tpu_custom_call" | custom-call | flops 167772160 | bytes 393216 | tf_op jit(solution)/shard_map/d_cat_parts/pallas_call | solution.py:536
  199.8 24.8 %attention_back.1 = (bf16[1024,3584]{1,0:T(8,128)(2,1)}, f32[1,512]{1,0:T(1,128)}, f32[1,512]{1,0:T(1,128)}, f32[1,512]{1,0:T(1,128)}) custom-call(bf16[1024,512]{1,0:T(8,128)(2,1)} %get-tuple-element.147.q_ref, bf16[1024,512]{1,0:T(8,128)(2,1)} %get-tuple-element.148.k_ref, ...), custom_call_target="tpu_custom_call", output_to_operand_aliasing={{0}: (9, {})} | custom-call | flops 83886080 | bytes 131072 | tf_op jit(solution)/shard_map/attention_back/pallas_call | solution.py:275
  224.6 22.5 %norm_back.1 = bf16[1024,2048]{1,0:T(8,128)(2,1)} custom-call(s32[8]{0:T(128)} %copy-done.33, bf16[1024,3584]{1,0:T(8,128)(2,1)} %get-tuple-element.160.x_ref.right_ref, bf16[2048,3584]{1,0:T(8,128)(2,1)} %get-tuple-element.161.w_ref), custom_call_target="tpu_custom_call" | custom-call | flops 234881024 | bytes 442368 | tf_op jit(solution)/shard_map/norm_back/pallas_call | solution.py:492
  247.1 19.0 %grads.5 = (bf16[1280,2048]{1,0:T(8,128)(2,1)}, bf16[1280,2048]{1,0:T(8,128)(2,1)}) custom-call(s32[1]{0:T(128)} %bitcast.2.f_ref, bf16[1024,2560]{1,0:T(8,128)(2,1)} %get-tuple-element.162.x_ref.att_ref.left_ref, bf16[1024,2048]{1,0:T(8,128)(2,1)} %get-tuple-element.163.right_ref), custom_call_target="tpu_custom_call" | custom-call | flops 167772160 | bytes 311296 | tf_op jit(solution)/shard_map/grads/pallas_call | solution.py:318
  266.3 9.3 %grads.6 = bf16[1024,2048]{1,0:T(8,128)(2,1)} custom-call(s32[1]{0:T(128)} %bitcast.2.f_ref, bf16[1024,2048]{1,0:T(8,128)(2,1)} %get-tuple-element.174.x_ref.left_ref, bf16[1024,3584]{1,0:T(8,128)(2,1)} %get-tuple-element.160.x_ref.right_ref), custom_call_target="tpu_custom_call" | custom-call | flops 67108864 | bytes 163840 | tf_op jit(solution)/shard_map/grads/pallas_call | solution.py:318
  275.7 2.1 add_convert_fusion.6
  280.0 9.1 %grads.7 = bf16[1024,2048]{1,0:T(8,128)(2,1)} custom-call(s32[1]{0:T(128)} %bitcast.2.f_ref, bf16[1024,2048]{1,0:T(8,128)(2,1)} %get-tuple-element.174.x_ref.left_ref, bf16[1024,3584]{1,0:T(8,128)(2,1)} %get-tuple-element.160.x_ref.right_ref, bf16[256,2048]{1,0:T(8,128)(2,1)} %reduce-scatter.3.cloned.1.call-done.refs_0_), custom_call_target="tpu_custom_call" | custom-call | flops 67108864 | bytes 163840 | tf_op jit(solution)/shard_map/grads/pallas_call | solution.py:318
  289.1 7.7 %grads.8 = bf16[1024,1536]{1,0:T(8,128)(2,1)} custom-call(s32[1]{0:T(128)} %bitcast.2.f_ref, bf16[1024,2048]{1,0:T(8,128)(2,1)} %get-tuple-element.174.x_ref.left_ref, bf16[1024,3584]{1,0:T(8,128)(2,1)} %get-tuple-element.160.x_ref.right_ref), custom_call_target="tpu_custom_call" | custom-call | flops 50331648 | bytes 131072 | tf_op jit(solution)/shard_map/grads/pallas_call | solution.py:318
  296.9 3.8 add_convert_fusion.3
  304.2 7.9 %grads.9 = bf16[1024,1536]{1,0:T(8,128)(2,1)} custom-call(s32[1]{0:T(128)} %bitcast.2.f_ref, bf16[1024,2048]{1,0:T(8,128)(2,1)} %get-tuple-element.174.x_ref.left_ref, bf16[1024,3584]{1,0:T(8,128)(2,1)} %get-tuple-element.160.x_ref.right_ref), custom_call_target="tpu_custom_call" | custom-call | flops 50331648 | bytes 131072 | tf_op jit(solution)/shard_map/grads/pallas_call | solution.py:318
  312.2 20.0 %collective-permute-done.24 = bf16[320,2048]{1,0:T(8,128)(2,1)} collective-permute-done((bf16[320,2048]{1,0:T(8,128)(2,1)S(1)}, bf16[320,2048]{1,0:T(8,128)(2,1)}, u32[]{:S(2)}, u32[]{:S(2)}) %collective-permute-start.24) | collective-permute-done | bytes 1310752 | tf_op jit(solution)/shard_map/ppermute | solution.py:604
  338.7 3.5 add_convert_fusion.1
  342.5 3.7 collective-permute-start.30
  346.2 3.2 collective-permute-done.27
  350.2 2.8 convert_element_type.281
  353.0 4.7 add_convert_fusion.11
  366.3 9.7 %collective-permute-done.29.refs_1_ = bf16[320,2048]{1,0:T(8,128)(2,1)} collective-permute-done((bf16[320,2048]{1,0:T(8,128)(2,1)S(1)}, bf16[320,2048]{1,0:T(8,128)(2,1)}, u32[]{:S(2)}, u32[]{:S(2)}) %collective-permute-start.29) | collective-permute-done | bytes 1310752 | tf_op jit(solution)/shard_map/ppermute | solution.py:595
  376.0 24.2 %collective-permute-done.30.refs_3_ = bf16[320,2048]{1,0:T(8,128)(2,1)} collective-permute-done((bf16[320,2048]{1,0:T(8,128)(2,1)S(1)}, bf16[320,2048]{1,0:T(8,128)(2,1)}, u32[]{:S(2)}, u32[]{:S(2)}) %collective-permute-start.30) | collective-permute-done | bytes 1310752 | tf_op jit(solution)/shard_map/ppermute | solution.py:595
  404.6 2.2 add_convert_fusion.9
  408.5 2.3 collective-permute-start.35
  410.8 2.3 collective-permute-done.37
  414.1 20.1 %collective-permute-done.36.refs_2_ = bf16[320,2048]{1,0:T(8,128)(2,1)} collective-permute-done((bf16[320,2048]{1,0:T(8,128)(2,1)}, bf16[320,2048]{1,0:T(8,128)(2,1)}, u32[]{:S(2)}, u32[]{:S(2)}) %collective-permute-start.36) | collective-permute-done | bytes 1310752 | tf_op jit(solution)/shard_map/ppermute | solution.py:595
  440.6 7.6 %join_rows.1 = f32[1280,2048]{1,0:T(8,128)} custom-call(s32[8]{0:T(128)} %stack.71.at_ref, bf16[320,2048]{1,0:T(8,128)(2,1)} %copy-done.7, bf16[320,2048]{1,0:T(8,128)(2,1)} %collective-permute-done.29.refs_1_, bf16[320,2048]{1,0:T(8,128)(2,1)} %collective-permute-done.36.refs_2_, bf16[320,2048]{1,0:T(8,128)(2,1)} %collective-permute-done.30.refs_3_), custom_call_target="tpu_custom_call" | custom-call | bytes 245760 | tf_op jit(solution)/shard_map/join_rows/pallas_call | solution.py:576
  448.3 8.3 %collective-permute-done.34.refs_1_ = bf16[256,2048]{1,0:T(8,128)(2,1)} collective-permute-done((bf16[256,2048]{1,0:T(8,128)(2,1)S(1)}, bf16[256,2048]{1,0:T(8,128)(2,1)}, u32[]{:S(2)}, u32[]{:S(2)}) %collective-permute-start.34) | collective-permute-done | bytes 1048608 | tf_op jit(solution)/shard_map/ppermute | solution.py:595
  456.6 19.6 %collective-permute-done.35.refs_3_ = bf16[256,2048]{1,0:T(8,128)(2,1)} collective-permute-done((bf16[256,2048]{1,0:T(8,128)(2,1)S(1)}, bf16[256,2048]{1,0:T(8,128)(2,1)}, u32[]{:S(2)}, u32[]{:S(2)}) %collective-permute-start.35) | collective-permute-done | bytes 1048608 | tf_op jit(solution)/shard_map/ppermute | solution.py:595
  476.8 2.2 add_convert_fusion.17
  479.7 3.2 collective-permute-start.43
  483.5 3.9 collective-permute-done.45
  487.5 17.0 %collective-permute-done.44.refs_2_ = bf16[256,2048]{1,0:T(8,128)(2,1)S(1)} collective-permute-done((bf16[256,2048]{1,0:T(8,128)(2,1)}, bf16[256,2048]{1,0:T(8,128)(2,1)S(1)}, u32[]{:S(2)}, u32[]{:S(2)}) %collective-permute-start.44) | collective-permute-done | bytes 1048608 | tf_op jit(solution)/shard_map/ppermute | solution.py:595
  505.3 3.6 collective-permute-done.46
  509.1 5.5 spread_columns.2.refs_4_
  514.6 6.7 %collective-permute-done.42.refs_1_ = bf16[256,1536]{1,0:T(8,128)(2,1)} collective-permute-done((bf16[256,1536]{1,0:T(8,128)(2,1)S(1)}, bf16[256,1536]{1,0:T(8,128)(2,1)}, u32[]{:S(2)}, u32[]{:S(2)}) %collective-permute-start.42) | collective-permute-done | bytes 786464 | tf_op jit(solution)/shard_map/ppermute | solution.py:595
  521.3 15.8 %collective-permute-done.43.refs_3_ = bf16[256,1536]{1,0:T(8,128)(2,1)S(1)} collective-permute-done((bf16[256,1536]{1,0:T(8,128)(2,1)S(1)}, bf16[256,1536]{1,0:T(8,128)(2,1)S(1)}, u32[]{:S(2)}, u32[]{:S(2)}) %collective-permute-start.43) | collective-permute-done | bytes 786464 | tf_op jit(solution)/shard_map/ppermute | solution.py:595
  541.6 21.2 %collective-permute-done.49 = f32[20480]{0:T(1024)S(1)} collective-permute-done((f32[20480]{0:T(1024)S(1)}, f32[20480]{0:T(1024)S(1)}, u32[]{:S(2)}, u32[]{:S(2)}) %collective-permute-start.49) | collective-permute-done | bytes 81952 | tf_op jit(solution)/shard_map/ppermute | solution.py:604
  562.8 4.5 spread_columns.3
  (285 shorter events, 86.0 us)
Async XLA Ops:
  7.2 169.7 %all-gather.2.cloned.1.call-start = ((), (), s32[]{:S(2)}) async-start(), calls=%async_computation.3 | async-start | bytes 5242880 | tf_op jit(solution)/shard_map/all_gather | solution.py:866
  15.4 29.4 %collective-permute-start = (bf16[256,2048]{1,0:T(8,128)(2,1)}, bf16[256,2048]{1,0:T(8,128)(2,1)}, u32[]{:S(2)}, u32[]{:S(2)}) collective-permute-start(bf16[256,2048]{1,0:T(8,128)(2,1)} %get-tuple-element.128.refs_0_), channel_id=1, source_target_pairs={{0,8},{8,16},{16,24},{24,0},{1,9},{9,17},{17,25},{25,1},{2,10},{10... | collective-permute-start | bytes 3145736 | tf_op jit(solution)/shard_map/ppermute | solution.py:595
  18.4 47.4 %collective-permute-start.1 = (bf16[256,2048]{1,0:T(8,128)(2,1)}, bf16[256,2048]{1,0:T(8,128)(2,1)}, u32[]{:S(2)}, u32[]{:S(2)}) collective-permute-start(bf16[256,2048]{1,0:T(8,128)(2,1)} %get-tuple-element.128.refs_0_), channel_id=1, source_target_pairs={{0,24},{8,0},{16,8},{24,16},{1,25},{9,1},{17,9},{25,17},{2,26},{10... | collective-permute-start | bytes 3145736 | tf_op jit(solution)/shard_map/ppermute | solution.py:595
  20.5 45.3 %collective-permute-start.2 = (bf16[256,3584]{1,0:T(8,128)(2,1)S(1)}, bf16[256,3584]{1,0:T(8,128)(2,1)}, u32[]{:S(2)}, u32[]{:S(2)}) collective-permute-start(bf16[256,3584]{1,0:T(8,128)(2,1)S(1)} %copy-done.3), channel_id=1, source_target_pairs={{0,2},{1,3},{2,0},{3,1},{4,6},{5,7},{6,4},{7,5},{8,10},{9,11},{10,... | collective-permute-start | bytes 5505032 | tf_op jit(solution)/shard_map/ppermute | solution.py:604
  22.1 43.7 %collective-permute-start.3 = (bf16[256,3584]{1,0:T(8,128)(2,1)S(1)}, bf16[256,3584]{1,0:T(8,128)(2,1)}, u32[]{:S(2)}, u32[]{:S(2)}) collective-permute-start(bf16[256,3584]{1,0:T(8,128)(2,1)S(1)} %copy-done.3), channel_id=1, source_target_pairs={{0,4},{1,5},{2,6},{3,7},{4,0},{5,1},{6,2},{7,3},{8,12},{9,13},{10,... | collective-permute-start | bytes 5505032 | tf_op jit(solution)/shard_map/ppermute | solution.py:604
  23.7 42.2 %collective-permute-start.4 = (bf16[256,3584]{1,0:T(8,128)(2,1)S(1)}, bf16[256,3584]{1,0:T(8,128)(2,1)}, u32[]{:S(2)}, u32[]{:S(2)}) collective-permute-start(bf16[256,3584]{1,0:T(8,128)(2,1)S(1)} %copy-done.3), channel_id=1, source_target_pairs={{0,1},{1,0},{2,3},{3,2},{4,5},{5,4},{6,7},{7,6},{8,9},{9,8},{10,11... | collective-permute-start | bytes 5505032 | tf_op jit(solution)/shard_map/ppermute | solution.py:604
  65.8 27.7 %collective-permute-start.8 = (bf16[256,3584]{1,0:T(8,128)(2,1)}, bf16[256,3584]{1,0:T(8,128)(2,1)S(1)}, u32[]{:S(2)}, u32[]{:S(2)}) collective-permute-start(bf16[256,3584]{1,0:T(8,128)(2,1)} %collective-permute-done.2.refs_5_.refs_1_), channel_id=1, source_target_pairs={{0,1},{1,0},{2,3},{3,2},{4,5},{5,4},{6,7},{7,6},{8,9},{9,8},{10,11... | collective-permute-start | bytes 5505032 | tf_op jit(solution)/shard_map/ppermute | solution.py:604
  65.9 27.7 %collective-permute-start.9 = (bf16[256,3584]{1,0:T(8,128)(2,1)}, bf16[256,3584]{1,0:T(8,128)(2,1)}, u32[]{:S(2)}, u32[]{:S(2)}) collective-permute-start(bf16[256,3584]{1,0:T(8,128)(2,1)} %collective-permute-done.3.refs_6_.refs_2_), channel_id=1, source_target_pairs={{0,1},{1,0},{2,3},{3,2},{4,5},{5,4},{6,7},{7,6},{8,9},{9,8},{10,11... | collective-permute-start | bytes 5505032 | tf_op jit(solution)/shard_map/ppermute | solution.py:604
  66.4 27.2 %collective-permute-start.5 = (bf16[256,2048]{1,0:T(8,128)(2,1)}, bf16[256,2048]{1,0:T(8,128)(2,1)S(1)}, u32[]{:S(2)}, u32[]{:S(2)}) collective-permute-start(bf16[256,2048]{1,0:T(8,128)(2,1)} %collective-permute-done.refs_1_), channel_id=1, source_target_pairs={{0,8},{8,16},{16,24},{24,0},{1,9},{9,17},{17,25},{25,1},{2,10},{10... | collective-permute-start | bytes 3145736 | tf_op jit(solution)/shard_map/ppermute | solution.py:595
  70.0 22.1 %collective-permute-start.6 = (bf16[128,3584]{1,0:T(8,128)(2,1)S(1)}, bf16[128,3584]{1,0:T(8,128)(2,1)S(1)}, u32[]{:S(2)}, u32[]{:S(2)}) collective-permute-start(bf16[128,3584]{1,0:T(8,128)(2,1)S(1)} %slice.575), channel_id=1, source_target_pairs={{0,4},{1,5},{2,6},{3,7},{4,0},{5,1},{6,2},{7,3},{8,12},{9,13},{10,... | collective-permute-start | bytes 2752520 | tf_op jit(solution)/shard_map/ppermute | solution.py:604
  71.6 21.8 %collective-permute-start.7 = (bf16[128,3584]{1,0:T(8,128)(2,1)S(1)}, bf16[128,3584]{1,0:T(8,128)(2,1)S(1)}, u32[]{:S(2)}, u32[]{:S(2)}) collective-permute-start(bf16[128,3584]{1,0:T(8,128)(2,1)S(1)} %slice.576), channel_id=1, source_target_pairs={{0,2},{1,3},{2,0},{3,1},{4,6},{5,7},{6,4},{7,5},{8,10},{9,11},{10,... | collective-permute-start | bytes 2752520 | tf_op jit(solution)/shard_map/ppermute | solution.py:604
  94.7 185.3 %reduce-scatter.3.cloned.1.call-start = ((), (), s32[]{:S(2)}) async-start(), calls=%async_computation.2 | async-start | bytes 5242880 | tf_op jit(solution)/shard_map/reduce_scatter | solution.py:905
  99.3 31.9 %collective-permute-start.12 = (bf16[320,2048]{1,0:T(8,128)(2,1)S(1)}, bf16[320,2048]{1,0:T(8,128)(2,1)S(1)}, u32[]{:S(2)}, u32[]{:S(2)}) collective-permute-start(bf16[320,2048]{1,0:T(8,128)(2,1)S(1)} %maximum_select_fusion.refs_0_), channel_id=1, source_target_pairs={{0,2},{1,3},{2,0},{3,1},{4,6},{5,7},{6,4},{7,5},{8,10},{9,11},{10,... | collective-permute-start | bytes 3932168 | tf_op jit(solution)/shard_map/ppermute | solution.py:604
  100.8 30.5 %collective-permute-start.13 = (bf16[320,2048]{1,0:T(8,128)(2,1)S(1)}, bf16[320,2048]{1,0:T(8,128)(2,1)S(1)}, u32[]{:S(2)}, u32[]{:S(2)}) collective-permute-start(bf16[320,2048]{1,0:T(8,128)(2,1)S(1)} %maximum_select_fusion.refs_0_), channel_id=1, source_target_pairs={{0,4},{1,5},{2,6},{3,7},{4,0},{5,1},{6,2},{7,3},{8,12},{9,13},{10,... | collective-permute-start | bytes 3932168 | tf_op jit(solution)/shard_map/ppermute | solution.py:604
  102.2 29.1 %collective-permute-start.14 = (bf16[320,2048]{1,0:T(8,128)(2,1)S(1)}, bf16[320,2048]{1,0:T(8,128)(2,1)}, u32[]{:S(2)}, u32[]{:S(2)}) collective-permute-start(bf16[320,2048]{1,0:T(8,128)(2,1)S(1)} %maximum_select_fusion.refs_0_), channel_id=1, source_target_pairs={{0,1},{1,0},{2,3},{3,2},{4,5},{5,4},{6,7},{7,6},{8,9},{9,8},{10,11... | collective-permute-start | bytes 3932168 | tf_op jit(solution)/shard_map/ppermute | solution.py:604
  131.3 22.1 %collective-permute-start.17 = (bf16[320,2048]{1,0:T(8,128)(2,1)S(1)}, bf16[320,2048]{1,0:T(8,128)(2,1)S(1)}, u32[]{:S(2)}, u32[]{:S(2)}) collective-permute-start(bf16[320,2048]{1,0:T(8,128)(2,1)S(1)} %collective-permute-done.12.refs_1_), channel_id=1, source_target_pairs={{0,1},{1,0},{2,3},{3,2},{4,5},{5,4},{6,7},{7,6},{8,9},{9,8},{10,11... | collective-permute-start | bytes 3932168 | tf_op jit(solution)/shard_map/ppermute | solution.py:604
  131.8 21.7 %collective-permute-start.18 = (bf16[320,2048]{1,0:T(8,128)(2,1)S(1)}, bf16[320,2048]{1,0:T(8,128)(2,1)S(1)}, u32[]{:S(2)}, u32[]{:S(2)}) collective-permute-start(bf16[320,2048]{1,0:T(8,128)(2,1)S(1)} %collective-permute-done.13.refs_2_), channel_id=1, source_target_pairs={{0,1},{1,0},{2,3},{3,2},{4,5},{5,4},{6,7},{7,6},{8,9},{9,8},{10,11... | collective-permute-start | bytes 3932168 | tf_op jit(solution)/shard_map/ppermute | solution.py:604
  133.0 20.5 %collective-permute-start.15 = (bf16[160,2048]{1,0:T(8,128)(2,1)}, bf16[160,2048]{1,0:T(8,128)(2,1)S(1)}, u32[]{:S(2)}, u32[]{:S(2)}) collective-permute-start(bf16[160,2048]{1,0:T(8,128)(2,1)} %slice.577), channel_id=1, source_target_pairs={{0,4},{1,5},{2,6},{3,7},{4,0},{5,1},{6,2},{7,3},{8,12},{9,13},{10,... | collective-permute-start | bytes 1966088 | tf_op jit(solution)/shard_map/ppermute | solution.py:604
  134.3 19.2 %collective-permute-start.16 = (bf16[160,2048]{1,0:T(8,128)(2,1)S(1)}, bf16[160,2048]{1,0:T(8,128)(2,1)S(1)}, u32[]{:S(2)}, u32[]{:S(2)}) collective-permute-start(bf16[160,2048]{1,0:T(8,128)(2,1)S(1)} %slice.578), channel_id=1, source_target_pairs={{0,2},{1,3},{2,0},{3,1},{4,6},{5,7},{6,4},{7,5},{8,10},{9,11},{10,... | collective-permute-start | bytes 1966088 | tf_op jit(solution)/shard_map/ppermute | solution.py:604
  176.7 173.6 %reduce-scatter.5.cloned.1.call-start = ((), (), s32[]{:S(2)}) async-start(), calls=%async_computation.4 | async-start | bytes 5242880 | tf_op jit(solution)/shard_map/reduce_scatter | solution.py:905
  266.2 9.5 %collective-permute-start.21 = (bf16[1280,2048]{1,0:T(8,128)(2,1)}, bf16[1280,2048]{1,0:T(8,128)(2,1)}, u32[]{:S(2)}, u32[]{:S(2)}) collective-permute-start(bf16[1280,2048]{1,0:T(8,128)(2,1)} %get-tuple-element.165), channel_id=1, source_target_pairs={{0,1},{1,0},{2,3},{3,2},{4,5},{5,4},{6,7},{7,6},{8,9},{9,8},{10,11... | collective-permute-start | bytes 15728648 | tf_op jit(solution)/shard_map/ppermute | solution.py:604
  277.8 19.0 %collective-permute-start.22 = (bf16[160,2048]{1,0:T(8,128)(2,1)S(1)}, bf16[160,2048]{1,0:T(8,128)(2,1)S(1)}, u32[]{:S(2)}, u32[]{:S(2)}) collective-permute-start(bf16[160,2048]{1,0:T(8,128)(2,1)S(1)} %get-tuple-element.263), channel_id=1, source_target_pairs={{0,4},{1,5},{2,6},{3,7},{4,0},{5,1},{6,2},{7,3},{8,12},{9,13},{10,... | collective-permute-start | bytes 1966088 | tf_op jit(solution)/shard_map/ppermute | solution.py:604
  278.9 17.9 %collective-permute-start.23 = (bf16[160,2048]{1,0:T(8,128)(2,1)S(1)}, bf16[160,2048]{1,0:T(8,128)(2,1)S(1)}, u32[]{:S(2)}, u32[]{:S(2)}) collective-permute-start(bf16[160,2048]{1,0:T(8,128)(2,1)S(1)} %get-tuple-element.262), channel_id=1, source_target_pairs={{0,2},{1,3},{2,0},{3,1},{4,6},{5,7},{6,4},{7,5},{8,10},{9,11},{10,... | collective-permute-start | bytes 1966088 | tf_op jit(solution)/shard_map/ppermute | solution.py:604
  296.8 37.3 %collective-permute-start.26 = (bf16[1024,2048]{1,0:T(8,128)(2,1)}, bf16[1024,2048]{1,0:T(8,128)(2,1)}, u32[]{:S(2)}, u32[]{:S(2)}) collective-permute-start(bf16[1024,2048]{1,0:T(8,128)(2,1)} %grads.6), channel_id=1, source_target_pairs={{0,1},{1,0},{2,3},{3,2},{4,5},{5,4},{6,7},{7,6},{8,9},{9,8},{10,11... | collective-permute-start | bytes 12582920 | tf_op jit(solution)/shard_map/ppermute | solution.py:604
  300.8 31.3 %collective-permute-start.24 = (bf16[320,2048]{1,0:T(8,128)(2,1)S(1)}, bf16[320,2048]{1,0:T(8,128)(2,1)}, u32[]{:S(2)}, u32[]{:S(2)}) collective-permute-start(bf16[320,2048]{1,0:T(8,128)(2,1)S(1)} %pad_maximum_fusion), channel_id=1, source_target_pairs={{0,2},{1,3},{2,0},{3,1},{4,6},{5,7},{6,4},{7,5},{8,10},{9,11},{10,... | collective-permute-start | bytes 3932168 | tf_op jit(solution)/shard_map/ppermute | solution.py:604
  302.9 31.2 %collective-permute-start.25 = (bf16[320,2048]{1,0:T(8,128)(2,1)}, bf16[320,2048]{1,0:T(8,128)(2,1)}, u32[]{:S(2)}, u32[]{:S(2)}) collective-permute-start(bf16[320,2048]{1,0:T(8,128)(2,1)} %pad_maximum_fusion.1), channel_id=1, source_target_pairs={{0,4},{1,5},{2,6},{3,7},{4,0},{5,1},{6,2},{7,3},{8,12},{9,13},{10,... | collective-permute-start | bytes 3932168 | tf_op jit(solution)/shard_map/ppermute | solution.py:604
  336.1 13.4 %collective-permute-start.27 = (bf16[128,2048]{1,0:T(8,128)(2,1)S(1)}, bf16[128,2048]{1,0:T(8,128)(2,1)}, u32[]{:S(2)}, u32[]{:S(2)}) collective-permute-start(bf16[128,2048]{1,0:T(8,128)(2,1)S(1)} %get-tuple-element.269), channel_id=1, source_target_pairs={{0,4},{1,5},{2,6},{3,7},{4,0},{5,1},{6,2},{7,3},{8,12},{9,13},{10,... | collective-permute-start | bytes 1572872 | tf_op jit(solution)/shard_map/ppermute | solution.py:604
  337.2 13.0 %collective-permute-start.28 = (bf16[128,2048]{1,0:T(8,128)(2,1)S(1)}, bf16[128,2048]{1,0:T(8,128)(2,1)}, u32[]{:S(2)}, u32[]{:S(2)}) collective-permute-start(bf16[128,2048]{1,0:T(8,128)(2,1)S(1)} %get-tuple-element.268), channel_id=1, source_target_pairs={{0,2},{1,3},{2,0},{3,1},{4,6},{5,7},{6,4},{7,5},{8,10},{9,11},{10,... | collective-permute-start | bytes 1572872 | tf_op jit(solution)/shard_map/ppermute | solution.py:604
  342.3 33.7 %collective-permute-start.29 = (bf16[320,2048]{1,0:T(8,128)(2,1)S(1)}, bf16[320,2048]{1,0:T(8,128)(2,1)}, u32[]{:S(2)}, u32[]{:S(2)}) collective-permute-start(bf16[320,2048]{1,0:T(8,128)(2,1)S(1)} %pad_maximum_fusion.2.refs_0_), channel_id=1, source_target_pairs={{0,8},{8,16},{16,24},{24,0},{1,9},{9,17},{17,25},{25,1},{2,10},{10... | collective-permute-start | bytes 3932168 | tf_op jit(solution)/shard_map/ppermute | solution.py:595
  342.5 57.7 %collective-permute-start.30 = (bf16[320,2048]{1,0:T(8,128)(2,1)S(1)}, bf16[320,2048]{1,0:T(8,128)(2,1)}, u32[]{:S(2)}, u32[]{:S(2)}) collective-permute-start(bf16[320,2048]{1,0:T(8,128)(2,1)S(1)} %pad_maximum_fusion.2.refs_0_), channel_id=1, source_target_pairs={{0,24},{8,0},{16,8},{24,16},{1,25},{9,1},{17,9},{25,17},{2,26},{10... | collective-permute-start | bytes 3932168 | tf_op jit(solution)/shard_map/ppermute | solution.py:595
  346.2 54.0 %collective-permute-start.33 = (bf16[1024,1536]{1,0:T(8,128)(2,1)}, bf16[1024,1536]{1,0:T(8,128)(2,1)}, u32[]{:S(2)}, u32[]{:S(2)}) collective-permute-start(bf16[1024,1536]{1,0:T(8,128)(2,1)} %grads.8), channel_id=1, source_target_pairs={{0,1},{1,0},{2,3},{3,2},{4,5},{5,4},{6,7},{7,6},{8,9},{9,8},{10,11... | collective-permute-start | bytes 9437192 | tf_op jit(solution)/shard_map/ppermute | solution.py:604
  359.4 40.8 %collective-permute-start.31 = (bf16[256,2048]{1,0:T(8,128)(2,1)S(1)}, bf16[256,2048]{1,0:T(8,128)(2,1)S(1)}, u32[]{:S(2)}, u32[]{:S(2)}) collective-permute-start(bf16[256,2048]{1,0:T(8,128)(2,1)S(1)} %pad_maximum_fusion.3), channel_id=1, source_target_pairs={{0,2},{1,3},{2,0},{3,1},{4,6},{5,7},{6,4},{7,5},{8,10},{9,11},{10,... | collective-permute-start | bytes 3145736 | tf_op jit(solution)/shard_map/ppermute | solution.py:604
  361.1 39.1 %collective-permute-start.32 = (bf16[256,2048]{1,0:T(8,128)(2,1)S(1)}, bf16[256,2048]{1,0:T(8,128)(2,1)S(1)}, u32[]{:S(2)}, u32[]{:S(2)}) collective-permute-start(bf16[256,2048]{1,0:T(8,128)(2,1)S(1)} %pad_maximum_fusion.4), channel_id=1, source_target_pairs={{0,4},{1,5},{2,6},{3,7},{4,0},{5,1},{6,2},{7,3},{8,12},{9,13},{10,... | collective-permute-start | bytes 3145736 | tf_op jit(solution)/shard_map/ppermute | solution.py:604
  400.2 34.0 %collective-permute-start.36 = (bf16[320,2048]{1,0:T(8,128)(2,1)}, bf16[320,2048]{1,0:T(8,128)(2,1)}, u32[]{:S(2)}, u32[]{:S(2)}) collective-permute-start(bf16[320,2048]{1,0:T(8,128)(2,1)} %collective-permute-done.29.refs_1_), channel_id=1, source_target_pairs={{0,8},{8,16},{16,24},{24,0},{1,9},{9,17},{17,25},{25,1},{2,10},{10... | collective-permute-start | bytes 3932168 | tf_op jit(solution)/shard_map/ppermute | solution.py:595
  403.1 9.9 %collective-permute-start.37 = (bf16[128,1536]{1,0:T(8,128)(2,1)S(1)}, bf16[128,1536]{1,0:T(8,128)(2,1)S(1)}, u32[]{:S(2)}, u32[]{:S(2)}) collective-permute-start(bf16[128,1536]{1,0:T(8,128)(2,1)S(1)} %get-tuple-element.277), channel_id=1, source_target_pairs={{0,4},{1,5},{2,6},{3,7},{4,0},{5,1},{6,2},{7,3},{8,12},{9,13},{10,... | collective-permute-start | bytes 1179656 | tf_op jit(solution)/shard_map/ppermute | solution.py:604
  404.2 9.9 %collective-permute-start.38 = (bf16[128,1536]{1,0:T(8,128)(2,1)S(1)}, bf16[128,1536]{1,0:T(8,128)(2,1)S(1)}, u32[]{:S(2)}, u32[]{:S(2)}) collective-permute-start(bf16[128,1536]{1,0:T(8,128)(2,1)S(1)} %get-tuple-element.276), channel_id=1, source_target_pairs={{0,2},{1,3},{2,0},{3,1},{4,6},{5,7},{6,4},{7,5},{8,10},{9,11},{10,... | collective-permute-start | bytes 1179656 | tf_op jit(solution)/shard_map/ppermute | solution.py:604
  406.9 49.7 %collective-permute-start.34 = (bf16[256,2048]{1,0:T(8,128)(2,1)S(1)}, bf16[256,2048]{1,0:T(8,128)(2,1)}, u32[]{:S(2)}, u32[]{:S(2)}) collective-permute-start(bf16[256,2048]{1,0:T(8,128)(2,1)S(1)} %pad_maximum_fusion.5.refs_0_), channel_id=1, source_target_pairs={{0,8},{8,16},{16,24},{24,0},{1,9},{9,17},{17,25},{25,1},{2,10},{10... | collective-permute-start | bytes 3145736 | tf_op jit(solution)/shard_map/ppermute | solution.py:595
  408.5 67.7 %collective-permute-start.35 = (bf16[256,2048]{1,0:T(8,128)(2,1)S(1)}, bf16[256,2048]{1,0:T(8,128)(2,1)}, u32[]{:S(2)}, u32[]{:S(2)}) collective-permute-start(bf16[256,2048]{1,0:T(8,128)(2,1)S(1)} %pad_maximum_fusion.5.refs_0_), channel_id=1, source_target_pairs={{0,24},{8,0},{16,8},{24,16},{1,25},{9,1},{17,9},{25,17},{2,26},{10... | collective-permute-start | bytes 3145736 | tf_op jit(solution)/shard_map/ppermute | solution.py:595
  437.0 39.2 %collective-permute-start.39 = (bf16[256,1536]{1,0:T(8,128)(2,1)}, bf16[256,1536]{1,0:T(8,128)(2,1)}, u32[]{:S(2)}, u32[]{:S(2)}) collective-permute-start(bf16[256,1536]{1,0:T(8,128)(2,1)} %pad_maximum_fusion.6), channel_id=1, source_target_pairs={{0,2},{1,3},{2,0},{3,1},{4,6},{5,7},{6,4},{7,5},{8,10},{9,11},{10,... | collective-permute-start | bytes 2359304 | tf_op jit(solution)/shard_map/ppermute | solution.py:604
  438.4 37.7 %collective-permute-start.40 = (bf16[256,1536]{1,0:T(8,128)(2,1)}, bf16[256,1536]{1,0:T(8,128)(2,1)}, u32[]{:S(2)}, u32[]{:S(2)}) collective-permute-start(bf16[256,1536]{1,0:T(8,128)(2,1)} %pad_maximum_fusion.7), channel_id=1, source_target_pairs={{0,4},{1,5},{2,6},{3,7},{4,0},{5,1},{6,2},{7,3},{8,12},{9,13},{10,... | collective-permute-start | bytes 2359304 | tf_op jit(solution)/shard_map/ppermute | solution.py:604
  439.8 36.3 %collective-permute-start.41 = (f32[20480]{0:T(1024)S(1)}, f32[20480]{0:T(1024)S(1)}, u32[]{:S(2)}, u32[]{:S(2)}) collective-permute-start(f32[20480]{0:T(1024)S(1)} %concatenate.101), channel_id=1, source_target_pairs={{0,1},{1,0},{2,3},{3,2},{4,5},{5,4},{6,7},{7,6},{8,9},{9,8},{10,11... | collective-permute-start | bytes 245768 | tf_op jit(solution)/shard_map/ppermute | solution.py:604
  476.2 28.3 %collective-permute-start.44 = (bf16[256,2048]{1,0:T(8,128)(2,1)}, bf16[256,2048]{1,0:T(8,128)(2,1)S(1)}, u32[]{:S(2)}, u32[]{:S(2)}) collective-permute-start(bf16[256,2048]{1,0:T(8,128)(2,1)} %collective-permute-done.34.refs_1_), channel_id=1, source_target_pairs={{0,8},{8,16},{16,24},{24,0},{1,9},{9,17},{17,25},{25,1},{2,10},{10... | collective-permute-start | bytes 3145736 | tf_op jit(solution)/shard_map/ppermute | solution.py:595
  479.1 42.2 %collective-permute-start.42 = (bf16[256,1536]{1,0:T(8,128)(2,1)S(1)}, bf16[256,1536]{1,0:T(8,128)(2,1)}, u32[]{:S(2)}, u32[]{:S(2)}) collective-permute-start(bf16[256,1536]{1,0:T(8,128)(2,1)S(1)} %pad_maximum_fusion.8.refs_0_), channel_id=1, source_target_pairs={{0,8},{8,16},{16,24},{24,0},{1,9},{9,17},{17,25},{25,1},{2,10},{10... | collective-permute-start | bytes 2359304 | tf_op jit(solution)/shard_map/ppermute | solution.py:595
  479.7 57.4 %collective-permute-start.43 = (bf16[256,1536]{1,0:T(8,128)(2,1)S(1)}, bf16[256,1536]{1,0:T(8,128)(2,1)S(1)}, u32[]{:S(2)}, u32[]{:S(2)}) collective-permute-start(bf16[256,1536]{1,0:T(8,128)(2,1)S(1)} %pad_maximum_fusion.8.refs_0_), channel_id=1, source_target_pairs={{0,24},{8,0},{16,8},{24,16},{1,25},{9,1},{17,9},{25,17},{2,26},{10... | collective-permute-start | bytes 2359304 | tf_op jit(solution)/shard_map/ppermute | solution.py:595
  483.0 4.5 collective-permute-start.45
  509.0 29.7 %collective-permute-start.47 = (f32[20480]{0:T(1024)S(1)}, f32[20480]{0:T(1024)S(1)}, u32[]{:S(2)}, u32[]{:S(2)}) collective-permute-start(f32[20480]{0:T(1024)S(1)} %add.384), channel_id=1, source_target_pairs={{0,8},{8,0},{16,24},{24,16},{1,9},{9,1},{17,25},{25,17},{2,10},{10... | collective-permute-start | bytes 245768 | tf_op jit(solution)/shard_map/ppermute | solution.py:604
  538.7 24.0 %collective-permute-start.48 = (bf16[256,1536]{1,0:T(8,128)(2,1)}, bf16[256,1536]{1,0:T(8,128)(2,1)}, u32[]{:S(2)}, u32[]{:S(2)}) collective-permute-start(bf16[256,1536]{1,0:T(8,128)(2,1)} %collective-permute-done.42.refs_1_), channel_id=1, source_target_pairs={{0,8},{8,16},{16,24},{24,0},{1,9},{9,17},{17,25},{25,1},{2,10},{10... | collective-permute-start | bytes 2359304 | tf_op jit(solution)/shard_map/ppermute | solution.py:595
  538.8 24.0 %collective-permute-start.49 = (f32[20480]{0:T(1024)S(1)}, f32[20480]{0:T(1024)S(1)}, u32[]{:S(2)}, u32[]{:S(2)}) collective-permute-start(f32[20480]{0:T(1024)S(1)} %add.385), channel_id=1, source_target_pairs={{0,16},{8,24},{16,0},{24,8},{1,17},{9,25},{17,1},{25,9},{2,18},{10... | collective-permute-start | bytes 245768 | tf_op jit(solution)/shard_map/ppermute | solution.py:604
  (59 other events, 455.3 us)
Sparse Core Ops, SparseCore 0:
  94.9 80.1 all-gather.1
  177.3 75.6 reduce-scatter.2
  266.5 76.1 reduce-scatter.4

commit v6 on v5

--- a/solution.py
+++ b/solution.py
@@ -161,10 +161,12 @@
     return lax.dot_general(a, b, (((ca,), (cb,)), ((), ())), preferred_element_type=F32)
 
 
-def causal(size, keys, first):
-    key_at = lax.broadcasted_iota(jnp.int32, (keys, size), 0)
-    query_at = lax.broadcasted_iota(jnp.int32, (keys, size), 1) + first
-    return key_at <= query_at
+def causal(s):
+    keys, size = s.shape
+    key_at = lax.broadcasted_iota(jnp.int32, (size, size), 0)
+    query_at = lax.broadcasted_iota(jnp.int32, (size, size), 1)
+    own = jnp.where(key_at <= query_at, s[keys - size :], NEG_BIG)
+    return own if keys == size else jnp.concatenate([s[: keys - size], own], axis=0)
 
 
 def att_kernel(q_ref, k_ref, v_ref, c_ref, u_ref, d_ref, qb_ref, kb_ref, vb_ref, att_ref, lse_ref):
@@ -174,15 +176,14 @@
     qb_ref[...] = turn(q_ref[...], c, su, sd).astype(BF)
     kb_ref[...] = turn(k_ref[...], c, su, sd).astype(BF)
     vb_ref[...] = v_ref[...].astype(BF)
-    scale = 1.0 / math.sqrt(HEAD_DIM)
+    scale = jnp.asarray(1.0 / math.sqrt(HEAD_DIM), BF)
     for i in range(seq // size):
         rows = slice(i * size, (i + 1) * size)
         keys = (i + 1) * size
         outs = []
         for h in range(2):
             lanes = slice(h * HEAD_DIM, (h + 1) * HEAD_DIM)
-            s = dot(kb_ref[:keys, lanes], qb_ref[rows, lanes], 1, 1) * scale
-            s = jnp.where(causal(size, keys, i * size), s, NEG_BIG)
+            s = causal(dot(kb_ref[:keys, lanes], qb_ref[rows, lanes] * scale, 1, 1))
             top = jnp.max(s, axis=0, keepdims=True)
             e = jnp.exp(s - top)
             total = jnp.sum(e, axis=0, keepdims=True)
@@ -223,7 +224,7 @@
     del dproj_in
     seq = q_ref.shape[0]
     size = math.gcd(seq, 256)
-    scale = 1.0 / math.sqrt(HEAD_DIM)
+    scale = jnp.asarray(1.0 / math.sqrt(HEAD_DIM), BF)
     ak[...] = jnp.zeros_like(ak)
     av[...] = jnp.zeros_like(av)
     for i in range(seq // size):
@@ -237,14 +238,14 @@
             q, do = q_ref[rows, lanes], datt_ref[rows, lanes]
             k, v = k_ref[:keys, lanes], v_ref[:keys, lanes]
             delta = jnp.sum(prod_t[lanes, :], axis=0, keepdims=True)
-            s = dot(k, q, 1, 1) * scale
-            s = jnp.where(causal(size, keys, i * size), s, NEG_BIG)
+            q = q * scale
+            s = causal(dot(k, q, 1, 1))
             p = jnp.exp(s - lse_ref[0, h : h + 1, rows])
             dp = dot(v, do, 1, 1)
-            ds = (p * (dp - delta) * scale).astype(BF)
+            ds = (p * (dp - delta)).astype(BF)
             dvs.append(dot(p.astype(BF), do, 1, 0))
             dks.append(dot(ds, q, 1, 0))
-            dqs.append(dot(ds, k, 0, 0))
+            dqs.append(dot(k, ds, 0, 0).T * scale.astype(F32))
         av[:keys, :] += jnp.concatenate(dvs, axis=1)
         ak[:keys, :] += jnp.concatenate(dks, axis=1)
         aq[rows, :] = jnp.concatenate(dqs, axis=1)
@@ -290,13 +291,8 @@
 
 
 def grads_kernel(n_split, n_late, f_ref, left_ref, right_ref, *refs):
-    outs, left_t = refs[n_late:-1], refs[-1]
-
-    @pl.when(pl.program_id(0) == 0)
-    def _():
-        left_t[...] = left_ref[...].T
-
-    g = dot(left_t[...], right_ref[...], 1, 0).astype(BF)
+    outs = refs[n_late:]
+    g = dot(left_ref[...], right_ref[...], 0, 0).astype(BF)
     if len(outs) == 1:
         outs[0][...] = g
         return
@@ -326,7 +322,6 @@
             ]
             + [pl.BlockSpec(memory_space=pl.ANY)] * len(late),
             out_specs=[pl.BlockSpec((wide // n_out, tile), lambda i, f_ref: (0, i))] * n_out,
-            scratch_shapes=[pltpu.VMEM((wide, rows), BF)],
         ),
         out_shape=[jax.ShapeDtypeStruct((wide // n_out, width), BF)] * n_out,
         **big("grads", 2 * rows * wide * width, 2 * rows * (wide + width) + 2 * wide * width),
@@ -442,17 +437,18 @@
     )(places, x, *ws, b, cat, w_all)
 
 
-def by_rank(at_ref, acc, out, blk_size):
-    for i in range(acc.shape[0] // blk_size):
-        at = pl.multiple_of(at_ref[i], blk_size)
-        out[i * blk_size : (i + 1) * blk_size, :] = acc[pl.ds(at, blk_size), :].astype(out.dtype)
+def by_rank(at_ref, x_ref, w, side, out, blk_size):
+    for rows in chunks(x_ref.shape[0]):
+        part = dot(x_ref[rows, :], w[...], 1, side).astype(out.dtype)
+        for at in range(0, part.shape[0], blk_size):
+            to = pl.multiple_of(at_ref[(rows.start + at) // blk_size], blk_size)
+            out[pl.ds(to, blk_size), :] = part[at : at + blk_size]
 
 
 def out_kernel(w_cuts, n_w, n_blk, blk_size, at_ref, x_ref, *refs):
-    ws, out_ref, w_ref, acc = refs[:n_w], refs[-3], refs[-2], refs[-1]
+    ws, out_ref, w_ref = refs[:n_w], refs[-2], refs[-1]
     lay(ws, w_cuts, at_ref, n_blk, w_ref)
-    acc[...] = dot(x_ref[...], w_ref[...], 1, 0)
-    by_rank(at_ref, acc, out_ref, blk_size)
+    by_rank(at_ref, x_ref, w_ref, 0, out_ref, blk_size)
 
 
 def out_project(x, ws, w_cuts, places, n_blk, blk_size):
@@ -470,7 +466,6 @@
                 pl.BlockSpec((rows, tile), lambda i, at: (0, i)),
                 pl.BlockSpec((deep, tile), lambda i, at: (0, i)),
             ],
-            scratch_shapes=[pltpu.VMEM((rows, tile), F32)],
         ),
         out_shape=[
             jax.ShapeDtypeStruct((rows, width), BF),
@@ -480,9 +475,8 @@
     )(places, x, *ws)
 
 
-def norm_kernel_back(blk_size, at_ref, x_ref, w_ref, out_ref, acc):
-    acc[...] = dot(x_ref[...], w_ref[...], 1, 1)
-    by_rank(at_ref, acc, out_ref, blk_size)
+def norm_kernel_back(blk_size, at_ref, x_ref, w_ref, out_ref):
+    by_rank(at_ref, x_ref, w_ref, 1, out_ref, blk_size)
 
 
 def norm_back(x, w, places, blk_size):
@@ -499,7 +493,6 @@
                 pl.BlockSpec((tile, deep), lambda i, at: (i, 0)),
             ],
             out_specs=pl.BlockSpec((rows, tile), lambda i, at: (0, i)),
-            scratch_shapes=[pltpu.VMEM((rows, tile), F32)],
         ),
         out_shape=jax.ShapeDtypeStruct((rows, width), BF),
         **big("norm_back", 2 * rows * deep * width, 2 * deep * (rows + width) + 3 * rows * width),
@@ -806,6 +799,11 @@
         return lax.shift_right_logical(k, 1) + lax.bitwise_and(k, 1) * (n_fsdp // 2)
 
     rank_places = blk_order * blk_size
+    blocks_at = jnp.arange(n_blk, dtype=jnp.int32)
+    slots = jnp.sum(
+        (blk_order[None, :] == blocks_at[:, None]).astype(jnp.int32) * blocks_at[None, :],
+        axis=1, dtype=jnp.int32,
+    ) * blk_size
     ranks = lax.rem(z - jnp.arange(n_ctx, dtype=jnp.int32) + n_ctx, n_ctx)
     picks = (ranks[:, None] == jnp.arange(n_ctx, dtype=jnp.int32)[None, :]).astype(jnp.int32)
     row_places = jnp.sum(
@@ -845,7 +843,7 @@
         [(h or 0) * (share // 2) for _, h in order], jnp.int32
     )
     qkv_at = jnp.concatenate([row_places, w_at])
-    o_at = jnp.concatenate([rank_places, o_at if even else jnp.zeros((1,), jnp.int32)])
+    o_at = jnp.concatenate([slots, o_at if even else jnp.zeros((1,), jnp.int32)])
 
     normed_parts, w_in_parts, w_out_parts = {}, [], []
     w_in_own = pick_columns(w_in, z, z_runs)
@@ -859,7 +857,7 @@
     b_in_z = jnp.stack([jnp.concatenate([b_in[s : s + n] for s, n in runs]) for runs in z_runs])[z]
     b_in_z = b_in_z[None]
     w_out_own = own_rows(line.tied(w_out)) if even else w_out
-    line.wait(w_out_own, b_in_z, qkv_at, o_at, w_at, rank_places, row_places)
+    line.wait(w_out_own, b_in_z, qkv_at, o_at, w_at, rank_places, slots)
 
     while normed_ring.flight is not None:
         normed_ring.step(w_in_move)
@@ -915,7 +913,7 @@
         q_b, k_b, v_b, cat_b, line.tied(d_att), lse, tables, d_proj, n_heads
     )
     line.wait(d_proj)
-    norm_part = norm_back(line.tied(d_proj), w_in_all, rank_places, blk_size)
+    norm_part = norm_back(line.tied(d_proj), w_in_all, slots, blk_size)
     line.wait(norm_part)
     norm_sum = ctx_sum(norm_part)
 

time: 583 us -> 576 us (0.988)
  Pallas kernels: 216 us -> 208 us
  transfers between devices with their start and end apart: 53 -> 53, of which waited for: 28 -> 29; matrix products, arithmetic and copies ran while one was open for 10% -> 11% of each run, Pallas kernels for 35% -> 34%
where the time goes in v6:
time: 576 us; the launch traced here: 571 us
  waiting for transfers between devices  230 us (40%)
  Pallas kernels  208 us (36%)
  starting transfers between devices  50.6 us (9%)
  other arithmetic  44 us (8%)
  local copies, waits for them, and re-layouts  23.3 us (4%)
  between operations  15.4 us (3%)
    ppermute x12, waiting for transfers between devices, pass_on(): return lax.ppermute(x, 'ctx', [(i, (i + hops) % n) for i in range(n)])  144 us
    ppermute x38, waiting for transfers between devices, swap(): return lax.ppermute(x, axis, [(i, i ^ bit) for i in range(n)])  85.6 us
    pallas_call x5, Pallas kernels, grads(): pl.pallas_call(functools.partial(grads_kernel, n_split, len(late)), grid_...  49.2 us
    ppermute x38, starting transfers between devices, swap(): return lax.ppermute(x, axis, [(i, i ^ bit) for i in range(n)])  29.8 us
    pallas_call x1, Pallas kernels, d_cat_parts(): pl.pallas_call(functools.partial(d_cat_kernel, cuts), grid_spec=pltpu.Pre...  23 us
    pallas_call x1, Pallas kernels, attention_back(): pl.pallas_call(functools.partial(back_kernel, pairs), grid=(pairs,), in_s...  22.7 us
    pallas_call x1, Pallas kernels, norm_back(): pl.pallas_call(functools.partial(norm_kernel_back, blk_size), grid_spec=p...  22.1 us
    ppermute x12, starting transfers between devices, pass_on(): return lax.ppermute(x, 'ctx', [(i, (i + hops) % n) for i in range(n)])  19.9 us
  transfers between devices with their start and end apart: 53, of which 29 were waited for; matrix products, arithmetic and copies ran while one was open for 11% of the time, Pallas kernels for 34%

profile of v6, /device:TPU:0, one launch (start us, length us, event | category | flops | bytes accessed | tf_op | source)
XLA Modules:
  0.0 570.6 jit_solution(1498947191292403598)
XLA Ops:
  7.2 4.3 pick_columns.1.refs_4_.refs_0_
  11.6 3.8 norm.1
  15.4 3.1 collective-permute-start
  18.4 2.1 collective-permute-start.1
  26.9 3.0 fusion
  30.0 2.6 concatenate.84.u_ref
  32.6 2.6 concatenate.85.d_ref
  44.8 21.0 %collective-permute-done.1.refs_3_ = bf16[256,2048]{1,0:T(8,128)(2,1)} collective-permute-done((bf16[256,2048]{1,0:T(8,128)(2,1)}, bf16[256,2048]{1,0:T(8,128)(2,1)}, u32[]{:S(2)}, u32[]{:S(2)}) %collective-permute-start.1) | collective-permute-done | bytes 1048608 | tf_op jit(solution)/shard_map/ppermute | solution.py:588
  73.1 19.0 %collective-permute-done.6.refs_8_.refs_4_ = bf16[128,3584]{1,0:T(8,128)(2,1)S(1)} collective-permute-done((bf16[128,3584]{1,0:T(8,128)(2,1)S(1)}, bf16[128,3584]{1,0:T(8,128)(2,1)S(1)}, u32[]{:S(2)}, u32[]{:S(2)}) %collective-permute-start.6) | collective-permute-done | bytes 917536 | tf_op jit(solution)/shard_map/ppermute | solution.py:597
  95.7 2.2 collective-permute-done.10.refs_12_.refs_8_
  102.2 13.8 %qkv_project.1 = (f32[1024,1536]{1,0:T(8,128)}, bf16[1024,2048]{1,0:T(8,128)(2,1)}, bf16[2048,3584]{1,0:T(8,128)(2,1)}) custom-call(s32[18]{0:T(128)} %get-tuple-element.353.at_ref, bf16[256,2048]{1,0:T(8,128)(2,1)} %get-tuple-element.128.refs_0_, bf16[256,2048]{1,0:T(8,128)(2,1)} %collective-permute-done.refs_1_, bf16[256,2048]{1,0:T(8,128)(2,1)} %copy-done.22, ...), custom_call_target="tpu_custom_call" | custom-call | flops 100663296 | bytes 262144 | tf_op jit(solution)/shard_map/qkv_project/pallas_call | solution.py:377
  116.0 14.8 %attention.1 = (bf16[1024,512]{1,0:T(8,128)(2,1)}, bf16[1024,512]{1,0:T(8,128)(2,1)}, bf16[1024,512]{1,0:T(8,128)(2,1)}, bf16[1024,2560]{1,0:T(8,128)(2,1)}, f32[4,2,1024]{2,1,0:T(2,128)}) custom-call(f32[1024,1536]{1,0:T(8,128)} %get-tuple-element.131.q_ref.k_ref.v_ref, f32[1024,1536]{1,0:T(8,128)} %get-tuple-element.131.q_ref.k_ref.v_ref, ...), custom_call_target="tpu_custom_call" | custom-call | flops 33554432 | bytes 163840 | tf_op jit(solution)/shard_map/attention/pallas_call | solution.py:206
  134.8 18.6 %pre_project.1 = (f32[1024,2048]{1,0:T(8,128)}, bf16[1024,2560]{1,0:T(8,128)(2,1)}, bf16[2048,3584]{1,0:T(8,128)(2,1)}) custom-call(s32[10]{0:T(128)} %constant.90.clone.at_ref, bf16[1024,2048]{1,0:T(8,128)(2,1)} %get-tuple-element.174.x_ref.left_ref, bf16[256,3584]{1,0:T(8,128)(2,1)} %pick_columns.1.refs_4_.refs_0_, ...), custom_call_target="tpu_custom_call", output_to_operand_aliasing={{1}: (13, {}), {2}: (14, {})} | custom-call | flops 134217728 | bytes 393216 | tf_op jit(solution)/shard_map/pre_project/pallas_call | solution.py:415
  157.5 17.8 %out_project.1 = (bf16[1024,2048]{1,0:T(8,128)(2,1)}, bf16[2560,2048]{1,0:T(8,128)(2,1)}) custom-call(s32[18]{0:T(128)} %get-tuple-element.352.at_ref, bf16[1024,2560]{1,0:T(8,128)(2,1)} %get-tuple-element.162.x_ref.att_ref.left_ref, bf16[320,2048]{1,0:T(8,128)(2,1)} %copy-done.8, bf16[320,2048]{1,0:T(8,128)(2,1)} %copy-done.16, ...), custom_call_target="tpu_custom_call" | custom-call | flops 167772160 | bytes 344064 | tf_op jit(solution)/shard_map/out_project/pallas_call | solution.py:458
  175.6 23.0 %d_cat_parts.1 = (bf16[1024,512]{1,0:T(8,128)(2,1)}, bf16[1024,3584]{1,0:T(8,128)(2,1)}, f32[1,2048]{1,0:T(1,128)}, bf16[1024,2048]{1,0:T(8,128)(2,1)}) custom-call(s32[8]{0:T(128)} %broadcast_multiply_fusion.3.at_ref, bf16[1024,2048]{1,0:T(8,128)(2,1)} %all-gather.2.cloned.1.call-done.g_ref, bf16[2560,2048]{1,0:T(8,128)(2,1)} %get-tuple-element.153.w_ref, ...), custom_call_target="tpu_custom_call" | custom-call | flops 167772160 | bytes 393216 | tf_op jit(solution)/shard_map/d_cat_parts/pallas_call | solution.py:529
  198.6 22.7 %attention_back.1 = (bf16[1024,3584]{1,0:T(8,128)(2,1)}, f32[1,512]{1,0:T(1,128)}, f32[1,512]{1,0:T(1,128)}, f32[1,512]{1,0:T(1,128)}) custom-call(bf16[1024,512]{1,0:T(8,128)(2,1)} %get-tuple-element.147.q_ref, bf16[1024,512]{1,0:T(8,128)(2,1)} %get-tuple-element.148.k_ref, ...), custom_call_target="tpu_custom_call", output_to_operand_aliasing={{0}: (9, {})} | custom-call | flops 83886080 | bytes 131072 | tf_op jit(solution)/shard_map/attention_back/pallas_call | solution.py:276
  221.3 22.1 %norm_back.1 = bf16[1024,2048]{1,0:T(8,128)(2,1)} custom-call(s32[8]{0:T(128)} %copy-done.46, bf16[1024,3584]{1,0:T(8,128)(2,1)} %get-tuple-element.160.x_ref.right_ref, bf16[2048,3584]{1,0:T(8,128)(2,1)} %get-tuple-element.161.w_ref), custom_call_target="tpu_custom_call" | custom-call | flops 234881024 | bytes 442368 | tf_op jit(solution)/shard_map/norm_back/pallas_call | solution.py:486
  243.4 17.6 %grads.5 = (bf16[1280,2048]{1,0:T(8,128)(2,1)}, bf16[1280,2048]{1,0:T(8,128)(2,1)}) custom-call(s32[1]{0:T(128)} %bitcast.2.f_ref, bf16[1024,2560]{1,0:T(8,128)(2,1)} %get-tuple-element.162.x_ref.att_ref.left_ref, bf16[1024,2048]{1,0:T(8,128)(2,1)} %get-tuple-element.163.right_ref), custom_call_target="tpu_custom_call" | custom-call | flops 167772160 | bytes 311296 | tf_op jit(solution)/shard_map/grads/pallas_call | solution.py:314
  261.1 8.8 %grads.6 = bf16[1024,2048]{1,0:T(8,128)(2,1)} custom-call(s32[1]{0:T(128)} %bitcast.2.f_ref, bf16[1024,2048]{1,0:T(8,128)(2,1)} %get-tuple-element.174.x_ref.left_ref, bf16[1024,3584]{1,0:T(8,128)(2,1)} %get-tuple-element.160.x_ref.right_ref), custom_call_target="tpu_custom_call" | custom-call | flops 67108864 | bytes 163840 | tf_op jit(solution)/shard_map/grads/pallas_call | solution.py:314
  270.0 2.1 add_convert_fusion.6
  274.7 8.5 %grads.7 = bf16[1024,2048]{1,0:T(8,128)(2,1)} custom-call(s32[1]{0:T(128)} %bitcast.2.f_ref, bf16[1024,2048]{1,0:T(8,128)(2,1)} %get-tuple-element.174.x_ref.left_ref, bf16[1024,3584]{1,0:T(8,128)(2,1)} %get-tuple-element.160.x_ref.right_ref, bf16[256,2048]{1,0:T(8,128)(2,1)} %reduce-scatter.3.cloned.1.call-done.refs_0_), custom_call_target="tpu_custom_call" | custom-call | flops 67108864 | bytes 163840 | tf_op jit(solution)/shard_map/grads/pallas_call | solution.py:314
  283.2 7.2 %grads.8 = bf16[1024,1536]{1,0:T(8,128)(2,1)} custom-call(s32[1]{0:T(128)} %bitcast.2.f_ref, bf16[1024,2048]{1,0:T(8,128)(2,1)} %get-tuple-element.174.x_ref.left_ref, bf16[1024,3584]{1,0:T(8,128)(2,1)} %get-tuple-element.160.x_ref.right_ref), custom_call_target="tpu_custom_call" | custom-call | flops 50331648 | bytes 131072 | tf_op jit(solution)/shard_map/grads/pallas_call | solution.py:314
  290.4 3.8 add_convert_fusion.3
  297.9 7.2 %grads.9 = bf16[1024,1536]{1,0:T(8,128)(2,1)} custom-call(s32[1]{0:T(128)} %bitcast.2.f_ref, bf16[1024,2048]{1,0:T(8,128)(2,1)} %get-tuple-element.174.x_ref.left_ref, bf16[1024,3584]{1,0:T(8,128)(2,1)} %get-tuple-element.160.x_ref.right_ref), custom_call_target="tpu_custom_call" | custom-call | flops 50331648 | bytes 131072 | tf_op jit(solution)/shard_map/grads/pallas_call | solution.py:314
  305.0 20.7 %collective-permute-done.24 = bf16[320,2048]{1,0:T(8,128)(2,1)} collective-permute-done((bf16[320,2048]{1,0:T(8,128)(2,1)S(1)}, bf16[320,2048]{1,0:T(8,128)(2,1)}, u32[]{:S(2)}, u32[]{:S(2)}) %collective-permute-start.24) | collective-permute-done | bytes 1310752 | tf_op jit(solution)/shard_map/ppermute | solution.py:597
  331.9 3.5 add_convert_fusion.1
  335.6 4.0 collective-permute-start.30
  339.6 3.3 collective-permute-done.27
  343.9 2.8 convert_element_type.282
  346.7 4.7 add_convert_fusion.11
  357.8 2.1 multiply_add_fusion
  359.8 9.4 %collective-permute-done.29.refs_1_ = bf16[320,2048]{1,0:T(8,128)(2,1)} collective-permute-done((bf16[320,2048]{1,0:T(8,128)(2,1)S(1)}, bf16[320,2048]{1,0:T(8,128)(2,1)}, u32[]{:S(2)}, u32[]{:S(2)}) %collective-permute-start.29) | collective-permute-done | bytes 1310752 | tf_op jit(solution)/shard_map/ppermute | solution.py:588
  369.2 24.5 %collective-permute-done.30.refs_3_ = bf16[320,2048]{1,0:T(8,128)(2,1)} collective-permute-done((bf16[320,2048]{1,0:T(8,128)(2,1)S(1)}, bf16[320,2048]{1,0:T(8,128)(2,1)}, u32[]{:S(2)}, u32[]{:S(2)}) %collective-permute-start.30) | collective-permute-done | bytes 1310752 | tf_op jit(solution)/shard_map/ppermute | solution.py:588
  398.6 2.2 add_convert_fusion.9
  407.6 20.2 %collective-permute-done.36.refs_2_ = bf16[320,2048]{1,0:T(8,128)(2,1)} collective-permute-done((bf16[320,2048]{1,0:T(8,128)(2,1)}, bf16[320,2048]{1,0:T(8,128)(2,1)}, u32[]{:S(2)}, u32[]{:S(2)}) %collective-permute-start.36) | collective-permute-done | bytes 1310752 | tf_op jit(solution)/shard_map/ppermute | solution.py:588
  434.3 7.6 %join_rows.1 = f32[1280,2048]{1,0:T(8,128)} custom-call(s32[8]{0:T(128)} %stack.71.at_ref, bf16[320,2048]{1,0:T(8,128)(2,1)} %copy-done.7, bf16[320,2048]{1,0:T(8,128)(2,1)} %collective-permute-done.29.refs_1_, bf16[320,2048]{1,0:T(8,128)(2,1)} %collective-permute-done.36.refs_2_, bf16[320,2048]{1,0:T(8,128)(2,1)} %collective-permute-done.30.refs_3_), custom_call_target="tpu_custom_call" | custom-call | bytes 245760 | tf_op jit(solution)/shard_map/join_rows/pallas_call | solution.py:569
  442.0 8.1 %collective-permute-done.34.refs_1_ = bf16[256,2048]{1,0:T(8,128)(2,1)} collective-permute-done((bf16[256,2048]{1,0:T(8,128)(2,1)S(1)}, bf16[256,2048]{1,0:T(8,128)(2,1)}, u32[]{:S(2)}, u32[]{:S(2)}) %collective-permute-start.34) | collective-permute-done | bytes 1048608 | tf_op jit(solution)/shard_map/ppermute | solution.py:588
  450.1 19.8 %collective-permute-done.35.refs_3_ = bf16[256,2048]{1,0:T(8,128)(2,1)} collective-permute-done((bf16[256,2048]{1,0:T(8,128)(2,1)S(1)}, bf16[256,2048]{1,0:T(8,128)(2,1)}, u32[]{:S(2)}, u32[]{:S(2)}) %collective-permute-start.35) | collective-permute-done | bytes 1048608 | tf_op jit(solution)/shard_map/ppermute | solution.py:588
  470.5 2.2 add_convert_fusion.17
  473.5 3.2 collective-permute-start.43
  477.6 3.7 collective-permute-done.45
  481.2 17.0 %collective-permute-done.44.refs_2_ = bf16[256,2048]{1,0:T(8,128)(2,1)S(1)} collective-permute-done((bf16[256,2048]{1,0:T(8,128)(2,1)}, bf16[256,2048]{1,0:T(8,128)(2,1)S(1)}, u32[]{:S(2)}, u32[]{:S(2)}) %collective-permute-start.44) | collective-permute-done | bytes 1048608 | tf_op jit(solution)/shard_map/ppermute | solution.py:588
  499.1 3.6 collective-permute-done.46
  502.8 5.5 spread_columns.2.refs_4_
  508.3 6.7 %collective-permute-done.42.refs_1_ = bf16[256,1536]{1,0:T(8,128)(2,1)} collective-permute-done((bf16[256,1536]{1,0:T(8,128)(2,1)S(1)}, bf16[256,1536]{1,0:T(8,128)(2,1)}, u32[]{:S(2)}, u32[]{:S(2)}) %collective-permute-start.42) | collective-permute-done | bytes 786464 | tf_op jit(solution)/shard_map/ppermute | solution.py:588
  515.0 15.8 %collective-permute-done.43.refs_3_ = bf16[256,1536]{1,0:T(8,128)(2,1)S(1)} collective-permute-done((bf16[256,1536]{1,0:T(8,128)(2,1)S(1)}, bf16[256,1536]{1,0:T(8,128)(2,1)S(1)}, u32[]{:S(2)}, u32[]{:S(2)}) %collective-permute-start.43) | collective-permute-done | bytes 786464 | tf_op jit(solution)/shard_map/ppermute | solution.py:588
  535.4 21.1 %collective-permute-done.49 = f32[20480]{0:T(1024)S(1)} collective-permute-done((f32[20480]{0:T(1024)S(1)}, f32[20480]{0:T(1024)S(1)}, u32[]{:S(2)}, u32[]{:S(2)}) %collective-permute-start.49) | collective-permute-done | bytes 81952 | tf_op jit(solution)/shard_map/ppermute | solution.py:597
  556.5 4.5 spread_columns.3
  (298 shorter events, 87.4 us)
Async XLA Ops:
  7.2 168.4 %all-gather.2.cloned.1.call-start = ((), (), s32[]{:S(2)}) async-start(), calls=%async_computation.3 | async-start | bytes 5242880 | tf_op jit(solution)/shard_map/all_gather | solution.py:864
  15.4 29.4 %collective-permute-start = (bf16[256,2048]{1,0:T(8,128)(2,1)}, bf16[256,2048]{1,0:T(8,128)(2,1)}, u32[]{:S(2)}, u32[]{:S(2)}) collective-permute-start(bf16[256,2048]{1,0:T(8,128)(2,1)} %get-tuple-element.128.refs_0_), channel_id=1, source_target_pairs={{0,8},{8,16},{16,24},{24,0},{1,9},{9,17},{17,25},{25,1},{2,10},{10... | collective-permute-start | bytes 3145736 | tf_op jit(solution)/shard_map/ppermute | solution.py:588
  18.4 47.4 %collective-permute-start.1 = (bf16[256,2048]{1,0:T(8,128)(2,1)}, bf16[256,2048]{1,0:T(8,128)(2,1)}, u32[]{:S(2)}, u32[]{:S(2)}) collective-permute-start(bf16[256,2048]{1,0:T(8,128)(2,1)} %get-tuple-element.128.refs_0_), channel_id=1, source_target_pairs={{0,24},{8,0},{16,8},{24,16},{1,25},{9,1},{17,9},{25,17},{2,26},{10... | collective-permute-start | bytes 3145736 | tf_op jit(solution)/shard_map/ppermute | solution.py:588
  20.5 45.3 %collective-permute-start.2 = (bf16[256,3584]{1,0:T(8,128)(2,1)S(1)}, bf16[256,3584]{1,0:T(8,128)(2,1)}, u32[]{:S(2)}, u32[]{:S(2)}) collective-permute-start(bf16[256,3584]{1,0:T(8,128)(2,1)S(1)} %copy-done.3), channel_id=1, source_target_pairs={{0,2},{1,3},{2,0},{3,1},{4,6},{5,7},{6,4},{7,5},{8,10},{9,11},{10,... | collective-permute-start | bytes 5505032 | tf_op jit(solution)/shard_map/ppermute | solution.py:597
  22.1 43.7 %collective-permute-start.3 = (bf16[256,3584]{1,0:T(8,128)(2,1)S(1)}, bf16[256,3584]{1,0:T(8,128)(2,1)}, u32[]{:S(2)}, u32[]{:S(2)}) collective-permute-start(bf16[256,3584]{1,0:T(8,128)(2,1)S(1)} %copy-done.3), channel_id=1, source_target_pairs={{0,4},{1,5},{2,6},{3,7},{4,0},{5,1},{6,2},{7,3},{8,12},{9,13},{10,... | collective-permute-start | bytes 5505032 | tf_op jit(solution)/shard_map/ppermute | solution.py:597
  23.6 42.2 %collective-permute-start.4 = (bf16[256,3584]{1,0:T(8,128)(2,1)S(1)}, bf16[256,3584]{1,0:T(8,128)(2,1)}, u32[]{:S(2)}, u32[]{:S(2)}) collective-permute-start(bf16[256,3584]{1,0:T(8,128)(2,1)S(1)} %copy-done.3), channel_id=1, source_target_pairs={{0,1},{1,0},{2,3},{3,2},{4,5},{5,4},{6,7},{7,6},{8,9},{9,8},{10,11... | collective-permute-start | bytes 5505032 | tf_op jit(solution)/shard_map/ppermute | solution.py:597
  65.8 27.7 %collective-permute-start.8 = (bf16[256,3584]{1,0:T(8,128)(2,1)}, bf16[256,3584]{1,0:T(8,128)(2,1)S(1)}, u32[]{:S(2)}, u32[]{:S(2)}) collective-permute-start(bf16[256,3584]{1,0:T(8,128)(2,1)} %collective-permute-done.2.refs_5_.refs_1_), channel_id=1, source_target_pairs={{0,1},{1,0},{2,3},{3,2},{4,5},{5,4},{6,7},{7,6},{8,9},{9,8},{10,11... | collective-permute-start | bytes 5505032 | tf_op jit(solution)/shard_map/ppermute | solution.py:597
  65.9 27.7 %collective-permute-start.9 = (bf16[256,3584]{1,0:T(8,128)(2,1)}, bf16[256,3584]{1,0:T(8,128)(2,1)}, u32[]{:S(2)}, u32[]{:S(2)}) collective-permute-start(bf16[256,3584]{1,0:T(8,128)(2,1)} %collective-permute-done.3.refs_6_.refs_2_), channel_id=1, source_target_pairs={{0,1},{1,0},{2,3},{3,2},{4,5},{5,4},{6,7},{7,6},{8,9},{9,8},{10,11... | collective-permute-start | bytes 5505032 | tf_op jit(solution)/shard_map/ppermute | solution.py:597
  66.4 27.2 %collective-permute-start.5 = (bf16[256,2048]{1,0:T(8,128)(2,1)}, bf16[256,2048]{1,0:T(8,128)(2,1)S(1)}, u32[]{:S(2)}, u32[]{:S(2)}) collective-permute-start(bf16[256,2048]{1,0:T(8,128)(2,1)} %collective-permute-done.refs_1_), channel_id=1, source_target_pairs={{0,8},{8,16},{16,24},{24,0},{1,9},{9,17},{17,25},{25,1},{2,10},{10... | collective-permute-start | bytes 3145736 | tf_op jit(solution)/shard_map/ppermute | solution.py:588
  70.0 22.1 %collective-permute-start.6 = (bf16[128,3584]{1,0:T(8,128)(2,1)S(1)}, bf16[128,3584]{1,0:T(8,128)(2,1)S(1)}, u32[]{:S(2)}, u32[]{:S(2)}) collective-permute-start(bf16[128,3584]{1,0:T(8,128)(2,1)S(1)} %slice.575), channel_id=1, source_target_pairs={{0,4},{1,5},{2,6},{3,7},{4,0},{5,1},{6,2},{7,3},{8,12},{9,13},{10,... | collective-permute-start | bytes 2752520 | tf_op jit(solution)/shard_map/ppermute | solution.py:597
  71.6 21.8 %collective-permute-start.7 = (bf16[128,3584]{1,0:T(8,128)(2,1)S(1)}, bf16[128,3584]{1,0:T(8,128)(2,1)S(1)}, u32[]{:S(2)}, u32[]{:S(2)}) collective-permute-start(bf16[128,3584]{1,0:T(8,128)(2,1)S(1)} %slice.576), channel_id=1, source_target_pairs={{0,2},{1,3},{2,0},{3,1},{4,6},{5,7},{6,4},{7,5},{8,10},{9,11},{10,... | collective-permute-start | bytes 2752520 | tf_op jit(solution)/shard_map/ppermute | solution.py:597
  94.7 180.0 %reduce-scatter.3.cloned.1.call-start = ((), (), s32[]{:S(2)}) async-start(), calls=%async_computation.2 | async-start | bytes 5242880 | tf_op jit(solution)/shard_map/reduce_scatter | solution.py:903
  99.2 31.6 %collective-permute-start.12 = (bf16[320,2048]{1,0:T(8,128)(2,1)S(1)}, bf16[320,2048]{1,0:T(8,128)(2,1)S(1)}, u32[]{:S(2)}, u32[]{:S(2)}) collective-permute-start(bf16[320,2048]{1,0:T(8,128)(2,1)S(1)} %maximum_select_fusion.refs_0_), channel_id=1, source_target_pairs={{0,2},{1,3},{2,0},{3,1},{4,6},{5,7},{6,4},{7,5},{8,10},{9,11},{10,... | collective-permute-start | bytes 3932168 | tf_op jit(solution)/shard_map/ppermute | solution.py:597
  100.7 30.5 %collective-permute-start.13 = (bf16[320,2048]{1,0:T(8,128)(2,1)S(1)}, bf16[320,2048]{1,0:T(8,128)(2,1)S(1)}, u32[]{:S(2)}, u32[]{:S(2)}) collective-permute-start(bf16[320,2048]{1,0:T(8,128)(2,1)S(1)} %maximum_select_fusion.refs_0_), channel_id=1, source_target_pairs={{0,4},{1,5},{2,6},{3,7},{4,0},{5,1},{6,2},{7,3},{8,12},{9,13},{10,... | collective-permute-start | bytes 3932168 | tf_op jit(solution)/shard_map/ppermute | solution.py:597
  102.2 29.1 %collective-permute-start.14 = (bf16[320,2048]{1,0:T(8,128)(2,1)S(1)}, bf16[320,2048]{1,0:T(8,128)(2,1)}, u32[]{:S(2)}, u32[]{:S(2)}) collective-permute-start(bf16[320,2048]{1,0:T(8,128)(2,1)S(1)} %maximum_select_fusion.refs_0_), channel_id=1, source_target_pairs={{0,1},{1,0},{2,3},{3,2},{4,5},{5,4},{6,7},{7,6},{8,9},{9,8},{10,11... | collective-permute-start | bytes 3932168 | tf_op jit(solution)/shard_map/ppermute | solution.py:597
  131.3 22.1 %collective-permute-start.17 = (bf16[320,2048]{1,0:T(8,128)(2,1)S(1)}, bf16[320,2048]{1,0:T(8,128)(2,1)S(1)}, u32[]{:S(2)}, u32[]{:S(2)}) collective-permute-start(bf16[320,2048]{1,0:T(8,128)(2,1)S(1)} %collective-permute-done.12.refs_1_), channel_id=1, source_target_pairs={{0,1},{1,0},{2,3},{3,2},{4,5},{5,4},{6,7},{7,6},{8,9},{9,8},{10,11... | collective-permute-start | bytes 3932168 | tf_op jit(solution)/shard_map/ppermute | solution.py:597
  131.4 22.1 %collective-permute-start.18 = (bf16[320,2048]{1,0:T(8,128)(2,1)S(1)}, bf16[320,2048]{1,0:T(8,128)(2,1)S(1)}, u32[]{:S(2)}, u32[]{:S(2)}) collective-permute-start(bf16[320,2048]{1,0:T(8,128)(2,1)S(1)} %collective-permute-done.13.refs_2_), channel_id=1, source_target_pairs={{0,1},{1,0},{2,3},{3,2},{4,5},{5,4},{6,7},{7,6},{8,9},{9,8},{10,11... | collective-permute-start | bytes 3932168 | tf_op jit(solution)/shard_map/ppermute | solution.py:597
  132.7 20.6 %collective-permute-start.15 = (bf16[160,2048]{1,0:T(8,128)(2,1)}, bf16[160,2048]{1,0:T(8,128)(2,1)S(1)}, u32[]{:S(2)}, u32[]{:S(2)}) collective-permute-start(bf16[160,2048]{1,0:T(8,128)(2,1)} %slice.577), channel_id=1, source_target_pairs={{0,4},{1,5},{2,6},{3,7},{4,0},{5,1},{6,2},{7,3},{8,12},{9,13},{10,... | collective-permute-start | bytes 1966088 | tf_op jit(solution)/shard_map/ppermute | solution.py:597
  134.2 19.2 %collective-permute-start.16 = (bf16[160,2048]{1,0:T(8,128)(2,1)S(1)}, bf16[160,2048]{1,0:T(8,128)(2,1)S(1)}, u32[]{:S(2)}, u32[]{:S(2)}) collective-permute-start(bf16[160,2048]{1,0:T(8,128)(2,1)S(1)} %slice.578), channel_id=1, source_target_pairs={{0,2},{1,3},{2,0},{3,1},{4,6},{5,7},{6,4},{7,5},{8,10},{9,11},{10,... | collective-permute-start | bytes 1966088 | tf_op jit(solution)/shard_map/ppermute | solution.py:597
  175.3 168.6 %reduce-scatter.5.cloned.1.call-start = ((), (), s32[]{:S(2)}) async-start(), calls=%async_computation.4 | async-start | bytes 5242880 | tf_op jit(solution)/shard_map/reduce_scatter | solution.py:903
  261.0 9.0 %collective-permute-start.21 = (bf16[1280,2048]{1,0:T(8,128)(2,1)}, bf16[1280,2048]{1,0:T(8,128)(2,1)}, u32[]{:S(2)}, u32[]{:S(2)}) collective-permute-start(bf16[1280,2048]{1,0:T(8,128)(2,1)} %get-tuple-element.165), channel_id=1, source_target_pairs={{0,1},{1,0},{2,3},{3,2},{4,5},{5,4},{6,7},{7,6},{8,9},{9,8},{10,11... | collective-permute-start | bytes 15728648 | tf_op jit(solution)/shard_map/ppermute | solution.py:597
  272.1 18.2 %collective-permute-start.22 = (bf16[160,2048]{1,0:T(8,128)(2,1)S(1)}, bf16[160,2048]{1,0:T(8,128)(2,1)S(1)}, u32[]{:S(2)}, u32[]{:S(2)}) collective-permute-start(bf16[160,2048]{1,0:T(8,128)(2,1)S(1)} %get-tuple-element.263), channel_id=1, source_target_pairs={{0,4},{1,5},{2,6},{3,7},{4,0},{5,1},{6,2},{7,3},{8,12},{9,13},{10,... | collective-permute-start | bytes 1966088 | tf_op jit(solution)/shard_map/ppermute | solution.py:597
  273.2 17.2 %collective-permute-start.23 = (bf16[160,2048]{1,0:T(8,128)(2,1)S(1)}, bf16[160,2048]{1,0:T(8,128)(2,1)S(1)}, u32[]{:S(2)}, u32[]{:S(2)}) collective-permute-start(bf16[160,2048]{1,0:T(8,128)(2,1)S(1)} %get-tuple-element.262), channel_id=1, source_target_pairs={{0,2},{1,3},{2,0},{3,1},{4,6},{5,7},{6,4},{7,5},{8,10},{9,11},{10,... | collective-permute-start | bytes 1966088 | tf_op jit(solution)/shard_map/ppermute | solution.py:597
  290.4 37.2 %collective-permute-start.26 = (bf16[1024,2048]{1,0:T(8,128)(2,1)}, bf16[1024,2048]{1,0:T(8,128)(2,1)}, u32[]{:S(2)}, u32[]{:S(2)}) collective-permute-start(bf16[1024,2048]{1,0:T(8,128)(2,1)} %grads.6), channel_id=1, source_target_pairs={{0,1},{1,0},{2,3},{3,2},{4,5},{5,4},{6,7},{7,6},{8,9},{9,8},{10,11... | collective-permute-start | bytes 12582920 | tf_op jit(solution)/shard_map/ppermute | solution.py:597
  294.4 31.3 %collective-permute-start.24 = (bf16[320,2048]{1,0:T(8,128)(2,1)S(1)}, bf16[320,2048]{1,0:T(8,128)(2,1)}, u32[]{:S(2)}, u32[]{:S(2)}) collective-permute-start(bf16[320,2048]{1,0:T(8,128)(2,1)S(1)} %pad_maximum_fusion), channel_id=1, source_target_pairs={{0,2},{1,3},{2,0},{3,1},{4,6},{5,7},{6,4},{7,5},{8,10},{9,11},{10,... | collective-permute-start | bytes 3932168 | tf_op jit(solution)/shard_map/ppermute | solution.py:597
  296.3 31.2 %collective-permute-start.25 = (bf16[320,2048]{1,0:T(8,128)(2,1)}, bf16[320,2048]{1,0:T(8,128)(2,1)}, u32[]{:S(2)}, u32[]{:S(2)}) collective-permute-start(bf16[320,2048]{1,0:T(8,128)(2,1)} %pad_maximum_fusion.1), channel_id=1, source_target_pairs={{0,4},{1,5},{2,6},{3,7},{4,0},{5,1},{6,2},{7,3},{8,12},{9,13},{10,... | collective-permute-start | bytes 3932168 | tf_op jit(solution)/shard_map/ppermute | solution.py:597
  329.5 13.4 %collective-permute-start.27 = (bf16[128,2048]{1,0:T(8,128)(2,1)S(1)}, bf16[128,2048]{1,0:T(8,128)(2,1)}, u32[]{:S(2)}, u32[]{:S(2)}) collective-permute-start(bf16[128,2048]{1,0:T(8,128)(2,1)S(1)} %get-tuple-element.269), channel_id=1, source_target_pairs={{0,4},{1,5},{2,6},{3,7},{4,0},{5,1},{6,2},{7,3},{8,12},{9,13},{10,... | collective-permute-start | bytes 1572872 | tf_op jit(solution)/shard_map/ppermute | solution.py:597
  330.8 13.1 %collective-permute-start.28 = (bf16[128,2048]{1,0:T(8,128)(2,1)S(1)}, bf16[128,2048]{1,0:T(8,128)(2,1)}, u32[]{:S(2)}, u32[]{:S(2)}) collective-permute-start(bf16[128,2048]{1,0:T(8,128)(2,1)S(1)} %get-tuple-element.268), channel_id=1, source_target_pairs={{0,2},{1,3},{2,0},{3,1},{4,6},{5,7},{6,4},{7,5},{8,10},{9,11},{10,... | collective-permute-start | bytes 1572872 | tf_op jit(solution)/shard_map/ppermute | solution.py:597
  335.5 33.7 %collective-permute-start.29 = (bf16[320,2048]{1,0:T(8,128)(2,1)S(1)}, bf16[320,2048]{1,0:T(8,128)(2,1)}, u32[]{:S(2)}, u32[]{:S(2)}) collective-permute-start(bf16[320,2048]{1,0:T(8,128)(2,1)S(1)} %pad_maximum_fusion.2.refs_0_), channel_id=1, source_target_pairs={{0,8},{8,16},{16,24},{24,0},{1,9},{9,17},{17,25},{25,1},{2,10},{10... | collective-permute-start | bytes 3932168 | tf_op jit(solution)/shard_map/ppermute | solution.py:588
  335.6 58.1 %collective-permute-start.30 = (bf16[320,2048]{1,0:T(8,128)(2,1)S(1)}, bf16[320,2048]{1,0:T(8,128)(2,1)}, u32[]{:S(2)}, u32[]{:S(2)}) collective-permute-start(bf16[320,2048]{1,0:T(8,128)(2,1)S(1)} %pad_maximum_fusion.2.refs_0_), channel_id=1, source_target_pairs={{0,24},{8,0},{16,8},{24,16},{1,25},{9,1},{17,9},{25,17},{2,26},{10... | collective-permute-start | bytes 3932168 | tf_op jit(solution)/shard_map/ppermute | solution.py:588
  339.6 54.1 %collective-permute-start.33 = (bf16[1024,1536]{1,0:T(8,128)(2,1)}, bf16[1024,1536]{1,0:T(8,128)(2,1)}, u32[]{:S(2)}, u32[]{:S(2)}) collective-permute-start(bf16[1024,1536]{1,0:T(8,128)(2,1)} %grads.8), channel_id=1, source_target_pairs={{0,1},{1,0},{2,3},{3,2},{4,5},{5,4},{6,7},{7,6},{8,9},{9,8},{10,11... | collective-permute-start | bytes 9437192 | tf_op jit(solution)/shard_map/ppermute | solution.py:597
  353.0 40.6 %collective-permute-start.31 = (bf16[256,2048]{1,0:T(8,128)(2,1)S(1)}, bf16[256,2048]{1,0:T(8,128)(2,1)S(1)}, u32[]{:S(2)}, u32[]{:S(2)}) collective-permute-start(bf16[256,2048]{1,0:T(8,128)(2,1)S(1)} %pad_maximum_fusion.3), channel_id=1, source_target_pairs={{0,2},{1,3},{2,0},{3,1},{4,6},{5,7},{6,4},{7,5},{8,10},{9,11},{10,... | collective-permute-start | bytes 3145736 | tf_op jit(solution)/shard_map/ppermute | solution.py:597
  354.3 39.4 %collective-permute-start.32 = (bf16[256,2048]{1,0:T(8,128)(2,1)S(1)}, bf16[256,2048]{1,0:T(8,128)(2,1)S(1)}, u32[]{:S(2)}, u32[]{:S(2)}) collective-permute-start(bf16[256,2048]{1,0:T(8,128)(2,1)S(1)} %pad_maximum_fusion.4), channel_id=1, source_target_pairs={{0,4},{1,5},{2,6},{3,7},{4,0},{5,1},{6,2},{7,3},{8,12},{9,13},{10,... | collective-permute-start | bytes 3145736 | tf_op jit(solution)/shard_map/ppermute | solution.py:597
  393.7 34.0 %collective-permute-start.36 = (bf16[320,2048]{1,0:T(8,128)(2,1)}, bf16[320,2048]{1,0:T(8,128)(2,1)}, u32[]{:S(2)}, u32[]{:S(2)}) collective-permute-start(bf16[320,2048]{1,0:T(8,128)(2,1)} %collective-permute-done.29.refs_1_), channel_id=1, source_target_pairs={{0,8},{8,16},{16,24},{24,0},{1,9},{9,17},{17,25},{25,1},{2,10},{10... | collective-permute-start | bytes 3932168 | tf_op jit(solution)/shard_map/ppermute | solution.py:588
  396.4 9.9 %collective-permute-start.37 = (bf16[128,1536]{1,0:T(8,128)(2,1)S(1)}, bf16[128,1536]{1,0:T(8,128)(2,1)S(1)}, u32[]{:S(2)}, u32[]{:S(2)}) collective-permute-start(bf16[128,1536]{1,0:T(8,128)(2,1)S(1)} %get-tuple-element.277), channel_id=1, source_target_pairs={{0,4},{1,5},{2,6},{3,7},{4,0},{5,1},{6,2},{7,3},{8,12},{9,13},{10,... | collective-permute-start | bytes 1179656 | tf_op jit(solution)/shard_map/ppermute | solution.py:597
  397.8 9.8 %collective-permute-start.38 = (bf16[128,1536]{1,0:T(8,128)(2,1)S(1)}, bf16[128,1536]{1,0:T(8,128)(2,1)S(1)}, u32[]{:S(2)}, u32[]{:S(2)}) collective-permute-start(bf16[128,1536]{1,0:T(8,128)(2,1)S(1)} %get-tuple-element.276), channel_id=1, source_target_pairs={{0,2},{1,3},{2,0},{3,1},{4,6},{5,7},{6,4},{7,5},{8,10},{9,11},{10,... | collective-permute-start | bytes 1179656 | tf_op jit(solution)/shard_map/ppermute | solution.py:597
  400.9 49.2 %collective-permute-start.34 = (bf16[256,2048]{1,0:T(8,128)(2,1)S(1)}, bf16[256,2048]{1,0:T(8,128)(2,1)}, u32[]{:S(2)}, u32[]{:S(2)}) collective-permute-start(bf16[256,2048]{1,0:T(8,128)(2,1)S(1)} %pad_maximum_fusion.5.refs_0_), channel_id=1, source_target_pairs={{0,8},{8,16},{16,24},{24,0},{1,9},{9,17},{17,25},{25,1},{2,10},{10... | collective-permute-start | bytes 3145736 | tf_op jit(solution)/shard_map/ppermute | solution.py:588
  402.8 67.1 %collective-permute-start.35 = (bf16[256,2048]{1,0:T(8,128)(2,1)S(1)}, bf16[256,2048]{1,0:T(8,128)(2,1)}, u32[]{:S(2)}, u32[]{:S(2)}) collective-permute-start(bf16[256,2048]{1,0:T(8,128)(2,1)S(1)} %pad_maximum_fusion.5.refs_0_), channel_id=1, source_target_pairs={{0,24},{8,0},{16,8},{24,16},{1,25},{9,1},{17,9},{25,17},{2,26},{10... | collective-permute-start | bytes 3145736 | tf_op jit(solution)/shard_map/ppermute | solution.py:588
  430.5 39.4 %collective-permute-start.39 = (bf16[256,1536]{1,0:T(8,128)(2,1)}, bf16[256,1536]{1,0:T(8,128)(2,1)}, u32[]{:S(2)}, u32[]{:S(2)}) collective-permute-start(bf16[256,1536]{1,0:T(8,128)(2,1)} %pad_maximum_fusion.6), channel_id=1, source_target_pairs={{0,2},{1,3},{2,0},{3,1},{4,6},{5,7},{6,4},{7,5},{8,10},{9,11},{10,... | collective-permute-start | bytes 2359304 | tf_op jit(solution)/shard_map/ppermute | solution.py:597
  432.4 37.5 %collective-permute-start.40 = (bf16[256,1536]{1,0:T(8,128)(2,1)}, bf16[256,1536]{1,0:T(8,128)(2,1)}, u32[]{:S(2)}, u32[]{:S(2)}) collective-permute-start(bf16[256,1536]{1,0:T(8,128)(2,1)} %pad_maximum_fusion.7), channel_id=1, source_target_pairs={{0,4},{1,5},{2,6},{3,7},{4,0},{5,1},{6,2},{7,3},{8,12},{9,13},{10,... | collective-permute-start | bytes 2359304 | tf_op jit(solution)/shard_map/ppermute | solution.py:597
  433.6 36.3 %collective-permute-start.41 = (f32[20480]{0:T(1024)S(1)}, f32[20480]{0:T(1024)S(1)}, u32[]{:S(2)}, u32[]{:S(2)}) collective-permute-start(f32[20480]{0:T(1024)S(1)} %concatenate.101), channel_id=1, source_target_pairs={{0,1},{1,0},{2,3},{3,2},{4,5},{5,4},{6,7},{7,6},{8,9},{9,8},{10,11... | collective-permute-start | bytes 245768 | tf_op jit(solution)/shard_map/ppermute | solution.py:597
  469.9 28.3 %collective-permute-start.44 = (bf16[256,2048]{1,0:T(8,128)(2,1)}, bf16[256,2048]{1,0:T(8,128)(2,1)S(1)}, u32[]{:S(2)}, u32[]{:S(2)}) collective-permute-start(bf16[256,2048]{1,0:T(8,128)(2,1)} %collective-permute-done.34.refs_1_), channel_id=1, source_target_pairs={{0,8},{8,16},{16,24},{24,0},{1,9},{9,17},{17,25},{25,1},{2,10},{10... | collective-permute-start | bytes 3145736 | tf_op jit(solution)/shard_map/ppermute | solution.py:588
  472.8 42.2 %collective-permute-start.42 = (bf16[256,1536]{1,0:T(8,128)(2,1)S(1)}, bf16[256,1536]{1,0:T(8,128)(2,1)}, u32[]{:S(2)}, u32[]{:S(2)}) collective-permute-start(bf16[256,1536]{1,0:T(8,128)(2,1)S(1)} %pad_maximum_fusion.8.refs_0_), channel_id=1, source_target_pairs={{0,8},{8,16},{16,24},{24,0},{1,9},{9,17},{17,25},{25,1},{2,10},{10... | collective-permute-start | bytes 2359304 | tf_op jit(solution)/shard_map/ppermute | solution.py:588
  473.5 57.3 %collective-permute-start.43 = (bf16[256,1536]{1,0:T(8,128)(2,1)S(1)}, bf16[256,1536]{1,0:T(8,128)(2,1)S(1)}, u32[]{:S(2)}, u32[]{:S(2)}) collective-permute-start(bf16[256,1536]{1,0:T(8,128)(2,1)S(1)} %pad_maximum_fusion.8.refs_0_), channel_id=1, source_target_pairs={{0,24},{8,0},{16,8},{24,16},{1,25},{9,1},{17,9},{25,17},{2,26},{10... | collective-permute-start | bytes 2359304 | tf_op jit(solution)/shard_map/ppermute | solution.py:588
  476.7 4.5 collective-permute-start.45
  502.7 29.7 %collective-permute-start.47 = (f32[20480]{0:T(1024)S(1)}, f32[20480]{0:T(1024)S(1)}, u32[]{:S(2)}, u32[]{:S(2)}) collective-permute-start(f32[20480]{0:T(1024)S(1)} %add.384), channel_id=1, source_target_pairs={{0,8},{8,0},{16,24},{24,16},{1,9},{9,1},{17,25},{25,17},{2,10},{10... | collective-permute-start | bytes 245768 | tf_op jit(solution)/shard_map/ppermute | solution.py:597
  532.5 24.0 %collective-permute-start.48 = (bf16[256,1536]{1,0:T(8,128)(2,1)}, bf16[256,1536]{1,0:T(8,128)(2,1)}, u32[]{:S(2)}, u32[]{:S(2)}) collective-permute-start(bf16[256,1536]{1,0:T(8,128)(2,1)} %collective-permute-done.42.refs_1_), channel_id=1, source_target_pairs={{0,8},{8,16},{16,24},{24,0},{1,9},{9,17},{17,25},{25,1},{2,10},{10... | collective-permute-start | bytes 2359304 | tf_op jit(solution)/shard_map/ppermute | solution.py:588
  532.5 24.0 %collective-permute-start.49 = (f32[20480]{0:T(1024)S(1)}, f32[20480]{0:T(1024)S(1)}, u32[]{:S(2)}, u32[]{:S(2)}) collective-permute-start(f32[20480]{0:T(1024)S(1)} %add.385), channel_id=1, source_target_pairs={{0,16},{8,24},{16,0},{24,8},{1,17},{9,25},{17,1},{25,9},{2,18},{10... | collective-permute-start | bytes 245768 | tf_op jit(solution)/shard_map/ppermute | solution.py:597
  (64 other events, 456.5 us)
Sparse Core Ops, SparseCore 0:
  94.8 80.1 all-gather.1
  177.3 75.2 reduce-scatter.2
  261.2 76.2 reduce-scatter.4

commit v7 on v6

--- a/solution.py
+++ b/solution.py
@@ -349,7 +349,7 @@
 def big(name_of, flops, nbytes):
     return {
         "compiler_params": pltpu.CompilerParams(vmem_limit_bytes=VMEM_BYTES),
-        "cost_estimate": cost(flops // 64, nbytes // 64),
+        "cost_estimate": cost(flops, nbytes),
         "name": name_of,
     }
 
@@ -846,12 +846,12 @@
     o_at = jnp.concatenate([slots, o_at if even else jnp.zeros((1,), jnp.int32)])
 
     normed_parts, w_in_parts, w_out_parts = {}, [], []
-    w_in_own = pick_columns(w_in, z, z_runs)
+    normed_own, dy_own = norm(seq_in, seq_grad, ln_gain, ln_beta, f, n_fsdp)
+    normed_ring = Move(line, ring_job(normed_own, normed_parts))
+    line.wait(normed_own)
+    w_in_own = pick_columns(line.tied(w_in), z, z_runs)
     w_in_move = Move(line, gather_job(w_in_own, w_in_parts))
     line.wait(w_in_own)
-    normed_own, dy_own = norm(line.tied(seq_in), seq_grad, ln_gain, ln_beta, f, n_fsdp)
-    normed_ring = Move(line, ring_job(normed_own, normed_parts))
-    line.wait(normed_own)
     tables = rotary_tables(line.tied(jnp.arange(seq_len, dtype=jnp.int32)))
     line.wait(*tables)
     b_in_z = jnp.stack([jnp.concatenate([b_in[s : s + n] for s, n in runs]) for runs in z_runs])[z]
@@ -859,6 +859,8 @@
     w_out_own = own_rows(line.tied(w_out)) if even else w_out
     line.wait(w_out_own, b_in_z, qkv_at, o_at, w_at, rank_places, slots)
 
+    normed_ring.step()
+    w_in_move.step()
     while normed_ring.flight is not None:
         normed_ring.step(w_in_move)
     dy_all = lax.all_gather(after(dy_own, *line.due), "ctx", axis=0, tiled=True)
@@ -937,10 +939,9 @@
     (qkv_home,) = grads(line.tied(normed), 0, half, d_proj, 0, wide_q, f)
     line.wait(qkv_home)
     if even:
-        out_scatter.step(pre_scatter)
+        out_scatter.end()
         out_ring = Move(line, ring_job(line.tied(out_own[0]), out_parts))
-    else:
-        pre_scatter.step()
+    pre_scatter.step()
     qkv_scatter = Move(line, scatter_job(line.tied(qkv_away), qkv_home, qkv_own))
     pre_scatter.step()
 

time: 576 us -> 574 us (level)
  waiting for transfers between devices: 230 us -> 236 us
    ppermute x12, waiting for transfers between devices: 144 us -> 165 us  [pass_on(): return lax.ppermute(x, 'ctx', [(i, (i + hops) % n) for i in range(n)])]
    ppermute x38, waiting for transfers between devices: 85.6 us -> 70.7 us  [swap(): return lax.ppermute(x, axis, [(i, i ^ bit) for i in range(n)])]
  transfers between devices with their start and end apart: 53 -> 53, of which waited for: 29 -> 31; matrix products, arithmetic and copies ran while one was open for 11% -> 10% of each run, Pallas kernels for 34% -> 35%
where the time goes in v7:
time: 574 us; the launch traced here: 568 us
  waiting for transfers between devices  236 us (41%)
  Pallas kernels  207 us (36%)
  starting transfers between devices  47 us (8%)
  other arithmetic  43.2 us (8%)
  local copies, waits for them, and re-layouts  19.4 us (3%)
  between operations  15.1 us (3%)
    ppermute x12, waiting for transfers between devices, pass_on(): return lax.ppermute(x, 'ctx', [(i, (i + hops) % n) for i in range(n)])  165 us
    ppermute x38, waiting for transfers between devices, swap(): return lax.ppermute(x, axis, [(i, i ^ bit) for i in range(n)])  70.7 us
    pallas_call x5, Pallas kernels, grads(): pl.pallas_call(functools.partial(grads_kernel, n_split, len(late)), grid_...  49.2 us
    ppermute x38, starting transfers between devices, swap(): return lax.ppermute(x, axis, [(i, i ^ bit) for i in range(n)])  28.5 us
    pallas_call x1, Pallas kernels, d_cat_parts(): pl.pallas_call(functools.partial(d_cat_kernel, cuts), grid_spec=pltpu.Pre...  22.9 us
    pallas_call x1, Pallas kernels, attention_back(): pl.pallas_call(functools.partial(back_kernel, pairs), grid=(pairs,), in_s...  22.7 us
    pallas_call x1, Pallas kernels, norm_back(): pl.pallas_call(functools.partial(norm_kernel_back, blk_size), grid_spec=p...  22.1 us
    pallas_call x1, Pallas kernels, pre_project(): pl.pallas_call(functools.partial(pre_kernel, w_cuts, n_w), grid_spec=pltp...  18.6 us
  transfers between devices with their start and end apart: 53, of which 31 were waited for; matrix products, arithmetic and copies ran while one was open for 10% of the time, Pallas kernels for 35%

profile of v7, /device:TPU:0, one launch (start us, length us, event | category | flops | bytes accessed | tf_op | source)
XLA Modules:
  0.0 567.5 jit_solution(12866047106993692193)
XLA Ops:
  7.2 3.7 norm.1
  10.9 3.0 collective-permute-start
  13.9 2.1 collective-permute-start.1
  16.0 4.3 pick_columns.1.refs_4_.refs_0_
  40.3 21.0 %collective-permute-done.1.refs_3_ = bf16[256,2048]{1,0:T(8,128)(2,1)} collective-permute-done((bf16[256,2048]{1,0:T(8,128)(2,1)}, bf16[256,2048]{1,0:T(8,128)(2,1)}, u32[]{:S(2)}, u32[]{:S(2)}) %collective-permute-start.1) | collective-permute-done | bytes 1048608 | tf_op jit(solution)/shard_map/ppermute | solution.py:588
  68.6 22.3 %collective-permute-done.2.refs_2_ = bf16[256,2048]{1,0:T(8,128)(2,1)S(1)} collective-permute-done((bf16[256,2048]{1,0:T(8,128)(2,1)}, bf16[256,2048]{1,0:T(8,128)(2,1)S(1)}, u32[]{:S(2)}, u32[]{:S(2)}) %collective-permute-start.2) | collective-permute-done | bytes 1048608 | tf_op jit(solution)/shard_map/ppermute | solution.py:588
  93.7 2.2 collective-permute-done.10.refs_12_.refs_8_
  99.3 13.6 %qkv_project.1 = (f32[1024,1536]{1,0:T(8,128)}, bf16[1024,2048]{1,0:T(8,128)(2,1)}, bf16[2048,3584]{1,0:T(8,128)(2,1)}) custom-call(s32[18]{0:T(128)} %get-tuple-element.353.at_ref, bf16[256,2048]{1,0:T(8,128)(2,1)} %get-tuple-element.128.refs_0_, bf16[256,2048]{1,0:T(8,128)(2,1)} %collective-permute-done.refs_1_, bf16[256,2048]{1,0:T(8,128)(2,1)} %copy-done.34, ...), custom_call_target="tpu_custom_call" | custom-call | flops 6442450944 | bytes 16777216 | tf_op jit(solution)/shard_map/qkv_project/pallas_call | solution.py:377
  112.8 14.8 %attention.1 = (bf16[1024,512]{1,0:T(8,128)(2,1)}, bf16[1024,512]{1,0:T(8,128)(2,1)}, bf16[1024,512]{1,0:T(8,128)(2,1)}, bf16[1024,2560]{1,0:T(8,128)(2,1)}, f32[4,2,1024]{2,1,0:T(2,128)}) custom-call(f32[1024,1536]{1,0:T(8,128)} %get-tuple-element.131.q_ref.k_ref.v_ref, f32[1024,1536]{1,0:T(8,128)} %get-tuple-element.131.q_ref.k_ref.v_ref, ...), custom_call_target="tpu_custom_call" | custom-call | flops 2147483648 | bytes 10485760 | tf_op jit(solution)/shard_map/attention/pallas_call | solution.py:206
  132.0 18.6 %pre_project.1 = (f32[1024,2048]{1,0:T(8,128)}, bf16[1024,2560]{1,0:T(8,128)(2,1)}, bf16[2048,3584]{1,0:T(8,128)(2,1)}) custom-call(s32[10]{0:T(128)} %constant.90.clone.at_ref, bf16[1024,2048]{1,0:T(8,128)(2,1)} %get-tuple-element.174.x_ref.left_ref, bf16[256,3584]{1,0:T(8,128)(2,1)} %pick_columns.1.refs_4_.refs_0_, ...), custom_call_target="tpu_custom_call", output_to_operand_aliasing={{1}: (13, {}), {2}: (14, {})} | custom-call | flops 8589934592 | bytes 25165824 | tf_op jit(solution)/shard_map/pre_project/pallas_call | solution.py:415
  154.8 17.9 %out_project.1 = (bf16[1024,2048]{1,0:T(8,128)(2,1)}, bf16[2560,2048]{1,0:T(8,128)(2,1)}) custom-call(s32[18]{0:T(128)} %get-tuple-element.352.at_ref, bf16[1024,2560]{1,0:T(8,128)(2,1)} %get-tuple-element.162.x_ref.att_ref.left_ref, bf16[320,2048]{1,0:T(8,128)(2,1)} %copy-done.12, bf16[320,2048]{1,0:T(8,128)(2,1)} %copy-done.19, ...), custom_call_target="tpu_custom_call" | custom-call | flops 10737418240 | bytes 22020096 | tf_op jit(solution)/shard_map/out_project/pallas_call | solution.py:458
  173.0 22.9 %d_cat_parts.1 = (bf16[1024,512]{1,0:T(8,128)(2,1)}, bf16[1024,3584]{1,0:T(8,128)(2,1)}, f32[1,2048]{1,0:T(1,128)}, bf16[1024,2048]{1,0:T(8,128)(2,1)}) custom-call(s32[8]{0:T(128)} %broadcast_multiply_fusion.3.at_ref, bf16[1024,2048]{1,0:T(8,128)(2,1)} %all-gather.2.cloned.1.call-done.g_ref, bf16[2560,2048]{1,0:T(8,128)(2,1)} %get-tuple-element.153.w_ref, ...), custom_call_target="tpu_custom_call" | custom-call | flops 10737418240 | bytes 25165824 | tf_op jit(solution)/shard_map/d_cat_parts/pallas_call | solution.py:529
  195.8 22.7 %attention_back.1 = (bf16[1024,3584]{1,0:T(8,128)(2,1)}, f32[1,512]{1,0:T(1,128)}, f32[1,512]{1,0:T(1,128)}, f32[1,512]{1,0:T(1,128)}) custom-call(bf16[1024,512]{1,0:T(8,128)(2,1)} %get-tuple-element.147.q_ref, bf16[1024,512]{1,0:T(8,128)(2,1)} %get-tuple-element.148.k_ref, ...), custom_call_target="tpu_custom_call", output_to_operand_aliasing={{0}: (9, {})} | custom-call | flops 5368709120 | bytes 8388608 | tf_op jit(solution)/shard_map/attention_back/pallas_call | solution.py:276
  218.5 22.1 %norm_back.1 = bf16[1024,2048]{1,0:T(8,128)(2,1)} custom-call(s32[8]{0:T(128)} %copy-done.29, bf16[1024,3584]{1,0:T(8,128)(2,1)} %get-tuple-element.160.x_ref.right_ref, bf16[2048,3584]{1,0:T(8,128)(2,1)} %get-tuple-element.161.w_ref), custom_call_target="tpu_custom_call" | custom-call | flops 15032385536 | bytes 28311552 | tf_op jit(solution)/shard_map/norm_back/pallas_call | solution.py:486
  240.6 17.6 %grads.5 = (bf16[1280,2048]{1,0:T(8,128)(2,1)}, bf16[1280,2048]{1,0:T(8,128)(2,1)}) custom-call(s32[1]{0:T(128)} %bitcast.2.f_ref, bf16[1024,2560]{1,0:T(8,128)(2,1)} %get-tuple-element.162.x_ref.att_ref.left_ref, bf16[1024,2048]{1,0:T(8,128)(2,1)} %get-tuple-element.163.right_ref), custom_call_target="tpu_custom_call" | custom-call | flops 10737418240 | bytes 19922944 | tf_op jit(solution)/shard_map/grads/pallas_call | solution.py:314
  258.4 8.6 %grads.6 = bf16[1024,2048]{1,0:T(8,128)(2,1)} custom-call(s32[1]{0:T(128)} %bitcast.2.f_ref, bf16[1024,2048]{1,0:T(8,128)(2,1)} %get-tuple-element.174.x_ref.left_ref, bf16[1024,3584]{1,0:T(8,128)(2,1)} %get-tuple-element.160.x_ref.right_ref), custom_call_target="tpu_custom_call" | custom-call | flops 4294967296 | bytes 10485760 | tf_op jit(solution)/shard_map/grads/pallas_call | solution.py:314
  267.2 2.1 add_convert_fusion.6
  270.6 8.5 %grads.7 = bf16[1024,2048]{1,0:T(8,128)(2,1)} custom-call(s32[1]{0:T(128)} %bitcast.2.f_ref, bf16[1024,2048]{1,0:T(8,128)(2,1)} %get-tuple-element.174.x_ref.left_ref, bf16[1024,3584]{1,0:T(8,128)(2,1)} %get-tuple-element.160.x_ref.right_ref, bf16[256,2048]{1,0:T(8,128)(2,1)} %reduce-scatter.3.cloned.1.call-done.refs_0_), custom_call_target="tpu_custom_call" | custom-call | flops 4294967296 | bytes 10485760 | tf_op jit(solution)/shard_map/grads/pallas_call | solution.py:314
  279.2 7.2 %grads.8 = bf16[1024,1536]{1,0:T(8,128)(2,1)} custom-call(s32[1]{0:T(128)} %bitcast.2.f_ref, bf16[1024,2048]{1,0:T(8,128)(2,1)} %get-tuple-element.174.x_ref.left_ref, bf16[1024,3584]{1,0:T(8,128)(2,1)} %get-tuple-element.160.x_ref.right_ref), custom_call_target="tpu_custom_call" | custom-call | flops 3221225472 | bytes 8388608 | tf_op jit(solution)/shard_map/grads/pallas_call | solution.py:314
  286.6 3.8 add_convert_fusion.3
  294.7 7.2 %grads.9 = bf16[1024,1536]{1,0:T(8,128)(2,1)} custom-call(s32[1]{0:T(128)} %bitcast.2.f_ref, bf16[1024,2048]{1,0:T(8,128)(2,1)} %get-tuple-element.174.x_ref.left_ref, bf16[1024,3584]{1,0:T(8,128)(2,1)} %get-tuple-element.160.x_ref.right_ref), custom_call_target="tpu_custom_call" | custom-call | flops 3221225472 | bytes 8388608 | tf_op jit(solution)/shard_map/grads/pallas_call | solution.py:314
  301.9 20.0 %collective-permute-done.25 = bf16[320,2048]{1,0:T(8,128)(2,1)} collective-permute-done((bf16[320,2048]{1,0:T(8,128)(2,1)S(1)}, bf16[320,2048]{1,0:T(8,128)(2,1)}, u32[]{:S(2)}, u32[]{:S(2)}) %collective-permute-start.25) | collective-permute-done | bytes 1310752 | tf_op jit(solution)/shard_map/ppermute | solution.py:597
  321.9 2.3 collective-permute-done.26
  324.2 3.5 add_convert_fusion.1
  327.8 2.4 add_convert_fusion.14
  332.6 4.0 collective-permute-start.30
  336.7 6.9 %collective-permute-done.27 = bf16[128,2048]{1,0:T(8,128)(2,1)} collective-permute-done((bf16[128,2048]{1,0:T(8,128)(2,1)S(1)}, bf16[128,2048]{1,0:T(8,128)(2,1)}, u32[]{:S(2)}, u32[]{:S(2)}) %collective-permute-start.27) | collective-permute-done | bytes 524320 | tf_op jit(solution)/shard_map/ppermute | solution.py:597
  344.8 2.8 convert_element_type.282
  347.6 4.7 add_convert_fusion.11
  357.9 2.1 multiply_add_fusion
  360.0 6.2 %collective-permute-done.29.refs_1_ = bf16[320,2048]{1,0:T(8,128)(2,1)} collective-permute-done((bf16[320,2048]{1,0:T(8,128)(2,1)S(1)}, bf16[320,2048]{1,0:T(8,128)(2,1)}, u32[]{:S(2)}, u32[]{:S(2)}) %collective-permute-start.29) | collective-permute-done | bytes 1310752 | tf_op jit(solution)/shard_map/ppermute | solution.py:588
  366.2 24.4 %collective-permute-done.30.refs_3_ = bf16[320,2048]{1,0:T(8,128)(2,1)} collective-permute-done((bf16[320,2048]{1,0:T(8,128)(2,1)S(1)}, bf16[320,2048]{1,0:T(8,128)(2,1)}, u32[]{:S(2)}, u32[]{:S(2)}) %collective-permute-start.30) | collective-permute-done | bytes 1310752 | tf_op jit(solution)/shard_map/ppermute | solution.py:588
  394.8 2.2 add_convert_fusion.9
  399.0 2.0 collective-permute-start.35
  403.1 21.6 %collective-permute-done.36.refs_2_ = bf16[320,2048]{1,0:T(8,128)(2,1)} collective-permute-done((bf16[320,2048]{1,0:T(8,128)(2,1)}, bf16[320,2048]{1,0:T(8,128)(2,1)}, u32[]{:S(2)}, u32[]{:S(2)}) %collective-permute-start.36) | collective-permute-done | bytes 1310752 | tf_op jit(solution)/shard_map/ppermute | solution.py:588
  431.4 7.6 %join_rows.1 = f32[1280,2048]{1,0:T(8,128)} custom-call(s32[8]{0:T(128)} %stack.71.at_ref, bf16[320,2048]{1,0:T(8,128)(2,1)} %copy-done.5, bf16[320,2048]{1,0:T(8,128)(2,1)} %collective-permute-done.29.refs_1_, bf16[320,2048]{1,0:T(8,128)(2,1)} %collective-permute-done.36.refs_2_, bf16[320,2048]{1,0:T(8,128)(2,1)} %collective-permute-done.30.refs_3_), custom_call_target="tpu_custom_call" | custom-call | bytes 15728640 | tf_op jit(solution)/shard_map/join_rows/pallas_call | solution.py:569
  439.0 8.1 %collective-permute-done.34.refs_1_ = bf16[256,2048]{1,0:T(8,128)(2,1)} collective-permute-done((bf16[256,2048]{1,0:T(8,128)(2,1)S(1)}, bf16[256,2048]{1,0:T(8,128)(2,1)}, u32[]{:S(2)}, u32[]{:S(2)}) %collective-permute-start.34) | collective-permute-done | bytes 1048608 | tf_op jit(solution)/shard_map/ppermute | solution.py:588
  447.1 19.8 %collective-permute-done.35.refs_3_ = bf16[256,2048]{1,0:T(8,128)(2,1)} collective-permute-done((bf16[256,2048]{1,0:T(8,128)(2,1)S(1)}, bf16[256,2048]{1,0:T(8,128)(2,1)}, u32[]{:S(2)}, u32[]{:S(2)}) %collective-permute-start.35) | collective-permute-done | bytes 1048608 | tf_op jit(solution)/shard_map/ppermute | solution.py:588
  467.5 2.2 add_convert_fusion.17
  470.4 3.2 collective-permute-start.43
  475.0 3.2 collective-permute-done.45
  478.2 17.0 %collective-permute-done.44.refs_2_ = bf16[256,2048]{1,0:T(8,128)(2,1)S(1)} collective-permute-done((bf16[256,2048]{1,0:T(8,128)(2,1)}, bf16[256,2048]{1,0:T(8,128)(2,1)S(1)}, u32[]{:S(2)}, u32[]{:S(2)}) %collective-permute-start.44) | collective-permute-done | bytes 1048608 | tf_op jit(solution)/shard_map/ppermute | solution.py:588
  495.8 3.9 collective-permute-done.46
  499.8 5.5 spread_columns.2.refs_4_
  505.3 6.7 %collective-permute-done.42.refs_1_ = bf16[256,1536]{1,0:T(8,128)(2,1)} collective-permute-done((bf16[256,1536]{1,0:T(8,128)(2,1)S(1)}, bf16[256,1536]{1,0:T(8,128)(2,1)}, u32[]{:S(2)}, u32[]{:S(2)}) %collective-permute-start.42) | collective-permute-done | bytes 786464 | tf_op jit(solution)/shard_map/ppermute | solution.py:588
  512.0 15.8 %collective-permute-done.43.refs_3_ = bf16[256,1536]{1,0:T(8,128)(2,1)S(1)} collective-permute-done((bf16[256,1536]{1,0:T(8,128)(2,1)S(1)}, bf16[256,1536]{1,0:T(8,128)(2,1)S(1)}, u32[]{:S(2)}, u32[]{:S(2)}) %collective-permute-start.43) | collective-permute-done | bytes 786464 | tf_op jit(solution)/shard_map/ppermute | solution.py:588
  532.3 21.1 %collective-permute-done.49 = f32[20480]{0:T(1024)S(1)} collective-permute-done((f32[20480]{0:T(1024)S(1)}, f32[20480]{0:T(1024)S(1)}, u32[]{:S(2)}, u32[]{:S(2)}) %collective-permute-start.49) | collective-permute-done | bytes 81952 | tf_op jit(solution)/shard_map/ppermute | solution.py:597
  553.5 4.5 spread_columns.3
  (258 shorter events, 82.5 us)
Async XLA Ops:
  7.2 165.8 %all-gather.2.cloned.1.call-start = ((), (), s32[]{:S(2)}) async-start(), calls=%async_computation.3 | async-start | bytes 5242880 | tf_op jit(solution)/shard_map/all_gather | solution.py:866
  10.9 29.4 %collective-permute-start = (bf16[256,2048]{1,0:T(8,128)(2,1)}, bf16[256,2048]{1,0:T(8,128)(2,1)}, u32[]{:S(2)}, u32[]{:S(2)}) collective-permute-start(bf16[256,2048]{1,0:T(8,128)(2,1)} %get-tuple-element.128.refs_0_), channel_id=1, source_target_pairs={{0,8},{8,16},{16,24},{24,0},{1,9},{9,17},{17,25},{25,1},{2,10},{10... | collective-permute-start | bytes 3145736 | tf_op jit(solution)/shard_map/ppermute | solution.py:588
  13.9 47.4 %collective-permute-start.1 = (bf16[256,2048]{1,0:T(8,128)(2,1)}, bf16[256,2048]{1,0:T(8,128)(2,1)}, u32[]{:S(2)}, u32[]{:S(2)}) collective-permute-start(bf16[256,2048]{1,0:T(8,128)(2,1)} %get-tuple-element.128.refs_0_), channel_id=1, source_target_pairs={{0,24},{8,0},{16,8},{24,16},{1,25},{9,1},{17,9},{25,17},{2,26},{10... | collective-permute-start | bytes 3145736 | tf_op jit(solution)/shard_map/ppermute | solution.py:588
  20.4 41.8 %collective-permute-start.3 = (bf16[256,3584]{1,0:T(8,128)(2,1)}, bf16[256,3584]{1,0:T(8,128)(2,1)}, u32[]{:S(2)}, u32[]{:S(2)}) collective-permute-start(bf16[256,3584]{1,0:T(8,128)(2,1)} %pick_columns.1.refs_4_.refs_0_), channel_id=1, source_target_pairs={{0,2},{1,3},{2,0},{3,1},{4,6},{5,7},{6,4},{7,5},{8,10},{9,11},{10,... | collective-permute-start | bytes 5505032 | tf_op jit(solution)/shard_map/ppermute | solution.py:597
  22.0 41.3 %collective-permute-start.4 = (bf16[256,3584]{1,0:T(8,128)(2,1)}, bf16[256,3584]{1,0:T(8,128)(2,1)}, u32[]{:S(2)}, u32[]{:S(2)}) collective-permute-start(bf16[256,3584]{1,0:T(8,128)(2,1)} %pick_columns.1.refs_4_.refs_0_), channel_id=1, source_target_pairs={{0,4},{1,5},{2,6},{3,7},{4,0},{5,1},{6,2},{7,3},{8,12},{9,13},{10,... | collective-permute-start | bytes 5505032 | tf_op jit(solution)/shard_map/ppermute | solution.py:597
  23.5 39.8 %collective-permute-start.5 = (bf16[256,3584]{1,0:T(8,128)(2,1)}, bf16[256,3584]{1,0:T(8,128)(2,1)}, u32[]{:S(2)}, u32[]{:S(2)}) collective-permute-start(bf16[256,3584]{1,0:T(8,128)(2,1)} %pick_columns.1.refs_4_.refs_0_), channel_id=1, source_target_pairs={{0,1},{1,0},{2,3},{3,2},{4,5},{5,4},{6,7},{7,6},{8,9},{9,8},{10,11... | collective-permute-start | bytes 5505032 | tf_op jit(solution)/shard_map/ppermute | solution.py:597
  63.4 27.6 %collective-permute-start.8 = (bf16[256,3584]{1,0:T(8,128)(2,1)}, bf16[256,3584]{1,0:T(8,128)(2,1)S(1)}, u32[]{:S(2)}, u32[]{:S(2)}) collective-permute-start(bf16[256,3584]{1,0:T(8,128)(2,1)} %collective-permute-done.3.refs_5_.refs_1_), channel_id=1, source_target_pairs={{0,1},{1,0},{2,3},{3,2},{4,5},{5,4},{6,7},{7,6},{8,9},{9,8},{10,11... | collective-permute-start | bytes 5505032 | tf_op jit(solution)/shard_map/ppermute | solution.py:597
  63.4 28.6 %collective-permute-start.9 = (bf16[256,3584]{1,0:T(8,128)(2,1)}, bf16[256,3584]{1,0:T(8,128)(2,1)}, u32[]{:S(2)}, u32[]{:S(2)}) collective-permute-start(bf16[256,3584]{1,0:T(8,128)(2,1)} %collective-permute-done.4.refs_6_.refs_2_), channel_id=1, source_target_pairs={{0,1},{1,0},{2,3},{3,2},{4,5},{5,4},{6,7},{7,6},{8,9},{9,8},{10,11... | collective-permute-start | bytes 5505032 | tf_op jit(solution)/shard_map/ppermute | solution.py:597
  63.9 27.1 %collective-permute-start.2 = (bf16[256,2048]{1,0:T(8,128)(2,1)}, bf16[256,2048]{1,0:T(8,128)(2,1)S(1)}, u32[]{:S(2)}, u32[]{:S(2)}) collective-permute-start(bf16[256,2048]{1,0:T(8,128)(2,1)} %collective-permute-done.refs_1_), channel_id=1, source_target_pairs={{0,8},{8,16},{16,24},{24,0},{1,9},{9,17},{17,25},{25,1},{2,10},{10... | collective-permute-start | bytes 3145736 | tf_op jit(solution)/shard_map/ppermute | solution.py:588
  66.4 24.6 %collective-permute-start.6 = (bf16[128,3584]{1,0:T(8,128)(2,1)S(1)}, bf16[128,3584]{1,0:T(8,128)(2,1)S(1)}, u32[]{:S(2)}, u32[]{:S(2)}) collective-permute-start(bf16[128,3584]{1,0:T(8,128)(2,1)S(1)} %slice.575), channel_id=1, source_target_pairs={{0,4},{1,5},{2,6},{3,7},{4,0},{5,1},{6,2},{7,3},{8,12},{9,13},{10,... | collective-permute-start | bytes 2752520 | tf_op jit(solution)/shard_map/ppermute | solution.py:597
  68.0 23.0 %collective-permute-start.7 = (bf16[128,3584]{1,0:T(8,128)(2,1)S(1)}, bf16[128,3584]{1,0:T(8,128)(2,1)S(1)}, u32[]{:S(2)}, u32[]{:S(2)}) collective-permute-start(bf16[128,3584]{1,0:T(8,128)(2,1)S(1)} %slice.576), channel_id=1, source_target_pairs={{0,2},{1,3},{2,0},{3,1},{4,6},{5,7},{6,4},{7,5},{8,10},{9,11},{10,... | collective-permute-start | bytes 2752520 | tf_op jit(solution)/shard_map/ppermute | solution.py:597
  92.6 178.1 %reduce-scatter.3.cloned.1.call-start = ((), (), s32[]{:S(2)}) async-start(), calls=%async_computation.2 | async-start | bytes 5242880 | tf_op jit(solution)/shard_map/reduce_scatter | solution.py:905
  97.2 30.8 %collective-permute-start.12 = (bf16[320,2048]{1,0:T(8,128)(2,1)S(1)}, bf16[320,2048]{1,0:T(8,128)(2,1)S(1)}, u32[]{:S(2)}, u32[]{:S(2)}) collective-permute-start(bf16[320,2048]{1,0:T(8,128)(2,1)S(1)} %maximum_select_fusion.refs_0_), channel_id=1, source_target_pairs={{0,2},{1,3},{2,0},{3,1},{4,6},{5,7},{6,4},{7,5},{8,10},{9,11},{10,... | collective-permute-start | bytes 3932168 | tf_op jit(solution)/shard_map/ppermute | solution.py:597
  97.7 30.5 %collective-permute-start.13 = (bf16[320,2048]{1,0:T(8,128)(2,1)S(1)}, bf16[320,2048]{1,0:T(8,128)(2,1)S(1)}, u32[]{:S(2)}, u32[]{:S(2)}) collective-permute-start(bf16[320,2048]{1,0:T(8,128)(2,1)S(1)} %maximum_select_fusion.refs_0_), channel_id=1, source_target_pairs={{0,4},{1,5},{2,6},{3,7},{4,0},{5,1},{6,2},{7,3},{8,12},{9,13},{10,... | collective-permute-start | bytes 3932168 | tf_op jit(solution)/shard_map/ppermute | solution.py:597
  99.2 29.0 %collective-permute-start.14 = (bf16[320,2048]{1,0:T(8,128)(2,1)S(1)}, bf16[320,2048]{1,0:T(8,128)(2,1)}, u32[]{:S(2)}, u32[]{:S(2)}) collective-permute-start(bf16[320,2048]{1,0:T(8,128)(2,1)S(1)} %maximum_select_fusion.refs_0_), channel_id=1, source_target_pairs={{0,1},{1,0},{2,3},{3,2},{4,5},{5,4},{6,7},{7,6},{8,9},{9,8},{10,11... | collective-permute-start | bytes 3932168 | tf_op jit(solution)/shard_map/ppermute | solution.py:597
  128.3 22.4 %collective-permute-start.17 = (bf16[320,2048]{1,0:T(8,128)(2,1)S(1)}, bf16[320,2048]{1,0:T(8,128)(2,1)S(1)}, u32[]{:S(2)}, u32[]{:S(2)}) collective-permute-start(bf16[320,2048]{1,0:T(8,128)(2,1)S(1)} %collective-permute-done.12.refs_1_), channel_id=1, source_target_pairs={{0,1},{1,0},{2,3},{3,2},{4,5},{5,4},{6,7},{7,6},{8,9},{9,8},{10,11... | collective-permute-start | bytes 3932168 | tf_op jit(solution)/shard_map/ppermute | solution.py:597
  128.3 22.4 %collective-permute-start.18 = (bf16[320,2048]{1,0:T(8,128)(2,1)S(1)}, bf16[320,2048]{1,0:T(8,128)(2,1)S(1)}, u32[]{:S(2)}, u32[]{:S(2)}) collective-permute-start(bf16[320,2048]{1,0:T(8,128)(2,1)S(1)} %collective-permute-done.13.refs_2_), channel_id=1, source_target_pairs={{0,1},{1,0},{2,3},{3,2},{4,5},{5,4},{6,7},{7,6},{8,9},{9,8},{10,11... | collective-permute-start | bytes 3932168 | tf_op jit(solution)/shard_map/ppermute | solution.py:597
  128.9 21.7 %collective-permute-start.15 = (bf16[160,2048]{1,0:T(8,128)(2,1)S(1)}, bf16[160,2048]{1,0:T(8,128)(2,1)S(1)}, u32[]{:S(2)}, u32[]{:S(2)}) collective-permute-start(bf16[160,2048]{1,0:T(8,128)(2,1)S(1)} %slice.577), channel_id=1, source_target_pairs={{0,4},{1,5},{2,6},{3,7},{4,0},{5,1},{6,2},{7,3},{8,12},{9,13},{10,... | collective-permute-start | bytes 1966088 | tf_op jit(solution)/shard_map/ppermute | solution.py:597
  130.5 20.1 %collective-permute-start.16 = (bf16[160,2048]{1,0:T(8,128)(2,1)S(1)}, bf16[160,2048]{1,0:T(8,128)(2,1)}, u32[]{:S(2)}, u32[]{:S(2)}) collective-permute-start(bf16[160,2048]{1,0:T(8,128)(2,1)S(1)} %slice.578), channel_id=1, source_target_pairs={{0,2},{1,3},{2,0},{3,1},{4,6},{5,7},{6,4},{7,5},{8,10},{9,11},{10,... | collective-permute-start | bytes 1966088 | tf_op jit(solution)/shard_map/ppermute | solution.py:597
  172.7 172.1 %reduce-scatter.5.cloned.1.call-start = ((), (), s32[]{:S(2)}) async-start(), calls=%async_computation.4 | async-start | bytes 5242880 | tf_op jit(solution)/shard_map/reduce_scatter | solution.py:905
  258.2 9.0 %collective-permute-start.21 = (bf16[1280,2048]{1,0:T(8,128)(2,1)}, bf16[1280,2048]{1,0:T(8,128)(2,1)}, u32[]{:S(2)}, u32[]{:S(2)}) collective-permute-start(bf16[1280,2048]{1,0:T(8,128)(2,1)} %get-tuple-element.165), channel_id=1, source_target_pairs={{0,1},{1,0},{2,3},{3,2},{4,5},{5,4},{6,7},{7,6},{8,9},{9,8},{10,11... | collective-permute-start | bytes 15728648 | tf_op jit(solution)/shard_map/ppermute | solution.py:597
  269.4 17.0 %collective-permute-start.22 = (bf16[160,2048]{1,0:T(8,128)(2,1)S(1)}, bf16[160,2048]{1,0:T(8,128)(2,1)S(1)}, u32[]{:S(2)}, u32[]{:S(2)}) collective-permute-start(bf16[160,2048]{1,0:T(8,128)(2,1)S(1)} %get-tuple-element.263), channel_id=1, source_target_pairs={{0,4},{1,5},{2,6},{3,7},{4,0},{5,1},{6,2},{7,3},{8,12},{9,13},{10,... | collective-permute-start | bytes 1966088 | tf_op jit(solution)/shard_map/ppermute | solution.py:597
  269.9 16.6 %collective-permute-start.23 = (bf16[160,2048]{1,0:T(8,128)(2,1)S(1)}, bf16[160,2048]{1,0:T(8,128)(2,1)S(1)}, u32[]{:S(2)}, u32[]{:S(2)}) collective-permute-start(bf16[160,2048]{1,0:T(8,128)(2,1)S(1)} %get-tuple-element.262), channel_id=1, source_target_pairs={{0,2},{1,3},{2,0},{3,1},{4,6},{5,7},{6,4},{7,5},{8,10},{9,11},{10,... | collective-permute-start | bytes 1966088 | tf_op jit(solution)/shard_map/ppermute | solution.py:597
  286.6 41.2 %collective-permute-start.24 = (bf16[1024,2048]{1,0:T(8,128)(2,1)}, bf16[1024,2048]{1,0:T(8,128)(2,1)}, u32[]{:S(2)}, u32[]{:S(2)}) collective-permute-start(bf16[1024,2048]{1,0:T(8,128)(2,1)} %grads.6), channel_id=1, source_target_pairs={{0,1},{1,0},{2,3},{3,2},{4,5},{5,4},{6,7},{7,6},{8,9},{9,8},{10,11... | collective-permute-start | bytes 12582920 | tf_op jit(solution)/shard_map/ppermute | solution.py:597
  290.5 31.4 %collective-permute-start.25 = (bf16[320,2048]{1,0:T(8,128)(2,1)S(1)}, bf16[320,2048]{1,0:T(8,128)(2,1)}, u32[]{:S(2)}, u32[]{:S(2)}) collective-permute-start(bf16[320,2048]{1,0:T(8,128)(2,1)S(1)} %pad_maximum_fusion), channel_id=1, source_target_pairs={{0,2},{1,3},{2,0},{3,1},{4,6},{5,7},{6,4},{7,5},{8,10},{9,11},{10,... | collective-permute-start | bytes 3932168 | tf_op jit(solution)/shard_map/ppermute | solution.py:597
  293.0 31.2 %collective-permute-start.26 = (bf16[320,2048]{1,0:T(8,128)(2,1)}, bf16[320,2048]{1,0:T(8,128)(2,1)}, u32[]{:S(2)}, u32[]{:S(2)}) collective-permute-start(bf16[320,2048]{1,0:T(8,128)(2,1)} %pad_maximum_fusion.1), channel_id=1, source_target_pairs={{0,4},{1,5},{2,6},{3,7},{4,0},{5,1},{6,2},{7,3},{8,12},{9,13},{10,... | collective-permute-start | bytes 3932168 | tf_op jit(solution)/shard_map/ppermute | solution.py:597
  330.1 13.4 %collective-permute-start.27 = (bf16[128,2048]{1,0:T(8,128)(2,1)S(1)}, bf16[128,2048]{1,0:T(8,128)(2,1)}, u32[]{:S(2)}, u32[]{:S(2)}) collective-permute-start(bf16[128,2048]{1,0:T(8,128)(2,1)S(1)} %get-tuple-element.269), channel_id=1, source_target_pairs={{0,4},{1,5},{2,6},{3,7},{4,0},{5,1},{6,2},{7,3},{8,12},{9,13},{10,... | collective-permute-start | bytes 1572872 | tf_op jit(solution)/shard_map/ppermute | solution.py:597
  331.7 13.0 %collective-permute-start.28 = (bf16[128,2048]{1,0:T(8,128)(2,1)S(1)}, bf16[128,2048]{1,0:T(8,128)(2,1)}, u32[]{:S(2)}, u32[]{:S(2)}) collective-permute-start(bf16[128,2048]{1,0:T(8,128)(2,1)S(1)} %get-tuple-element.268), channel_id=1, source_target_pairs={{0,2},{1,3},{2,0},{3,1},{4,6},{5,7},{6,4},{7,5},{8,10},{9,11},{10,... | collective-permute-start | bytes 1572872 | tf_op jit(solution)/shard_map/ppermute | solution.py:597
  332.6 33.7 %collective-permute-start.29 = (bf16[320,2048]{1,0:T(8,128)(2,1)S(1)}, bf16[320,2048]{1,0:T(8,128)(2,1)}, u32[]{:S(2)}, u32[]{:S(2)}) collective-permute-start(bf16[320,2048]{1,0:T(8,128)(2,1)S(1)} %pad_maximum_fusion.2.refs_0_), channel_id=1, source_target_pairs={{0,8},{8,16},{16,24},{24,0},{1,9},{9,17},{17,25},{25,1},{2,10},{10... | collective-permute-start | bytes 3932168 | tf_op jit(solution)/shard_map/ppermute | solution.py:588
  332.6 58.0 %collective-permute-start.30 = (bf16[320,2048]{1,0:T(8,128)(2,1)S(1)}, bf16[320,2048]{1,0:T(8,128)(2,1)}, u32[]{:S(2)}, u32[]{:S(2)}) collective-permute-start(bf16[320,2048]{1,0:T(8,128)(2,1)S(1)} %pad_maximum_fusion.2.refs_0_), channel_id=1, source_target_pairs={{0,24},{8,0},{16,8},{24,16},{1,25},{9,1},{17,9},{25,17},{2,26},{10... | collective-permute-start | bytes 3932168 | tf_op jit(solution)/shard_map/ppermute | solution.py:588
  336.7 54.0 %collective-permute-start.33 = (bf16[1024,1536]{1,0:T(8,128)(2,1)}, bf16[1024,1536]{1,0:T(8,128)(2,1)}, u32[]{:S(2)}, u32[]{:S(2)}) collective-permute-start(bf16[1024,1536]{1,0:T(8,128)(2,1)} %grads.8), channel_id=1, source_target_pairs={{0,1},{1,0},{2,3},{3,2},{4,5},{5,4},{6,7},{7,6},{8,9},{9,8},{10,11... | collective-permute-start | bytes 9437192 | tf_op jit(solution)/shard_map/ppermute | solution.py:597
  353.9 36.7 %collective-permute-start.31 = (bf16[256,2048]{1,0:T(8,128)(2,1)S(1)}, bf16[256,2048]{1,0:T(8,128)(2,1)S(1)}, u32[]{:S(2)}, u32[]{:S(2)}) collective-permute-start(bf16[256,2048]{1,0:T(8,128)(2,1)S(1)} %pad_maximum_fusion.3), channel_id=1, source_target_pairs={{0,2},{1,3},{2,0},{3,1},{4,6},{5,7},{6,4},{7,5},{8,10},{9,11},{10,... | collective-permute-start | bytes 3145736 | tf_op jit(solution)/shard_map/ppermute | solution.py:597
  354.9 35.8 %collective-permute-start.32 = (bf16[256,2048]{1,0:T(8,128)(2,1)S(1)}, bf16[256,2048]{1,0:T(8,128)(2,1)S(1)}, u32[]{:S(2)}, u32[]{:S(2)}) collective-permute-start(bf16[256,2048]{1,0:T(8,128)(2,1)S(1)} %pad_maximum_fusion.4), channel_id=1, source_target_pairs={{0,4},{1,5},{2,6},{3,7},{4,0},{5,1},{6,2},{7,3},{8,12},{9,13},{10,... | collective-permute-start | bytes 3145736 | tf_op jit(solution)/shard_map/ppermute | solution.py:597
  390.7 34.0 %collective-permute-start.36 = (bf16[320,2048]{1,0:T(8,128)(2,1)}, bf16[320,2048]{1,0:T(8,128)(2,1)}, u32[]{:S(2)}, u32[]{:S(2)}) collective-permute-start(bf16[320,2048]{1,0:T(8,128)(2,1)} %collective-permute-done.29.refs_1_), channel_id=1, source_target_pairs={{0,8},{8,16},{16,24},{24,0},{1,9},{9,17},{17,25},{25,1},{2,10},{10... | collective-permute-start | bytes 3932168 | tf_op jit(solution)/shard_map/ppermute | solution.py:588
  392.3 9.4 %collective-permute-start.37 = (bf16[128,1536]{1,0:T(8,128)(2,1)S(1)}, bf16[128,1536]{1,0:T(8,128)(2,1)S(1)}, u32[]{:S(2)}, u32[]{:S(2)}) collective-permute-start(bf16[128,1536]{1,0:T(8,128)(2,1)S(1)} %get-tuple-element.277), channel_id=1, source_target_pairs={{0,4},{1,5},{2,6},{3,7},{4,0},{5,1},{6,2},{7,3},{8,12},{9,13},{10,... | collective-permute-start | bytes 1179656 | tf_op jit(solution)/shard_map/ppermute | solution.py:597
  393.8 9.4 %collective-permute-start.38 = (bf16[128,1536]{1,0:T(8,128)(2,1)S(1)}, bf16[128,1536]{1,0:T(8,128)(2,1)S(1)}, u32[]{:S(2)}, u32[]{:S(2)}) collective-permute-start(bf16[128,1536]{1,0:T(8,128)(2,1)S(1)} %get-tuple-element.276), channel_id=1, source_target_pairs={{0,2},{1,3},{2,0},{3,1},{4,6},{5,7},{6,4},{7,5},{8,10},{9,11},{10,... | collective-permute-start | bytes 1179656 | tf_op jit(solution)/shard_map/ppermute | solution.py:597
  397.1 49.9 %collective-permute-start.34 = (bf16[256,2048]{1,0:T(8,128)(2,1)S(1)}, bf16[256,2048]{1,0:T(8,128)(2,1)}, u32[]{:S(2)}, u32[]{:S(2)}) collective-permute-start(bf16[256,2048]{1,0:T(8,128)(2,1)S(1)} %pad_maximum_fusion.5.refs_0_), channel_id=1, source_target_pairs={{0,8},{8,16},{16,24},{24,0},{1,9},{9,17},{17,25},{25,1},{2,10},{10... | collective-permute-start | bytes 3145736 | tf_op jit(solution)/shard_map/ppermute | solution.py:588
  399.0 67.9 %collective-permute-start.35 = (bf16[256,2048]{1,0:T(8,128)(2,1)S(1)}, bf16[256,2048]{1,0:T(8,128)(2,1)}, u32[]{:S(2)}, u32[]{:S(2)}) collective-permute-start(bf16[256,2048]{1,0:T(8,128)(2,1)S(1)} %pad_maximum_fusion.5.refs_0_), channel_id=1, source_target_pairs={{0,24},{8,0},{16,8},{24,16},{1,25},{9,1},{17,9},{25,17},{2,26},{10... | collective-permute-start | bytes 3145736 | tf_op jit(solution)/shard_map/ppermute | solution.py:588
  427.5 39.4 %collective-permute-start.39 = (bf16[256,1536]{1,0:T(8,128)(2,1)}, bf16[256,1536]{1,0:T(8,128)(2,1)}, u32[]{:S(2)}, u32[]{:S(2)}) collective-permute-start(bf16[256,1536]{1,0:T(8,128)(2,1)} %pad_maximum_fusion.6), channel_id=1, source_target_pairs={{0,2},{1,3},{2,0},{3,1},{4,6},{5,7},{6,4},{7,5},{8,10},{9,11},{10,... | collective-permute-start | bytes 2359304 | tf_op jit(solution)/shard_map/ppermute | solution.py:597
  429.7 37.2 %collective-permute-start.40 = (bf16[256,1536]{1,0:T(8,128)(2,1)}, bf16[256,1536]{1,0:T(8,128)(2,1)}, u32[]{:S(2)}, u32[]{:S(2)}) collective-permute-start(bf16[256,1536]{1,0:T(8,128)(2,1)} %pad_maximum_fusion.7), channel_id=1, source_target_pairs={{0,4},{1,5},{2,6},{3,7},{4,0},{5,1},{6,2},{7,3},{8,12},{9,13},{10,... | collective-permute-start | bytes 2359304 | tf_op jit(solution)/shard_map/ppermute | solution.py:597
  430.6 36.3 %collective-permute-start.41 = (f32[20480]{0:T(1024)S(1)}, f32[20480]{0:T(1024)S(1)}, u32[]{:S(2)}, u32[]{:S(2)}) collective-permute-start(f32[20480]{0:T(1024)S(1)} %concatenate.101), channel_id=1, source_target_pairs={{0,1},{1,0},{2,3},{3,2},{4,5},{5,4},{6,7},{7,6},{8,9},{9,8},{10,11... | collective-permute-start | bytes 245768 | tf_op jit(solution)/shard_map/ppermute | solution.py:597
  466.9 28.3 %collective-permute-start.44 = (bf16[256,2048]{1,0:T(8,128)(2,1)}, bf16[256,2048]{1,0:T(8,128)(2,1)S(1)}, u32[]{:S(2)}, u32[]{:S(2)}) collective-permute-start(bf16[256,2048]{1,0:T(8,128)(2,1)} %collective-permute-done.34.refs_1_), channel_id=1, source_target_pairs={{0,8},{8,16},{16,24},{24,0},{1,9},{9,17},{17,25},{25,1},{2,10},{10... | collective-permute-start | bytes 3145736 | tf_op jit(solution)/shard_map/ppermute | solution.py:588
  469.8 42.2 %collective-permute-start.42 = (bf16[256,1536]{1,0:T(8,128)(2,1)S(1)}, bf16[256,1536]{1,0:T(8,128)(2,1)}, u32[]{:S(2)}, u32[]{:S(2)}) collective-permute-start(bf16[256,1536]{1,0:T(8,128)(2,1)S(1)} %pad_maximum_fusion.8.refs_0_), channel_id=1, source_target_pairs={{0,8},{8,16},{16,24},{24,0},{1,9},{9,17},{17,25},{25,1},{2,10},{10... | collective-permute-start | bytes 2359304 | tf_op jit(solution)/shard_map/ppermute | solution.py:588
  470.4 57.3 %collective-permute-start.43 = (bf16[256,1536]{1,0:T(8,128)(2,1)S(1)}, bf16[256,1536]{1,0:T(8,128)(2,1)S(1)}, u32[]{:S(2)}, u32[]{:S(2)}) collective-permute-start(bf16[256,1536]{1,0:T(8,128)(2,1)S(1)} %pad_maximum_fusion.8.refs_0_), channel_id=1, source_target_pairs={{0,24},{8,0},{16,8},{24,16},{1,25},{9,1},{17,9},{25,17},{2,26},{10... | collective-permute-start | bytes 2359304 | tf_op jit(solution)/shard_map/ppermute | solution.py:588
  473.7 4.5 collective-permute-start.45
  499.7 29.7 %collective-permute-start.47 = (f32[20480]{0:T(1024)S(1)}, f32[20480]{0:T(1024)S(1)}, u32[]{:S(2)}, u32[]{:S(2)}) collective-permute-start(f32[20480]{0:T(1024)S(1)} %add.384), channel_id=1, source_target_pairs={{0,8},{8,0},{16,24},{24,16},{1,9},{9,1},{17,25},{25,17},{2,10},{10... | collective-permute-start | bytes 245768 | tf_op jit(solution)/shard_map/ppermute | solution.py:597
  529.4 24.0 %collective-permute-start.48 = (bf16[256,1536]{1,0:T(8,128)(2,1)}, bf16[256,1536]{1,0:T(8,128)(2,1)}, u32[]{:S(2)}, u32[]{:S(2)}) collective-permute-start(bf16[256,1536]{1,0:T(8,128)(2,1)} %collective-permute-done.42.refs_1_), channel_id=1, source_target_pairs={{0,8},{8,16},{16,24},{24,0},{1,9},{9,17},{17,25},{25,1},{2,10},{10... | collective-permute-start | bytes 2359304 | tf_op jit(solution)/shard_map/ppermute | solution.py:588
  529.4 24.0 %collective-permute-start.49 = (f32[20480]{0:T(1024)S(1)}, f32[20480]{0:T(1024)S(1)}, u32[]{:S(2)}, u32[]{:S(2)}) collective-permute-start(f32[20480]{0:T(1024)S(1)} %add.385), channel_id=1, source_target_pairs={{0,16},{8,24},{16,0},{24,8},{1,17},{9,25},{17,1},{25,9},{2,18},{10... | collective-permute-start | bytes 245768 | tf_op jit(solution)/shard_map/ppermute | solution.py:597
  (44 other events, 395.7 us)
Sparse Core Ops, SparseCore 0:
  92.7 78.3 all-gather.1
  173.4 75.2 reduce-scatter.2
  258.6 74.2 reduce-scatter.4

commit v8 on v7

--- a/solution.py
+++ b/solution.py
@@ -336,9 +336,9 @@
 def gelu_parts(u):
     c = math.sqrt(2.0 / math.pi)
     square = u * u
-    t = jnp.tanh(c * (u + 0.044715 * u * square))
-    value = 0.5 * u * (1.0 + t)
-    slope = 0.5 * (1.0 + t) + 0.5 * u * (1.0 - t * t) * (c * (1.0 + 3 * 0.044715 * square))
+    half = 0.5 * jnp.tanh(u * (c + (c * 0.044715) * square)) + 0.5
+    value = u * half
+    slope = half + half * (1.0 - half) * (u * (2.0 * c + (6.0 * c * 0.044715) * square))
     return value, slope
 
 

time: 574 us -> 573 us (level)
  no operation moved by 1% of the time
where the time goes in v8:
time: 573 us; the launch traced here: 567 us
  waiting for transfers between devices  235 us (41%)
  Pallas kernels  206 us (36%)
  starting transfers between devices  47.1 us (8%)
  other arithmetic  43.2 us (8%)
  local copies, waits for them, and re-layouts  19.4 us (3%)
  between operations  15.1 us (3%)
    ppermute x12, waiting for transfers between devices, pass_on(): return lax.ppermute(x, 'ctx', [(i, (i + hops) % n) for i in range(n)])  164 us
    ppermute x38, waiting for transfers between devices, swap(): return lax.ppermute(x, axis, [(i, i ^ bit) for i in range(n)])  71.1 us
    pallas_call x5, Pallas kernels, grads(): pl.pallas_call(functools.partial(grads_kernel, n_split, len(late)), grid_...  49.1 us
    ppermute x38, starting transfers between devices, swap(): return lax.ppermute(x, axis, [(i, i ^ bit) for i in range(n)])  28.4 us
    pallas_call x1, Pallas kernels, attention_back(): pl.pallas_call(functools.partial(back_kernel, pairs), grid=(pairs,), in_s...  22.7 us
    pallas_call x1, Pallas kernels, norm_back(): pl.pallas_call(functools.partial(norm_kernel_back, blk_size), grid_spec=p...  22.1 us
    pallas_call x1, Pallas kernels, d_cat_parts(): pl.pallas_call(functools.partial(d_cat_kernel, cuts), grid_spec=pltpu.Pre...  22.1 us
    pallas_call x1, Pallas kernels, pre_project(): pl.pallas_call(functools.partial(pre_kernel, w_cuts, n_w), grid_spec=pltp...  18.4 us
  transfers between devices with their start and end apart: 53, of which 31 were waited for; matrix products, arithmetic and copies ran while one was open for 10% of the time, Pallas kernels for 35%

profile of v8, /device:TPU:0, one launch (start us, length us, event | category | flops | bytes accessed | tf_op | source)
XLA Modules:
  0.0 566.5 jit_solution(4329221534186138320)
XLA Ops:
  7.2 3.7 norm.1
  10.9 3.0 collective-permute-start
  13.9 2.1 collective-permute-start.1
  16.0 4.3 pick_columns.1.refs_4_.refs_0_
  40.3 21.0 %collective-permute-done.1.refs_3_ = bf16[256,2048]{1,0:T(8,128)(2,1)} collective-permute-done((bf16[256,2048]{1,0:T(8,128)(2,1)}, bf16[256,2048]{1,0:T(8,128)(2,1)}, u32[]{:S(2)}, u32[]{:S(2)}) %collective-permute-start.1) | collective-permute-done | bytes 1048608 | tf_op jit(solution)/shard_map/ppermute | solution.py:588
  68.6 22.3 %collective-permute-done.2.refs_2_ = bf16[256,2048]{1,0:T(8,128)(2,1)S(1)} collective-permute-done((bf16[256,2048]{1,0:T(8,128)(2,1)}, bf16[256,2048]{1,0:T(8,128)(2,1)S(1)}, u32[]{:S(2)}, u32[]{:S(2)}) %collective-permute-start.2) | collective-permute-done | bytes 1048608 | tf_op jit(solution)/shard_map/ppermute | solution.py:588
  93.7 2.2 collective-permute-done.10.refs_12_.refs_8_
  99.3 13.6 %qkv_project.1 = (f32[1024,1536]{1,0:T(8,128)}, bf16[1024,2048]{1,0:T(8,128)(2,1)}, bf16[2048,3584]{1,0:T(8,128)(2,1)}) custom-call(s32[18]{0:T(128)} %get-tuple-element.353.at_ref, bf16[256,2048]{1,0:T(8,128)(2,1)} %get-tuple-element.128.refs_0_, bf16[256,2048]{1,0:T(8,128)(2,1)} %collective-permute-done.refs_1_, bf16[256,2048]{1,0:T(8,128)(2,1)} %copy-done.34, ...), custom_call_target="tpu_custom_call" | custom-call | flops 6442450944 | bytes 16777216 | tf_op jit(solution)/shard_map/qkv_project/pallas_call | solution.py:377
  112.8 14.8 %attention.1 = (bf16[1024,512]{1,0:T(8,128)(2,1)}, bf16[1024,512]{1,0:T(8,128)(2,1)}, bf16[1024,512]{1,0:T(8,128)(2,1)}, bf16[1024,2560]{1,0:T(8,128)(2,1)}, f32[4,2,1024]{2,1,0:T(2,128)}) custom-call(f32[1024,1536]{1,0:T(8,128)} %get-tuple-element.131.q_ref.k_ref.v_ref, f32[1024,1536]{1,0:T(8,128)} %get-tuple-element.131.q_ref.k_ref.v_ref, ...), custom_call_target="tpu_custom_call" | custom-call | flops 2147483648 | bytes 10485760 | tf_op jit(solution)/shard_map/attention/pallas_call | solution.py:206
  132.0 18.4 %pre_project.1 = (f32[1024,2048]{1,0:T(8,128)}, bf16[1024,2560]{1,0:T(8,128)(2,1)}, bf16[2048,3584]{1,0:T(8,128)(2,1)}) custom-call(s32[10]{0:T(128)} %constant.90.clone.at_ref, bf16[1024,2048]{1,0:T(8,128)(2,1)} %get-tuple-element.174.x_ref.left_ref, bf16[256,3584]{1,0:T(8,128)(2,1)} %pick_columns.1.refs_4_.refs_0_, ...), custom_call_target="tpu_custom_call", output_to_operand_aliasing={{1}: (13, {}), {2}: (14, {})} | custom-call | flops 8589934592 | bytes 25165824 | tf_op jit(solution)/shard_map/pre_project/pallas_call | solution.py:415
  154.6 17.9 %out_project.1 = (bf16[1024,2048]{1,0:T(8,128)(2,1)}, bf16[2560,2048]{1,0:T(8,128)(2,1)}) custom-call(s32[18]{0:T(128)} %get-tuple-element.352.at_ref, bf16[1024,2560]{1,0:T(8,128)(2,1)} %get-tuple-element.162.x_ref.att_ref.left_ref, bf16[320,2048]{1,0:T(8,128)(2,1)} %copy-done.12, bf16[320,2048]{1,0:T(8,128)(2,1)} %copy-done.19, ...), custom_call_target="tpu_custom_call" | custom-call | flops 10737418240 | bytes 22020096 | tf_op jit(solution)/shard_map/out_project/pallas_call | solution.py:458
  172.7 22.1 %d_cat_parts.1 = (bf16[1024,512]{1,0:T(8,128)(2,1)}, bf16[1024,3584]{1,0:T(8,128)(2,1)}, f32[1,2048]{1,0:T(1,128)}, bf16[1024,2048]{1,0:T(8,128)(2,1)}) custom-call(s32[8]{0:T(128)} %broadcast_multiply_fusion.3.at_ref, bf16[1024,2048]{1,0:T(8,128)(2,1)} %all-gather.2.cloned.1.call-done.g_ref, bf16[2560,2048]{1,0:T(8,128)(2,1)} %get-tuple-element.153.w_ref, ...), custom_call_target="tpu_custom_call" | custom-call | flops 10737418240 | bytes 25165824 | tf_op jit(solution)/shard_map/d_cat_parts/pallas_call | solution.py:529
  194.8 22.7 %attention_back.1 = (bf16[1024,3584]{1,0:T(8,128)(2,1)}, f32[1,512]{1,0:T(1,128)}, f32[1,512]{1,0:T(1,128)}, f32[1,512]{1,0:T(1,128)}) custom-call(bf16[1024,512]{1,0:T(8,128)(2,1)} %get-tuple-element.147.q_ref, bf16[1024,512]{1,0:T(8,128)(2,1)} %get-tuple-element.148.k_ref, ...), custom_call_target="tpu_custom_call", output_to_operand_aliasing={{0}: (9, {})} | custom-call | flops 5368709120 | bytes 8388608 | tf_op jit(solution)/shard_map/attention_back/pallas_call | solution.py:276
  217.5 22.1 %norm_back.1 = bf16[1024,2048]{1,0:T(8,128)(2,1)} custom-call(s32[8]{0:T(128)} %copy-done.29, bf16[1024,3584]{1,0:T(8,128)(2,1)} %get-tuple-element.160.x_ref.right_ref, bf16[2048,3584]{1,0:T(8,128)(2,1)} %get-tuple-element.161.w_ref), custom_call_target="tpu_custom_call" | custom-call | flops 15032385536 | bytes 28311552 | tf_op jit(solution)/shard_map/norm_back/pallas_call | solution.py:486
  239.6 17.6 %grads.5 = (bf16[1280,2048]{1,0:T(8,128)(2,1)}, bf16[1280,2048]{1,0:T(8,128)(2,1)}) custom-call(s32[1]{0:T(128)} %bitcast.2.f_ref, bf16[1024,2560]{1,0:T(8,128)(2,1)} %get-tuple-element.162.x_ref.att_ref.left_ref, bf16[1024,2048]{1,0:T(8,128)(2,1)} %get-tuple-element.163.right_ref), custom_call_target="tpu_custom_call" | custom-call | flops 10737418240 | bytes 19922944 | tf_op jit(solution)/shard_map/grads/pallas_call | solution.py:314
  257.3 8.7 %grads.6 = bf16[1024,2048]{1,0:T(8,128)(2,1)} custom-call(s32[1]{0:T(128)} %bitcast.2.f_ref, bf16[1024,2048]{1,0:T(8,128)(2,1)} %get-tuple-element.174.x_ref.left_ref, bf16[1024,3584]{1,0:T(8,128)(2,1)} %get-tuple-element.160.x_ref.right_ref), custom_call_target="tpu_custom_call" | custom-call | flops 4294967296 | bytes 10485760 | tf_op jit(solution)/shard_map/grads/pallas_call | solution.py:314
  266.2 2.1 add_convert_fusion.6
  269.8 8.5 %grads.7 = bf16[1024,2048]{1,0:T(8,128)(2,1)} custom-call(s32[1]{0:T(128)} %bitcast.2.f_ref, bf16[1024,2048]{1,0:T(8,128)(2,1)} %get-tuple-element.174.x_ref.left_ref, bf16[1024,3584]{1,0:T(8,128)(2,1)} %get-tuple-element.160.x_ref.right_ref, bf16[256,2048]{1,0:T(8,128)(2,1)} %reduce-scatter.3.cloned.1.call-done.refs_0_), custom_call_target="tpu_custom_call" | custom-call | flops 4294967296 | bytes 10485760 | tf_op jit(solution)/shard_map/grads/pallas_call | solution.py:314
  278.4 7.2 %grads.8 = bf16[1024,1536]{1,0:T(8,128)(2,1)} custom-call(s32[1]{0:T(128)} %bitcast.2.f_ref, bf16[1024,2048]{1,0:T(8,128)(2,1)} %get-tuple-element.174.x_ref.left_ref, bf16[1024,3584]{1,0:T(8,128)(2,1)} %get-tuple-element.160.x_ref.right_ref), custom_call_target="tpu_custom_call" | custom-call | flops 3221225472 | bytes 8388608 | tf_op jit(solution)/shard_map/grads/pallas_call | solution.py:314
  285.6 3.8 add_convert_fusion.3
  293.7 7.2 %grads.9 = bf16[1024,1536]{1,0:T(8,128)(2,1)} custom-call(s32[1]{0:T(128)} %bitcast.2.f_ref, bf16[1024,2048]{1,0:T(8,128)(2,1)} %get-tuple-element.174.x_ref.left_ref, bf16[1024,3584]{1,0:T(8,128)(2,1)} %get-tuple-element.160.x_ref.right_ref), custom_call_target="tpu_custom_call" | custom-call | flops 3221225472 | bytes 8388608 | tf_op jit(solution)/shard_map/grads/pallas_call | solution.py:314
  300.9 20.0 %collective-permute-done.25 = bf16[320,2048]{1,0:T(8,128)(2,1)} collective-permute-done((bf16[320,2048]{1,0:T(8,128)(2,1)S(1)}, bf16[320,2048]{1,0:T(8,128)(2,1)}, u32[]{:S(2)}, u32[]{:S(2)}) %collective-permute-start.25) | collective-permute-done | bytes 1310752 | tf_op jit(solution)/shard_map/ppermute | solution.py:597
  320.9 2.3 collective-permute-done.26
  323.2 3.5 add_convert_fusion.1
  326.8 2.4 add_convert_fusion.14
  331.6 4.0 collective-permute-start.30
  335.6 6.9 %collective-permute-done.27 = bf16[128,2048]{1,0:T(8,128)(2,1)} collective-permute-done((bf16[128,2048]{1,0:T(8,128)(2,1)S(1)}, bf16[128,2048]{1,0:T(8,128)(2,1)}, u32[]{:S(2)}, u32[]{:S(2)}) %collective-permute-start.27) | collective-permute-done | bytes 524320 | tf_op jit(solution)/shard_map/ppermute | solution.py:597
  343.7 2.8 convert_element_type.282
  346.5 4.7 add_convert_fusion.11
  357.0 2.1 multiply_add_fusion
  359.0 6.2 %collective-permute-done.29.refs_1_ = bf16[320,2048]{1,0:T(8,128)(2,1)} collective-permute-done((bf16[320,2048]{1,0:T(8,128)(2,1)S(1)}, bf16[320,2048]{1,0:T(8,128)(2,1)}, u32[]{:S(2)}, u32[]{:S(2)}) %collective-permute-start.29) | collective-permute-done | bytes 1310752 | tf_op jit(solution)/shard_map/ppermute | solution.py:588
  365.2 24.4 %collective-permute-done.30.refs_3_ = bf16[320,2048]{1,0:T(8,128)(2,1)} collective-permute-done((bf16[320,2048]{1,0:T(8,128)(2,1)S(1)}, bf16[320,2048]{1,0:T(8,128)(2,1)}, u32[]{:S(2)}, u32[]{:S(2)}) %collective-permute-start.30) | collective-permute-done | bytes 1310752 | tf_op jit(solution)/shard_map/ppermute | solution.py:588
  393.8 2.2 add_convert_fusion.9
  398.0 1.9 collective-permute-start.35
  402.5 21.1 %collective-permute-done.36.refs_2_ = bf16[320,2048]{1,0:T(8,128)(2,1)} collective-permute-done((bf16[320,2048]{1,0:T(8,128)(2,1)}, bf16[320,2048]{1,0:T(8,128)(2,1)}, u32[]{:S(2)}, u32[]{:S(2)}) %collective-permute-start.36) | collective-permute-done | bytes 1310752 | tf_op jit(solution)/shard_map/ppermute | solution.py:588
  430.4 7.6 %join_rows.1 = f32[1280,2048]{1,0:T(8,128)} custom-call(s32[8]{0:T(128)} %stack.71.at_ref, bf16[320,2048]{1,0:T(8,128)(2,1)} %copy-done.5, bf16[320,2048]{1,0:T(8,128)(2,1)} %collective-permute-done.29.refs_1_, bf16[320,2048]{1,0:T(8,128)(2,1)} %collective-permute-done.36.refs_2_, bf16[320,2048]{1,0:T(8,128)(2,1)} %collective-permute-done.30.refs_3_), custom_call_target="tpu_custom_call" | custom-call | bytes 15728640 | tf_op jit(solution)/shard_map/join_rows/pallas_call | solution.py:569
  438.1 8.0 %collective-permute-done.34.refs_1_ = bf16[256,2048]{1,0:T(8,128)(2,1)} collective-permute-done((bf16[256,2048]{1,0:T(8,128)(2,1)S(1)}, bf16[256,2048]{1,0:T(8,128)(2,1)}, u32[]{:S(2)}, u32[]{:S(2)}) %collective-permute-start.34) | collective-permute-done | bytes 1048608 | tf_op jit(solution)/shard_map/ppermute | solution.py:588
  446.0 19.8 %collective-permute-done.35.refs_3_ = bf16[256,2048]{1,0:T(8,128)(2,1)} collective-permute-done((bf16[256,2048]{1,0:T(8,128)(2,1)S(1)}, bf16[256,2048]{1,0:T(8,128)(2,1)}, u32[]{:S(2)}, u32[]{:S(2)}) %collective-permute-start.35) | collective-permute-done | bytes 1048608 | tf_op jit(solution)/shard_map/ppermute | solution.py:588
  466.5 2.2 add_convert_fusion.17
  469.4 3.2 collective-permute-start.43
  474.0 3.2 collective-permute-done.45
  477.2 17.0 %collective-permute-done.44.refs_2_ = bf16[256,2048]{1,0:T(8,128)(2,1)S(1)} collective-permute-done((bf16[256,2048]{1,0:T(8,128)(2,1)}, bf16[256,2048]{1,0:T(8,128)(2,1)S(1)}, u32[]{:S(2)}, u32[]{:S(2)}) %collective-permute-start.44) | collective-permute-done | bytes 1048608 | tf_op jit(solution)/shard_map/ppermute | solution.py:588
  494.8 3.8 collective-permute-done.46
  498.8 5.5 spread_columns.2.refs_4_
  504.3 6.7 %collective-permute-done.42.refs_1_ = bf16[256,1536]{1,0:T(8,128)(2,1)} collective-permute-done((bf16[256,1536]{1,0:T(8,128)(2,1)S(1)}, bf16[256,1536]{1,0:T(8,128)(2,1)}, u32[]{:S(2)}, u32[]{:S(2)}) %collective-permute-start.42) | collective-permute-done | bytes 786464 | tf_op jit(solution)/shard_map/ppermute | solution.py:588
  511.0 15.8 %collective-permute-done.43.refs_3_ = bf16[256,1536]{1,0:T(8,128)(2,1)S(1)} collective-permute-done((bf16[256,1536]{1,0:T(8,128)(2,1)S(1)}, bf16[256,1536]{1,0:T(8,128)(2,1)S(1)}, u32[]{:S(2)}, u32[]{:S(2)}) %collective-permute-start.43) | collective-permute-done | bytes 786464 | tf_op jit(solution)/shard_map/ppermute | solution.py:588
  531.3 21.1 %collective-permute-done.49 = f32[20480]{0:T(1024)S(1)} collective-permute-done((f32[20480]{0:T(1024)S(1)}, f32[20480]{0:T(1024)S(1)}, u32[]{:S(2)}, u32[]{:S(2)}) %collective-permute-start.49) | collective-permute-done | bytes 81952 | tf_op jit(solution)/shard_map/ppermute | solution.py:597
  552.5 4.5 spread_columns.3
  (258 shorter events, 83.1 us)
Async XLA Ops:
  7.2 165.6 %all-gather.2.cloned.1.call-start = ((), (), s32[]{:S(2)}) async-start(), calls=%async_computation.3 | async-start | bytes 5242880 | tf_op jit(solution)/shard_map/all_gather | solution.py:866
  10.9 29.4 %collective-permute-start = (bf16[256,2048]{1,0:T(8,128)(2,1)}, bf16[256,2048]{1,0:T(8,128)(2,1)}, u32[]{:S(2)}, u32[]{:S(2)}) collective-permute-start(bf16[256,2048]{1,0:T(8,128)(2,1)} %get-tuple-element.128.refs_0_), channel_id=1, source_target_pairs={{0,8},{8,16},{16,24},{24,0},{1,9},{9,17},{17,25},{25,1},{2,10},{10... | collective-permute-start | bytes 3145736 | tf_op jit(solution)/shard_map/ppermute | solution.py:588
  13.9 47.4 %collective-permute-start.1 = (bf16[256,2048]{1,0:T(8,128)(2,1)}, bf16[256,2048]{1,0:T(8,128)(2,1)}, u32[]{:S(2)}, u32[]{:S(2)}) collective-permute-start(bf16[256,2048]{1,0:T(8,128)(2,1)} %get-tuple-element.128.refs_0_), channel_id=1, source_target_pairs={{0,24},{8,0},{16,8},{24,16},{1,25},{9,1},{17,9},{25,17},{2,26},{10... | collective-permute-start | bytes 3145736 | tf_op jit(solution)/shard_map/ppermute | solution.py:588
  20.4 41.8 %collective-permute-start.3 = (bf16[256,3584]{1,0:T(8,128)(2,1)}, bf16[256,3584]{1,0:T(8,128)(2,1)}, u32[]{:S(2)}, u32[]{:S(2)}) collective-permute-start(bf16[256,3584]{1,0:T(8,128)(2,1)} %pick_columns.1.refs_4_.refs_0_), channel_id=1, source_target_pairs={{0,2},{1,3},{2,0},{3,1},{4,6},{5,7},{6,4},{7,5},{8,10},{9,11},{10,... | collective-permute-start | bytes 5505032 | tf_op jit(solution)/shard_map/ppermute | solution.py:597
  22.0 41.3 %collective-permute-start.4 = (bf16[256,3584]{1,0:T(8,128)(2,1)}, bf16[256,3584]{1,0:T(8,128)(2,1)}, u32[]{:S(2)}, u32[]{:S(2)}) collective-permute-start(bf16[256,3584]{1,0:T(8,128)(2,1)} %pick_columns.1.refs_4_.refs_0_), channel_id=1, source_target_pairs={{0,4},{1,5},{2,6},{3,7},{4,0},{5,1},{6,2},{7,3},{8,12},{9,13},{10,... | collective-permute-start | bytes 5505032 | tf_op jit(solution)/shard_map/ppermute | solution.py:597
  23.5 39.8 %collective-permute-start.5 = (bf16[256,3584]{1,0:T(8,128)(2,1)}, bf16[256,3584]{1,0:T(8,128)(2,1)}, u32[]{:S(2)}, u32[]{:S(2)}) collective-permute-start(bf16[256,3584]{1,0:T(8,128)(2,1)} %pick_columns.1.refs_4_.refs_0_), channel_id=1, source_target_pairs={{0,1},{1,0},{2,3},{3,2},{4,5},{5,4},{6,7},{7,6},{8,9},{9,8},{10,11... | collective-permute-start | bytes 5505032 | tf_op jit(solution)/shard_map/ppermute | solution.py:597
  63.4 27.6 %collective-permute-start.8 = (bf16[256,3584]{1,0:T(8,128)(2,1)}, bf16[256,3584]{1,0:T(8,128)(2,1)S(1)}, u32[]{:S(2)}, u32[]{:S(2)}) collective-permute-start(bf16[256,3584]{1,0:T(8,128)(2,1)} %collective-permute-done.3.refs_5_.refs_1_), channel_id=1, source_target_pairs={{0,1},{1,0},{2,3},{3,2},{4,5},{5,4},{6,7},{7,6},{8,9},{9,8},{10,11... | collective-permute-start | bytes 5505032 | tf_op jit(solution)/shard_map/ppermute | solution.py:597
  63.4 28.6 %collective-permute-start.9 = (bf16[256,3584]{1,0:T(8,128)(2,1)}, bf16[256,3584]{1,0:T(8,128)(2,1)}, u32[]{:S(2)}, u32[]{:S(2)}) collective-permute-start(bf16[256,3584]{1,0:T(8,128)(2,1)} %collective-permute-done.4.refs_6_.refs_2_), channel_id=1, source_target_pairs={{0,1},{1,0},{2,3},{3,2},{4,5},{5,4},{6,7},{7,6},{8,9},{9,8},{10,11... | collective-permute-start | bytes 5505032 | tf_op jit(solution)/shard_map/ppermute | solution.py:597
  63.9 27.1 %collective-permute-start.2 = (bf16[256,2048]{1,0:T(8,128)(2,1)}, bf16[256,2048]{1,0:T(8,128)(2,1)S(1)}, u32[]{:S(2)}, u32[]{:S(2)}) collective-permute-start(bf16[256,2048]{1,0:T(8,128)(2,1)} %collective-permute-done.refs_1_), channel_id=1, source_target_pairs={{0,8},{8,16},{16,24},{24,0},{1,9},{9,17},{17,25},{25,1},{2,10},{10... | collective-permute-start | bytes 3145736 | tf_op jit(solution)/shard_map/ppermute | solution.py:588
  66.4 24.6 %collective-permute-start.6 = (bf16[128,3584]{1,0:T(8,128)(2,1)S(1)}, bf16[128,3584]{1,0:T(8,128)(2,1)S(1)}, u32[]{:S(2)}, u32[]{:S(2)}) collective-permute-start(bf16[128,3584]{1,0:T(8,128)(2,1)S(1)} %slice.575), channel_id=1, source_target_pairs={{0,4},{1,5},{2,6},{3,7},{4,0},{5,1},{6,2},{7,3},{8,12},{9,13},{10,... | collective-permute-start | bytes 2752520 | tf_op jit(solution)/shard_map/ppermute | solution.py:597
  68.0 23.0 %collective-permute-start.7 = (bf16[128,3584]{1,0:T(8,128)(2,1)S(1)}, bf16[128,3584]{1,0:T(8,128)(2,1)S(1)}, u32[]{:S(2)}, u32[]{:S(2)}) collective-permute-start(bf16[128,3584]{1,0:T(8,128)(2,1)S(1)} %slice.576), channel_id=1, source_target_pairs={{0,2},{1,3},{2,0},{3,1},{4,6},{5,7},{6,4},{7,5},{8,10},{9,11},{10,... | collective-permute-start | bytes 2752520 | tf_op jit(solution)/shard_map/ppermute | solution.py:597
  92.6 177.2 %reduce-scatter.3.cloned.1.call-start = ((), (), s32[]{:S(2)}) async-start(), calls=%async_computation.2 | async-start | bytes 5242880 | tf_op jit(solution)/shard_map/reduce_scatter | solution.py:905
  97.2 30.8 %collective-permute-start.12 = (bf16[320,2048]{1,0:T(8,128)(2,1)S(1)}, bf16[320,2048]{1,0:T(8,128)(2,1)S(1)}, u32[]{:S(2)}, u32[]{:S(2)}) collective-permute-start(bf16[320,2048]{1,0:T(8,128)(2,1)S(1)} %maximum_select_fusion.refs_0_), channel_id=1, source_target_pairs={{0,2},{1,3},{2,0},{3,1},{4,6},{5,7},{6,4},{7,5},{8,10},{9,11},{10,... | collective-permute-start | bytes 3932168 | tf_op jit(solution)/shard_map/ppermute | solution.py:597
  97.7 30.5 %collective-permute-start.13 = (bf16[320,2048]{1,0:T(8,128)(2,1)S(1)}, bf16[320,2048]{1,0:T(8,128)(2,1)S(1)}, u32[]{:S(2)}, u32[]{:S(2)}) collective-permute-start(bf16[320,2048]{1,0:T(8,128)(2,1)S(1)} %maximum_select_fusion.refs_0_), channel_id=1, source_target_pairs={{0,4},{1,5},{2,6},{3,7},{4,0},{5,1},{6,2},{7,3},{8,12},{9,13},{10,... | collective-permute-start | bytes 3932168 | tf_op jit(solution)/shard_map/ppermute | solution.py:597
  99.2 29.0 %collective-permute-start.14 = (bf16[320,2048]{1,0:T(8,128)(2,1)S(1)}, bf16[320,2048]{1,0:T(8,128)(2,1)}, u32[]{:S(2)}, u32[]{:S(2)}) collective-permute-start(bf16[320,2048]{1,0:T(8,128)(2,1)S(1)} %maximum_select_fusion.refs_0_), channel_id=1, source_target_pairs={{0,1},{1,0},{2,3},{3,2},{4,5},{5,4},{6,7},{7,6},{8,9},{9,8},{10,11... | collective-permute-start | bytes 3932168 | tf_op jit(solution)/shard_map/ppermute | solution.py:597
  128.3 22.1 %collective-permute-start.17 = (bf16[320,2048]{1,0:T(8,128)(2,1)S(1)}, bf16[320,2048]{1,0:T(8,128)(2,1)S(1)}, u32[]{:S(2)}, u32[]{:S(2)}) collective-permute-start(bf16[320,2048]{1,0:T(8,128)(2,1)S(1)} %collective-permute-done.12.refs_1_), channel_id=1, source_target_pairs={{0,1},{1,0},{2,3},{3,2},{4,5},{5,4},{6,7},{7,6},{8,9},{9,8},{10,11... | collective-permute-start | bytes 3932168 | tf_op jit(solution)/shard_map/ppermute | solution.py:597
  128.3 22.2 %collective-permute-start.18 = (bf16[320,2048]{1,0:T(8,128)(2,1)S(1)}, bf16[320,2048]{1,0:T(8,128)(2,1)S(1)}, u32[]{:S(2)}, u32[]{:S(2)}) collective-permute-start(bf16[320,2048]{1,0:T(8,128)(2,1)S(1)} %collective-permute-done.13.refs_2_), channel_id=1, source_target_pairs={{0,1},{1,0},{2,3},{3,2},{4,5},{5,4},{6,7},{7,6},{8,9},{9,8},{10,11... | collective-permute-start | bytes 3932168 | tf_op jit(solution)/shard_map/ppermute | solution.py:597
  128.9 21.5 %collective-permute-start.15 = (bf16[160,2048]{1,0:T(8,128)(2,1)S(1)}, bf16[160,2048]{1,0:T(8,128)(2,1)S(1)}, u32[]{:S(2)}, u32[]{:S(2)}) collective-permute-start(bf16[160,2048]{1,0:T(8,128)(2,1)S(1)} %slice.577), channel_id=1, source_target_pairs={{0,4},{1,5},{2,6},{3,7},{4,0},{5,1},{6,2},{7,3},{8,12},{9,13},{10,... | collective-permute-start | bytes 1966088 | tf_op jit(solution)/shard_map/ppermute | solution.py:597
  130.5 19.9 %collective-permute-start.16 = (bf16[160,2048]{1,0:T(8,128)(2,1)S(1)}, bf16[160,2048]{1,0:T(8,128)(2,1)}, u32[]{:S(2)}, u32[]{:S(2)}) collective-permute-start(bf16[160,2048]{1,0:T(8,128)(2,1)S(1)} %slice.578), channel_id=1, source_target_pairs={{0,2},{1,3},{2,0},{3,1},{4,6},{5,7},{6,4},{7,5},{8,10},{9,11},{10,... | collective-permute-start | bytes 1966088 | tf_op jit(solution)/shard_map/ppermute | solution.py:597
  172.5 171.2 %reduce-scatter.5.cloned.1.call-start = ((), (), s32[]{:S(2)}) async-start(), calls=%async_computation.4 | async-start | bytes 5242880 | tf_op jit(solution)/shard_map/reduce_scatter | solution.py:905
  257.2 9.0 %collective-permute-start.21 = (bf16[1280,2048]{1,0:T(8,128)(2,1)}, bf16[1280,2048]{1,0:T(8,128)(2,1)}, u32[]{:S(2)}, u32[]{:S(2)}) collective-permute-start(bf16[1280,2048]{1,0:T(8,128)(2,1)} %get-tuple-element.165), channel_id=1, source_target_pairs={{0,1},{1,0},{2,3},{3,2},{4,5},{5,4},{6,7},{7,6},{8,9},{9,8},{10,11... | collective-permute-start | bytes 15728648 | tf_op jit(solution)/shard_map/ppermute | solution.py:597
  268.4 17.2 %collective-permute-start.22 = (bf16[160,2048]{1,0:T(8,128)(2,1)S(1)}, bf16[160,2048]{1,0:T(8,128)(2,1)S(1)}, u32[]{:S(2)}, u32[]{:S(2)}) collective-permute-start(bf16[160,2048]{1,0:T(8,128)(2,1)S(1)} %get-tuple-element.263), channel_id=1, source_target_pairs={{0,4},{1,5},{2,6},{3,7},{4,0},{5,1},{6,2},{7,3},{8,12},{9,13},{10,... | collective-permute-start | bytes 1966088 | tf_op jit(solution)/shard_map/ppermute | solution.py:597
  269.0 16.6 %collective-permute-start.23 = (bf16[160,2048]{1,0:T(8,128)(2,1)S(1)}, bf16[160,2048]{1,0:T(8,128)(2,1)S(1)}, u32[]{:S(2)}, u32[]{:S(2)}) collective-permute-start(bf16[160,2048]{1,0:T(8,128)(2,1)S(1)} %get-tuple-element.262), channel_id=1, source_target_pairs={{0,2},{1,3},{2,0},{3,1},{4,6},{5,7},{6,4},{7,5},{8,10},{9,11},{10,... | collective-permute-start | bytes 1966088 | tf_op jit(solution)/shard_map/ppermute | solution.py:597
  285.6 41.2 %collective-permute-start.24 = (bf16[1024,2048]{1,0:T(8,128)(2,1)}, bf16[1024,2048]{1,0:T(8,128)(2,1)}, u32[]{:S(2)}, u32[]{:S(2)}) collective-permute-start(bf16[1024,2048]{1,0:T(8,128)(2,1)} %grads.6), channel_id=1, source_target_pairs={{0,1},{1,0},{2,3},{3,2},{4,5},{5,4},{6,7},{7,6},{8,9},{9,8},{10,11... | collective-permute-start | bytes 12582920 | tf_op jit(solution)/shard_map/ppermute | solution.py:597
  289.6 31.4 %collective-permute-start.25 = (bf16[320,2048]{1,0:T(8,128)(2,1)S(1)}, bf16[320,2048]{1,0:T(8,128)(2,1)}, u32[]{:S(2)}, u32[]{:S(2)}) collective-permute-start(bf16[320,2048]{1,0:T(8,128)(2,1)S(1)} %pad_maximum_fusion), channel_id=1, source_target_pairs={{0,2},{1,3},{2,0},{3,1},{4,6},{5,7},{6,4},{7,5},{8,10},{9,11},{10,... | collective-permute-start | bytes 3932168 | tf_op jit(solution)/shard_map/ppermute | solution.py:597
  292.0 31.2 %collective-permute-start.26 = (bf16[320,2048]{1,0:T(8,128)(2,1)}, bf16[320,2048]{1,0:T(8,128)(2,1)}, u32[]{:S(2)}, u32[]{:S(2)}) collective-permute-start(bf16[320,2048]{1,0:T(8,128)(2,1)} %pad_maximum_fusion.1), channel_id=1, source_target_pairs={{0,4},{1,5},{2,6},{3,7},{4,0},{5,1},{6,2},{7,3},{8,12},{9,13},{10,... | collective-permute-start | bytes 3932168 | tf_op jit(solution)/shard_map/ppermute | solution.py:597
  329.2 13.4 %collective-permute-start.27 = (bf16[128,2048]{1,0:T(8,128)(2,1)S(1)}, bf16[128,2048]{1,0:T(8,128)(2,1)}, u32[]{:S(2)}, u32[]{:S(2)}) collective-permute-start(bf16[128,2048]{1,0:T(8,128)(2,1)S(1)} %get-tuple-element.269), channel_id=1, source_target_pairs={{0,4},{1,5},{2,6},{3,7},{4,0},{5,1},{6,2},{7,3},{8,12},{9,13},{10,... | collective-permute-start | bytes 1572872 | tf_op jit(solution)/shard_map/ppermute | solution.py:597
  330.7 13.0 %collective-permute-start.28 = (bf16[128,2048]{1,0:T(8,128)(2,1)S(1)}, bf16[128,2048]{1,0:T(8,128)(2,1)}, u32[]{:S(2)}, u32[]{:S(2)}) collective-permute-start(bf16[128,2048]{1,0:T(8,128)(2,1)S(1)} %get-tuple-element.268), channel_id=1, source_target_pairs={{0,2},{1,3},{2,0},{3,1},{4,6},{5,7},{6,4},{7,5},{8,10},{9,11},{10,... | collective-permute-start | bytes 1572872 | tf_op jit(solution)/shard_map/ppermute | solution.py:597
  331.5 33.7 %collective-permute-start.29 = (bf16[320,2048]{1,0:T(8,128)(2,1)S(1)}, bf16[320,2048]{1,0:T(8,128)(2,1)}, u32[]{:S(2)}, u32[]{:S(2)}) collective-permute-start(bf16[320,2048]{1,0:T(8,128)(2,1)S(1)} %pad_maximum_fusion.2.refs_0_), channel_id=1, source_target_pairs={{0,8},{8,16},{16,24},{24,0},{1,9},{9,17},{17,25},{25,1},{2,10},{10... | collective-permute-start | bytes 3932168 | tf_op jit(solution)/shard_map/ppermute | solution.py:588
  331.6 58.0 %collective-permute-start.30 = (bf16[320,2048]{1,0:T(8,128)(2,1)S(1)}, bf16[320,2048]{1,0:T(8,128)(2,1)}, u32[]{:S(2)}, u32[]{:S(2)}) collective-permute-start(bf16[320,2048]{1,0:T(8,128)(2,1)S(1)} %pad_maximum_fusion.2.refs_0_), channel_id=1, source_target_pairs={{0,24},{8,0},{16,8},{24,16},{1,25},{9,1},{17,9},{25,17},{2,26},{10... | collective-permute-start | bytes 3932168 | tf_op jit(solution)/shard_map/ppermute | solution.py:588
  335.6 54.0 %collective-permute-start.33 = (bf16[1024,1536]{1,0:T(8,128)(2,1)}, bf16[1024,1536]{1,0:T(8,128)(2,1)}, u32[]{:S(2)}, u32[]{:S(2)}) collective-permute-start(bf16[1024,1536]{1,0:T(8,128)(2,1)} %grads.8), channel_id=1, source_target_pairs={{0,1},{1,0},{2,3},{3,2},{4,5},{5,4},{6,7},{7,6},{8,9},{9,8},{10,11... | collective-permute-start | bytes 9437192 | tf_op jit(solution)/shard_map/ppermute | solution.py:597
  352.9 36.7 %collective-permute-start.31 = (bf16[256,2048]{1,0:T(8,128)(2,1)S(1)}, bf16[256,2048]{1,0:T(8,128)(2,1)S(1)}, u32[]{:S(2)}, u32[]{:S(2)}) collective-permute-start(bf16[256,2048]{1,0:T(8,128)(2,1)S(1)} %pad_maximum_fusion.3), channel_id=1, source_target_pairs={{0,2},{1,3},{2,0},{3,1},{4,6},{5,7},{6,4},{7,5},{8,10},{9,11},{10,... | collective-permute-start | bytes 3145736 | tf_op jit(solution)/shard_map/ppermute | solution.py:597
  353.8 35.8 %collective-permute-start.32 = (bf16[256,2048]{1,0:T(8,128)(2,1)S(1)}, bf16[256,2048]{1,0:T(8,128)(2,1)S(1)}, u32[]{:S(2)}, u32[]{:S(2)}) collective-permute-start(bf16[256,2048]{1,0:T(8,128)(2,1)S(1)} %pad_maximum_fusion.4), channel_id=1, source_target_pairs={{0,4},{1,5},{2,6},{3,7},{4,0},{5,1},{6,2},{7,3},{8,12},{9,13},{10,... | collective-permute-start | bytes 3145736 | tf_op jit(solution)/shard_map/ppermute | solution.py:597
  389.6 34.0 %collective-permute-start.36 = (bf16[320,2048]{1,0:T(8,128)(2,1)}, bf16[320,2048]{1,0:T(8,128)(2,1)}, u32[]{:S(2)}, u32[]{:S(2)}) collective-permute-start(bf16[320,2048]{1,0:T(8,128)(2,1)} %collective-permute-done.29.refs_1_), channel_id=1, source_target_pairs={{0,8},{8,16},{16,24},{24,0},{1,9},{9,17},{17,25},{25,1},{2,10},{10... | collective-permute-start | bytes 3932168 | tf_op jit(solution)/shard_map/ppermute | solution.py:588
  391.5 9.5 %collective-permute-start.37 = (bf16[128,1536]{1,0:T(8,128)(2,1)S(1)}, bf16[128,1536]{1,0:T(8,128)(2,1)S(1)}, u32[]{:S(2)}, u32[]{:S(2)}) collective-permute-start(bf16[128,1536]{1,0:T(8,128)(2,1)S(1)} %get-tuple-element.277), channel_id=1, source_target_pairs={{0,4},{1,5},{2,6},{3,7},{4,0},{5,1},{6,2},{7,3},{8,12},{9,13},{10,... | collective-permute-start | bytes 1179656 | tf_op jit(solution)/shard_map/ppermute | solution.py:597
  393.0 9.5 %collective-permute-start.38 = (bf16[128,1536]{1,0:T(8,128)(2,1)S(1)}, bf16[128,1536]{1,0:T(8,128)(2,1)S(1)}, u32[]{:S(2)}, u32[]{:S(2)}) collective-permute-start(bf16[128,1536]{1,0:T(8,128)(2,1)S(1)} %get-tuple-element.276), channel_id=1, source_target_pairs={{0,2},{1,3},{2,0},{3,1},{4,6},{5,7},{6,4},{7,5},{8,10},{9,11},{10,... | collective-permute-start | bytes 1179656 | tf_op jit(solution)/shard_map/ppermute | solution.py:597
  396.1 50.0 %collective-permute-start.34 = (bf16[256,2048]{1,0:T(8,128)(2,1)S(1)}, bf16[256,2048]{1,0:T(8,128)(2,1)}, u32[]{:S(2)}, u32[]{:S(2)}) collective-permute-start(bf16[256,2048]{1,0:T(8,128)(2,1)S(1)} %pad_maximum_fusion.5.refs_0_), channel_id=1, source_target_pairs={{0,8},{8,16},{16,24},{24,0},{1,9},{9,17},{17,25},{25,1},{2,10},{10... | collective-permute-start | bytes 3145736 | tf_op jit(solution)/shard_map/ppermute | solution.py:588
  398.0 67.8 %collective-permute-start.35 = (bf16[256,2048]{1,0:T(8,128)(2,1)S(1)}, bf16[256,2048]{1,0:T(8,128)(2,1)}, u32[]{:S(2)}, u32[]{:S(2)}) collective-permute-start(bf16[256,2048]{1,0:T(8,128)(2,1)S(1)} %pad_maximum_fusion.5.refs_0_), channel_id=1, source_target_pairs={{0,24},{8,0},{16,8},{24,16},{1,25},{9,1},{17,9},{25,17},{2,26},{10... | collective-permute-start | bytes 3145736 | tf_op jit(solution)/shard_map/ppermute | solution.py:588
  426.5 39.4 %collective-permute-start.39 = (bf16[256,1536]{1,0:T(8,128)(2,1)}, bf16[256,1536]{1,0:T(8,128)(2,1)}, u32[]{:S(2)}, u32[]{:S(2)}) collective-permute-start(bf16[256,1536]{1,0:T(8,128)(2,1)} %pad_maximum_fusion.6), channel_id=1, source_target_pairs={{0,2},{1,3},{2,0},{3,1},{4,6},{5,7},{6,4},{7,5},{8,10},{9,11},{10,... | collective-permute-start | bytes 2359304 | tf_op jit(solution)/shard_map/ppermute | solution.py:597
  428.7 37.2 %collective-permute-start.40 = (bf16[256,1536]{1,0:T(8,128)(2,1)}, bf16[256,1536]{1,0:T(8,128)(2,1)}, u32[]{:S(2)}, u32[]{:S(2)}) collective-permute-start(bf16[256,1536]{1,0:T(8,128)(2,1)} %pad_maximum_fusion.7), channel_id=1, source_target_pairs={{0,4},{1,5},{2,6},{3,7},{4,0},{5,1},{6,2},{7,3},{8,12},{9,13},{10,... | collective-permute-start | bytes 2359304 | tf_op jit(solution)/shard_map/ppermute | solution.py:597
  429.6 36.2 %collective-permute-start.41 = (f32[20480]{0:T(1024)S(1)}, f32[20480]{0:T(1024)S(1)}, u32[]{:S(2)}, u32[]{:S(2)}) collective-permute-start(f32[20480]{0:T(1024)S(1)} %concatenate.101), channel_id=1, source_target_pairs={{0,1},{1,0},{2,3},{3,2},{4,5},{5,4},{6,7},{7,6},{8,9},{9,8},{10,11... | collective-permute-start | bytes 245768 | tf_op jit(solution)/shard_map/ppermute | solution.py:597
  465.9 28.3 %collective-permute-start.44 = (bf16[256,2048]{1,0:T(8,128)(2,1)}, bf16[256,2048]{1,0:T(8,128)(2,1)S(1)}, u32[]{:S(2)}, u32[]{:S(2)}) collective-permute-start(bf16[256,2048]{1,0:T(8,128)(2,1)} %collective-permute-done.34.refs_1_), channel_id=1, source_target_pairs={{0,8},{8,16},{16,24},{24,0},{1,9},{9,17},{17,25},{25,1},{2,10},{10... | collective-permute-start | bytes 3145736 | tf_op jit(solution)/shard_map/ppermute | solution.py:588
  468.8 42.2 %collective-permute-start.42 = (bf16[256,1536]{1,0:T(8,128)(2,1)S(1)}, bf16[256,1536]{1,0:T(8,128)(2,1)}, u32[]{:S(2)}, u32[]{:S(2)}) collective-permute-start(bf16[256,1536]{1,0:T(8,128)(2,1)S(1)} %pad_maximum_fusion.8.refs_0_), channel_id=1, source_target_pairs={{0,8},{8,16},{16,24},{24,0},{1,9},{9,17},{17,25},{25,1},{2,10},{10... | collective-permute-start | bytes 2359304 | tf_op jit(solution)/shard_map/ppermute | solution.py:588
  469.4 57.3 %collective-permute-start.43 = (bf16[256,1536]{1,0:T(8,128)(2,1)S(1)}, bf16[256,1536]{1,0:T(8,128)(2,1)S(1)}, u32[]{:S(2)}, u32[]{:S(2)}) collective-permute-start(bf16[256,1536]{1,0:T(8,128)(2,1)S(1)} %pad_maximum_fusion.8.refs_0_), channel_id=1, source_target_pairs={{0,24},{8,0},{16,8},{24,16},{1,25},{9,1},{17,9},{25,17},{2,26},{10... | collective-permute-start | bytes 2359304 | tf_op jit(solution)/shard_map/ppermute | solution.py:588
  472.7 4.5 collective-permute-start.45
  498.7 29.7 %collective-permute-start.47 = (f32[20480]{0:T(1024)S(1)}, f32[20480]{0:T(1024)S(1)}, u32[]{:S(2)}, u32[]{:S(2)}) collective-permute-start(f32[20480]{0:T(1024)S(1)} %add.384), channel_id=1, source_target_pairs={{0,8},{8,0},{16,24},{24,16},{1,9},{9,1},{17,25},{25,17},{2,10},{10... | collective-permute-start | bytes 245768 | tf_op jit(solution)/shard_map/ppermute | solution.py:597
  528.4 24.0 %collective-permute-start.48 = (bf16[256,1536]{1,0:T(8,128)(2,1)}, bf16[256,1536]{1,0:T(8,128)(2,1)}, u32[]{:S(2)}, u32[]{:S(2)}) collective-permute-start(bf16[256,1536]{1,0:T(8,128)(2,1)} %collective-permute-done.42.refs_1_), channel_id=1, source_target_pairs={{0,8},{8,16},{16,24},{24,0},{1,9},{9,17},{17,25},{25,1},{2,10},{10... | collective-permute-start | bytes 2359304 | tf_op jit(solution)/shard_map/ppermute | solution.py:588
  528.4 24.0 %collective-permute-start.49 = (f32[20480]{0:T(1024)S(1)}, f32[20480]{0:T(1024)S(1)}, u32[]{:S(2)}, u32[]{:S(2)}) collective-permute-start(f32[20480]{0:T(1024)S(1)} %add.385), channel_id=1, source_target_pairs={{0,16},{8,24},{16,0},{24,8},{1,17},{9,25},{17,1},{25,9},{2,18},{10... | collective-permute-start | bytes 245768 | tf_op jit(solution)/shard_map/ppermute | solution.py:597
  (44 other events, 395.1 us)
Sparse Core Ops, SparseCore 0:
  92.7 78.3 all-gather.1
  173.4 75.2 reduce-scatter.2
  257.5 74.3 reduce-scatter.4

commit v9 on v8

--- a/solution.py
+++ b/solution.py
@@ -915,20 +915,19 @@
         q_b, k_b, v_b, cat_b, line.tied(d_att), lse, tables, d_proj, n_heads
     )
     line.wait(d_proj)
-    norm_part = norm_back(line.tied(d_proj), w_in_all, slots, blk_size)
-    line.wait(norm_part)
-    norm_sum = ctx_sum(norm_part)
-
     half = D // 2
     out_own, pre_own, qkv_own = [], [], []
     out_parts, pre_parts, qkv_parts = {}, {}, {}
     away, home = grads(line.tied(cat_b), 0, cat_rows // n_ctx, dy, 0, D, f, n_fsdp)
     line.wait(away)
     out_scatter = Move(line, scatter_job(line.tied(away), home, out_own)) if even else None
+    norm_part = norm_back(line.tied(d_proj), w_in_all, slots, blk_size)
+    line.wait(norm_part)
+    norm_sum = ctx_sum(norm_part)
+    if even:
+        out_scatter.step()
     (pre_away,) = grads(line.tied(normed), 1, half, d_proj, wide_q, wide_m, f)
     line.wait(pre_away)
-    if even:
-        out_scatter.step()
     (pre_home,) = grads(line.tied(normed), 0, half, d_proj, wide_q, wide_m, f, late=(out_sum,))
     line.wait(pre_home)
     (qkv_away,) = grads(line.tied(normed), 1, half, d_proj, 0, wide_q, f)

time: 573 us -> 573 us (level)
  no operation moved by 1% of the time
where the time goes in v9:
time: 573 us; the launch traced here: 567 us
  waiting for transfers between devices  236 us (41%)
  Pallas kernels  207 us (36%)
  starting transfers between devices  46.5 us (8%)
  other arithmetic  43.3 us (8%)
  local copies, waits for them, and re-layouts  19.3 us (3%)
  between operations  15.1 us (3%)
    ppermute x12, waiting for transfers between devices, pass_on(): return lax.ppermute(x, 'ctx', [(i, (i + hops) % n) for i in range(n)])  165 us
    ppermute x38, waiting for transfers between devices, swap(): return lax.ppermute(x, axis, [(i, i ^ bit) for i in range(n)])  70.5 us
    pallas_call x5, Pallas kernels, grads(): pl.pallas_call(functools.partial(grads_kernel, n_split, len(late)), grid_...  49 us
    ppermute x38, starting transfers between devices, swap(): return lax.ppermute(x, axis, [(i, i ^ bit) for i in range(n)])  28.1 us
    pallas_call x1, Pallas kernels, attention_back(): pl.pallas_call(functools.partial(back_kernel, pairs), grid=(pairs,), in_s...  22.7 us
    pallas_call x1, Pallas kernels, norm_back(): pl.pallas_call(functools.partial(norm_kernel_back, blk_size), grid_spec=p...  22.4 us
    pallas_call x1, Pallas kernels, d_cat_parts(): pl.pallas_call(functools.partial(d_cat_kernel, cuts), grid_spec=pltpu.Pre...  22.2 us
    pallas_call x1, Pallas kernels, pre_project(): pl.pallas_call(functools.partial(pre_kernel, w_cuts, n_w), grid_spec=pltp...  18.4 us
  transfers between devices with their start and end apart: 53, of which 31 were waited for; matrix products, arithmetic and copies ran while one was open for 10% of the time, Pallas kernels for 35%

profile of v9, /device:TPU:0, one launch (start us, length us, event | category | flops | bytes accessed | tf_op | source)
XLA Modules:
  0.0 566.7 jit_solution(11828161276680117532)
XLA Ops:
  7.2 3.7 norm.1
  10.9 3.0 collective-permute-start
  13.9 2.1 collective-permute-start.1
  16.0 4.3 pick_columns.1.refs_4_.refs_0_
  40.3 21.0 %collective-permute-done.1.refs_3_ = bf16[256,2048]{1,0:T(8,128)(2,1)} collective-permute-done((bf16[256,2048]{1,0:T(8,128)(2,1)}, bf16[256,2048]{1,0:T(8,128)(2,1)}, u32[]{:S(2)}, u32[]{:S(2)}) %collective-permute-start.1) | collective-permute-done | bytes 1048608 | tf_op jit(solution)/shard_map/ppermute | solution.py:588
  68.6 22.3 %collective-permute-done.2.refs_2_ = bf16[256,2048]{1,0:T(8,128)(2,1)S(1)} collective-permute-done((bf16[256,2048]{1,0:T(8,128)(2,1)}, bf16[256,2048]{1,0:T(8,128)(2,1)S(1)}, u32[]{:S(2)}, u32[]{:S(2)}) %collective-permute-start.2) | collective-permute-done | bytes 1048608 | tf_op jit(solution)/shard_map/ppermute | solution.py:588
  93.6 2.2 collective-permute-done.10.refs_12_.refs_8_
  99.1 13.6 %qkv_project.1 = (f32[1024,1536]{1,0:T(8,128)}, bf16[1024,2048]{1,0:T(8,128)(2,1)}, bf16[2048,3584]{1,0:T(8,128)(2,1)}) custom-call(s32[18]{0:T(128)} %get-tuple-element.353.at_ref, bf16[256,2048]{1,0:T(8,128)(2,1)} %get-tuple-element.128.refs_0_, bf16[256,2048]{1,0:T(8,128)(2,1)} %collective-permute-done.refs_1_, bf16[256,2048]{1,0:T(8,128)(2,1)} %copy-done.34, ...), custom_call_target="tpu_custom_call" | custom-call | flops 6442450944 | bytes 16777216 | tf_op jit(solution)/shard_map/qkv_project/pallas_call | solution.py:377
  112.7 14.8 %attention.1 = (bf16[1024,512]{1,0:T(8,128)(2,1)}, bf16[1024,512]{1,0:T(8,128)(2,1)}, bf16[1024,512]{1,0:T(8,128)(2,1)}, bf16[1024,2560]{1,0:T(8,128)(2,1)}, f32[4,2,1024]{2,1,0:T(2,128)}) custom-call(f32[1024,1536]{1,0:T(8,128)} %get-tuple-element.131.q_ref.k_ref.v_ref, f32[1024,1536]{1,0:T(8,128)} %get-tuple-element.131.q_ref.k_ref.v_ref, ...), custom_call_target="tpu_custom_call" | custom-call | flops 2147483648 | bytes 10485760 | tf_op jit(solution)/shard_map/attention/pallas_call | solution.py:206
  131.9 18.4 %pre_project.1 = (f32[1024,2048]{1,0:T(8,128)}, bf16[1024,2560]{1,0:T(8,128)(2,1)}, bf16[2048,3584]{1,0:T(8,128)(2,1)}) custom-call(s32[10]{0:T(128)} %constant.90.clone.at_ref, bf16[1024,2048]{1,0:T(8,128)(2,1)} %get-tuple-element.174.x_ref.left_ref, bf16[256,3584]{1,0:T(8,128)(2,1)} %pick_columns.1.refs_4_.refs_0_, ...), custom_call_target="tpu_custom_call", output_to_operand_aliasing={{1}: (13, {}), {2}: (14, {})} | custom-call | flops 8589934592 | bytes 25165824 | tf_op jit(solution)/shard_map/pre_project/pallas_call | solution.py:415
  154.6 17.8 %out_project.1 = (bf16[1024,2048]{1,0:T(8,128)(2,1)}, bf16[2560,2048]{1,0:T(8,128)(2,1)}) custom-call(s32[18]{0:T(128)} %get-tuple-element.352.at_ref, bf16[1024,2560]{1,0:T(8,128)(2,1)} %get-tuple-element.160.x_ref.att_ref.left_ref, bf16[320,2048]{1,0:T(8,128)(2,1)} %copy-done.12, bf16[320,2048]{1,0:T(8,128)(2,1)} %copy-done.19, ...), custom_call_target="tpu_custom_call" | custom-call | flops 10737418240 | bytes 22020096 | tf_op jit(solution)/shard_map/out_project/pallas_call | solution.py:458
  172.7 22.2 %d_cat_parts.1 = (bf16[1024,512]{1,0:T(8,128)(2,1)}, bf16[1024,3584]{1,0:T(8,128)(2,1)}, f32[1,2048]{1,0:T(1,128)}, bf16[1024,2048]{1,0:T(8,128)(2,1)}) custom-call(s32[8]{0:T(128)} %broadcast_multiply_fusion.3.at_ref, bf16[1024,2048]{1,0:T(8,128)(2,1)} %all-gather.2.cloned.1.call-done.g_ref, bf16[2560,2048]{1,0:T(8,128)(2,1)} %get-tuple-element.153.w_ref, ...), custom_call_target="tpu_custom_call" | custom-call | flops 10737418240 | bytes 25165824 | tf_op jit(solution)/shard_map/d_cat_parts/pallas_call | solution.py:529
  194.9 22.7 %attention_back.1 = (bf16[1024,3584]{1,0:T(8,128)(2,1)}, f32[1,512]{1,0:T(1,128)}, f32[1,512]{1,0:T(1,128)}, f32[1,512]{1,0:T(1,128)}) custom-call(bf16[1024,512]{1,0:T(8,128)(2,1)} %get-tuple-element.147.q_ref, bf16[1024,512]{1,0:T(8,128)(2,1)} %get-tuple-element.148.k_ref, ...), custom_call_target="tpu_custom_call", output_to_operand_aliasing={{0}: (9, {})} | custom-call | flops 5368709120 | bytes 8388608 | tf_op jit(solution)/shard_map/attention_back/pallas_call | solution.py:276
  217.6 17.5 %grads.5 = (bf16[1280,2048]{1,0:T(8,128)(2,1)}, bf16[1280,2048]{1,0:T(8,128)(2,1)}) custom-call(s32[1]{0:T(128)} %bitcast.2.f_ref, bf16[1024,2560]{1,0:T(8,128)(2,1)} %get-tuple-element.160.x_ref.att_ref.left_ref, bf16[1024,2048]{1,0:T(8,128)(2,1)} %get-tuple-element.161.right_ref), custom_call_target="tpu_custom_call" | custom-call | flops 10737418240 | bytes 19922944 | tf_op jit(solution)/shard_map/grads/pallas_call | solution.py:314
  235.2 22.4 %norm_back.1 = bf16[1024,2048]{1,0:T(8,128)(2,1)} custom-call(s32[8]{0:T(128)} %copy-done.29, bf16[1024,3584]{1,0:T(8,128)(2,1)} %get-tuple-element.164.x_ref.right_ref, bf16[2048,3584]{1,0:T(8,128)(2,1)} %get-tuple-element.165.w_ref), custom_call_target="tpu_custom_call" | custom-call | flops 15032385536 | bytes 28311552 | tf_op jit(solution)/shard_map/norm_back/pallas_call | solution.py:486
  257.6 8.6 %grads.6 = bf16[1024,2048]{1,0:T(8,128)(2,1)} custom-call(s32[1]{0:T(128)} %bitcast.2.f_ref, bf16[1024,2048]{1,0:T(8,128)(2,1)} %get-tuple-element.174.x_ref.left_ref, bf16[1024,3584]{1,0:T(8,128)(2,1)} %get-tuple-element.164.x_ref.right_ref), custom_call_target="tpu_custom_call" | custom-call | flops 4294967296 | bytes 10485760 | tf_op jit(solution)/shard_map/grads/pallas_call | solution.py:314
  266.2 2.1 add_convert_fusion.6
  269.6 8.6 %grads.7 = bf16[1024,2048]{1,0:T(8,128)(2,1)} custom-call(s32[1]{0:T(128)} %bitcast.2.f_ref, bf16[1024,2048]{1,0:T(8,128)(2,1)} %get-tuple-element.174.x_ref.left_ref, bf16[1024,3584]{1,0:T(8,128)(2,1)} %get-tuple-element.164.x_ref.right_ref, bf16[256,2048]{1,0:T(8,128)(2,1)} %reduce-scatter.3.cloned.1.call-done.refs_0_), custom_call_target="tpu_custom_call" | custom-call | flops 4294967296 | bytes 10485760 | tf_op jit(solution)/shard_map/grads/pallas_call | solution.py:314
  278.2 7.2 %grads.8 = bf16[1024,1536]{1,0:T(8,128)(2,1)} custom-call(s32[1]{0:T(128)} %bitcast.2.f_ref, bf16[1024,2048]{1,0:T(8,128)(2,1)} %get-tuple-element.174.x_ref.left_ref, bf16[1024,3584]{1,0:T(8,128)(2,1)} %get-tuple-element.164.x_ref.right_ref), custom_call_target="tpu_custom_call" | custom-call | flops 3221225472 | bytes 8388608 | tf_op jit(solution)/shard_map/grads/pallas_call | solution.py:314
  285.7 3.8 add_convert_fusion.3
  293.7 7.2 %grads.9 = bf16[1024,1536]{1,0:T(8,128)(2,1)} custom-call(s32[1]{0:T(128)} %bitcast.2.f_ref, bf16[1024,2048]{1,0:T(8,128)(2,1)} %get-tuple-element.174.x_ref.left_ref, bf16[1024,3584]{1,0:T(8,128)(2,1)} %get-tuple-element.164.x_ref.right_ref), custom_call_target="tpu_custom_call" | custom-call | flops 3221225472 | bytes 8388608 | tf_op jit(solution)/shard_map/grads/pallas_call | solution.py:314
  300.9 20.1 %collective-permute-done.25 = bf16[320,2048]{1,0:T(8,128)(2,1)} collective-permute-done((bf16[320,2048]{1,0:T(8,128)(2,1)S(1)}, bf16[320,2048]{1,0:T(8,128)(2,1)}, u32[]{:S(2)}, u32[]{:S(2)}) %collective-permute-start.25) | collective-permute-done | bytes 1310752 | tf_op jit(solution)/shard_map/ppermute | solution.py:597
  321.0 2.2 collective-permute-done.26
  323.2 3.5 add_convert_fusion.1
  326.8 2.4 add_convert_fusion.14
  331.8 4.0 collective-permute-start.30
  335.8 6.8 %collective-permute-done.27 = bf16[128,2048]{1,0:T(8,128)(2,1)} collective-permute-done((bf16[128,2048]{1,0:T(8,128)(2,1)S(1)}, bf16[128,2048]{1,0:T(8,128)(2,1)}, u32[]{:S(2)}, u32[]{:S(2)}) %collective-permute-start.27) | collective-permute-done | bytes 524320 | tf_op jit(solution)/shard_map/ppermute | solution.py:597
  343.8 2.8 convert_element_type.282
  346.6 4.7 add_convert_fusion.11
  357.1 2.1 multiply_add_fusion
  359.1 6.3 %collective-permute-done.29.refs_1_ = bf16[320,2048]{1,0:T(8,128)(2,1)} collective-permute-done((bf16[320,2048]{1,0:T(8,128)(2,1)S(1)}, bf16[320,2048]{1,0:T(8,128)(2,1)}, u32[]{:S(2)}, u32[]{:S(2)}) %collective-permute-start.29) | collective-permute-done | bytes 1310752 | tf_op jit(solution)/shard_map/ppermute | solution.py:588
  365.4 24.4 %collective-permute-done.30.refs_3_ = bf16[320,2048]{1,0:T(8,128)(2,1)} collective-permute-done((bf16[320,2048]{1,0:T(8,128)(2,1)S(1)}, bf16[320,2048]{1,0:T(8,128)(2,1)}, u32[]{:S(2)}, u32[]{:S(2)}) %collective-permute-start.30) | collective-permute-done | bytes 1310752 | tf_op jit(solution)/shard_map/ppermute | solution.py:588
  393.7 2.2 add_convert_fusion.9
  396.0 2.0 collective-permute-start.34
  401.8 22.1 %collective-permute-done.36.refs_2_ = bf16[320,2048]{1,0:T(8,128)(2,1)} collective-permute-done((bf16[320,2048]{1,0:T(8,128)(2,1)}, bf16[320,2048]{1,0:T(8,128)(2,1)}, u32[]{:S(2)}, u32[]{:S(2)}) %collective-permute-start.36) | collective-permute-done | bytes 1310752 | tf_op jit(solution)/shard_map/ppermute | solution.py:588
  430.3 7.6 %join_rows.1 = f32[1280,2048]{1,0:T(8,128)} custom-call(s32[8]{0:T(128)} %stack.71.at_ref, bf16[320,2048]{1,0:T(8,128)(2,1)} %copy-done.5, bf16[320,2048]{1,0:T(8,128)(2,1)} %collective-permute-done.29.refs_1_, bf16[320,2048]{1,0:T(8,128)(2,1)} %collective-permute-done.36.refs_2_, bf16[320,2048]{1,0:T(8,128)(2,1)} %collective-permute-done.30.refs_3_), custom_call_target="tpu_custom_call" | custom-call | bytes 15728640 | tf_op jit(solution)/shard_map/join_rows/pallas_call | solution.py:569
  438.0 8.2 %collective-permute-done.34.refs_1_ = bf16[256,2048]{1,0:T(8,128)(2,1)} collective-permute-done((bf16[256,2048]{1,0:T(8,128)(2,1)S(1)}, bf16[256,2048]{1,0:T(8,128)(2,1)}, u32[]{:S(2)}, u32[]{:S(2)}) %collective-permute-start.34) | collective-permute-done | bytes 1048608 | tf_op jit(solution)/shard_map/ppermute | solution.py:588
  446.2 19.8 %collective-permute-done.35.refs_3_ = bf16[256,2048]{1,0:T(8,128)(2,1)} collective-permute-done((bf16[256,2048]{1,0:T(8,128)(2,1)S(1)}, bf16[256,2048]{1,0:T(8,128)(2,1)}, u32[]{:S(2)}, u32[]{:S(2)}) %collective-permute-start.35) | collective-permute-done | bytes 1048608 | tf_op jit(solution)/shard_map/ppermute | solution.py:588
  466.7 2.2 add_convert_fusion.17
  469.6 3.2 collective-permute-start.43
  474.0 3.4 collective-permute-done.45
  477.3 17.0 %collective-permute-done.44.refs_2_ = bf16[256,2048]{1,0:T(8,128)(2,1)S(1)} collective-permute-done((bf16[256,2048]{1,0:T(8,128)(2,1)}, bf16[256,2048]{1,0:T(8,128)(2,1)S(1)}, u32[]{:S(2)}, u32[]{:S(2)}) %collective-permute-start.44) | collective-permute-done | bytes 1048608 | tf_op jit(solution)/shard_map/ppermute | solution.py:588
  494.9 3.9 collective-permute-done.46
  498.9 5.5 spread_columns.2.refs_4_
  504.4 6.7 %collective-permute-done.42.refs_1_ = bf16[256,1536]{1,0:T(8,128)(2,1)} collective-permute-done((bf16[256,1536]{1,0:T(8,128)(2,1)S(1)}, bf16[256,1536]{1,0:T(8,128)(2,1)}, u32[]{:S(2)}, u32[]{:S(2)}) %collective-permute-start.42) | collective-permute-done | bytes 786464 | tf_op jit(solution)/shard_map/ppermute | solution.py:588
  511.2 15.8 %collective-permute-done.43.refs_3_ = bf16[256,1536]{1,0:T(8,128)(2,1)S(1)} collective-permute-done((bf16[256,1536]{1,0:T(8,128)(2,1)S(1)}, bf16[256,1536]{1,0:T(8,128)(2,1)S(1)}, u32[]{:S(2)}, u32[]{:S(2)}) %collective-permute-start.43) | collective-permute-done | bytes 786464 | tf_op jit(solution)/shard_map/ppermute | solution.py:588
  531.5 21.1 %collective-permute-done.49 = f32[20480]{0:T(1024)S(1)} collective-permute-done((f32[20480]{0:T(1024)S(1)}, f32[20480]{0:T(1024)S(1)}, u32[]{:S(2)}, u32[]{:S(2)}) %collective-permute-start.49) | collective-permute-done | bytes 81952 | tf_op jit(solution)/shard_map/ppermute | solution.py:597
  552.7 4.5 spread_columns.3
  (258 shorter events, 81.6 us)
Async XLA Ops:
  7.2 165.5 %all-gather.2.cloned.1.call-start = ((), (), s32[]{:S(2)}) async-start(), calls=%async_computation.3 | async-start | bytes 5242880 | tf_op jit(solution)/shard_map/all_gather | solution.py:866
  10.9 29.4 %collective-permute-start = (bf16[256,2048]{1,0:T(8,128)(2,1)}, bf16[256,2048]{1,0:T(8,128)(2,1)}, u32[]{:S(2)}, u32[]{:S(2)}) collective-permute-start(bf16[256,2048]{1,0:T(8,128)(2,1)} %get-tuple-element.128.refs_0_), channel_id=1, source_target_pairs={{0,8},{8,16},{16,24},{24,0},{1,9},{9,17},{17,25},{25,1},{2,10},{10... | collective-permute-start | bytes 3145736 | tf_op jit(solution)/shard_map/ppermute | solution.py:588
  13.9 47.4 %collective-permute-start.1 = (bf16[256,2048]{1,0:T(8,128)(2,1)}, bf16[256,2048]{1,0:T(8,128)(2,1)}, u32[]{:S(2)}, u32[]{:S(2)}) collective-permute-start(bf16[256,2048]{1,0:T(8,128)(2,1)} %get-tuple-element.128.refs_0_), channel_id=1, source_target_pairs={{0,24},{8,0},{16,8},{24,16},{1,25},{9,1},{17,9},{25,17},{2,26},{10... | collective-permute-start | bytes 3145736 | tf_op jit(solution)/shard_map/ppermute | solution.py:588
  20.3 41.8 %collective-permute-start.3 = (bf16[256,3584]{1,0:T(8,128)(2,1)}, bf16[256,3584]{1,0:T(8,128)(2,1)}, u32[]{:S(2)}, u32[]{:S(2)}) collective-permute-start(bf16[256,3584]{1,0:T(8,128)(2,1)} %pick_columns.1.refs_4_.refs_0_), channel_id=1, source_target_pairs={{0,2},{1,3},{2,0},{3,1},{4,6},{5,7},{6,4},{7,5},{8,10},{9,11},{10,... | collective-permute-start | bytes 5505032 | tf_op jit(solution)/shard_map/ppermute | solution.py:597
  22.0 41.3 %collective-permute-start.4 = (bf16[256,3584]{1,0:T(8,128)(2,1)}, bf16[256,3584]{1,0:T(8,128)(2,1)}, u32[]{:S(2)}, u32[]{:S(2)}) collective-permute-start(bf16[256,3584]{1,0:T(8,128)(2,1)} %pick_columns.1.refs_4_.refs_0_), channel_id=1, source_target_pairs={{0,4},{1,5},{2,6},{3,7},{4,0},{5,1},{6,2},{7,3},{8,12},{9,13},{10,... | collective-permute-start | bytes 5505032 | tf_op jit(solution)/shard_map/ppermute | solution.py:597
  23.5 39.8 %collective-permute-start.5 = (bf16[256,3584]{1,0:T(8,128)(2,1)}, bf16[256,3584]{1,0:T(8,128)(2,1)}, u32[]{:S(2)}, u32[]{:S(2)}) collective-permute-start(bf16[256,3584]{1,0:T(8,128)(2,1)} %pick_columns.1.refs_4_.refs_0_), channel_id=1, source_target_pairs={{0,1},{1,0},{2,3},{3,2},{4,5},{5,4},{6,7},{7,6},{8,9},{9,8},{10,11... | collective-permute-start | bytes 5505032 | tf_op jit(solution)/shard_map/ppermute | solution.py:597
  63.3 27.6 %collective-permute-start.8 = (bf16[256,3584]{1,0:T(8,128)(2,1)}, bf16[256,3584]{1,0:T(8,128)(2,1)S(1)}, u32[]{:S(2)}, u32[]{:S(2)}) collective-permute-start(bf16[256,3584]{1,0:T(8,128)(2,1)} %collective-permute-done.3.refs_5_.refs_1_), channel_id=1, source_target_pairs={{0,1},{1,0},{2,3},{3,2},{4,5},{5,4},{6,7},{7,6},{8,9},{9,8},{10,11... | collective-permute-start | bytes 5505032 | tf_op jit(solution)/shard_map/ppermute | solution.py:597
  63.3 28.5 %collective-permute-start.9 = (bf16[256,3584]{1,0:T(8,128)(2,1)}, bf16[256,3584]{1,0:T(8,128)(2,1)}, u32[]{:S(2)}, u32[]{:S(2)}) collective-permute-start(bf16[256,3584]{1,0:T(8,128)(2,1)} %collective-permute-done.4.refs_6_.refs_2_), channel_id=1, source_target_pairs={{0,1},{1,0},{2,3},{3,2},{4,5},{5,4},{6,7},{7,6},{8,9},{9,8},{10,11... | collective-permute-start | bytes 5505032 | tf_op jit(solution)/shard_map/ppermute | solution.py:597
  63.9 27.1 %collective-permute-start.2 = (bf16[256,2048]{1,0:T(8,128)(2,1)}, bf16[256,2048]{1,0:T(8,128)(2,1)S(1)}, u32[]{:S(2)}, u32[]{:S(2)}) collective-permute-start(bf16[256,2048]{1,0:T(8,128)(2,1)} %collective-permute-done.refs_1_), channel_id=1, source_target_pairs={{0,8},{8,16},{16,24},{24,0},{1,9},{9,17},{17,25},{25,1},{2,10},{10... | collective-permute-start | bytes 3145736 | tf_op jit(solution)/shard_map/ppermute | solution.py:588
  66.3 24.6 %collective-permute-start.6 = (bf16[128,3584]{1,0:T(8,128)(2,1)S(1)}, bf16[128,3584]{1,0:T(8,128)(2,1)S(1)}, u32[]{:S(2)}, u32[]{:S(2)}) collective-permute-start(bf16[128,3584]{1,0:T(8,128)(2,1)S(1)} %slice.575), channel_id=1, source_target_pairs={{0,4},{1,5},{2,6},{3,7},{4,0},{5,1},{6,2},{7,3},{8,12},{9,13},{10,... | collective-permute-start | bytes 2752520 | tf_op jit(solution)/shard_map/ppermute | solution.py:597
  67.9 23.0 %collective-permute-start.7 = (bf16[128,3584]{1,0:T(8,128)(2,1)S(1)}, bf16[128,3584]{1,0:T(8,128)(2,1)S(1)}, u32[]{:S(2)}, u32[]{:S(2)}) collective-permute-start(bf16[128,3584]{1,0:T(8,128)(2,1)S(1)} %slice.576), channel_id=1, source_target_pairs={{0,2},{1,3},{2,0},{3,1},{4,6},{5,7},{6,4},{7,5},{8,10},{9,11},{10,... | collective-permute-start | bytes 2752520 | tf_op jit(solution)/shard_map/ppermute | solution.py:597
  92.5 177.2 %reduce-scatter.3.cloned.1.call-start = ((), (), s32[]{:S(2)}) async-start(), calls=%async_computation.2 | async-start | bytes 5242880 | tf_op jit(solution)/shard_map/reduce_scatter | solution.py:905
  97.1 30.8 %collective-permute-start.12 = (bf16[320,2048]{1,0:T(8,128)(2,1)S(1)}, bf16[320,2048]{1,0:T(8,128)(2,1)S(1)}, u32[]{:S(2)}, u32[]{:S(2)}) collective-permute-start(bf16[320,2048]{1,0:T(8,128)(2,1)S(1)} %maximum_select_fusion.refs_0_), channel_id=1, source_target_pairs={{0,2},{1,3},{2,0},{3,1},{4,6},{5,7},{6,4},{7,5},{8,10},{9,11},{10,... | collective-permute-start | bytes 3932168 | tf_op jit(solution)/shard_map/ppermute | solution.py:597
  97.6 30.5 %collective-permute-start.13 = (bf16[320,2048]{1,0:T(8,128)(2,1)S(1)}, bf16[320,2048]{1,0:T(8,128)(2,1)S(1)}, u32[]{:S(2)}, u32[]{:S(2)}) collective-permute-start(bf16[320,2048]{1,0:T(8,128)(2,1)S(1)} %maximum_select_fusion.refs_0_), channel_id=1, source_target_pairs={{0,4},{1,5},{2,6},{3,7},{4,0},{5,1},{6,2},{7,3},{8,12},{9,13},{10,... | collective-permute-start | bytes 3932168 | tf_op jit(solution)/shard_map/ppermute | solution.py:597
  99.1 29.0 %collective-permute-start.14 = (bf16[320,2048]{1,0:T(8,128)(2,1)S(1)}, bf16[320,2048]{1,0:T(8,128)(2,1)}, u32[]{:S(2)}, u32[]{:S(2)}) collective-permute-start(bf16[320,2048]{1,0:T(8,128)(2,1)S(1)} %maximum_select_fusion.refs_0_), channel_id=1, source_target_pairs={{0,1},{1,0},{2,3},{3,2},{4,5},{5,4},{6,7},{7,6},{8,9},{9,8},{10,11... | collective-permute-start | bytes 3932168 | tf_op jit(solution)/shard_map/ppermute | solution.py:597
  128.1 22.2 %collective-permute-start.17 = (bf16[320,2048]{1,0:T(8,128)(2,1)S(1)}, bf16[320,2048]{1,0:T(8,128)(2,1)S(1)}, u32[]{:S(2)}, u32[]{:S(2)}) collective-permute-start(bf16[320,2048]{1,0:T(8,128)(2,1)S(1)} %collective-permute-done.12.refs_1_), channel_id=1, source_target_pairs={{0,1},{1,0},{2,3},{3,2},{4,5},{5,4},{6,7},{7,6},{8,9},{9,8},{10,11... | collective-permute-start | bytes 3932168 | tf_op jit(solution)/shard_map/ppermute | solution.py:597
  128.2 22.2 %collective-permute-start.18 = (bf16[320,2048]{1,0:T(8,128)(2,1)S(1)}, bf16[320,2048]{1,0:T(8,128)(2,1)S(1)}, u32[]{:S(2)}, u32[]{:S(2)}) collective-permute-start(bf16[320,2048]{1,0:T(8,128)(2,1)S(1)} %collective-permute-done.13.refs_2_), channel_id=1, source_target_pairs={{0,1},{1,0},{2,3},{3,2},{4,5},{5,4},{6,7},{7,6},{8,9},{9,8},{10,11... | collective-permute-start | bytes 3932168 | tf_op jit(solution)/shard_map/ppermute | solution.py:597
  128.8 21.5 %collective-permute-start.15 = (bf16[160,2048]{1,0:T(8,128)(2,1)S(1)}, bf16[160,2048]{1,0:T(8,128)(2,1)S(1)}, u32[]{:S(2)}, u32[]{:S(2)}) collective-permute-start(bf16[160,2048]{1,0:T(8,128)(2,1)S(1)} %slice.577), channel_id=1, source_target_pairs={{0,4},{1,5},{2,6},{3,7},{4,0},{5,1},{6,2},{7,3},{8,12},{9,13},{10,... | collective-permute-start | bytes 1966088 | tf_op jit(solution)/shard_map/ppermute | solution.py:597
  130.4 19.9 %collective-permute-start.16 = (bf16[160,2048]{1,0:T(8,128)(2,1)S(1)}, bf16[160,2048]{1,0:T(8,128)(2,1)}, u32[]{:S(2)}, u32[]{:S(2)}) collective-permute-start(bf16[160,2048]{1,0:T(8,128)(2,1)S(1)} %slice.578), channel_id=1, source_target_pairs={{0,2},{1,3},{2,0},{3,1},{4,6},{5,7},{6,4},{7,5},{8,10},{9,11},{10,... | collective-permute-start | bytes 1966088 | tf_op jit(solution)/shard_map/ppermute | solution.py:597
  172.5 171.3 %reduce-scatter.5.cloned.1.call-start = ((), (), s32[]{:S(2)}) async-start(), calls=%async_computation.4 | async-start | bytes 5242880 | tf_op jit(solution)/shard_map/reduce_scatter | solution.py:905
  235.1 22.5 %collective-permute-start.21 = (bf16[1280,2048]{1,0:T(8,128)(2,1)}, bf16[1280,2048]{1,0:T(8,128)(2,1)}, u32[]{:S(2)}, u32[]{:S(2)}) collective-permute-start(bf16[1280,2048]{1,0:T(8,128)(2,1)} %get-tuple-element.163), channel_id=1, source_target_pairs={{0,1},{1,0},{2,3},{3,2},{4,5},{5,4},{6,7},{7,6},{8,9},{9,8},{10,11... | collective-permute-start | bytes 15728648 | tf_op jit(solution)/shard_map/ppermute | solution.py:597
  268.4 17.1 %collective-permute-start.22 = (bf16[160,2048]{1,0:T(8,128)(2,1)S(1)}, bf16[160,2048]{1,0:T(8,128)(2,1)S(1)}, u32[]{:S(2)}, u32[]{:S(2)}) collective-permute-start(bf16[160,2048]{1,0:T(8,128)(2,1)S(1)} %get-tuple-element.263), channel_id=1, source_target_pairs={{0,4},{1,5},{2,6},{3,7},{4,0},{5,1},{6,2},{7,3},{8,12},{9,13},{10,... | collective-permute-start | bytes 1966088 | tf_op jit(solution)/shard_map/ppermute | solution.py:597
  269.0 16.7 %collective-permute-start.23 = (bf16[160,2048]{1,0:T(8,128)(2,1)S(1)}, bf16[160,2048]{1,0:T(8,128)(2,1)S(1)}, u32[]{:S(2)}, u32[]{:S(2)}) collective-permute-start(bf16[160,2048]{1,0:T(8,128)(2,1)S(1)} %get-tuple-element.262), channel_id=1, source_target_pairs={{0,2},{1,3},{2,0},{3,1},{4,6},{5,7},{6,4},{7,5},{8,10},{9,11},{10,... | collective-permute-start | bytes 1966088 | tf_op jit(solution)/shard_map/ppermute | solution.py:597
  285.7 41.1 %collective-permute-start.24 = (bf16[1024,2048]{1,0:T(8,128)(2,1)}, bf16[1024,2048]{1,0:T(8,128)(2,1)}, u32[]{:S(2)}, u32[]{:S(2)}) collective-permute-start(bf16[1024,2048]{1,0:T(8,128)(2,1)} %grads.6), channel_id=1, source_target_pairs={{0,1},{1,0},{2,3},{3,2},{4,5},{5,4},{6,7},{7,6},{8,9},{9,8},{10,11... | collective-permute-start | bytes 12582920 | tf_op jit(solution)/shard_map/ppermute | solution.py:597
  289.6 31.4 %collective-permute-start.25 = (bf16[320,2048]{1,0:T(8,128)(2,1)S(1)}, bf16[320,2048]{1,0:T(8,128)(2,1)}, u32[]{:S(2)}, u32[]{:S(2)}) collective-permute-start(bf16[320,2048]{1,0:T(8,128)(2,1)S(1)} %pad_maximum_fusion), channel_id=1, source_target_pairs={{0,2},{1,3},{2,0},{3,1},{4,6},{5,7},{6,4},{7,5},{8,10},{9,11},{10,... | collective-permute-start | bytes 3932168 | tf_op jit(solution)/shard_map/ppermute | solution.py:597
  292.0 31.2 %collective-permute-start.26 = (bf16[320,2048]{1,0:T(8,128)(2,1)}, bf16[320,2048]{1,0:T(8,128)(2,1)}, u32[]{:S(2)}, u32[]{:S(2)}) collective-permute-start(bf16[320,2048]{1,0:T(8,128)(2,1)} %pad_maximum_fusion.1), channel_id=1, source_target_pairs={{0,4},{1,5},{2,6},{3,7},{4,0},{5,1},{6,2},{7,3},{8,12},{9,13},{10,... | collective-permute-start | bytes 3932168 | tf_op jit(solution)/shard_map/ppermute | solution.py:597
  329.2 13.4 %collective-permute-start.27 = (bf16[128,2048]{1,0:T(8,128)(2,1)S(1)}, bf16[128,2048]{1,0:T(8,128)(2,1)}, u32[]{:S(2)}, u32[]{:S(2)}) collective-permute-start(bf16[128,2048]{1,0:T(8,128)(2,1)S(1)} %get-tuple-element.269), channel_id=1, source_target_pairs={{0,4},{1,5},{2,6},{3,7},{4,0},{5,1},{6,2},{7,3},{8,12},{9,13},{10,... | collective-permute-start | bytes 1572872 | tf_op jit(solution)/shard_map/ppermute | solution.py:597
  330.7 13.0 %collective-permute-start.28 = (bf16[128,2048]{1,0:T(8,128)(2,1)S(1)}, bf16[128,2048]{1,0:T(8,128)(2,1)}, u32[]{:S(2)}, u32[]{:S(2)}) collective-permute-start(bf16[128,2048]{1,0:T(8,128)(2,1)S(1)} %get-tuple-element.268), channel_id=1, source_target_pairs={{0,2},{1,3},{2,0},{3,1},{4,6},{5,7},{6,4},{7,5},{8,10},{9,11},{10,... | collective-permute-start | bytes 1572872 | tf_op jit(solution)/shard_map/ppermute | solution.py:597
  331.7 33.7 %collective-permute-start.29 = (bf16[320,2048]{1,0:T(8,128)(2,1)S(1)}, bf16[320,2048]{1,0:T(8,128)(2,1)}, u32[]{:S(2)}, u32[]{:S(2)}) collective-permute-start(bf16[320,2048]{1,0:T(8,128)(2,1)S(1)} %pad_maximum_fusion.2.refs_0_), channel_id=1, source_target_pairs={{0,8},{8,16},{16,24},{24,0},{1,9},{9,17},{17,25},{25,1},{2,10},{10... | collective-permute-start | bytes 3932168 | tf_op jit(solution)/shard_map/ppermute | solution.py:588
  331.8 58.0 %collective-permute-start.30 = (bf16[320,2048]{1,0:T(8,128)(2,1)S(1)}, bf16[320,2048]{1,0:T(8,128)(2,1)}, u32[]{:S(2)}, u32[]{:S(2)}) collective-permute-start(bf16[320,2048]{1,0:T(8,128)(2,1)S(1)} %pad_maximum_fusion.2.refs_0_), channel_id=1, source_target_pairs={{0,24},{8,0},{16,8},{24,16},{1,25},{9,1},{17,9},{25,17},{2,26},{10... | collective-permute-start | bytes 3932168 | tf_op jit(solution)/shard_map/ppermute | solution.py:588
  335.8 54.0 %collective-permute-start.33 = (bf16[1024,1536]{1,0:T(8,128)(2,1)}, bf16[1024,1536]{1,0:T(8,128)(2,1)}, u32[]{:S(2)}, u32[]{:S(2)}) collective-permute-start(bf16[1024,1536]{1,0:T(8,128)(2,1)} %grads.8), channel_id=1, source_target_pairs={{0,1},{1,0},{2,3},{3,2},{4,5},{5,4},{6,7},{7,6},{8,9},{9,8},{10,11... | collective-permute-start | bytes 9437192 | tf_op jit(solution)/shard_map/ppermute | solution.py:597
  352.9 36.9 %collective-permute-start.31 = (bf16[256,2048]{1,0:T(8,128)(2,1)S(1)}, bf16[256,2048]{1,0:T(8,128)(2,1)S(1)}, u32[]{:S(2)}, u32[]{:S(2)}) collective-permute-start(bf16[256,2048]{1,0:T(8,128)(2,1)S(1)} %pad_maximum_fusion.3), channel_id=1, source_target_pairs={{0,2},{1,3},{2,0},{3,1},{4,6},{5,7},{6,4},{7,5},{8,10},{9,11},{10,... | collective-permute-start | bytes 3145736 | tf_op jit(solution)/shard_map/ppermute | solution.py:597
  354.0 35.8 %collective-permute-start.32 = (bf16[256,2048]{1,0:T(8,128)(2,1)S(1)}, bf16[256,2048]{1,0:T(8,128)(2,1)S(1)}, u32[]{:S(2)}, u32[]{:S(2)}) collective-permute-start(bf16[256,2048]{1,0:T(8,128)(2,1)S(1)} %pad_maximum_fusion.4), channel_id=1, source_target_pairs={{0,4},{1,5},{2,6},{3,7},{4,0},{5,1},{6,2},{7,3},{8,12},{9,13},{10,... | collective-permute-start | bytes 3145736 | tf_op jit(solution)/shard_map/ppermute | solution.py:597
  389.8 34.0 %collective-permute-start.36 = (bf16[320,2048]{1,0:T(8,128)(2,1)}, bf16[320,2048]{1,0:T(8,128)(2,1)}, u32[]{:S(2)}, u32[]{:S(2)}) collective-permute-start(bf16[320,2048]{1,0:T(8,128)(2,1)} %collective-permute-done.29.refs_1_), channel_id=1, source_target_pairs={{0,8},{8,16},{16,24},{24,0},{1,9},{9,17},{17,25},{25,1},{2,10},{10... | collective-permute-start | bytes 3932168 | tf_op jit(solution)/shard_map/ppermute | solution.py:588
  391.3 9.5 %collective-permute-start.37 = (bf16[128,1536]{1,0:T(8,128)(2,1)S(1)}, bf16[128,1536]{1,0:T(8,128)(2,1)S(1)}, u32[]{:S(2)}, u32[]{:S(2)}) collective-permute-start(bf16[128,1536]{1,0:T(8,128)(2,1)S(1)} %get-tuple-element.277), channel_id=1, source_target_pairs={{0,4},{1,5},{2,6},{3,7},{4,0},{5,1},{6,2},{7,3},{8,12},{9,13},{10,... | collective-permute-start | bytes 1179656 | tf_op jit(solution)/shard_map/ppermute | solution.py:597
  392.7 9.1 %collective-permute-start.38 = (bf16[128,1536]{1,0:T(8,128)(2,1)S(1)}, bf16[128,1536]{1,0:T(8,128)(2,1)S(1)}, u32[]{:S(2)}, u32[]{:S(2)}) collective-permute-start(bf16[128,1536]{1,0:T(8,128)(2,1)S(1)} %get-tuple-element.276), channel_id=1, source_target_pairs={{0,2},{1,3},{2,0},{3,1},{4,6},{5,7},{6,4},{7,5},{8,10},{9,11},{10,... | collective-permute-start | bytes 1179656 | tf_op jit(solution)/shard_map/ppermute | solution.py:597
  396.0 50.2 %collective-permute-start.34 = (bf16[256,2048]{1,0:T(8,128)(2,1)S(1)}, bf16[256,2048]{1,0:T(8,128)(2,1)}, u32[]{:S(2)}, u32[]{:S(2)}) collective-permute-start(bf16[256,2048]{1,0:T(8,128)(2,1)S(1)} %pad_maximum_fusion.5.refs_0_), channel_id=1, source_target_pairs={{0,8},{8,16},{16,24},{24,0},{1,9},{9,17},{17,25},{25,1},{2,10},{10... | collective-permute-start | bytes 3145736 | tf_op jit(solution)/shard_map/ppermute | solution.py:588
  398.1 68.0 %collective-permute-start.35 = (bf16[256,2048]{1,0:T(8,128)(2,1)S(1)}, bf16[256,2048]{1,0:T(8,128)(2,1)}, u32[]{:S(2)}, u32[]{:S(2)}) collective-permute-start(bf16[256,2048]{1,0:T(8,128)(2,1)S(1)} %pad_maximum_fusion.5.refs_0_), channel_id=1, source_target_pairs={{0,24},{8,0},{16,8},{24,16},{1,25},{9,1},{17,9},{25,17},{2,26},{10... | collective-permute-start | bytes 3145736 | tf_op jit(solution)/shard_map/ppermute | solution.py:588
  426.6 39.4 %collective-permute-start.39 = (bf16[256,1536]{1,0:T(8,128)(2,1)}, bf16[256,1536]{1,0:T(8,128)(2,1)}, u32[]{:S(2)}, u32[]{:S(2)}) collective-permute-start(bf16[256,1536]{1,0:T(8,128)(2,1)} %pad_maximum_fusion.6), channel_id=1, source_target_pairs={{0,2},{1,3},{2,0},{3,1},{4,6},{5,7},{6,4},{7,5},{8,10},{9,11},{10,... | collective-permute-start | bytes 2359304 | tf_op jit(solution)/shard_map/ppermute | solution.py:597
  428.7 37.4 %collective-permute-start.40 = (bf16[256,1536]{1,0:T(8,128)(2,1)}, bf16[256,1536]{1,0:T(8,128)(2,1)}, u32[]{:S(2)}, u32[]{:S(2)}) collective-permute-start(bf16[256,1536]{1,0:T(8,128)(2,1)} %pad_maximum_fusion.7), channel_id=1, source_target_pairs={{0,4},{1,5},{2,6},{3,7},{4,0},{5,1},{6,2},{7,3},{8,12},{9,13},{10,... | collective-permute-start | bytes 2359304 | tf_op jit(solution)/shard_map/ppermute | solution.py:597
  429.6 36.4 %collective-permute-start.41 = (f32[20480]{0:T(1024)S(1)}, f32[20480]{0:T(1024)S(1)}, u32[]{:S(2)}, u32[]{:S(2)}) collective-permute-start(f32[20480]{0:T(1024)S(1)} %concatenate.101), channel_id=1, source_target_pairs={{0,1},{1,0},{2,3},{3,2},{4,5},{5,4},{6,7},{7,6},{8,9},{9,8},{10,11... | collective-permute-start | bytes 245768 | tf_op jit(solution)/shard_map/ppermute | solution.py:597
  466.0 28.3 %collective-permute-start.44 = (bf16[256,2048]{1,0:T(8,128)(2,1)}, bf16[256,2048]{1,0:T(8,128)(2,1)S(1)}, u32[]{:S(2)}, u32[]{:S(2)}) collective-permute-start(bf16[256,2048]{1,0:T(8,128)(2,1)} %collective-permute-done.34.refs_1_), channel_id=1, source_target_pairs={{0,8},{8,16},{16,24},{24,0},{1,9},{9,17},{17,25},{25,1},{2,10},{10... | collective-permute-start | bytes 3145736 | tf_op jit(solution)/shard_map/ppermute | solution.py:588
  468.9 42.2 %collective-permute-start.42 = (bf16[256,1536]{1,0:T(8,128)(2,1)S(1)}, bf16[256,1536]{1,0:T(8,128)(2,1)}, u32[]{:S(2)}, u32[]{:S(2)}) collective-permute-start(bf16[256,1536]{1,0:T(8,128)(2,1)S(1)} %pad_maximum_fusion.8.refs_0_), channel_id=1, source_target_pairs={{0,8},{8,16},{16,24},{24,0},{1,9},{9,17},{17,25},{25,1},{2,10},{10... | collective-permute-start | bytes 2359304 | tf_op jit(solution)/shard_map/ppermute | solution.py:588
  469.6 57.3 %collective-permute-start.43 = (bf16[256,1536]{1,0:T(8,128)(2,1)S(1)}, bf16[256,1536]{1,0:T(8,128)(2,1)S(1)}, u32[]{:S(2)}, u32[]{:S(2)}) collective-permute-start(bf16[256,1536]{1,0:T(8,128)(2,1)S(1)} %pad_maximum_fusion.8.refs_0_), channel_id=1, source_target_pairs={{0,24},{8,0},{16,8},{24,16},{1,25},{9,1},{17,9},{25,17},{2,26},{10... | collective-permute-start | bytes 2359304 | tf_op jit(solution)/shard_map/ppermute | solution.py:588
  472.8 4.5 collective-permute-start.45
  498.9 29.7 %collective-permute-start.47 = (f32[20480]{0:T(1024)S(1)}, f32[20480]{0:T(1024)S(1)}, u32[]{:S(2)}, u32[]{:S(2)}) collective-permute-start(f32[20480]{0:T(1024)S(1)} %add.384), channel_id=1, source_target_pairs={{0,8},{8,0},{16,24},{24,16},{1,9},{9,1},{17,25},{25,17},{2,10},{10... | collective-permute-start | bytes 245768 | tf_op jit(solution)/shard_map/ppermute | solution.py:597
  528.6 24.0 %collective-permute-start.48 = (bf16[256,1536]{1,0:T(8,128)(2,1)}, bf16[256,1536]{1,0:T(8,128)(2,1)}, u32[]{:S(2)}, u32[]{:S(2)}) collective-permute-start(bf16[256,1536]{1,0:T(8,128)(2,1)} %collective-permute-done.42.refs_1_), channel_id=1, source_target_pairs={{0,8},{8,16},{16,24},{24,0},{1,9},{9,17},{17,25},{25,1},{2,10},{10... | collective-permute-start | bytes 2359304 | tf_op jit(solution)/shard_map/ppermute | solution.py:588
  528.6 24.0 %collective-permute-start.49 = (f32[20480]{0:T(1024)S(1)}, f32[20480]{0:T(1024)S(1)}, u32[]{:S(2)}, u32[]{:S(2)}) collective-permute-start(f32[20480]{0:T(1024)S(1)} %add.385), channel_id=1, source_target_pairs={{0,16},{8,24},{16,0},{24,8},{1,17},{9,25},{17,1},{25,9},{2,18},{10... | collective-permute-start | bytes 245768 | tf_op jit(solution)/shard_map/ppermute | solution.py:597
  (44 other events, 395.0 us)
Sparse Core Ops, SparseCore 0:
  92.6 78.4 all-gather.1
  173.4 75.2 reduce-scatter.2
  257.7 74.2 reduce-scatter.4
